TPU v7x, 32 devices: a whole 2x2x4 slice. The times are simulated.
32 devices in a mesh: frame: 16 (over z, x, core), mod: 2 (over y).
Axes of the slice: x: 2, y: 2, z: 4, core: 2. Of those that a mesh axis runs over, the one named last changes fastest.
Arguments:
- frames: bfloat16 [2048, 8192], P('frame', 'mod'), may hold values from 0.2 to 64, as said below
- cycle_label: int32 [8192], P('mod'), may hold values from 0 to 15, as said below
- good_pixel: int32 [8192], P('mod'), may hold values from 0 to 1
Outputs:
- correlation: float32 [16, 2048, 1024], P('mod', 'frame')
Inputs may be any that keep to these rules, and one draw needn't show every extreme that they name: `cycle_label`: on every block of 4096 consecutive pixels each of the 16 cycles holds exactly 256 pixels, at least one of them with good_pixel 1. `frames`: positive intensities.
All inputs are finite; a program needn't handle non-finite values.
Results may differ from a plain program's by a relative error of at most 0.0003.
Values may be sent and summed in bfloat16 or wider, within the bound.
No kernel may reach another device: no remote copies, remote signals or barrier semaphores. Data moves between devices by JAX's collectives and lax.ppermute only.
A program may use at most 64 MiB of HBM per device.

v0:
```python
import jax
import jax.numpy as jnp
from jax import lax
from jax.sharding import PartitionSpec as P

CYCLES = 16
LAG = 1024


def passed_along(value, axis, steps):
    count = lax.axis_size(axis)
    first, last = (max(0, -steps), min(count, count - steps))
    return lax.ppermute(value, axis, [(source, source + steps) for source in range(first, last)])


def frame_window(frame_block):
    distance_count = LAG // frame_block.shape[0]
    pieces = [frame_block]
    moving = frame_block
    for distance in range(distance_count):
        moving = passed_along(moving, "frame", -1)
        pieces.append(moving)
    return jnp.concatenate(pieces, axis=0)


def correlate(gram_tile, window_sums, cycle_counts):
    block_rows = gram_tile.shape[1]
    window_width = gram_tile.shape[2]
    frame_at = lax.axis_index("frame") * block_rows + jnp.arange(window_width, dtype=jnp.int32)
    in_range = frame_at < block_rows * lax.axis_size("frame")
    earlier = window_sums[:, :block_rows]
    safe_sums = jnp.where(in_range[None, :], window_sums, 1.0)
    normalized = (
        gram_tile * cycle_counts[:, None, None] / (earlier[:, :, None] * safe_sums[:, None, :])
    )
    normalized = jnp.where(in_range[None, None, :], normalized, 0.0)
    cycle_number = normalized.shape[0]
    flattened = jnp.pad(
        normalized.reshape(cycle_number, block_rows * window_width), ((0, 0), (0, block_rows))
    )
    return flattened.reshape(cycle_number, block_rows, window_width + 1)[:, :, :LAG]


def shards(frames, cycle_label, good_pixel):
    mod_count = lax.axis_size("mod")
    cycle_dev = CYCLES // mod_count
    first_cycle = lax.axis_index("mod") * cycle_dev
    block_rows = frames.shape[0]
    pix_count = frames.shape[1]
    per_cycle = pix_count // CYCLES
    ordering = jnp.argsort(cycle_label, stable=True)
    sorted_frames = jnp.take(frames, ordering, axis=1)
    sorted_good = jnp.take(good_pixel, ordering, axis=0).astype(jnp.bfloat16)
    window = frame_window(sorted_frames)
    window_width = window.shape[0]
    block_three = sorted_frames.reshape(block_rows, CYCLES, per_cycle)
    good_two = sorted_good.reshape(CYCLES, per_cycle)
    window_three = window.reshape(window_width, CYCLES, per_cycle)
    weighted = block_three * good_two[None]
    gram_tile = lax.psum_scatter(
        jnp.einsum("frc,grc->rfg", weighted, window_three, preferred_element_type=jnp.float32),
        "mod",
        scatter_dimension=0,
        tiled=True,
    )
    partial_sums = jnp.einsum(
        "grc,rc->gr", window_three, good_two, preferred_element_type=jnp.float32
    )
    partial_counts = jnp.sum(good_two.astype(jnp.float32), axis=1)
    all_sums, all_counts = lax.psum((partial_sums, partial_counts), "mod")
    window_sums = lax.dynamic_slice_in_dim(all_sums, first_cycle, cycle_dev, 1).T
    cycle_counts = lax.dynamic_slice_in_dim(all_counts, first_cycle, cycle_dev, 0)
    return correlate(gram_tile, window_sums, cycle_counts)


def solution(mesh):
    placed = (P("frame", "mod"), P("mod"), P("mod"))
    return jax.shard_map(
        shards, mesh=mesh, in_specs=placed, out_specs=P("mod", "frame", None), check_vma=False
    )
```

profile of v0, /device:TPU:0, one launch (start us, length us, event | category | flops | bytes accessed | tf_op | source)
XLA Modules:
  0.0 349.2 jit_solution(4954578220545902130)
XLA Ops:
  6.5 0.0 copy-start
  6.5 0.0 all-reduce.3.cloned.1.call-start
  6.5 6.5 %sort.17 = (s32[4096]{0:T(1024)}, s32[4096]{0:T(1024)S(1)}) sort(s32[4096]{0:T(1024)} %param.4, s32[4096]{0:T(1024)S(1)} %iota.12), dimensions={0}, to_apply=%region_0.0 | sort | flops 49152 | bytes 65536 | tf_op jit(solution)/shard_map/jit(argsort)/sort | solution.py:51
  13.1 1.6 copy.6
  14.7 12.1 %gather_fusion = bf16[4096,128]{1,0:T(8,128)(2,1)S(1)} fusion(bf16[128,4096]{0,1:T(8,128)(2,1)S(1)} %copy.6, s32[4096]{0:T(1024)S(1)} %fusion.8), kind=kCustom, calls=%fused_computation | custom fusion | bytes 2113536 | tf_op jit(solution)/shard_map/jit(_take)/gather | solution.py:52
  26.8 3.0 constant_dynamic-update-slice_fusion.8
  29.8 1.3 collective-permute-start
  31.1 3.3 collective-permute-done
  34.3 0.0 copy-start.1
  34.3 1.3 collective-permute-start.1
  35.6 15.6 %collective-permute-done.1 = bf16[128,4096]{0,1:T(8,128)(2,1)S(1)} collective-permute-done((bf16[128,4096]{0,1:T(8,128)(2,1)S(1)}, bf16[128,4096]{0,1:T(8,128)(2,1)S(1)}, u32[]{:S(2)}, u32[]{:S(2)}) %collective-permute-start.1) | collective-permute-done | bytes 1048608 | tf_op jit(solution)/shard_map/ppermute | solution.py:13
  51.3 1.3 collective-permute-start.2
  52.6 14.8 %collective-permute-done.2 = bf16[128,4096]{0,1:T(8,128)(2,1)S(1)} collective-permute-done((bf16[128,4096]{0,1:T(8,128)(2,1)S(1)}, bf16[128,4096]{0,1:T(8,128)(2,1)S(1)}, u32[]{:S(2)}, u32[]{:S(2)}) %collective-permute-start.2) | collective-permute-done | bytes 1048608 | tf_op jit(solution)/shard_map/ppermute | solution.py:13
  67.4 0.0 copy-done.1
  67.4 0.0 copy-start.2
  67.4 1.3 collective-permute-start.3
  68.7 0.0 copy-done.2
  68.7 14.8 %collective-permute-done.3 = bf16[128,4096]{0,1:T(8,128)(2,1)S(1)} collective-permute-done((bf16[128,4096]{0,1:T(8,128)(2,1)S(1)}, bf16[128,4096]{0,1:T(8,128)(2,1)S(1)}, u32[]{:S(2)}, u32[]{:S(2)}) %collective-permute-start.3) | collective-permute-done | bytes 1048608 | tf_op jit(solution)/shard_map/ppermute | solution.py:13
  83.5 0.0 copy-start.3
  83.5 1.0 copy-done.3
  84.5 1.3 collective-permute-start.4
  85.8 15.0 %collective-permute-done.4 = bf16[128,4096]{0,1:T(8,128)(2,1)} collective-permute-done((bf16[128,4096]{0,1:T(8,128)(2,1)S(1)}, bf16[128,4096]{0,1:T(8,128)(2,1)}, u32[]{:S(2)}, u32[]{:S(2)}) %collective-permute-start.4) | collective-permute-done | bytes 1048608 | tf_op jit(solution)/shard_map/ppermute | solution.py:13
  100.7 1.3 collective-permute-start.5
  102.0 0.0 copy-done
  102.0 23.0 %gather_fusion.1 = s32[4096]{0:T(1024)S(1)} fusion(s32[4096]{0:T(1024)S(1)} %copy-done, s32[4096]{0:T(1024)S(1)} %fusion.8), kind=kCustom, calls=%fused_computation.1 | custom fusion | bytes 49152 | tf_op jit(solution)/shard_map/jit(_take)/gather | solution.py:53
  125.1 0.5 copy.7
  125.6 0.1 convert_reduce_fusion
  125.7 2.3 constant_dynamic-update-slice_fusion.7
  128.1 0.0 collective-permute-done.5
  128.1 1.3 collective-permute-start.6
  129.4 1.1 constant_dynamic-update-slice_fusion.6
  130.5 2.3 constant_dynamic-update-slice_fusion.5
  132.8 2.4 constant_dynamic-update-slice_fusion.4
  135.2 9.8 %collective-permute-done.6 = bf16[128,4096]{0,1:T(8,128)(2,1)S(1)} collective-permute-done((bf16[128,4096]{0,1:T(8,128)(2,1)}, bf16[128,4096]{0,1:T(8,128)(2,1)S(1)}, u32[]{:S(2)}, u32[]{:S(2)}) %collective-permute-start.6) | collective-permute-done | bytes 1048608 | tf_op jit(solution)/shard_map/ppermute | solution.py:13
  145.0 1.3 collective-permute-start.7
  146.3 2.4 constant_dynamic-update-slice_fusion.3
  148.7 2.4 constant_dynamic-update-slice_fusion.2
  151.1 1.1 constant_dynamic-update-slice_fusion.1
  152.2 8.9 %collective-permute-done.7 = bf16[128,4096]{0,1:T(8,128)(2,1)S(1)} collective-permute-done((bf16[128,4096]{0,1:T(8,128)(2,1)S(1)}, bf16[128,4096]{0,1:T(8,128)(2,1)S(1)}, u32[]{:S(2)}, u32[]{:S(2)}) %collective-permute-start.7) | collective-permute-done | bytes 1048608 | tf_op jit(solution)/shard_map/ppermute | solution.py:13
  161.1 1.1 constant_dynamic-update-slice_fusion
  162.2 5.0 %fusion.6 = f32[16,1,1152]{2,1,0:T(1,128)S(1)} fusion(bf16[1152,16,256]{0,2,1:T(8,128)(2,1)} %bitcast.20, bf16[16,256,1]{1,0,2:T(8,128)(2,1)S(1)} %bitcast.24), kind=kOutput, calls=%fused_computation.23 | convolution fusion | flops 9437184 | bytes 9519104 | tf_op jit(solution)/shard_map/grc,rc->gr/dot_general | solution.py:66
  167.2 0.6 copy.16
  167.9 0.0 all-reduce.3.cloned.1.call-update
  167.9 0.0 reduce-scatter.2.cloned.1.call-start
  167.9 8.9 %fusion = f32[16,128,1152]{2,1,0:T(8,128)} fusion(bf16[1152,16,256]{0,2,1:T(8,128)(2,1)} %bitcast.21, bf16[128,16,256]{2,0,1:T(8,128)(2,1)S(1)} %copy.7, pred[16,256]{1,0:T(8,128)(4,1)S(1)} %broadcast_in_dim.54, bf16[16,256]{1,0:T(8,128)(2,1)S(1)} %get-tuple-element.8), kind=kOutput, calls=%fused_computation.4 | convolution fusion | flops 1209008128 | bytes 19935232 | tf_op jit(solution)/shard_map/frc,grc->rfg/dot_general | solution.py:61
  176.8 0.0 reduce-scatter.2.cloned.1.call-update
  176.9 5.1 %psum.14 = f32[16]{0:T(128)S(1)} all-reduce(f32[16]{0:T(128)S(1)} %get-tuple-element.7), channel_id=1, replica_groups=mesh['frame'=16,'mod'=2] {'mod'}, use_global_device_ids=true, to_apply=%region_3.4 | all-reduce | flops 16 | bytes 128 | tf_op jit(solution)/shard_map/psum | solution.py:70
  182.0 0.1 dynamic_slice.6
  182.1 24.8 %all-reduce.3.cloned.1.call-done = f32[1152,16]{0,1:T(8,128)} async-done(((f32[1152,16]{0,1:T(8,128)}), f32[1152,16]{0,1:T(8,128)}) %all-reduce.3.cloned.1.call-update) | async-done | bytes 73744 | tf_op jit(solution)/shard_map/psum | solution.py:70
  206.9 0.8 broadcast_select_fusion
  207.7 112.3 %reduce-scatter.2.cloned.1.call-done = f32[8,128,1152]{2,1,0:T(8,128)} async-done(((f32[16,128,1152]{2,1,0:T(8,128)}), f32[8,128,1152]{2,1,0:T(8,128)}) %reduce-scatter.2.cloned.1.call-update) | async-done | bytes 4718608 | tf_op jit(solution)/shard_map/reduce_scatter | solution.py:60
  320.0 3.2 select_bitcast_fusion
  323.2 2.7 copy.12
  325.9 2.4 pad.4
  328.3 9.3 %reshape.52 = f32[8,128,1153]{2,1,0:T(8,128)} reshape(f32[8,147584]{1,0:T(8,128)} %pad.4) | data formatting | bytes 9445376 | tf_op jit(solution)/shard_map/reshape | solution.py:41
  337.5 4.8 %slice.13 = f32[8,128,1024]{2,1,0:T(8,128)} slice(f32[8,128,1153]{2,1,0:T(8,128)} %reshape.52), slice={[0:8], [0:128], [0:1024]} | slice | bytes 8388608 | tf_op jit(solution)/shard_map/slice | solution.py:41
  (7 shorter events, 0.0 us)
Async XLA Ops:
  6.5 95.5 %copy-start = (s32[4096]{0:T(1024)S(1)}, s32[4096]{0:T(1024)}, u32[]{:S(2)}) copy-start(s32[4096]{0:T(1024)} %param.5) | copy-start | bytes 49156
  6.5 200.4 %all-reduce.3.cloned.1.call-start = ((), (), s32[]{:S(2)}) async-start(), calls=%async_computation.2 | async-start | bytes 147456 | tf_op jit(solution)/shard_map/psum | solution.py:70
  29.8 4.5 %collective-permute-start = (bf16[128,4096]{0,1:T(8,128)(2,1)S(1)}, bf16[128,4096]{0,1:T(8,128)(2,1)S(1)}, u32[]{:S(2)}, u32[]{:S(2)}) collective-permute-start(bf16[128,4096]{0,1:T(8,128)(2,1)S(1)} %get-tuple-element.12), channel_id=1, source_target_pairs={{2,0},{4,2},{6,4},{8,6},{10,8},{12,10},{14,12},{16,14},{18,16},{20... | collective-permute-start | bytes 3145736 | tf_op jit(solution)/shard_map/ppermute | solution.py:13
  34.3 33.0 %copy-start.1 = (bf16[128,4096]{0,1:T(8,128)(2,1)}, bf16[128,4096]{0,1:T(8,128)(2,1)S(1)}, u32[]{:S(2)}) copy-start(bf16[128,4096]{0,1:T(8,128)(2,1)S(1)} %collective-permute-done) | copy-start | bytes 3145732
  34.3 16.9 %collective-permute-start.1 = (bf16[128,4096]{0,1:T(8,128)(2,1)S(1)}, bf16[128,4096]{0,1:T(8,128)(2,1)S(1)}, u32[]{:S(2)}, u32[]{:S(2)}) collective-permute-start(bf16[128,4096]{0,1:T(8,128)(2,1)S(1)} %collective-permute-done), channel_id=1, source_target_pairs={{2,0},{4,2},{6,4},{8,6},{10,8},{12,10},{14,12},{16,14},{18,16},{20... | collective-permute-start | bytes 3145736 | tf_op jit(solution)/shard_map/ppermute | solution.py:13
  51.3 16.1 %collective-permute-start.2 = (bf16[128,4096]{0,1:T(8,128)(2,1)S(1)}, bf16[128,4096]{0,1:T(8,128)(2,1)S(1)}, u32[]{:S(2)}, u32[]{:S(2)}) collective-permute-start(bf16[128,4096]{0,1:T(8,128)(2,1)S(1)} %collective-permute-done.1), channel_id=1, source_target_pairs={{2,0},{4,2},{6,4},{8,6},{10,8},{12,10},{14,12},{16,14},{18,16},{20... | collective-permute-start | bytes 3145736 | tf_op jit(solution)/shard_map/ppermute | solution.py:13
  67.4 1.3 copy-start.2
  67.4 16.1 %collective-permute-start.3 = (bf16[128,4096]{0,1:T(8,128)(2,1)S(1)}, bf16[128,4096]{0,1:T(8,128)(2,1)S(1)}, u32[]{:S(2)}, u32[]{:S(2)}) collective-permute-start(bf16[128,4096]{0,1:T(8,128)(2,1)S(1)} %collective-permute-done.2), channel_id=1, source_target_pairs={{2,0},{4,2},{6,4},{8,6},{10,8},{12,10},{14,12},{16,14},{18,16},{20... | collective-permute-start | bytes 3145736 | tf_op jit(solution)/shard_map/ppermute | solution.py:13
  83.5 1.0 copy-start.3
  84.5 16.2 %collective-permute-start.4 = (bf16[128,4096]{0,1:T(8,128)(2,1)S(1)}, bf16[128,4096]{0,1:T(8,128)(2,1)}, u32[]{:S(2)}, u32[]{:S(2)}) collective-permute-start(bf16[128,4096]{0,1:T(8,128)(2,1)S(1)} %collective-permute-done.3), channel_id=1, source_target_pairs={{2,0},{4,2},{6,4},{8,6},{10,8},{12,10},{14,12},{16,14},{18,16},{20... | collective-permute-start | bytes 3145736 | tf_op jit(solution)/shard_map/ppermute | solution.py:13
  100.7 27.4 %collective-permute-start.5 = (bf16[128,4096]{0,1:T(8,128)(2,1)}, bf16[128,4096]{0,1:T(8,128)(2,1)}, u32[]{:S(2)}, u32[]{:S(2)}) collective-permute-start(bf16[128,4096]{0,1:T(8,128)(2,1)} %collective-permute-done.4), channel_id=1, source_target_pairs={{2,0},{4,2},{6,4},{8,6},{10,8},{12,10},{14,12},{16,14},{18,16},{20... | collective-permute-start | bytes 3145736 | tf_op jit(solution)/shard_map/ppermute | solution.py:13
  128.1 16.9 %collective-permute-start.6 = (bf16[128,4096]{0,1:T(8,128)(2,1)}, bf16[128,4096]{0,1:T(8,128)(2,1)S(1)}, u32[]{:S(2)}, u32[]{:S(2)}) collective-permute-start(bf16[128,4096]{0,1:T(8,128)(2,1)} %collective-permute-done.5), channel_id=1, source_target_pairs={{2,0},{4,2},{6,4},{8,6},{10,8},{12,10},{14,12},{16,14},{18,16},{20... | collective-permute-start | bytes 3145736 | tf_op jit(solution)/shard_map/ppermute | solution.py:13
  145.0 16.1 %collective-permute-start.7 = (bf16[128,4096]{0,1:T(8,128)(2,1)S(1)}, bf16[128,4096]{0,1:T(8,128)(2,1)S(1)}, u32[]{:S(2)}, u32[]{:S(2)}) collective-permute-start(bf16[128,4096]{0,1:T(8,128)(2,1)S(1)} %collective-permute-done.6), channel_id=1, source_target_pairs={{2,0},{4,2},{6,4},{8,6},{10,8},{12,10},{14,12},{16,14},{18,16},{20... | collective-permute-start | bytes 3145736 | tf_op jit(solution)/shard_map/ppermute | solution.py:13
  167.9 152.1 %reduce-scatter.2.cloned.1.call-start = ((), (), s32[]{:S(2)}) async-start(), calls=%async_computation.1 | async-start | bytes 14155776 | tf_op jit(solution)/shard_map/reduce_scatter | solution.py:60
Sparse Core Ops, SparseCore 0:
  168.0 38.8 all-reduce.2
  209.2 110.7 reduce-scatter.1
where the time goes:
time: 350 us; the launch traced here: 349 us
  waiting for transfers between devices  219 us (63%)
  local copies, waits for them, and re-layouts  73.3 us (21%)
  matrix products  13.9 us (4%)
  between operations  13.6 us (4%)
  other arithmetic  13.5 us (4%)
  starting transfers between devices  10.3 us (3%)
  blocking collectives  5.12 us (1%)
    reduce_scatter x1, waiting for transfers between devices, shards(): lax.psum_scatter(jnp.einsum('frc,grc->rfg', weighted, window_three, prefe...  112 us
    ppermute x8, waiting for transfers between devices, passed_along(): lax.ppermute(value, axis, [(source, source + steps) for source in range(f...  82.2 us
    psum x1, waiting for transfers between devices, shards(): all_sums, all_counts = lax.psum((partial_sums, partial_counts), 'mod')  24.8 us
    gather x2, local copies, waits for them, and re-layouts, shards(): sorted_good = jnp.take(good_pixel, ordering, axis=0).astype(jnp.bfloat16)  23 us
    unnamed x17, local copies, waits for them, and re-layouts  19.4 us
    gather x2, local copies, waits for them, and re-layouts, shards(): sorted_frames = jnp.take(frames, ordering, axis=1)  12.7 us
    ppermute x8, starting transfers between devices, passed_along(): lax.ppermute(value, axis, [(source, source + steps) for source in range(f...  10.2 us
    reshape x1, local copies, waits for them, and re-layouts, correlate(): flattened.reshape(cycle_number, block_rows, window_width + 1)[:, :, :LAG]  9.25 us
  transfers between devices with their start and end apart: 10, of which 9 were waited for; matrix products, arithmetic and copies ran while one was open for 14% of the time, Pallas kernels for 0%

commit v1 on v0

v1 whole, which is shorter than its diff:
```python
import functools

import jax
import jax.numpy as jnp
from jax import lax
from jax.experimental import pallas as pl
from jax.experimental.pallas import tpu as pltpu
from jax.sharding import PartitionSpec as P

CYCLES = 16
LAG = 1024
LANES = 128
SUBLANES = 8
CHUNK = 256
VMEM_LIMIT = 48 * 1024 * 1024


def order_kernel(groups_ref, frames_ref, label_ref, good_ref, *rest, group_cycles):
    group_refs, (counts_ref, key_ref) = rest[:-2], rest[-2:]
    chunks = label_ref.shape[0]
    rows = chunks * CYCLES
    per_cycle = frames_ref.shape[1] // CYCLES
    cycle_iota = lax.broadcasted_iota(jnp.int32, (CYCLES, CHUNK), 0)
    member = jnp.concatenate(
        [
            jnp.where(label_ref[chunk : chunk + 1, :] == cycle_iota, 1.0, 0.0)
            for chunk in range(chunks)
        ],
        axis=0,
    )
    good = jnp.concatenate(
        [
            jnp.broadcast_to(good_ref[chunk : chunk + 1, :], (CYCLES, CHUNK))
            for chunk in range(chunks)
        ],
        axis=0,
    )
    member_b = member.astype(jnp.bfloat16)
    up = lax.broadcasted_iota(jnp.int32, (rows, rows), 0)
    across = lax.broadcasted_iota(jnp.int32, (rows, rows), 1)
    same = lax.rem(up, CYCLES) == lax.rem(across, CYCLES)
    chunk_before = jnp.where(same & (across < up), 1.0, 0.0).astype(jnp.bfloat16)
    before = (
        lax.broadcasted_iota(jnp.int32, (CHUNK, CHUNK), 0)
        < lax.broadcasted_iota(jnp.int32, (CHUNK, CHUNK), 1)
    )
    before = jnp.where(before, 1.0, 0.0).astype(jnp.bfloat16)
    ones = jnp.ones((CHUNK, CHUNK), jnp.bfloat16)
    dot = functools.partial(jnp.dot, preferred_element_type=jnp.float32)
    earlier = dot(chunk_before, member_b).astype(jnp.bfloat16)
    rank = dot(member_b, before) + dot(earlier, ones)
    used = (member > 0.0) & (good > 0)
    key_ref[...] = jnp.where(used, rank, -1.0)

    of_cycle = jnp.where(
        lax.broadcasted_iota(jnp.int32, (CYCLES, rows), 0)
        == lax.rem(lax.broadcasted_iota(jnp.int32, (CYCLES, rows), 1), CYCLES),
        1.0,
        0.0,
    ).astype(jnp.bfloat16)
    per_lane = dot(of_cycle, jnp.where(used, 1.0, 0.0).astype(jnp.bfloat16))
    counts_ref[...] = dot(per_lane.astype(jnp.bfloat16), jnp.ones((CHUNK, LANES), jnp.bfloat16))

    slots = [
        (lax.broadcasted_iota(jnp.int32, (16, CHUNK), 0) + first).astype(jnp.float32).astype(jnp.bfloat16)
        for first in range(0, per_cycle, 16)
    ]
    one = jnp.ones((16, CHUNK), jnp.bfloat16)
    zero = jnp.zeros((16, CHUNK), jnp.bfloat16)
    frames = frames_ref[...]
    for number, group_ref in enumerate(group_refs):
        first_cycle = groups_ref[number] * group_cycles

        @pl.loop(0, group_cycles)
        def _(cycle):
            tiles = []
            for chunk in range(chunks):
                key = key_ref[pl.ds(chunk * CYCLES + first_cycle + cycle, 1), :]
                key = jnp.broadcast_to(key, (16, CHUNK)).astype(jnp.bfloat16)
                tiles.append(
                    jnp.concatenate([jnp.where(key == slot, one, zero) for slot in slots], axis=0)
                )
            chosen = jnp.concatenate(tiles, axis=1)
            picked = lax.dot_general(
                chosen, frames, (((1,), (1,)), ((), ())), preferred_element_type=jnp.float32
            )
            start = pl.multiple_of(cycle * per_cycle, per_cycle)
            group_ref[pl.ds(start, per_cycle), :] = picked.astype(jnp.bfloat16)


def order_pixels(groups, frames, label, good, group_cycles):
    block_rows, pix_count = frames.shape
    pixels = group_cycles * (pix_count // CYCLES)
    rows = pix_count // CHUNK * CYCLES
    vmem = pl.BlockSpec(memory_space=pltpu.VMEM)
    out_shape = [
        jax.ShapeDtypeStruct((pixels, block_rows), jnp.bfloat16) for _ in range(groups.shape[0])
    ] + [jax.ShapeDtypeStruct((CYCLES, LANES), jnp.float32)]
    return pl.pallas_call(
        functools.partial(order_kernel, group_cycles=group_cycles),
        out_shape=out_shape,
        in_specs=[pl.BlockSpec(memory_space=pltpu.SMEM), vmem, vmem, vmem],
        out_specs=[vmem] * len(out_shape),
        scratch_shapes=[pltpu.VMEM((rows, CHUNK), jnp.float32)],
        compiler_params=pltpu.CompilerParams(vmem_limit_bytes=VMEM_LIMIT),
        cost_estimate=pl.CostEstimate(
            flops=2 * pixels * groups.shape[0] * pix_count * block_rows,
            bytes_accessed=2 * pix_count * block_rows,
            transcendentals=0,
        ),
    )(groups, frames, label.reshape(-1, CHUNK), good.reshape(-1, CHUNK))


def gram_kernel(place_ref, counts_ref, *rest, pieces, frame_count, first_cycle_step):
    window_refs, (mine_ref, theirs_ref, window, gram, later, earlier) = rest[:-6], rest[-6:]
    core, chip, first_cycle = place_ref[0], place_ref[1], place_ref[2]
    block = mine_ref.shape[1]
    pieces_count = len(pieces)
    pair_count = len(window_refs) // pieces_count
    for pair in range(pair_count):
        for relative in range(2):
            at = pl.multiple_of((2 * pair) * block + (relative ^ core) * block, block)
            row = 0
            for piece in range(pieces_count):
                ref = window_refs[pair * pieces_count + piece]
                for source in range(ref.shape[1]):
                    height = ref.shape[2]
                    window[row : row + height, pl.ds(at, block)] = ref[relative, source]
                    row += height
    whole = window[...]
    own = window[:, : 2 * block]
    gram[...] = lax.dot_general(
        own, whole, (((0,), (0,)), ((), ())), preferred_element_type=jnp.float32
    )
    depth, width = whole.shape
    sums = lax.dot_general(
        jnp.ones((SUBLANES, depth), jnp.bfloat16),
        whole,
        (((1,), (0,)), ((), ())),
        preferred_element_type=jnp.float32,
    )
    frame_at = chip * (2 * block) + lax.broadcasted_iota(jnp.int32, (SUBLANES, width), 1)
    later[...] = jnp.where(frame_at < frame_count, 1.0 / sums, 0.0)
    cycle = first_cycle + pl.program_id(0)
    count = counts_ref[pl.ds(cycle, 1), :]
    own_sums = lax.dot_general(
        own,
        jnp.ones((depth, LANES), jnp.bfloat16),
        (((0,), (0,)), ((), ())),
        preferred_element_type=jnp.float32,
    )
    earlier[...] = count / own_sums
    lane = lax.broadcasted_iota(jnp.int32, (SUBLANES, LANES), 1)
    sublane = lax.broadcasted_iota(jnp.int32, (SUBLANES, LANES), 0)
    tiles = LAG // LANES
    for out_ref, position in ((mine_ref, core), (theirs_ref, 1 - core)):
        base = pl.multiple_of(position * block, block)
        for first in range(0, block, SUBLANES):
            factor = earlier[pl.ds(base + first, SUBLANES), :]
            skip = first % LANES
            kept = lane + sublane < LANES - skip
            turned = lax.rem(lane + sublane + skip, LANES)
            rolled = []
            for tile in range(tiles + 1):
                column = pl.multiple_of(base + (first // LANES + tile) * LANES, LANES)
                value = gram[pl.ds(base + first, SUBLANES), pl.ds(column, LANES)]
                value = value * factor * later[:, pl.ds(column, LANES)]
                rolled.append(
                    jnp.take_along_axis(value, turned, axis=1, mode="promise_in_bounds")
                )
            for tile in range(tiles):
                out_ref[0, first : first + SUBLANES, tile * LANES : (tile + 1) * LANES] = jnp.where(
                    kept, rolled[tile], rolled[tile + 1]
                )


def grams(place, counts, windows, frame_count, group_cycles, out_cycles):
    flat = [piece for pair in windows for piece in pair]
    pieces = [piece.shape[1] for piece in windows[0]]
    block = flat[0].shape[-1]
    per_cycle = flat[0].shape[2] // group_cycles
    depth = sum(pieces) * per_cycle
    width = 2 * len(windows) * block
    kernel = functools.partial(
        gram_kernel, pieces=pieces, frame_count=frame_count, first_cycle_step=group_cycles
    )
    in_specs = [pl.BlockSpec((CYCLES, LANES), lambda i, place: (0, 0))]
    in_specs += [
        pl.BlockSpec((2, piece.shape[1], per_cycle, block), lambda i, place: (0, 0, i, 0))
        for piece in flat
    ]
    grid_spec = pltpu.PrefetchScalarGridSpec(
        num_scalar_prefetch=1,
        grid=(group_cycles,),
        in_specs=in_specs,
        out_specs=[
            pl.BlockSpec((1, block, LAG), lambda i, place: (place[0] * group_cycles + i, 0, 0)),
            pl.BlockSpec((1, block, LAG), lambda i, place: (i, 0, 0)),
        ],
        scratch_shapes=[
            pltpu.VMEM((depth, width), jnp.bfloat16),
            pltpu.VMEM((2 * block, width), jnp.float32),
            pltpu.VMEM((SUBLANES, width), jnp.float32),
            pltpu.VMEM((2 * block, LANES), jnp.float32),
        ],
    )
    return pl.pallas_call(
        kernel,
        grid_spec=grid_spec,
        out_shape=[
            jax.ShapeDtypeStruct((out_cycles, block, LAG), jnp.float32),
            jax.ShapeDtypeStruct((group_cycles, block, LAG), jnp.float32),
        ],
        compiler_params=pltpu.CompilerParams(vmem_limit_bytes=VMEM_LIMIT),
        cost_estimate=pl.CostEstimate(
            flops=2 * group_cycles * depth * width * 2 * block,
            bytes_accessed=2 * group_cycles * (depth * width + 4 * block * LAG),
            transcendentals=0,
        ),
    )(place, counts, *flat)


def fill_kernel(place_ref, whole_ref, part_ref, out_ref):
    out_ref[...] = part_ref[...]


def fill(place, whole, part):
    count, block, lags = part.shape
    grid_spec = pltpu.PrefetchScalarGridSpec(
        num_scalar_prefetch=1,
        grid=(count,),
        in_specs=[
            pl.BlockSpec(memory_space=pl.ANY),
            pl.BlockSpec((1, block, lags), lambda i, place: (i, 0, 0)),
        ],
        out_specs=pl.BlockSpec(
            (1, block, lags), lambda i, place: ((1 - place[0]) * count + i, 0, 0)
        ),
    )
    return pl.pallas_call(
        fill_kernel,
        grid_spec=grid_spec,
        out_shape=jax.ShapeDtypeStruct(whole.shape, whole.dtype),
        input_output_aliases={1: 0},
        cost_estimate=pl.CostEstimate(flops=0, bytes_accessed=8 * part.size, transcendentals=0),
    )(place, whole, part)


def shifted(value, pairs_down):
    step = 2 * pairs_down
    count = lax.axis_size("frame")
    return lax.ppermute(value, "frame", [(source, source - step) for source in range(step, count)])


def other_pair(value):
    count = lax.axis_size("frame")
    return lax.ppermute(value, "frame", [(source, source ^ 2) for source in range(count)])


def other_core(value):
    count = lax.axis_size("frame")
    return lax.ppermute(value, "frame", [(source, source ^ 1) for source in range(count)])


def to_mod(value, step, core_flip):
    frames, mods = lax.axis_size("frame"), lax.axis_size("mod")
    pairs = [
        (frame * mods + mod, (frame ^ core_flip) * mods + (mod + step) % mods)
        for frame in range(frames)
        for mod in range(mods)
    ]
    return lax.ppermute(value, ("frame", "mod"), pairs)


def shards(frames, cycle_label, good_pixel):
    mods = lax.axis_size("mod")
    cycle_dev = CYCLES // mods
    group_cycles = cycle_dev // 2
    mod, frame = lax.axis_index("mod"), lax.axis_index("frame")
    core, chip = frame % 2, frame // 2
    block = frames.shape[0]
    assert LAG == 8 * block and block == LANES

    def ordered(step):
        target = (mod + step) % mods
        groups = jnp.stack([target * 2 + core, target * 2 + 1 - core]).astype(jnp.int32)
        return order_pixels(groups, frames, cycle_label, good_pixel, group_cycles)

    kept, sent, counts = ordered(0)
    counts = lax.psum(counts, "mod")
    first = jnp.stack([kept, other_core(sent)])[:, None]
    rest = []
    for step in range(1, mods):
        same, flipped, _ = ordered(step)
        rest.append(jnp.stack([to_mod(same, step, 0), to_mod(flipped, step, 1)]))
    pieces = [first, jnp.stack(rest, axis=1)]
    later_chip = chip % 2 == 1
    windows = [[] for _ in range(5)]
    for own in pieces:
        two = shifted(own, 2)
        four = shifted(two, 2)
        one = other_pair(jnp.where(later_chip, own, two))
        three = other_pair(jnp.where(later_chip, two, four))
        for window, value in zip(windows, (own, one, two, three, four)):
            window.append(value)
    place = jnp.stack([core, chip, mod * cycle_dev + core * group_cycles]).astype(jnp.int32)
    frame_count = block * lax.axis_size("frame")
    whole, theirs = grams(place, counts, windows, frame_count, group_cycles, cycle_dev)
    return fill(place, whole, other_core(theirs))


def solution(mesh):
    placed = (P("frame", "mod"), P("mod"), P("mod"))
    return jax.shard_map(
        shards, mesh=mesh, in_specs=placed, out_specs=P("mod", "frame", None), check_vma=False
    )
```

time: 350 us -> 129 us (0.37)
  waiting for transfers between devices: 219 us -> 75 us
  local copies, waits for them, and re-layouts: 73.3 us -> 4.02 us
  Pallas kernels: 0 us -> 27.2 us
  matrix products: 13.9 us -> 0 us
  between operations: 13.6 us -> 0.1 us
  other arithmetic: 13.5 us -> 4.51 us
    reduce_scatter x1 -> x0, waiting for transfers between devices: 112 us -> none  [shards(): lax.psum_scatter(jnp.einsum('frc,grc->rfg', weighted, window_three, prefe...]
    gather x4 -> x0, local copies, waits for them, and re-layouts: 35.7 us -> none  [the longest x2 23 us: shards(): sorted_good = jnp.take(good_pixel, ordering, axis=0).astype(jnp.bfloat16)]
    pallas_call x0 -> x4, Pallas kernels: none -> 27.2 us  [the longest x2 13.7 us: order_pixels(): pl.pallas_call(functools.partial(order_kernel, group_cycles=group_cycles)...]
    psum x1 -> x0, waiting for transfers between devices: 24.8 us -> none  [shards(): all_sums, all_counts = lax.psum((partial_sums, partial_counts), 'mod')]
    unnamed x17 -> x14, local copies, waits for them, and re-layouts: 19.4 us -> 2.57 us
    dot_general x2 -> x0, matrix products: 13.9 us -> none  [the longest x1 8.89 us: shards(): jnp.einsum('frc,grc->rfg', weighted, window_three, preferred_element_type...]
    reshape x1 -> x2, local copies, waits for them, and re-layouts: 9.25 us -> 1.44 us  [the longest x1 0.72 us: order_pixels(): label.reshape(-1, CHUNK)]
    ppermute x8 -> x12, waiting for transfers between devices: 82.2 us -> 75 us  [the longest x4 30.6 us: shifted(): lax.ppermute(value, 'frame', [(source, source - step) for source in range...]
  transfers between devices with their start and end apart: 10 -> 12, of which waited for: 9 -> 10; matrix products, arithmetic and copies ran while one was open for 14% -> 3% of each run, Pallas kernels for 0% -> 5%
where the time goes in v1:
time: 129 us; the launch traced here: 128 us
  waiting for transfers between devices  75 us (58%)
  Pallas kernels  27.2 us (21%)
  starting transfers between devices  12.4 us (10%)
  blocking collectives  4.96 us (4%)
  other arithmetic  4.51 us (3%)
  local copies, waits for them, and re-layouts  4.02 us (3%)
    ppermute x4, waiting for transfers between devices, shifted(): lax.ppermute(value, 'frame', [(source, source - step) for source in range...  30.6 us
    ppermute x4, waiting for transfers between devices, other_pair(): lax.ppermute(value, 'frame', [(source, source ^ 2) for source in range(co...  29.1 us
    pallas_call x2, Pallas kernels, order_pixels(): pl.pallas_call(functools.partial(order_kernel, group_cycles=group_cycles)...  13.7 us
    ppermute x2, waiting for transfers between devices, to_mod(): return lax.ppermute(value, ('frame', 'mod'), pairs)  10.9 us
    pallas_call x1, Pallas kernels, grams(): pl.pallas_call(kernel, grid_spec=grid_spec, out_shape=[jax.ShapeDtypeStru...  9.03 us
    ppermute x4, starting transfers between devices, shifted(): lax.ppermute(value, 'frame', [(source, source - step) for source in range...  5.15 us
    psum x1, blocking collectives, shards(): counts = lax.psum(counts, 'mod')  4.96 us
    pallas_call x1, Pallas kernels, fill(): pl.pallas_call(fill_kernel, grid_spec=grid_spec, out_shape=jax.ShapeDtype...  4.45 us
  transfers between devices with their start and end apart: 12, of which 10 were waited for; matrix products, arithmetic and copies ran while one was open for 3% of the time, Pallas kernels for 5%

profile of v1, /device:TPU:0, one launch (start us, length us, event | category | flops | bytes accessed | tf_op | source)
XLA Modules:
  0.0 128.1 jit_solution(11547330303616992180)
XLA Ops:
  0.0 0.7 reshape.8.label_ref
  0.7 0.7 reshape.9.good_ref
  1.4 0.1 pad_add_fusion.1.groups_ref
  1.5 0.0 copy-start.1
  1.5 1.2 copy-done.1
  2.7 0.0 copy-start.2
  2.7 6.8 %shard_map.37 = (bf16[1024,128]{1,0:T(8,128)(2,1)S(1)}, bf16[1024,128]{1,0:T(8,128)(2,1)S(1)}, f32[16,128]{1,0:T(8,128)S(1)}) custom-call(s32[2]{0:T(128)S(1)} %pad_add_fusion.1.groups_ref, bf16[128,4096]{1,0:T(8,128)(2,1)S(1)} %copy-done.1, s32[16,256]{1,0:T(8,128)S(1)} %reshape.8.label_ref, s32[16,256]{1,0:T(8,128)S(1)} %reshape.9.good_ref), custom_call_target="tpu_custom_call" | custom-call | flops 2147483648 | bytes 1048576 | tf_op jit(solution)/shard_map/pallas_call | solution.py:99
  9.5 0.5 collective-permute-start
  10.0 0.1 pad_add_fusion.2.groups_ref
  10.1 0.0 copy-done.2
  10.1 7.0 %shard_map.38 = (bf16[1024,128]{1,0:T(8,128)(2,1)S(1)}, bf16[1024,128]{1,0:T(8,128)(2,1)S(1)}, f32[16,128]{1,0:T(8,128)}) custom-call(s32[2]{0:T(128)S(1)} %pad_add_fusion.2.groups_ref, bf16[128,4096]{1,0:T(8,128)(2,1)S(1)} %copy-done.2, s32[16,256]{1,0:T(8,128)S(1)} %reshape.8.label_ref, s32[16,256]{1,0:T(8,128)S(1)} %reshape.9.good_ref), custom_call_target="tpu_custom_call" | custom-call | flops 2147483648 | bytes 1048576 | tf_op jit(solution)/shard_map/pallas_call | solution.py:99
  17.1 2.5 %collective-permute-start.1 = (bf16[1024,128]{1,0:T(8,128)(2,1)S(1)}, bf16[1024,128]{1,0:T(8,128)(2,1)S(1)}, u32[]{:S(2)}, u32[]{:S(2)}) collective-permute-start(bf16[1024,128]{1,0:T(8,128)(2,1)S(1)} %get-tuple-element.15), channel_id=1, source_target_pairs={{0,1},{1,0},{2,3},{3,2},{4,5},{5,4},{6,7},{7,6},{8,9},{9,8},{10,11... | collective-permute-start | bytes 786440 | tf_op jit(solution)/shard_map/ppermute | solution.py:272
  19.6 0.1 collective-permute-start.2
  19.7 0.0 collective-permute-done
  19.7 0.0 copy-start.4
  19.7 0.1 maximum_bitcast_fusion.rest_0_
  19.8 1.3 %collective-permute-start.3 = (bf16[2,1,1024,128]{3,2,1,0:T(8,128)(2,1)S(1)}, bf16[2,1,1024,128]{3,2,1,0:T(8,128)(2,1)S(1)}, u32[]{:S(2)}, u32[]{:S(2)}) collective-permute-start(bf16[2,1,1024,128]{3,2,1,0:T(8,128)(2,1)S(1)} %maximum_bitcast_fusion.rest_0_), channel_id=1, source_target_pairs={{8,0},{10,2},{12,4},{14,6},{16,8},{18,10},{20,12},{22,14},{24,16},... | collective-permute-start | bytes 1572872 | tf_op jit(solution)/shard_map/ppermute | solution.py:252
  21.1 5.7 %collective-permute-done.1 = bf16[1024,128]{1,0:T(8,128)(2,1)S(1)} collective-permute-done((bf16[1024,128]{1,0:T(8,128)(2,1)S(1)}, bf16[1024,128]{1,0:T(8,128)(2,1)S(1)}, u32[]{:S(2)}, u32[]{:S(2)}) %collective-permute-start.1) | collective-permute-done | bytes 262176 | tf_op jit(solution)/shard_map/ppermute | solution.py:272
  26.8 0.0 copy-start.5
  26.8 5.2 %collective-permute-done.2 = bf16[1024,128]{1,0:T(8,128)(2,1)S(1)} collective-permute-done((bf16[1024,128]{1,0:T(8,128)(2,1)S(1)}, bf16[1024,128]{1,0:T(8,128)(2,1)S(1)}, u32[]{:S(2)}, u32[]{:S(2)}) %collective-permute-start.2) | collective-permute-done | bytes 262176 | tf_op jit(solution)/shard_map/ppermute | solution.py:272
  32.0 0.0 copy-start.6
  32.0 0.0 copy-done.4
  32.0 0.1 maximum_bitcast_fusion.1.rest_1_
  32.0 1.3 %collective-permute-start.5 = (bf16[2,1,1024,128]{3,2,1,0:T(8,128)(2,1)S(1)}, bf16[2,1,1024,128]{3,2,1,0:T(8,128)(2,1)S(1)}, u32[]{:S(2)}, u32[]{:S(2)}) collective-permute-start(bf16[2,1,1024,128]{3,2,1,0:T(8,128)(2,1)S(1)} %maximum_bitcast_fusion.1.rest_1_), channel_id=1, source_target_pairs={{8,0},{10,2},{12,4},{14,6},{16,8},{18,10},{20,12},{22,14},{24,16},... | collective-permute-start | bytes 1572872 | tf_op jit(solution)/shard_map/ppermute | solution.py:252
  33.3 2.6 %collective-permute-done.3.rest_4_ = bf16[2,1,1024,128]{3,2,1,0:T(8,128)(2,1)S(1)} collective-permute-done((bf16[2,1,1024,128]{3,2,1,0:T(8,128)(2,1)S(1)}, bf16[2,1,1024,128]{3,2,1,0:T(8,128)(2,1)S(1)}, u32[]{:S(2)}, u32[]{:S(2)}) %collective-permute-start.3) | collective-permute-done | bytes 524320 | tf_op jit(solution)/shard_map/ppermute | solution.py:252
  35.9 1.3 collective-permute-start.7
  37.2 11.5 %collective-permute-done.5.rest_5_ = bf16[2,1,1024,128]{3,2,1,0:T(8,128)(2,1)S(1)} collective-permute-done((bf16[2,1,1024,128]{3,2,1,0:T(8,128)(2,1)S(1)}, bf16[2,1,1024,128]{3,2,1,0:T(8,128)(2,1)S(1)}, u32[]{:S(2)}, u32[]{:S(2)}) %collective-permute-start.5) | collective-permute-done | bytes 524320 | tf_op jit(solution)/shard_map/ppermute | solution.py:252
  48.6 0.0 copy-done.5
  48.6 0.0 copy-done.6
  48.7 1.3 %collective-permute-start.9 = (bf16[2,1,1024,128]{3,2,1,0:T(8,128)(2,1)S(1)}, bf16[2,1,1024,128]{3,2,1,0:T(8,128)(2,1)S(1)}, u32[]{:S(2)}, u32[]{:S(2)}) collective-permute-start(bf16[2,1,1024,128]{3,2,1,0:T(8,128)(2,1)S(1)} %collective-permute-done.5.rest_5_), channel_id=1, source_target_pairs={{8,0},{10,2},{12,4},{14,6},{16,8},{18,10},{20,12},{22,14},{24,16},... | collective-permute-start | bytes 1572872 | tf_op jit(solution)/shard_map/ppermute | solution.py:252
  50.0 9.9 %collective-permute-done.7.rest_8_ = bf16[2,1,1024,128]{3,2,1,0:T(8,128)(2,1)S(1)} collective-permute-done((bf16[2,1,1024,128]{3,2,1,0:T(8,128)(2,1)S(1)}, bf16[2,1,1024,128]{3,2,1,0:T(8,128)(2,1)S(1)}, u32[]{:S(2)}, u32[]{:S(2)}) %collective-permute-start.7) | collective-permute-done | bytes 524320 | tf_op jit(solution)/shard_map/ppermute | solution.py:252
  59.9 2.0 %broadcast_select_fusion.1 = (bf16[2,1,1024,128]{3,2,1,0:T(8,128)(2,1)}, bf16[2,1,1024,128]{3,2,1,0:T(8,128)(2,1)}) fusion(bf16[2,1,1024,128]{3,2,1,0:T(8,128)(2,1)S(1)} %collective-permute-done.3.rest_4_, bf16[2,1,1024,128]{3,2,1,0:T(8,128)(2,1)S(1)} %collective-permute-done.7.rest_8_, pred[]{:T(512)S(6)} %eq.8, bf16[1,1024,128]{2,1,0:T(8,128)(2,1)} %bitcast.22, ...), kind=kLoop, calls=%fused_computation.3 | loop fusion | flops 786432 | bytes 2621441 | tf_op jit(solution)/shard_map/jit(_where)/select_n | solution.py:303
  61.9 1.5 %collective-permute-start.8 = (bf16[2,1,1024,128]{3,2,1,0:T(8,128)(2,1)}, bf16[2,1,1024,128]{3,2,1,0:T(8,128)(2,1)}, u32[]{:S(2)}, u32[]{:S(2)}) collective-permute-start(bf16[2,1,1024,128]{3,2,1,0:T(8,128)(2,1)} %get-tuple-element.21), channel_id=1, source_target_pairs={{0,4},{2,6},{4,0},{6,2},{8,12},{10,14},{12,8},{14,10},{16,20},{18,... | collective-permute-start | bytes 1572872 | tf_op jit(solution)/shard_map/ppermute | solution.py:257
  63.4 0.5 collective-permute-start.4
  63.9 6.7 %collective-permute-done.9.rest_9_ = bf16[2,1,1024,128]{3,2,1,0:T(8,128)(2,1)S(1)} collective-permute-done((bf16[2,1,1024,128]{3,2,1,0:T(8,128)(2,1)S(1)}, bf16[2,1,1024,128]{3,2,1,0:T(8,128)(2,1)S(1)}, u32[]{:S(2)}, u32[]{:S(2)}) %collective-permute-start.9) | collective-permute-done | bytes 524320 | tf_op jit(solution)/shard_map/ppermute | solution.py:252
  70.6 2.1 %broadcast_select_fusion = (bf16[2,1,1024,128]{3,2,1,0:T(8,128)(2,1)}, bf16[2,1,1024,128]{3,2,1,0:T(8,128)(2,1)}) fusion(bf16[2,1,1024,128]{3,2,1,0:T(8,128)(2,1)S(1)} %collective-permute-done.5.rest_5_, bf16[2,1,1024,128]{3,2,1,0:T(8,128)(2,1)S(1)} %collective-permute-done.9.rest_9_, pred[]{:T(512)S(6)} %eq.8, bf16[1,1024,128]{2,1,0:T(8,128)(2,1)} %bitcast.26, ...), kind=kLoop, calls=%fused_computation.2 | loop fusion | flops 786432 | bytes 2621441 | tf_op jit(solution)/shard_map/jit(_where)/select_n | solution.py:303
  72.8 1.6 %collective-permute-start.10 = (bf16[2,1,1024,128]{3,2,1,0:T(8,128)(2,1)}, bf16[2,1,1024,128]{3,2,1,0:T(8,128)(2,1)}, u32[]{:S(2)}, u32[]{:S(2)}) collective-permute-start(bf16[2,1,1024,128]{3,2,1,0:T(8,128)(2,1)} %get-tuple-element.19), channel_id=1, source_target_pairs={{0,4},{2,6},{4,0},{6,2},{8,12},{10,14},{12,8},{14,10},{16,20},{18,... | collective-permute-start | bytes 1572872 | tf_op jit(solution)/shard_map/ppermute | solution.py:257
  74.4 0.4 collective-permute-start.6
  74.8 5.0 %psum.7.counts_ref = f32[16,128]{1,0:T(8,128)S(1)} all-reduce(f32[16,128]{1,0:T(8,128)S(1)} %get-tuple-element.12), channel_id=1, replica_groups=mesh['frame'=16,'mod'=2] {'mod'}, use_global_device_ids=true, to_apply=%region_0.1 | all-reduce | flops 2048 | bytes 16384 | tf_op jit(solution)/shard_map/psum | solution.py:290
  79.8 0.1 pad_add_fusion.place_ref
  79.9 0.0 copy-start
  79.9 0.0 collective-permute-done.8.rest_6_
  79.9 8.5 %collective-permute-done.4.rest_2_ = bf16[2,1,1024,128]{3,2,1,0:T(8,128)(2,1)} collective-permute-done((bf16[2,1,1024,128]{3,2,1,0:T(8,128)(2,1)}, bf16[2,1,1024,128]{3,2,1,0:T(8,128)(2,1)}, u32[]{:S(2)}, u32[]{:S(2)}) %collective-permute-start.4) | collective-permute-done | bytes 524320 | tf_op jit(solution)/shard_map/ppermute | solution.py:257
  88.3 11.2 %collective-permute-done.10.rest_7_ = bf16[2,1,1024,128]{3,2,1,0:T(8,128)(2,1)} collective-permute-done((bf16[2,1,1024,128]{3,2,1,0:T(8,128)(2,1)}, bf16[2,1,1024,128]{3,2,1,0:T(8,128)(2,1)}, u32[]{:S(2)}, u32[]{:S(2)}) %collective-permute-start.10) | collective-permute-done | bytes 524320 | tf_op jit(solution)/shard_map/ppermute | solution.py:257
  99.6 9.4 %collective-permute-done.6.rest_3_ = bf16[2,1,1024,128]{3,2,1,0:T(8,128)(2,1)} collective-permute-done((bf16[2,1,1024,128]{3,2,1,0:T(8,128)(2,1)}, bf16[2,1,1024,128]{3,2,1,0:T(8,128)(2,1)}, u32[]{:S(2)}, u32[]{:S(2)}) %collective-permute-start.6) | collective-permute-done | bytes 524320 | tf_op jit(solution)/shard_map/ppermute | solution.py:257
  109.0 9.0 %shard_map.39 = (f32[8,128,1024]{2,1,0:T(8,128)}, f32[4,128,1024]{2,1,0:T(8,128)}) custom-call(s32[3]{0:T(128)S(1)} %pad_add_fusion.place_ref, f32[16,128]{1,0:T(8,128)S(1)} %psum.7.counts_ref, bf16[2,1,1024,128]{3,2,1,0:T(8,128)(2,1)S(1)} %maximum_bitcast_fusion.rest_0_, bf16[2,1,1024,128]{3,2,1,0:T(8,128)(2,1)S(1)} %maximum_bitcast_fusion.1.rest_1_, ...), custom_call_target="tpu_custom_call" | custom-call | flops 1342177280 | bytes 9437184 | tf_op jit(solution)/shard_map/pallas_call | solution.py:207
  118.0 0.0 collective-permute-start.11
  118.0 4.4 %collective-permute-done.11.part_ref = f32[4,128,1024]{2,1,0:T(8,128)S(1)} collective-permute-done((f32[4,128,1024]{2,1,0:T(8,128)}, f32[4,128,1024]{2,1,0:T(8,128)S(1)}, u32[]{:S(2)}, u32[]{:S(2)}) %collective-permute-start.11) | collective-permute-done | bytes 2097184 | tf_op jit(solution)/shard_map/ppermute | solution.py:262
  122.4 0.0 copy-start.3
  122.4 0.0 copy-done
  122.4 1.3 %copy-done.3 = f32[4,128,1024]{2,1,0:T(8,128)} copy-done((f32[4,128,1024]{2,1,0:T(8,128)}, f32[4,128,1024]{2,1,0:T(8,128)S(1)}, u32[]{:S(2)}) %copy-start.3) | copy-done | bytes 2097176
  123.7 4.4 %shard_map.40 = f32[8,128,1024]{2,1,0:T(8,128)} custom-call(s32[3]{0:T(128)} %copy-done, f32[8,128,1024]{2,1,0:T(8,128)} %get-tuple-element.17.whole_ref, f32[4,128,1024]{2,1,0:T(8,128)} %copy-done.3), custom_call_target="tpu_custom_call", output_to_operand_aliasing={{}: (1, {})} | custom-call | bytes 4194304 | tf_op jit(solution)/shard_map/pallas_call | solution.py:240
Async XLA Ops:
  1.5 1.2 copy-start.1
  2.7 7.4 %copy-start.2 = (bf16[128,4096]{1,0:T(8,128)(2,1)S(1)}, bf16[128,4096]{1,0:T(8,128)(2,1)}, u32[]{:S(2)}) copy-start(bf16[128,4096]{1,0:T(8,128)(2,1)} %frames_ref.3) | copy-start | bytes 3145732
  9.5 10.2 %collective-permute-start = (bf16[1024,128]{1,0:T(8,128)(2,1)S(1)}, bf16[1024,128]{1,0:T(8,128)(2,1)S(1)}, u32[]{:S(2)}, u32[]{:S(2)}) collective-permute-start(bf16[1024,128]{1,0:T(8,128)(2,1)S(1)} %get-tuple-element.14), channel_id=1, source_target_pairs={{0,2},{2,0},{4,6},{6,4},{8,10},{10,8},{12,14},{14,12},{16,18},{18,... | collective-permute-start | bytes 786440 | tf_op jit(solution)/shard_map/ppermute | solution.py:262
  17.1 9.7 %collective-permute-start.1 = (bf16[1024,128]{1,0:T(8,128)(2,1)S(1)}, bf16[1024,128]{1,0:T(8,128)(2,1)S(1)}, u32[]{:S(2)}, u32[]{:S(2)}) collective-permute-start(bf16[1024,128]{1,0:T(8,128)(2,1)S(1)} %get-tuple-element.15), channel_id=1, source_target_pairs={{0,1},{1,0},{2,3},{3,2},{4,5},{5,4},{6,7},{7,6},{8,9},{9,8},{10,11... | collective-permute-start | bytes 786440 | tf_op jit(solution)/shard_map/ppermute | solution.py:272
  19.6 12.3 %collective-permute-start.2 = (bf16[1024,128]{1,0:T(8,128)(2,1)S(1)}, bf16[1024,128]{1,0:T(8,128)(2,1)S(1)}, u32[]{:S(2)}, u32[]{:S(2)}) collective-permute-start(bf16[1024,128]{1,0:T(8,128)(2,1)S(1)} %get-tuple-element.16), channel_id=1, source_target_pairs={{0,3},{1,2},{2,1},{3,0},{4,7},{5,6},{6,5},{7,4},{8,11},{9,10},{10,... | collective-permute-start | bytes 786440 | tf_op jit(solution)/shard_map/ppermute | solution.py:272
  19.7 12.2 %copy-start.4 = (bf16[1024,128]{1,0:T(8,128)(2,1)}, bf16[1024,128]{1,0:T(8,128)(2,1)S(1)}, u32[]{:S(2)}) copy-start(bf16[1024,128]{1,0:T(8,128)(2,1)S(1)} %collective-permute-done) | copy-start | bytes 786436
  19.8 16.1 %collective-permute-start.3 = (bf16[2,1,1024,128]{3,2,1,0:T(8,128)(2,1)S(1)}, bf16[2,1,1024,128]{3,2,1,0:T(8,128)(2,1)S(1)}, u32[]{:S(2)}, u32[]{:S(2)}) collective-permute-start(bf16[2,1,1024,128]{3,2,1,0:T(8,128)(2,1)S(1)} %maximum_bitcast_fusion.rest_0_), channel_id=1, source_target_pairs={{8,0},{10,2},{12,4},{14,6},{16,8},{18,10},{20,12},{22,14},{24,16},... | collective-permute-start | bytes 1572872 | tf_op jit(solution)/shard_map/ppermute | solution.py:252
  26.8 21.9 %copy-start.5 = (bf16[1024,128]{1,0:T(8,128)(2,1)}, bf16[1024,128]{1,0:T(8,128)(2,1)S(1)}, u32[]{:S(2)}) copy-start(bf16[1024,128]{1,0:T(8,128)(2,1)S(1)} %collective-permute-done.1) | copy-start | bytes 786436
  32.0 16.7 %copy-start.6 = (bf16[1024,128]{1,0:T(8,128)(2,1)}, bf16[1024,128]{1,0:T(8,128)(2,1)S(1)}, u32[]{:S(2)}) copy-start(bf16[1024,128]{1,0:T(8,128)(2,1)S(1)} %collective-permute-done.2) | copy-start | bytes 786436
  32.0 16.6 %collective-permute-start.5 = (bf16[2,1,1024,128]{3,2,1,0:T(8,128)(2,1)S(1)}, bf16[2,1,1024,128]{3,2,1,0:T(8,128)(2,1)S(1)}, u32[]{:S(2)}, u32[]{:S(2)}) collective-permute-start(bf16[2,1,1024,128]{3,2,1,0:T(8,128)(2,1)S(1)} %maximum_bitcast_fusion.1.rest_1_), channel_id=1, source_target_pairs={{8,0},{10,2},{12,4},{14,6},{16,8},{18,10},{20,12},{22,14},{24,16},... | collective-permute-start | bytes 1572872 | tf_op jit(solution)/shard_map/ppermute | solution.py:252
  35.9 24.0 %collective-permute-start.7 = (bf16[2,1,1024,128]{3,2,1,0:T(8,128)(2,1)S(1)}, bf16[2,1,1024,128]{3,2,1,0:T(8,128)(2,1)S(1)}, u32[]{:S(2)}, u32[]{:S(2)}) collective-permute-start(bf16[2,1,1024,128]{3,2,1,0:T(8,128)(2,1)S(1)} %collective-permute-done.3.rest_4_), channel_id=1, source_target_pairs={{8,0},{10,2},{12,4},{14,6},{16,8},{18,10},{20,12},{22,14},{24,16},... | collective-permute-start | bytes 1572872 | tf_op jit(solution)/shard_map/ppermute | solution.py:252
  48.7 22.0 %collective-permute-start.9 = (bf16[2,1,1024,128]{3,2,1,0:T(8,128)(2,1)S(1)}, bf16[2,1,1024,128]{3,2,1,0:T(8,128)(2,1)S(1)}, u32[]{:S(2)}, u32[]{:S(2)}) collective-permute-start(bf16[2,1,1024,128]{3,2,1,0:T(8,128)(2,1)S(1)} %collective-permute-done.5.rest_5_), channel_id=1, source_target_pairs={{8,0},{10,2},{12,4},{14,6},{16,8},{18,10},{20,12},{22,14},{24,16},... | collective-permute-start | bytes 1572872 | tf_op jit(solution)/shard_map/ppermute | solution.py:252
  61.9 17.9 %collective-permute-start.8 = (bf16[2,1,1024,128]{3,2,1,0:T(8,128)(2,1)}, bf16[2,1,1024,128]{3,2,1,0:T(8,128)(2,1)}, u32[]{:S(2)}, u32[]{:S(2)}) collective-permute-start(bf16[2,1,1024,128]{3,2,1,0:T(8,128)(2,1)} %get-tuple-element.21), channel_id=1, source_target_pairs={{0,4},{2,6},{4,0},{6,2},{8,12},{10,14},{12,8},{14,10},{16,20},{18,... | collective-permute-start | bytes 1572872 | tf_op jit(solution)/shard_map/ppermute | solution.py:257
  63.4 24.9 %collective-permute-start.4 = (bf16[2,1,1024,128]{3,2,1,0:T(8,128)(2,1)}, bf16[2,1,1024,128]{3,2,1,0:T(8,128)(2,1)}, u32[]{:S(2)}, u32[]{:S(2)}) collective-permute-start(bf16[2,1,1024,128]{3,2,1,0:T(8,128)(2,1)} %get-tuple-element.22), channel_id=1, source_target_pairs={{0,4},{2,6},{4,0},{6,2},{8,12},{10,14},{12,8},{14,10},{16,20},{18,... | collective-permute-start | bytes 1572872 | tf_op jit(solution)/shard_map/ppermute | solution.py:257
  72.8 26.8 %collective-permute-start.10 = (bf16[2,1,1024,128]{3,2,1,0:T(8,128)(2,1)}, bf16[2,1,1024,128]{3,2,1,0:T(8,128)(2,1)}, u32[]{:S(2)}, u32[]{:S(2)}) collective-permute-start(bf16[2,1,1024,128]{3,2,1,0:T(8,128)(2,1)} %get-tuple-element.19), channel_id=1, source_target_pairs={{0,4},{2,6},{4,0},{6,2},{8,12},{10,14},{12,8},{14,10},{16,20},{18,... | collective-permute-start | bytes 1572872 | tf_op jit(solution)/shard_map/ppermute | solution.py:257
  74.4 34.5 %collective-permute-start.6 = (bf16[2,1,1024,128]{3,2,1,0:T(8,128)(2,1)}, bf16[2,1,1024,128]{3,2,1,0:T(8,128)(2,1)}, u32[]{:S(2)}, u32[]{:S(2)}) collective-permute-start(bf16[2,1,1024,128]{3,2,1,0:T(8,128)(2,1)} %get-tuple-element.20), channel_id=1, source_target_pairs={{0,4},{2,6},{4,0},{6,2},{8,12},{10,14},{12,8},{14,10},{16,20},{18,... | collective-permute-start | bytes 1572872 | tf_op jit(solution)/shard_map/ppermute | solution.py:257
  79.9 42.5 %copy-start = (s32[3]{0:T(128)}, s32[3]{0:T(128)S(1)}, u32[]{:S(2)}) copy-start(s32[3]{0:T(128)S(1)} %pad_add_fusion.place_ref) | copy-start | bytes 40
  118.0 4.4 %collective-permute-start.11 = (f32[4,128,1024]{2,1,0:T(8,128)}, f32[4,128,1024]{2,1,0:T(8,128)S(1)}, u32[]{:S(2)}, u32[]{:S(2)}) collective-permute-start(f32[4,128,1024]{2,1,0:T(8,128)} %get-tuple-element.18), channel_id=1, source_target_pairs={{0,2},{2,0},{4,6},{6,4},{8,10},{10,8},{12,14},{14,12},{16,18},{18,... | collective-permute-start | bytes 6291464 | tf_op jit(solution)/shard_map/ppermute | solution.py:262
  122.4 1.3 %copy-start.3 = (f32[4,128,1024]{2,1,0:T(8,128)}, f32[4,128,1024]{2,1,0:T(8,128)S(1)}, u32[]{:S(2)}) copy-start(f32[4,128,1024]{2,1,0:T(8,128)S(1)} %collective-permute-done.11.part_ref) | copy-start | bytes 6291460

commit v2 on v0

v2 whole, which is shorter than its diff:
```python
import functools

import jax
import jax.numpy as jnp
from jax import lax
from jax.experimental import pallas as pl
from jax.experimental.pallas import tpu as pltpu
from jax.sharding import PartitionSpec as P

CYCLES = 16
LAG = 1024
LANES = 128
SUBLANES = 8
PACKED = 16
CHUNK = 256
VMEM_LIMIT = 40 * 1024 * 1024

SMEM_SPEC = pl.BlockSpec(memory_space=pltpu.SMEM)
VMEM_SPEC = pl.BlockSpec(memory_space=pltpu.VMEM)
ANY_SPEC = pl.BlockSpec(memory_space=pl.ANY)

dot = functools.partial(jnp.dot, preferred_element_type=jnp.float32)


def params():
    return pltpu.CompilerParams(vmem_limit_bytes=VMEM_LIMIT)


def estimate(flops, moved):
    return pl.CostEstimate(flops=flops, bytes_accessed=moved, transcendentals=0)


def ones_where(condition):
    return jnp.where(condition, 1.0, 0.0).astype(jnp.bfloat16)


def iota(shape, dimension):
    return lax.broadcasted_iota(jnp.int32, shape, dimension)


def rank_kernel(label_ref, good_ref, key_ref, counts_ref):
    chunks = label_ref.shape[0] // CHUNK
    rows = chunks * CYCLES
    cycle_at = iota((CYCLES, CHUNK), 0)
    labels = [label_ref[pl.ds(at * CHUNK, CHUNK)].reshape(1, CHUNK) for at in range(chunks)]
    goods = [good_ref[pl.ds(at * CHUNK, CHUNK)].reshape(1, CHUNK) for at in range(chunks)]
    member = jnp.concatenate([jnp.where(one == cycle_at, 1.0, 0.0) for one in labels], axis=0)
    good = jnp.concatenate([jnp.broadcast_to(one, (CYCLES, CHUNK)) for one in goods], axis=0)
    member_b = member.astype(jnp.bfloat16)
    up, across = iota((rows, rows), 0), iota((rows, rows), 1)
    same = lax.rem(up, CYCLES) == lax.rem(across, CYCLES)
    chunk_before = ones_where(same & (across < up))
    before = ones_where(iota((CHUNK, CHUNK), 0) < iota((CHUNK, CHUNK), 1))
    earlier = dot(chunk_before, member_b).astype(jnp.bfloat16)
    rank = dot(member_b, before) + dot(earlier, jnp.ones((CHUNK, CHUNK), jnp.bfloat16))
    used = (member > 0.0) & (good > 0)
    key_ref[...] = jnp.where(used, rank, -1.0)
    of_cycle = ones_where(iota((CYCLES, rows), 0) == lax.rem(iota((CYCLES, rows), 1), CYCLES))
    per_lane = dot(of_cycle, ones_where(used))
    counts_ref[...] = dot(per_lane.astype(jnp.bfloat16), jnp.ones((CHUNK, LANES), jnp.bfloat16))


def rank_pixels(label, good):
    rows = label.shape[0] // CHUNK * CYCLES
    return pl.pallas_call(
        rank_kernel,
        out_shape=[
            jax.ShapeDtypeStruct((rows, CHUNK), jnp.float32),
            jax.ShapeDtypeStruct((CYCLES, LANES), jnp.float32),
        ],
        in_specs=[VMEM_SPEC, VMEM_SPEC],
        out_specs=[VMEM_SPEC, VMEM_SPEC],
        compiler_params=params(),
        cost_estimate=estimate(6 * rows * CHUNK * CHUNK, 8 * label.shape[0]),
    )(label, good)


def order_kernel(place_ref, key_ref, own_ref, other_ref, *rest, step, mods, parts):
    part_refs, frames_ref = rest[:-1], rest[-1]
    block = own_ref.shape[0]
    chunks = key_ref.shape[0] // CYCLES
    per_cycle = own_ref.shape[1] // CYCLES
    core, mod = place_ref[0], place_ref[2]
    group_cycles = sum(parts)
    first_cycle = (lax.rem(mod + step, mods) * 2 + core) * group_cycles
    frames_ref[pl.ds(pl.multiple_of(core * block, block), block), :] = own_ref[...]
    frames_ref[pl.ds(pl.multiple_of((1 - core) * block, block), block), :] = other_ref[...]
    frames = frames_ref[...]
    slots = [
        (iota((PACKED, CHUNK), 0) + first).astype(jnp.float32).astype(jnp.bfloat16)
        for first in range(0, per_cycle, PACKED)
    ]
    one = jnp.ones((PACKED, CHUNK), jnp.bfloat16)
    zero = jnp.zeros((PACKED, CHUNK), jnp.bfloat16)
    done = 0
    for part_ref, part in zip(part_refs, parts):
        for cycle in range(part):
            tiles = []
            for chunk in range(chunks):
                key = key_ref[pl.ds(chunk * CYCLES + first_cycle + done + cycle, 1), :]
                key = jnp.broadcast_to(key, (PACKED, CHUNK)).astype(jnp.bfloat16)
                tiles.append(
                    jnp.concatenate([jnp.where(key == slot, one, zero) for slot in slots], axis=0)
                )
            picked = lax.dot_general(
                jnp.concatenate(tiles, axis=1),
                frames,
                (((1,), (1,)), ((), ())),
                preferred_element_type=jnp.float32,
            )
            part_ref[cycle * per_cycle : (cycle + 1) * per_cycle, :] = picked.astype(jnp.bfloat16)
        done += part


def order_pixels(place, key, own, other, step, mods, parts):
    block, pix_count = own.shape
    per_cycle = pix_count // CYCLES
    return pl.pallas_call(
        functools.partial(order_kernel, step=step, mods=mods, parts=parts),
        out_shape=[
            jax.ShapeDtypeStruct((part * per_cycle, 2 * block), jnp.bfloat16) for part in parts
        ],
        in_specs=[SMEM_SPEC] + [VMEM_SPEC] * 3,
        out_specs=[VMEM_SPEC] * len(parts),
        scratch_shapes=[pltpu.VMEM((2 * block, pix_count), jnp.bfloat16)],
        compiler_params=params(),
        cost_estimate=estimate(
            4 * sum(parts) * per_cycle * pix_count * block, 4 * pix_count * block
        ),
    )(place, key, own, other)


def gram_kernel(place_ref, counts_ref, *rest, pieces, pairs, choice, frame_count, cycle_step, offset, phase, chained):
    inputs = rest[: (1 + pairs) * pieces]
    mine_ref, theirs_ref, gram, later, earlier = rest[-5:]
    core, chip, mod = place_ref[0], place_ref[1], place_ref[2]
    block = mine_ref.shape[1]
    lags = mine_ref.shape[2]

    def piece_rows(number):
        refs = inputs[number * pieces : (number + 1) * pieces]
        return jnp.concatenate([ref[at] for ref in refs for at in range(ref.shape[0])], axis=0)

    own = piece_rows(0)
    columns = [piece_rows(1 + number) for number in range(pairs)]
    at, even, odd = choice
    chosen = jnp.where(lax.rem(chip, 2) == 0, columns[even], columns[odd])
    columns = [value for number, value in enumerate(columns) if number not in (even, odd)]
    columns.insert(at, chosen)
    if phase == 0:
        columns.insert(0, own)
    whole = jnp.concatenate(columns, axis=1)
    depth, width = whole.shape
    own_rows = own.T
    gram[...] = dot(own_rows, whole)
    sums = dot(jnp.ones((PACKED, depth), jnp.bfloat16), whole)[:SUBLANES]
    frame_at = chip * (2 * block) + phase * lags + iota((SUBLANES, width), 1)
    later[...] = jnp.where(frame_at < frame_count, 1.0 / sums, 0.0)
    cycle = (mod * 2 + core) * cycle_step + offset + pl.program_id(0)
    count = counts_ref[pl.ds(cycle, 1), :]
    earlier[...] = count / dot(own_rows, jnp.ones((depth, LANES), jnp.bfloat16))
    lane, sublane = iota((SUBLANES, LANES), 1), iota((SUBLANES, LANES), 0)
    tiles = lags // LANES
    for out_ref, position in ((mine_ref, core), (theirs_ref, 1 - core)):
        base = pl.multiple_of(position * block, block)
        for first in range(0, block, SUBLANES):
            factor = earlier[pl.ds(base + first, SUBLANES), :]
            kept = lane + sublane < LANES - first
            turned = lax.rem(lane + sublane + first, LANES)
            rolled = []
            for tile in range(tiles + 1):
                column = pl.multiple_of(base + tile * LANES, LANES)
                value = gram[pl.ds(base + first, SUBLANES), pl.ds(column, LANES)]
                value = value * factor * later[:, pl.ds(column, LANES)]
                rolled.append(jnp.take_along_axis(value, turned, axis=1, mode="promise_in_bounds"))
            for tile in range(tiles):
                out_ref[0, first : first + SUBLANES, tile * LANES : (tile + 1) * LANES] = jnp.where(
                    kept, rolled[tile], rolled[tile + 1]
                )


def grams(place, counts, whole, windows, choice, sizes, phase, frame_count):
    group_cycles, cycle_dev, offset, count, per_cycle = sizes
    flat = [piece for pair in windows for piece in pair]
    pieces = len(windows[0])
    chip_block = flat[0][0].shape[-1]
    block = chip_block // 2
    depth = sum(piece.shape[0] for piece, _ in windows[0]) * per_cycle
    lags = LAG // 2
    width = lags + chip_block
    kernel = functools.partial(
        gram_kernel,
        pieces=pieces,
        pairs=len(windows) - 1,
        choice=choice,
        frame_count=frame_count,
        cycle_step=group_cycles,
        offset=offset,
        phase=phase,
        chained=whole is not None,
    )

    def piece_spec(piece, first):
        return pl.BlockSpec(
            (piece.shape[0], per_cycle, chip_block), lambda i, place: (0, first + i, 0)
        )

    in_specs = [pl.BlockSpec((CYCLES, LANES), lambda i, place: (0, 0))]
    in_specs += [piece_spec(piece, first) for piece, first in flat]
    operands = [place, counts] + [piece for piece, _ in flat]
    aliases = {}
    if whole is not None:
        aliases = {len(operands): 0}
        operands.append(whole)
        in_specs.append(ANY_SPEC)
    grid_spec = pltpu.PrefetchScalarGridSpec(
        num_scalar_prefetch=1,
        grid=(count,),
        in_specs=in_specs,
        out_specs=[
            pl.BlockSpec(
                (1, block, lags), lambda i, place: (place[0] * group_cycles + offset + i, 0, phase)
            ),
            pl.BlockSpec((1, block, lags), lambda i, place: (i, 0, 0)),
        ],
        scratch_shapes=[
            pltpu.VMEM((chip_block, width), jnp.float32),
            pltpu.VMEM((SUBLANES, width), jnp.float32),
            pltpu.VMEM((chip_block, LANES), jnp.float32),
        ],
    )
    return pl.pallas_call(
        kernel,
        grid_spec=grid_spec,
        out_shape=[
            jax.ShapeDtypeStruct((cycle_dev, block, LAG), jnp.float32),
            jax.ShapeDtypeStruct((count, block, lags), jnp.float32),
        ],
        input_output_aliases=aliases,
        compiler_params=params(),
        cost_estimate=estimate(
            2 * count * depth * width * chip_block, 8 * count * chip_block * lags
        ),
    )(*operands)


def fill_kernel(place_ref, *rest, spots):
    count = len(spots)
    part_refs, out_ref, sems = rest[:count], rest[-2], rest[-1]
    copies = []
    for number, (part_ref, (group, offset, lag)) in enumerate(zip(part_refs, spots)):
        cycles, _, lags = part_ref.shape
        first = (1 - place_ref[0]) * group + offset
        copies.append(
            pltpu.make_async_copy(
                part_ref,
                out_ref.at[pl.ds(first, cycles), :, pl.ds(lag, lags)],
                sems.at[number],
            )
        )
    for copy in copies:
        copy.start()
    for copy in copies:
        copy.wait()


def fill(place, whole, parts, spots):
    return pl.pallas_call(
        functools.partial(fill_kernel, spots=spots),
        out_shape=jax.ShapeDtypeStruct(whole.shape, whole.dtype),
        in_specs=[SMEM_SPEC] + [ANY_SPEC] * (len(parts) + 1),
        out_specs=ANY_SPEC,
        scratch_shapes=[pltpu.SemaphoreType.DMA((len(parts),))],
        input_output_aliases={1 + len(parts): 0},
        compiler_params=params(),
        cost_estimate=estimate(0, 8 * sum(part.size for part in parts)),
    )(place, *parts, whole)


def shifted(value, pairs_down):
    step = 2 * pairs_down
    count = lax.axis_size("frame")
    return lax.ppermute(value, "frame", [(source, source - step) for source in range(step, count)])


def other_pair(value, parity=None):
    count = lax.axis_size("frame")
    sources = [at for at in range(count) if parity is None or at // 2 % 2 == parity]
    return lax.ppermute(value, "frame", [(source, source ^ 2) for source in sources])


def other_core(value):
    count = lax.axis_size("frame")
    return lax.ppermute(value, "frame", [(source, source ^ 1) for source in range(count)])


def along_mod(value, step):
    mods = lax.axis_size("mod")
    return lax.ppermute(value, "mod", [(mod, (mod + step) % mods) for mod in range(mods)])


def shards(frames, cycle_label, good_pixel):
    mods = lax.axis_size("mod")
    cycle_dev = CYCLES // mods
    group_cycles = cycle_dev // 2
    mod, frame = lax.axis_index("mod"), lax.axis_index("frame")
    core, chip = frame % 2, frame // 2
    block, pix_count = frames.shape
    per_cycle = pix_count // CYCLES
    frame_count = block * lax.axis_size("frame")
    assert LAG == 8 * block and block == LANES
    place = jnp.stack([core, chip, mod]).astype(jnp.int32)
    half = group_cycles // 2
    parts = [half, group_cycles - half] if half else [group_cycles]

    other = other_core(frames)
    key, counts = rank_pixels(cycle_label, good_pixel)
    (first,) = order_pixels(place, key, frames, other, 0, mods, [group_cycles])
    arrived = [[] for _ in parts]
    counted = [counts]
    for step in range(1, mods):
        sent = order_pixels(place, key, frames, other, step, mods, parts)
        for part, value in zip(arrived, sent):
            part.append(along_mod(value, step))
        counted.append(along_mod(counts, step))
    counts = sum(counted)
    units = [first[None]] + [jnp.stack(part) for part in arrived]
    windows = []
    for own in units:
        two = shifted(own, 2)
        four = shifted(two, 2)
        windows.append(
            (own, two, four, other_pair(own, 1), other_pair(two), other_pair(four, 0))
        )
    whole = None
    swapped = {}
    for phase in range(2):
        for number, count in enumerate(parts):
            offset = sum(parts[:number])
            own, two, four, from_own, from_two, from_four = (
                [(early, offset), (late, 0)]
                for early, late in zip(windows[0], windows[1 + number])
            )
            if phase == 0:
                used, choice = [own, two, from_own, from_two], (0, 1, 2)
            else:
                used, choice = [own, two, four, from_two, from_four], (1, 2, 3)
            sizes = (group_cycles, cycle_dev, offset, count, per_cycle)
            whole, theirs = grams(
                place, counts, whole, used, choice, sizes, phase, frame_count
            )
            swapped[phase, number] = other_core(theirs), (group_cycles, offset, phase * LAG // 2)
    values, spots = zip(*swapped.values())
    return fill(place, whole, list(values), list(spots))


def solution(mesh):
    placed = (P("frame", "mod"), P("mod"), P("mod"))
    return jax.shard_map(
        shards, mesh=mesh, in_specs=placed, out_specs=P("mod", "frame", None), check_vma=False
    )
```

time: 350 us -> 90.7 us (0.26)
  waiting for transfers between devices: 219 us -> 33.5 us
  local copies, waits for them, and re-layouts: 73.3 us -> 2.66 us
  starting transfers between devices: 10.3 us -> 31.9 us
  Pallas kernels: 0 us -> 21 us
  matrix products: 13.9 us -> 0 us
  other arithmetic: 13.5 us -> 0.08 us
  between operations: 13.6 us -> 0.18 us
  blocking collectives: 5.12 us -> 0 us
    reduce_scatter x1 -> x0, waiting for transfers between devices: 112 us -> none  [shards(): lax.psum_scatter(jnp.einsum('frc,grc->rfg', weighted, window_three, prefe...]
    ppermute x8 -> x23, waiting for transfers between devices: 82.2 us -> 33.5 us  [the longest x6 24.6 us: shifted(): lax.ppermute(value, 'frame', [(source, source - step) for source in range...]
    gather x4 -> x0, local copies, waits for them, and re-layouts: 35.7 us -> none  [the longest x2 23 us: shards(): sorted_good = jnp.take(good_pixel, ordering, axis=0).astype(jnp.bfloat16)]
    psum x1 -> x0, waiting for transfers between devices: 24.8 us -> none  [shards(): all_sums, all_counts = lax.psum((partial_sums, partial_counts), 'mod')]
    ppermute x8 -> x23, starting transfers between devices: 10.2 us -> 31.9 us  [the longest x9 18.5 us: other_pair(): lax.ppermute(value, 'frame', [(source, source ^ 2) for source in sources])]
    pallas_call x0 -> x8, Pallas kernels: none -> 21 us  [the longest x4 12.5 us: grams(): pl.pallas_call(kernel, grid_spec=grid_spec, out_shape=[jax.ShapeDtypeStru...]
    unnamed x17 -> x6, local copies, waits for them, and re-layouts: 19.4 us -> 2.66 us
    dot_general x2 -> x0, matrix products: 13.9 us -> none  [the longest x1 8.89 us: shards(): jnp.einsum('frc,grc->rfg', weighted, window_three, preferred_element_type...]
  transfers between devices with their start and end apart: 10 -> 23, of which waited for: 9 -> 10; matrix products, arithmetic and copies ran while one was open for 14% -> 0% of each run, Pallas kernels for 0% -> 18%
where the time goes in v2:
time: 90.7 us; the launch traced here: 89.3 us
  waiting for transfers between devices  33.5 us (37%)
  starting transfers between devices  31.9 us (35%)
  Pallas kernels  21 us (23%)
  local copies, waits for them, and re-layouts  2.66 us (3%)
    ppermute x6, waiting for transfers between devices, shifted(): lax.ppermute(value, 'frame', [(source, source - step) for source in range...  24.6 us
    ppermute x9, starting transfers between devices, other_pair(): lax.ppermute(value, 'frame', [(source, source ^ 2) for source in sources])  18.5 us
    pallas_call x4, Pallas kernels, grams(): pl.pallas_call(kernel, grid_spec=grid_spec, out_shape=[jax.ShapeDtypeStru...  12.5 us
    ppermute x6, starting transfers between devices, shifted(): lax.ppermute(value, 'frame', [(source, source - step) for source in range...  7.71 us
    ppermute x9, waiting for transfers between devices, other_pair(): lax.ppermute(value, 'frame', [(source, source ^ 2) for source in sources])  6.23 us
    pallas_call x2, Pallas kernels, order_pixels(): pl.pallas_call(functools.partial(order_kernel, step=step, mods=mods, part...  6.08 us
    ppermute x3, starting transfers between devices, along_mod(): lax.ppermute(value, 'mod', [(mod, (mod + step) % mods) for mod in range(m...  4.77 us
    unnamed x6, local copies, waits for them, and re-layouts  2.66 us
  transfers between devices with their start and end apart: 23, of which 10 were waited for; matrix products, arithmetic and copies ran while one was open for 0% of the time, Pallas kernels for 18%

profile of v2, /device:TPU:0, one launch (start us, length us, event | category | flops | bytes accessed | tf_op | source)
XLA Modules:
  0.0 89.3 jit_solution(10063914014104109919)
XLA Ops:
  0.0 0.5 collective-permute-start.1
  0.5 0.0 copy-start.1
  0.5 0.7 copy-done.1
  1.2 0.0 copy-start.2
  1.2 0.7 copy-done.2
  1.9 0.5 shard_map.37
  2.4 0.1 pad_add_fusion.place_ref
  2.5 0.4 collective-permute-done.1.other_ref
  3.0 0.0 copy-start
  3.0 1.2 %copy-done = bf16[128,4096]{1,0:T(8,128)(2,1)S(1)} copy-done((bf16[128,4096]{1,0:T(8,128)(2,1)S(1)}, bf16[128,4096]{1,0:T(8,128)(2,1)}, u32[]{:S(2)}) %copy-start) | copy-done | bytes 1048600
  4.2 3.0 %shard_map.38 = bf16[1024,256]{1,0:T(8,128)(2,1)S(1)} custom-call(s32[3]{0:T(128)S(1)} %pad_add_fusion.place_ref, f32[256,256]{1,0:T(8,128)S(1)} %get-tuple-element.18.key_ref, bf16[128,4096]{1,0:T(8,128)(2,1)S(1)} %copy-done, bf16[128,4096]{1,0:T(8,128)(2,1)S(1)} %collective-permute-done.1.other_ref), custom_call_target="tpu_custom_call" | custom-call | flops 2147483648 | bytes 2097152 | tf_op jit(solution)/shard_map/pallas_call | solution.py:118
  7.2 1.3 %collective-permute-start.3 = (bf16[1,1024,256]{2,1,0:T(8,128)(2,1)S(1)}, bf16[1,1024,256]{2,1,0:T(8,128)(2,1)S(1)}, u32[]{:S(2)}, u32[]{:S(2)}) collective-permute-start(bf16[1,1024,256]{2,1,0:T(8,128)(2,1)S(1)} %bitcast.6), channel_id=1, source_target_pairs={{8,0},{10,2},{12,4},{14,6},{16,8},{18,10},{20,12},{22,14},{24,16},... | collective-permute-start | bytes 1572872 | tf_op jit(solution)/shard_map/ppermute | solution.py:283
  8.5 1.3 %collective-permute-start.5 = (bf16[1,1024,256]{2,1,0:T(8,128)(2,1)S(1)}, bf16[1,1024,256]{2,1,0:T(8,128)(2,1)S(1)}, u32[]{:S(2)}, u32[]{:S(2)}) collective-permute-start(bf16[1,1024,256]{2,1,0:T(8,128)(2,1)S(1)} %bitcast.7), channel_id=1, source_target_pairs={{4,0},{6,2},{12,8},{14,10},{20,16},{22,18},{28,24},{30,26},{5,1},{... | collective-permute-start | bytes 1572872 | tf_op jit(solution)/shard_map/ppermute | solution.py:289
  9.8 3.0 %shard_map.39 = (bf16[512,256]{1,0:T(8,128)(2,1)S(1)}, bf16[512,256]{1,0:T(8,128)(2,1)S(1)}) custom-call(s32[3]{0:T(128)S(1)} %pad_add_fusion.place_ref, f32[256,256]{1,0:T(8,128)S(1)} %get-tuple-element.18.key_ref, bf16[128,4096]{1,0:T(8,128)(2,1)S(1)} %copy-done, bf16[128,4096]{1,0:T(8,128)(2,1)S(1)} %collective-permute-done.1.other_ref), custom_call_target="tpu_custom_call" | custom-call | flops 2147483648 | bytes 2097152 | tf_op jit(solution)/shard_map/pallas_call | solution.py:118
  12.9 3.0 %collective-permute-start.2 = (bf16[512,256]{1,0:T(8,128)(2,1)S(1)}, bf16[512,256]{1,0:T(8,128)(2,1)S(1)}, u32[]{:S(2)}, u32[]{:S(2)}) collective-permute-start(bf16[512,256]{1,0:T(8,128)(2,1)S(1)} %get-tuple-element.19), channel_id=1, source_target_pairs={{0,1},{1,0},{2,3},{3,2},{4,5},{5,4},{6,7},{7,6},{8,9},{9,8},{10,11... | collective-permute-start | bytes 786440 | tf_op jit(solution)/shard_map/ppermute | solution.py:299
  15.8 0.1 collective-permute-start.10
  15.9 8.4 %collective-permute-done.3.rest_2_ = bf16[1,1024,256]{2,1,0:T(8,128)(2,1)S(1)} collective-permute-done((bf16[1,1024,256]{2,1,0:T(8,128)(2,1)S(1)}, bf16[1,1024,256]{2,1,0:T(8,128)(2,1)S(1)}, u32[]{:S(2)}, u32[]{:S(2)}) %collective-permute-start.3) | collective-permute-done | bytes 524320 | tf_op jit(solution)/shard_map/ppermute | solution.py:283
  24.3 1.3 %collective-permute-start.15 = (bf16[1,1024,256]{2,1,0:T(8,128)(2,1)S(1)}, bf16[1,1024,256]{2,1,0:T(8,128)(2,1)S(1)}, u32[]{:S(2)}, u32[]{:S(2)}) collective-permute-start(bf16[1,1024,256]{2,1,0:T(8,128)(2,1)S(1)} %collective-permute-done.3.rest_2_), channel_id=1, source_target_pairs={{8,0},{10,2},{12,4},{14,6},{16,8},{18,10},{20,12},{22,14},{24,16},... | collective-permute-start | bytes 1572872 | tf_op jit(solution)/shard_map/ppermute | solution.py:283
  25.6 1.7 %collective-permute-start = (f32[16,128]{1,0:T(8,128)S(1)}, f32[16,128]{1,0:T(8,128)S(1)}, u32[]{:S(2)}, u32[]{:S(2)}) collective-permute-start(f32[16,128]{1,0:T(8,128)S(1)} %get-tuple-element.17), channel_id=1, source_target_pairs={{0,1},{1,0},{2,3},{3,2},{4,5},{5,4},{6,7},{7,6},{8,9},{9,8},{10,11... | collective-permute-start | bytes 24584 | tf_op jit(solution)/shard_map/ppermute | solution.py:299
  27.3 0.0 collective-permute-done.2
  27.3 1.3 %collective-permute-start.4 = (bf16[1,512,256]{2,1,0:T(8,128)(2,1)S(1)}, bf16[1,512,256]{2,1,0:T(8,128)(2,1)S(1)}, u32[]{:S(2)}, u32[]{:S(2)}) collective-permute-start(bf16[1,512,256]{2,1,0:T(8,128)(2,1)S(1)} %bitcast.16), channel_id=1, source_target_pairs={{8,0},{10,2},{12,4},{14,6},{16,8},{18,10},{20,12},{22,14},{24,16},... | collective-permute-start | bytes 786440 | tf_op jit(solution)/shard_map/ppermute | solution.py:283
  28.6 0.7 collective-permute-done
  29.3 1.3 %collective-permute-start.6 = (bf16[1,512,256]{2,1,0:T(8,128)(2,1)S(1)}, bf16[1,512,256]{2,1,0:T(8,128)(2,1)S(1)}, u32[]{:S(2)}, u32[]{:S(2)}) collective-permute-start(bf16[1,512,256]{2,1,0:T(8,128)(2,1)S(1)} %bitcast.17), channel_id=1, source_target_pairs={{4,0},{6,2},{12,8},{14,10},{20,16},{22,18},{28,24},{30,26},{5,1},{... | collective-permute-start | bytes 786440 | tf_op jit(solution)/shard_map/ppermute | solution.py:289
  30.6 0.0 collective-permute-done.10
  30.6 1.3 %collective-permute-start.11 = (bf16[1,512,256]{2,1,0:T(8,128)(2,1)S(1)}, bf16[1,512,256]{2,1,0:T(8,128)(2,1)S(1)}, u32[]{:S(2)}, u32[]{:S(2)}) collective-permute-start(bf16[1,512,256]{2,1,0:T(8,128)(2,1)S(1)} %bitcast.12), channel_id=1, source_target_pairs={{8,0},{10,2},{12,4},{14,6},{16,8},{18,10},{20,12},{22,14},{24,16},... | collective-permute-start | bytes 786440 | tf_op jit(solution)/shard_map/ppermute | solution.py:283
  31.9 0.0 collective-permute-done.5.rest_4_
  31.9 2.7 %collective-permute-start.7 = (bf16[1,1024,256]{2,1,0:T(8,128)(2,1)S(1)}, bf16[1,1024,256]{2,1,0:T(8,128)(2,1)S(1)}, u32[]{:S(2)}, u32[]{:S(2)}) collective-permute-start(bf16[1,1024,256]{2,1,0:T(8,128)(2,1)S(1)} %collective-permute-done.3.rest_2_), channel_id=1, source_target_pairs={{0,4},{2,6},{4,0},{6,2},{8,12},{10,14},{12,8},{14,10},{16,20},{18,... | collective-permute-start | bytes 1572872 | tf_op jit(solution)/shard_map/ppermute | solution.py:289
  34.6 12.0 %collective-permute-done.4.rest_3_ = bf16[1,512,256]{2,1,0:T(8,128)(2,1)S(1)} collective-permute-done((bf16[1,512,256]{2,1,0:T(8,128)(2,1)S(1)}, bf16[1,512,256]{2,1,0:T(8,128)(2,1)S(1)}, u32[]{:S(2)}, u32[]{:S(2)}) %collective-permute-start.4) | collective-permute-done | bytes 262176 | tf_op jit(solution)/shard_map/ppermute | solution.py:283
  46.6 1.7 %collective-permute-start.8 = (bf16[1,512,256]{2,1,0:T(8,128)(2,1)S(1)}, bf16[1,512,256]{2,1,0:T(8,128)(2,1)S(1)}, u32[]{:S(2)}, u32[]{:S(2)}) collective-permute-start(bf16[1,512,256]{2,1,0:T(8,128)(2,1)S(1)} %collective-permute-done.4.rest_3_), channel_id=1, source_target_pairs={{0,4},{2,6},{4,0},{6,2},{8,12},{10,14},{12,8},{14,10},{16,20},{18,... | collective-permute-start | bytes 786440 | tf_op jit(solution)/shard_map/ppermute | solution.py:289
  48.3 0.0 collective-permute-done.6.rest_5_
  48.3 1.3 %collective-permute-start.16 = (bf16[1,512,256]{2,1,0:T(8,128)(2,1)S(1)}, bf16[1,512,256]{2,1,0:T(8,128)(2,1)S(1)}, u32[]{:S(2)}, u32[]{:S(2)}) collective-permute-start(bf16[1,512,256]{2,1,0:T(8,128)(2,1)S(1)} %collective-permute-done.4.rest_3_), channel_id=1, source_target_pairs={{8,0},{10,2},{12,4},{14,6},{16,8},{18,10},{20,12},{22,14},{24,16},... | collective-permute-start | bytes 786440 | tf_op jit(solution)/shard_map/ppermute | solution.py:283
  49.6 2.7 %collective-permute-done.11.rest_3_ = bf16[1,512,256]{2,1,0:T(8,128)(2,1)S(1)} collective-permute-done((bf16[1,512,256]{2,1,0:T(8,128)(2,1)S(1)}, bf16[1,512,256]{2,1,0:T(8,128)(2,1)S(1)}, u32[]{:S(2)}, u32[]{:S(2)}) %collective-permute-start.11) | collective-permute-done | bytes 262176 | tf_op jit(solution)/shard_map/ppermute | solution.py:283
  52.3 1.3 %collective-permute-start.20 = (bf16[1,512,256]{2,1,0:T(8,128)(2,1)S(1)}, bf16[1,512,256]{2,1,0:T(8,128)(2,1)S(1)}, u32[]{:S(2)}, u32[]{:S(2)}) collective-permute-start(bf16[1,512,256]{2,1,0:T(8,128)(2,1)S(1)} %collective-permute-done.11.rest_3_), channel_id=1, source_target_pairs={{8,0},{10,2},{12,4},{14,6},{16,8},{18,10},{20,12},{22,14},{24,16},... | collective-permute-start | bytes 786440 | tf_op jit(solution)/shard_map/ppermute | solution.py:283
  53.5 0.0 collective-permute-done.15.rest_4_
  53.5 3.6 %collective-permute-start.17 = (bf16[1,1024,256]{2,1,0:T(8,128)(2,1)S(1)}, bf16[1,1024,256]{2,1,0:T(8,128)(2,1)S(1)}, u32[]{:S(2)}, u32[]{:S(2)}) collective-permute-start(bf16[1,1024,256]{2,1,0:T(8,128)(2,1)S(1)} %collective-permute-done.15.rest_4_), channel_id=1, source_target_pairs={{0,4},{2,6},{8,12},{10,14},{16,20},{18,22},{24,28},{26,30},{1,5},{... | collective-permute-start | bytes 1572872 | tf_op jit(solution)/shard_map/ppermute | solution.py:289
  57.2 0.0 collective-permute-done.8.rest_7_
  57.2 1.3 %collective-permute-start.12 = (bf16[1,512,256]{2,1,0:T(8,128)(2,1)S(1)}, bf16[1,512,256]{2,1,0:T(8,128)(2,1)S(1)}, u32[]{:S(2)}, u32[]{:S(2)}) collective-permute-start(bf16[1,512,256]{2,1,0:T(8,128)(2,1)S(1)} %bitcast.13), channel_id=1, source_target_pairs={{4,0},{6,2},{12,8},{14,10},{20,16},{22,18},{28,24},{30,26},{5,1},{... | collective-permute-start | bytes 786440 | tf_op jit(solution)/shard_map/ppermute | solution.py:289
  58.5 0.6 collective-permute-done.16.rest_5_
  59.0 2.2 %collective-permute-start.13 = (bf16[1,512,256]{2,1,0:T(8,128)(2,1)S(1)}, bf16[1,512,256]{2,1,0:T(8,128)(2,1)S(1)}, u32[]{:S(2)}, u32[]{:S(2)}) collective-permute-start(bf16[1,512,256]{2,1,0:T(8,128)(2,1)S(1)} %collective-permute-done.11.rest_3_), channel_id=1, source_target_pairs={{0,4},{2,6},{4,0},{6,2},{8,12},{10,14},{12,8},{14,10},{16,20},{18,... | collective-permute-start | bytes 786440 | tf_op jit(solution)/shard_map/ppermute | solution.py:289
  61.2 1.0 %collective-permute-done.20.rest_5_ = bf16[1,512,256]{2,1,0:T(8,128)(2,1)S(1)} collective-permute-done((bf16[1,512,256]{2,1,0:T(8,128)(2,1)S(1)}, bf16[1,512,256]{2,1,0:T(8,128)(2,1)S(1)}, u32[]{:S(2)}, u32[]{:S(2)}) %collective-permute-start.20) | collective-permute-done | bytes 262176 | tf_op jit(solution)/shard_map/ppermute | solution.py:283
  62.2 3.2 %collective-permute-start.18 = (bf16[1,512,256]{2,1,0:T(8,128)(2,1)S(1)}, bf16[1,512,256]{2,1,0:T(8,128)(2,1)S(1)}, u32[]{:S(2)}, u32[]{:S(2)}) collective-permute-start(bf16[1,512,256]{2,1,0:T(8,128)(2,1)S(1)} %collective-permute-done.16.rest_5_), channel_id=1, source_target_pairs={{0,4},{2,6},{8,12},{10,14},{16,20},{18,22},{24,28},{26,30},{1,5},{... | collective-permute-start | bytes 786440 | tf_op jit(solution)/shard_map/ppermute | solution.py:289
  65.3 0.0 collective-permute-done.7.rest_6_
  65.4 1.3 %collective-permute-start.21 = (bf16[1,512,256]{2,1,0:T(8,128)(2,1)S(1)}, bf16[1,512,256]{2,1,0:T(8,128)(2,1)S(1)}, u32[]{:S(2)}, u32[]{:S(2)}) collective-permute-start(bf16[1,512,256]{2,1,0:T(8,128)(2,1)S(1)} %collective-permute-done.20.rest_5_), channel_id=1, source_target_pairs={{0,4},{2,6},{8,12},{10,14},{16,20},{18,22},{24,28},{26,30},{1,5},{... | collective-permute-start | bytes 786440 | tf_op jit(solution)/shard_map/ppermute | solution.py:289
  66.7 3.1 %shard_map.40 = (f32[8,128,1024]{2,1,0:T(8,128)}, f32[2,128,512]{2,1,0:T(8,128)S(1)}) custom-call(s32[3]{0:T(128)S(1)} %pad_add_fusion.place_ref, f32[16,128]{1,0:T(8,128)S(1)} %add.9.counts_ref, bf16[1,1024,256]{2,1,0:T(8,128)(2,1)S(1)} %bitcast.8, bf16[1,512,256]{2,1,0:T(8,128)(2,1)S(1)} %bitcast.18, ...), custom_call_target="tpu_custom_call" | custom-call | flops 402653184 | bytes 2097152 | tf_op jit(solution)/shard_map/pallas_call | solution.py:232
  69.8 0.0 collective-permute-done.12.rest_5_
  69.8 0.0 collective-permute-start.9
  69.8 5.3 %collective-permute-done.13.rest_7_ = bf16[1,512,256]{2,1,0:T(8,128)(2,1)S(1)} collective-permute-done((bf16[1,512,256]{2,1,0:T(8,128)(2,1)S(1)}, bf16[1,512,256]{2,1,0:T(8,128)(2,1)S(1)}, u32[]{:S(2)}, u32[]{:S(2)}) %collective-permute-start.13) | collective-permute-done | bytes 262176 | tf_op jit(solution)/shard_map/ppermute | solution.py:289
  75.1 3.1 %shard_map.41 = (f32[8,128,1024]{2,1,0:T(8,128)}, f32[2,128,512]{2,1,0:T(8,128)S(1)}) custom-call(s32[3]{0:T(128)S(1)} %pad_add_fusion.place_ref, f32[16,128]{1,0:T(8,128)S(1)} %add.9.counts_ref, bf16[1,1024,256]{2,1,0:T(8,128)(2,1)S(1)} %bitcast.9, bf16[1,512,256]{2,1,0:T(8,128)(2,1)S(1)} %bitcast.14, ...), custom_call_target="tpu_custom_call", output_to_operand_aliasing={{0}: (10, {})} | custom-call | flops 402653184 | bytes 2097152 | tf_op jit(solution)/shard_map/pallas_call | solution.py:232
  78.2 0.0 collective-permute-start.14
  78.2 0.9 %collective-permute-done.18.rest_9_ = bf16[1,512,256]{2,1,0:T(8,128)(2,1)S(1)} collective-permute-done((bf16[1,512,256]{2,1,0:T(8,128)(2,1)S(1)}, bf16[1,512,256]{2,1,0:T(8,128)(2,1)S(1)}, u32[]{:S(2)}, u32[]{:S(2)}) %collective-permute-start.18) | collective-permute-done | bytes 262176 | tf_op jit(solution)/shard_map/ppermute | solution.py:289
  79.2 0.0 collective-permute-done.17.rest_8_
  79.2 3.1 %shard_map.42 = (f32[8,128,1024]{2,1,0:T(8,128)}, f32[2,128,512]{2,1,0:T(8,128)S(1)}) custom-call(s32[3]{0:T(128)S(1)} %pad_add_fusion.place_ref, f32[16,128]{1,0:T(8,128)S(1)} %add.9.counts_ref, bf16[1,1024,256]{2,1,0:T(8,128)(2,1)S(1)} %bitcast.10, bf16[1,512,256]{2,1,0:T(8,128)(2,1)S(1)} %bitcast.19, ...), custom_call_target="tpu_custom_call", output_to_operand_aliasing={{0}: (12, {})} | custom-call | flops 402653184 | bytes 2097152 | tf_op jit(solution)/shard_map/pallas_call | solution.py:232
  82.3 0.0 collective-permute-start.19
  82.3 0.0 collective-permute-done.21.rest_9_
  82.3 3.1 %shard_map.43 = (f32[8,128,1024]{2,1,0:T(8,128)}, f32[2,128,512]{2,1,0:T(8,128)S(1)}) custom-call(s32[3]{0:T(128)S(1)} %pad_add_fusion.place_ref, f32[16,128]{1,0:T(8,128)S(1)} %add.9.counts_ref, bf16[1,1024,256]{2,1,0:T(8,128)(2,1)S(1)} %bitcast.11, bf16[1,512,256]{2,1,0:T(8,128)(2,1)S(1)} %bitcast.15, ...), custom_call_target="tpu_custom_call", output_to_operand_aliasing={{0}: (12, {})} | custom-call | flops 402653184 | bytes 2097152 | tf_op jit(solution)/shard_map/pallas_call | solution.py:232
  85.4 0.5 collective-permute-start.22
  85.9 0.0 collective-permute-done.9.rest_0_
  85.9 0.0 collective-permute-done.14.rest_1_
  85.9 0.0 collective-permute-done.19.rest_2_
  85.9 1.5 %collective-permute-done.22.rest_3_ = f32[2,128,512]{2,1,0:T(8,128)S(1)} collective-permute-done((f32[2,128,512]{2,1,0:T(8,128)S(1)}, f32[2,128,512]{2,1,0:T(8,128)S(1)}, u32[]{:S(2)}, u32[]{:S(2)}) %collective-permute-start.22) | collective-permute-done | bytes 524320 | tf_op jit(solution)/shard_map/ppermute | solution.py:294
  87.4 1.9 %shard_map.44 = f32[8,128,1024]{2,1,0:T(8,128)} custom-call(s32[3]{0:T(128)S(1)} %pad_add_fusion.place_ref, f32[2,128,512]{2,1,0:T(8,128)S(1)} %collective-permute-done.9.rest_0_, f32[2,128,512]{2,1,0:T(8,128)S(1)} %collective-permute-done.14.rest_1_, f32[2,128,512]{2,1,0:T(8,128)S(1)} %collective-permute-done.19.rest_2_, ...), custom_call_target="tpu_custom_call", output_to_operand_aliasing={{}: (5, {})} | custom-call | bytes 4194304 | tf_op jit(solution)/shard_map/pallas_call | solution.py:268
  (1 shorter events, 0.0 us)
Async XLA Ops:
  0.0 3.0 %collective-permute-start.1 = (bf16[128,4096]{1,0:T(8,128)(2,1)}, bf16[128,4096]{1,0:T(8,128)(2,1)S(1)}, u32[]{:S(2)}, u32[]{:S(2)}) collective-permute-start(bf16[128,4096]{1,0:T(8,128)(2,1)} %own_ref.3), channel_id=1, source_target_pairs={{0,2},{2,0},{4,6},{6,4},{8,10},{10,8},{12,14},{14,12},{16,18},{18,... | collective-permute-start | bytes 3145736 | tf_op jit(solution)/shard_map/ppermute | solution.py:294
  0.5 0.7 copy-start.1
  1.2 0.7 copy-start.2
  3.0 1.2 %copy-start = (bf16[128,4096]{1,0:T(8,128)(2,1)S(1)}, bf16[128,4096]{1,0:T(8,128)(2,1)}, u32[]{:S(2)}) copy-start(bf16[128,4096]{1,0:T(8,128)(2,1)} %own_ref.3) | copy-start | bytes 3145732
  7.2 17.1 %collective-permute-start.3 = (bf16[1,1024,256]{2,1,0:T(8,128)(2,1)S(1)}, bf16[1,1024,256]{2,1,0:T(8,128)(2,1)S(1)}, u32[]{:S(2)}, u32[]{:S(2)}) collective-permute-start(bf16[1,1024,256]{2,1,0:T(8,128)(2,1)S(1)} %bitcast.6), channel_id=1, source_target_pairs={{8,0},{10,2},{12,4},{14,6},{16,8},{18,10},{20,12},{22,14},{24,16},... | collective-permute-start | bytes 1572872 | tf_op jit(solution)/shard_map/ppermute | solution.py:283
  8.5 23.4 %collective-permute-start.5 = (bf16[1,1024,256]{2,1,0:T(8,128)(2,1)S(1)}, bf16[1,1024,256]{2,1,0:T(8,128)(2,1)S(1)}, u32[]{:S(2)}, u32[]{:S(2)}) collective-permute-start(bf16[1,1024,256]{2,1,0:T(8,128)(2,1)S(1)} %bitcast.7), channel_id=1, source_target_pairs={{4,0},{6,2},{12,8},{14,10},{20,16},{22,18},{28,24},{30,26},{5,1},{... | collective-permute-start | bytes 1572872 | tf_op jit(solution)/shard_map/ppermute | solution.py:289
  12.9 14.5 %collective-permute-start.2 = (bf16[512,256]{1,0:T(8,128)(2,1)S(1)}, bf16[512,256]{1,0:T(8,128)(2,1)S(1)}, u32[]{:S(2)}, u32[]{:S(2)}) collective-permute-start(bf16[512,256]{1,0:T(8,128)(2,1)S(1)} %get-tuple-element.19), channel_id=1, source_target_pairs={{0,1},{1,0},{2,3},{3,2},{4,5},{5,4},{6,7},{7,6},{8,9},{9,8},{10,11... | collective-permute-start | bytes 786440 | tf_op jit(solution)/shard_map/ppermute | solution.py:299
  15.8 14.8 %collective-permute-start.10 = (bf16[512,256]{1,0:T(8,128)(2,1)S(1)}, bf16[512,256]{1,0:T(8,128)(2,1)S(1)}, u32[]{:S(2)}, u32[]{:S(2)}) collective-permute-start(bf16[512,256]{1,0:T(8,128)(2,1)S(1)} %get-tuple-element.21), channel_id=1, source_target_pairs={{0,1},{1,0},{2,3},{3,2},{4,5},{5,4},{6,7},{7,6},{8,9},{9,8},{10,11... | collective-permute-start | bytes 786440 | tf_op jit(solution)/shard_map/ppermute | solution.py:299
  24.3 29.2 %collective-permute-start.15 = (bf16[1,1024,256]{2,1,0:T(8,128)(2,1)S(1)}, bf16[1,1024,256]{2,1,0:T(8,128)(2,1)S(1)}, u32[]{:S(2)}, u32[]{:S(2)}) collective-permute-start(bf16[1,1024,256]{2,1,0:T(8,128)(2,1)S(1)} %collective-permute-done.3.rest_2_), channel_id=1, source_target_pairs={{8,0},{10,2},{12,4},{14,6},{16,8},{18,10},{20,12},{22,14},{24,16},... | collective-permute-start | bytes 1572872 | tf_op jit(solution)/shard_map/ppermute | solution.py:283
  25.6 3.7 %collective-permute-start = (f32[16,128]{1,0:T(8,128)S(1)}, f32[16,128]{1,0:T(8,128)S(1)}, u32[]{:S(2)}, u32[]{:S(2)}) collective-permute-start(f32[16,128]{1,0:T(8,128)S(1)} %get-tuple-element.17), channel_id=1, source_target_pairs={{0,1},{1,0},{2,3},{3,2},{4,5},{5,4},{6,7},{7,6},{8,9},{9,8},{10,11... | collective-permute-start | bytes 24584 | tf_op jit(solution)/shard_map/ppermute | solution.py:299
  27.3 19.3 %collective-permute-start.4 = (bf16[1,512,256]{2,1,0:T(8,128)(2,1)S(1)}, bf16[1,512,256]{2,1,0:T(8,128)(2,1)S(1)}, u32[]{:S(2)}, u32[]{:S(2)}) collective-permute-start(bf16[1,512,256]{2,1,0:T(8,128)(2,1)S(1)} %bitcast.16), channel_id=1, source_target_pairs={{8,0},{10,2},{12,4},{14,6},{16,8},{18,10},{20,12},{22,14},{24,16},... | collective-permute-start | bytes 786440 | tf_op jit(solution)/shard_map/ppermute | solution.py:283
  29.3 19.0 %collective-permute-start.6 = (bf16[1,512,256]{2,1,0:T(8,128)(2,1)S(1)}, bf16[1,512,256]{2,1,0:T(8,128)(2,1)S(1)}, u32[]{:S(2)}, u32[]{:S(2)}) collective-permute-start(bf16[1,512,256]{2,1,0:T(8,128)(2,1)S(1)} %bitcast.17), channel_id=1, source_target_pairs={{4,0},{6,2},{12,8},{14,10},{20,16},{22,18},{28,24},{30,26},{5,1},{... | collective-permute-start | bytes 786440 | tf_op jit(solution)/shard_map/ppermute | solution.py:289
  30.6 21.7 %collective-permute-start.11 = (bf16[1,512,256]{2,1,0:T(8,128)(2,1)S(1)}, bf16[1,512,256]{2,1,0:T(8,128)(2,1)S(1)}, u32[]{:S(2)}, u32[]{:S(2)}) collective-permute-start(bf16[1,512,256]{2,1,0:T(8,128)(2,1)S(1)} %bitcast.12), channel_id=1, source_target_pairs={{8,0},{10,2},{12,4},{14,6},{16,8},{18,10},{20,12},{22,14},{24,16},... | collective-permute-start | bytes 786440 | tf_op jit(solution)/shard_map/ppermute | solution.py:283
  31.9 33.4 %collective-permute-start.7 = (bf16[1,1024,256]{2,1,0:T(8,128)(2,1)S(1)}, bf16[1,1024,256]{2,1,0:T(8,128)(2,1)S(1)}, u32[]{:S(2)}, u32[]{:S(2)}) collective-permute-start(bf16[1,1024,256]{2,1,0:T(8,128)(2,1)S(1)} %collective-permute-done.3.rest_2_), channel_id=1, source_target_pairs={{0,4},{2,6},{4,0},{6,2},{8,12},{10,14},{12,8},{14,10},{16,20},{18,... | collective-permute-start | bytes 1572872 | tf_op jit(solution)/shard_map/ppermute | solution.py:289
  46.6 10.5 %collective-permute-start.8 = (bf16[1,512,256]{2,1,0:T(8,128)(2,1)S(1)}, bf16[1,512,256]{2,1,0:T(8,128)(2,1)S(1)}, u32[]{:S(2)}, u32[]{:S(2)}) collective-permute-start(bf16[1,512,256]{2,1,0:T(8,128)(2,1)S(1)} %collective-permute-done.4.rest_3_), channel_id=1, source_target_pairs={{0,4},{2,6},{4,0},{6,2},{8,12},{10,14},{12,8},{14,10},{16,20},{18,... | collective-permute-start | bytes 786440 | tf_op jit(solution)/shard_map/ppermute | solution.py:289
  48.3 10.7 %collective-permute-start.16 = (bf16[1,512,256]{2,1,0:T(8,128)(2,1)S(1)}, bf16[1,512,256]{2,1,0:T(8,128)(2,1)S(1)}, u32[]{:S(2)}, u32[]{:S(2)}) collective-permute-start(bf16[1,512,256]{2,1,0:T(8,128)(2,1)S(1)} %collective-permute-done.4.rest_3_), channel_id=1, source_target_pairs={{8,0},{10,2},{12,4},{14,6},{16,8},{18,10},{20,12},{22,14},{24,16},... | collective-permute-start | bytes 786440 | tf_op jit(solution)/shard_map/ppermute | solution.py:283
  52.3 9.9 %collective-permute-start.20 = (bf16[1,512,256]{2,1,0:T(8,128)(2,1)S(1)}, bf16[1,512,256]{2,1,0:T(8,128)(2,1)S(1)}, u32[]{:S(2)}, u32[]{:S(2)}) collective-permute-start(bf16[1,512,256]{2,1,0:T(8,128)(2,1)S(1)} %collective-permute-done.11.rest_3_), channel_id=1, source_target_pairs={{8,0},{10,2},{12,4},{14,6},{16,8},{18,10},{20,12},{22,14},{24,16},... | collective-permute-start | bytes 786440 | tf_op jit(solution)/shard_map/ppermute | solution.py:283
  53.5 25.6 %collective-permute-start.17 = (bf16[1,1024,256]{2,1,0:T(8,128)(2,1)S(1)}, bf16[1,1024,256]{2,1,0:T(8,128)(2,1)S(1)}, u32[]{:S(2)}, u32[]{:S(2)}) collective-permute-start(bf16[1,1024,256]{2,1,0:T(8,128)(2,1)S(1)} %collective-permute-done.15.rest_4_), channel_id=1, source_target_pairs={{0,4},{2,6},{8,12},{10,14},{16,20},{18,22},{24,28},{26,30},{1,5},{... | collective-permute-start | bytes 1572872 | tf_op jit(solution)/shard_map/ppermute | solution.py:289
  57.2 12.6 %collective-permute-start.12 = (bf16[1,512,256]{2,1,0:T(8,128)(2,1)S(1)}, bf16[1,512,256]{2,1,0:T(8,128)(2,1)S(1)}, u32[]{:S(2)}, u32[]{:S(2)}) collective-permute-start(bf16[1,512,256]{2,1,0:T(8,128)(2,1)S(1)} %bitcast.13), channel_id=1, source_target_pairs={{4,0},{6,2},{12,8},{14,10},{20,16},{22,18},{28,24},{30,26},{5,1},{... | collective-permute-start | bytes 786440 | tf_op jit(solution)/shard_map/ppermute | solution.py:289
  59.0 16.1 %collective-permute-start.13 = (bf16[1,512,256]{2,1,0:T(8,128)(2,1)S(1)}, bf16[1,512,256]{2,1,0:T(8,128)(2,1)S(1)}, u32[]{:S(2)}, u32[]{:S(2)}) collective-permute-start(bf16[1,512,256]{2,1,0:T(8,128)(2,1)S(1)} %collective-permute-done.11.rest_3_), channel_id=1, source_target_pairs={{0,4},{2,6},{4,0},{6,2},{8,12},{10,14},{12,8},{14,10},{16,20},{18,... | collective-permute-start | bytes 786440 | tf_op jit(solution)/shard_map/ppermute | solution.py:289
  62.2 17.0 %collective-permute-start.18 = (bf16[1,512,256]{2,1,0:T(8,128)(2,1)S(1)}, bf16[1,512,256]{2,1,0:T(8,128)(2,1)S(1)}, u32[]{:S(2)}, u32[]{:S(2)}) collective-permute-start(bf16[1,512,256]{2,1,0:T(8,128)(2,1)S(1)} %collective-permute-done.16.rest_5_), channel_id=1, source_target_pairs={{0,4},{2,6},{8,12},{10,14},{16,20},{18,22},{24,28},{26,30},{1,5},{... | collective-permute-start | bytes 786440 | tf_op jit(solution)/shard_map/ppermute | solution.py:289
  65.4 16.9 %collective-permute-start.21 = (bf16[1,512,256]{2,1,0:T(8,128)(2,1)S(1)}, bf16[1,512,256]{2,1,0:T(8,128)(2,1)S(1)}, u32[]{:S(2)}, u32[]{:S(2)}) collective-permute-start(bf16[1,512,256]{2,1,0:T(8,128)(2,1)S(1)} %collective-permute-done.20.rest_5_), channel_id=1, source_target_pairs={{0,4},{2,6},{8,12},{10,14},{16,20},{18,22},{24,28},{26,30},{1,5},{... | collective-permute-start | bytes 786440 | tf_op jit(solution)/shard_map/ppermute | solution.py:289
  69.8 16.1 %collective-permute-start.9 = (f32[2,128,512]{2,1,0:T(8,128)S(1)}, f32[2,128,512]{2,1,0:T(8,128)S(1)}, u32[]{:S(2)}, u32[]{:S(2)}) collective-permute-start(f32[2,128,512]{2,1,0:T(8,128)S(1)} %get-tuple-element.20), channel_id=1, source_target_pairs={{0,2},{2,0},{4,6},{6,4},{8,10},{10,8},{12,14},{14,12},{16,18},{18,... | collective-permute-start | bytes 1572872 | tf_op jit(solution)/shard_map/ppermute | solution.py:294
  78.2 7.7 %collective-permute-start.14 = (f32[2,128,512]{2,1,0:T(8,128)S(1)}, f32[2,128,512]{2,1,0:T(8,128)S(1)}, u32[]{:S(2)}, u32[]{:S(2)}) collective-permute-start(f32[2,128,512]{2,1,0:T(8,128)S(1)} %get-tuple-element.23), channel_id=1, source_target_pairs={{0,2},{2,0},{4,6},{6,4},{8,10},{10,8},{12,14},{14,12},{16,18},{18,... | collective-permute-start | bytes 1572872 | tf_op jit(solution)/shard_map/ppermute | solution.py:294
  82.3 3.6 %collective-permute-start.19 = (f32[2,128,512]{2,1,0:T(8,128)S(1)}, f32[2,128,512]{2,1,0:T(8,128)S(1)}, u32[]{:S(2)}, u32[]{:S(2)}) collective-permute-start(f32[2,128,512]{2,1,0:T(8,128)S(1)} %get-tuple-element.25), channel_id=1, source_target_pairs={{0,2},{2,0},{4,6},{6,4},{8,10},{10,8},{12,14},{14,12},{16,18},{18,... | collective-permute-start | bytes 1572872 | tf_op jit(solution)/shard_map/ppermute | solution.py:294
  85.4 2.0 %collective-permute-start.22 = (f32[2,128,512]{2,1,0:T(8,128)S(1)}, f32[2,128,512]{2,1,0:T(8,128)S(1)}, u32[]{:S(2)}, u32[]{:S(2)}) collective-permute-start(f32[2,128,512]{2,1,0:T(8,128)S(1)} %get-tuple-element.27), channel_id=1, source_target_pairs={{0,2},{2,0},{4,6},{6,4},{8,10},{10,8},{12,14},{14,12},{16,18},{18,... | collective-permute-start | bytes 1572872 | tf_op jit(solution)/shard_map/ppermute | solution.py:294

commit v3 on v2

v3 whole, which is shorter than its diff:
```python
import functools

import jax
import jax.numpy as jnp
from jax import lax
from jax.experimental import pallas as pl
from jax.experimental.pallas import tpu as pltpu
from jax.sharding import PartitionSpec as P

CYCLES = 16
LAG = 1024
LANES = 128
SUBLANES = 8
PACKED = 16
CHUNK = 256
VMEM_LIMIT = 24 * 1024 * 1024

TIES = {
    "z2": ("z0",),
    "w0": ("z1",),
    "z3": ("z2",),
    "w1": ("w0",),
    "w2": ("z3",),
    "w3": ("w1",),
    "x2": ("x0", "o0"),
    "v0": ("x1",),
    "x3": ("x2", "o1"),
    "v1": ("v0",),
    "v2": ("x3",),
    "v3": ("v1",),
    "o1": ("y1",),
    "g00": ("v1",),
    "g01": ("w3", "v1"),
}
OWN_SPLIT = True

SMEM_SPEC = pl.BlockSpec(memory_space=pltpu.SMEM)
VMEM_SPEC = pl.BlockSpec(memory_space=pltpu.VMEM)
HBM_SPEC = pl.BlockSpec(memory_space=pltpu.HBM)
ANY_SPEC = pl.BlockSpec(memory_space=pl.ANY)

dot = functools.partial(jnp.dot, preferred_element_type=jnp.float32)


def params():
    return pltpu.CompilerParams(vmem_limit_bytes=VMEM_LIMIT)


def estimate(flops, moved):
    return pl.CostEstimate(flops=flops, bytes_accessed=moved, transcendentals=0)


def ones_where(condition):
    return jnp.where(condition, 1.0, 0.0).astype(jnp.bfloat16)


def iota(shape, dimension):
    return lax.broadcasted_iota(jnp.int32, shape, dimension)


def rank_kernel(label_ref, frames_hbm, key_ref, counts_ref, frames_ref, sem):
    copy = pltpu.make_async_copy(frames_hbm, frames_ref, sem)
    copy.start()
    chunks = label_ref.shape[0] // CHUNK
    rows = chunks * CYCLES
    up, across = iota((rows, rows), 0), iota((rows, rows), 1)
    same = lax.rem(up, CYCLES) == lax.rem(across, CYCLES)
    chunk_before = ones_where(same & (across < up))
    before = ones_where(iota((CHUNK, CHUNK), 0) < iota((CHUNK, CHUNK), 1))
    of_cycle = ones_where(iota((CYCLES, rows), 0) == lax.rem(iota((CYCLES, rows), 1), CYCLES))
    cycle_at = iota((CYCLES, CHUNK), 0)
    labels = [label_ref[pl.ds(at * CHUNK, CHUNK)].reshape(1, CHUNK) for at in range(chunks)]
    used = jnp.concatenate([jnp.where(one == cycle_at, 1.0, 0.0) for one in labels], axis=0)
    member = used.astype(jnp.bfloat16)
    earlier = dot(chunk_before, member).astype(jnp.bfloat16)
    rank = dot(member, before) + dot(earlier, jnp.ones((CHUNK, CHUNK), jnp.bfloat16))
    key_ref[...] = jnp.where(used > 0.0, rank, -1.0)
    per_lane = dot(of_cycle, member).astype(jnp.bfloat16)
    counts_ref[...] = dot(per_lane, jnp.ones((CHUNK, LANES), jnp.bfloat16))
    copy.wait()


def rank_pixels(label, frames):
    rows = label.shape[0] // CHUNK * CYCLES
    return pl.pallas_call(
        rank_kernel,
        out_shape=[
            jax.ShapeDtypeStruct((rows, CHUNK), jnp.float32),
            jax.ShapeDtypeStruct((CYCLES, LANES), jnp.float32),
            jax.ShapeDtypeStruct(frames.shape, frames.dtype),
        ],
        in_specs=[VMEM_SPEC, HBM_SPEC],
        out_specs=[VMEM_SPEC] * 3,
        scratch_shapes=[pltpu.SemaphoreType.DMA],
        compiler_params=params(),
        cost_estimate=estimate(6 * rows * CHUNK * CHUNK, 8 * label.shape[0]),
    )(label, pltpu.with_memory_space_constraint(frames, pltpu.HBM))


def order_kernel(place_ref, key_ref, *rest, step, mods, parts, joined):
    rest = list(rest)
    core, mod = place_ref[0], place_ref[2]
    if joined:
        frames_ref = rest.pop(0)
    else:
        own_ref, other_ref, frames_ref = rest.pop(0), rest.pop(0), rest.pop()
        block = own_ref.shape[0]
        frames_ref[pl.ds(pl.multiple_of(core * block, block), block), :] = own_ref[...]
        frames_ref[pl.ds(pl.multiple_of((1 - core) * block, block), block), :] = other_ref[...]
    frames = frames_ref[...]
    all_ref, part_refs = rest[0], rest[1:]
    chunks = key_ref.shape[0] // CYCLES
    per_cycle = frames.shape[1] // CYCLES
    first_cycle = (lax.rem(mod + step, mods) * 2 + core) * sum(parts)
    slots = [
        (iota((PACKED, CHUNK), 0) + first).astype(jnp.float32).astype(jnp.bfloat16)
        for first in range(0, per_cycle, PACKED)
    ]
    one = jnp.ones((PACKED, CHUNK), jnp.bfloat16)
    zero = jnp.zeros((PACKED, CHUNK), jnp.bfloat16)
    spots = [(number, at) for number, part in enumerate(parts) for at in range(part)]
    for cycle, (number, at) in enumerate(spots):
        tiles = []
        for chunk in range(chunks):
            key = key_ref[pl.ds(chunk * CYCLES + first_cycle + cycle, 1), :]
            key = jnp.broadcast_to(key, (PACKED, CHUNK)).astype(jnp.bfloat16)
            tiles.append(
                jnp.concatenate([jnp.where(key == slot, one, zero) for slot in slots], axis=0)
            )
        picked = lax.dot_general(
            jnp.concatenate(tiles, axis=1),
            frames,
            (((1,), (1,)), ((), ())),
            preferred_element_type=jnp.float32,
        ).astype(jnp.bfloat16)
        all_ref[cycle * per_cycle : (cycle + 1) * per_cycle, :] = picked
        if part_refs:
            part_refs[number][at * per_cycle : (at + 1) * per_cycle, :] = picked


def order_pixels(place, key, frames, step, mods, parts, split):
    joined = len(frames) == 1
    chip_block = frames[0].shape[0] * (1 if joined else 2)
    pix_count = frames[0].shape[1]
    per_cycle = pix_count // CYCLES
    counts = [sum(parts)] + (list(parts) if split else [])
    out_shape = [
        jax.ShapeDtypeStruct((count * per_cycle, chip_block), jnp.bfloat16) for count in counts
    ]
    if not joined:
        out_shape.append(jax.ShapeDtypeStruct((chip_block, pix_count), jnp.bfloat16))
    return pl.pallas_call(
        functools.partial(order_kernel, step=step, mods=mods, parts=parts, joined=joined),
        out_shape=out_shape,
        in_specs=[SMEM_SPEC] + [VMEM_SPEC] * (1 + len(frames)),
        out_specs=[VMEM_SPEC] * len(out_shape),
        compiler_params=params(),
        cost_estimate=estimate(
            2 * sum(parts) * per_cycle * pix_count * chip_block, 2 * pix_count * chip_block
        ),
    )(place, key, *frames)


def gram_kernel(place_ref, counts_ref, *rest, layout, choice, frame_count, group, offset, count, phase, spots, chained):
    rest = list(rest)
    windows = [[(rest.pop(0), first) for first in pieces] for pieces in layout]
    ready_refs = [rest.pop(0) for _ in spots]
    if chained:
        rest.pop(0)
    out_ref, theirs_ref, mine_ref, gram, later, earlier, sems, fill_sems = rest
    core, chip, mod = place_ref[0], place_ref[1], place_ref[2]
    fills = fill_copies(core, ready_refs, spots, out_ref, fill_sems)
    for copy in fills:
        copy.start()
    _, block, lags = theirs_ref.shape
    chip_block = 2 * block
    per_cycle = CHUNK
    lane, sublane = iota((SUBLANES, LANES), 1), iota((SUBLANES, LANES), 0)
    tiles = lags // LANES
    stores = []
    for cycle in range(count):

        def rows_of(number):
            return jnp.concatenate(
                [
                    ref[source, (first + cycle) * per_cycle : (first + cycle + 1) * per_cycle, :]
                    for ref, first in windows[number]
                    for source in range(ref.shape[0])
                ],
                axis=0,
            )

        columns = [rows_of(number) for number in range(len(windows))]
        own = columns[0]
        at, even, odd = choice
        chosen = jnp.where(lax.rem(chip, 2) == 0, columns[even], columns[odd])
        columns = [
            value
            for number, value in enumerate(columns)
            if number not in (even, odd) and (number or phase == 0)
        ]
        columns.insert(at, chosen)
        whole = jnp.concatenate(columns, axis=1)
        depth, width = whole.shape
        own_rows = own.T
        gram[cycle] = dot(own_rows, whole)
        sums = dot(jnp.ones((PACKED, depth), jnp.bfloat16), whole)[:SUBLANES]
        frame_at = chip * chip_block + phase * lags + iota((SUBLANES, width), 1)
        later[cycle] = jnp.where(frame_at < frame_count, 1.0 / sums, 0.0)
        label = (mod * 2 + core) * group + offset + cycle
        total = counts_ref[pl.ds(label, 1), :]
        earlier[cycle] = total / dot(own_rows, jnp.ones((depth, LANES), jnp.bfloat16))
        for target, position in ((theirs_ref, 1 - core), (mine_ref, core)):
            base = pl.multiple_of(position * block, block)
            for first in range(0, block, SUBLANES):
                factor = earlier[cycle, pl.ds(base + first, SUBLANES), :]
                kept = lane + sublane < LANES - first
                turned = lax.rem(lane + sublane + first, LANES)
                rolled = []
                for tile in range(tiles + 1):
                    column = pl.multiple_of(base + tile * LANES, LANES)
                    value = gram[cycle, pl.ds(base + first, SUBLANES), pl.ds(column, LANES)]
                    value = value * factor * later[cycle, :, pl.ds(column, LANES)]
                    rolled.append(
                        jnp.take_along_axis(value, turned, axis=1, mode="promise_in_bounds")
                    )
                for tile in range(tiles):
                    target[
                        cycle, first : first + SUBLANES, tile * LANES : (tile + 1) * LANES
                    ] = jnp.where(kept, rolled[tile], rolled[tile + 1])
        store = pltpu.make_async_copy(
            mine_ref.at[cycle],
            out_ref.at[core * group + offset + cycle, :, pl.ds(phase * lags, lags)],
            sems.at[cycle],
        )
        store.start()
        stores.append(store)
    for copy in stores + fills:
        copy.wait()


def grams(place, counts, whole, windows, choice, sizes, phase, frame_count, ready):
    group_cycles, cycle_dev, offset, count = sizes
    flat = [piece for pieces in windows for piece, _ in pieces]
    chip_block = flat[0].shape[-1]
    block = chip_block // 2
    depth = sum(piece.shape[0] for piece, _ in windows[0]) * CHUNK
    lags = LAG // 2
    width = lags + chip_block
    kernel = functools.partial(
        gram_kernel,
        layout=[[first for _, first in pieces] for pieces in windows],
        choice=choice,
        frame_count=frame_count,
        group=group_cycles,
        offset=offset,
        count=count,
        phase=phase,
        spots=[spot for _, spot in ready],
        chained=whole is not None,
    )
    operands = [place, counts] + flat + [part for part, _ in ready]
    in_specs = [SMEM_SPEC] + [VMEM_SPEC] * (1 + len(flat)) + [ANY_SPEC] * len(ready)
    aliases = {}
    if whole is not None:
        aliases = {len(operands): 0}
        operands.append(whole)
        in_specs.append(ANY_SPEC)
    return pl.pallas_call(
        kernel,
        out_shape=[
            jax.ShapeDtypeStruct((cycle_dev, block, LAG), jnp.float32),
            jax.ShapeDtypeStruct((count, block, lags), jnp.float32),
        ],
        in_specs=in_specs,
        out_specs=[ANY_SPEC, VMEM_SPEC],
        scratch_shapes=[
            pltpu.VMEM((count, block, lags), jnp.float32),
            pltpu.VMEM((count, chip_block, width), jnp.float32),
            pltpu.VMEM((count, SUBLANES, width), jnp.float32),
            pltpu.VMEM((count, chip_block, LANES), jnp.float32),
            pltpu.SemaphoreType.DMA((count,)),
            pltpu.SemaphoreType.DMA((max(1, len(ready)),)),
        ],
        input_output_aliases=aliases,
        compiler_params=params(),
        cost_estimate=estimate(
            2 * count * depth * width * chip_block, 4 * count * chip_block * lags
        ),
    )(*operands)


def fill_copies(core, part_refs, spots, out_ref, sems):
    copies = []
    for number, (part_ref, (group, offset, lag)) in enumerate(zip(part_refs, spots)):
        cycles, _, lags = part_ref.shape
        first = (1 - core) * group + offset
        copies.append(
            pltpu.make_async_copy(
                part_ref,
                out_ref.at[pl.ds(first, cycles), :, pl.ds(lag, lags)],
                sems.at[number],
            )
        )
    return copies


def fill_kernel(place_ref, *rest, spots):
    part_refs, out_ref, sems = rest[: len(spots)], rest[-2], rest[-1]
    copies = fill_copies(place_ref[0], part_refs, spots, out_ref, sems)
    for copy in copies:
        copy.start()
    for copy in copies:
        copy.wait()


def fill(place, whole, ready):
    parts, spots = zip(*ready)
    return pl.pallas_call(
        functools.partial(fill_kernel, spots=spots),
        out_shape=jax.ShapeDtypeStruct(whole.shape, whole.dtype),
        in_specs=[SMEM_SPEC] + [ANY_SPEC] * (len(parts) + 1),
        out_specs=ANY_SPEC,
        scratch_shapes=[pltpu.SemaphoreType.DMA((len(parts),))],
        input_output_aliases={1 + len(parts): 0},
        compiler_params=params(),
        cost_estimate=estimate(0, 8 * sum(part.size for part in parts)),
    )(place, *parts, whole)


def shifted(value, pairs_down):
    step = 2 * pairs_down
    count = lax.axis_size("frame")
    return lax.ppermute(value, "frame", [(source, source - step) for source in range(step, count)])


def other_pair(value, parity=None):
    count = lax.axis_size("frame")
    sources = [at for at in range(count) if parity is None or at // 2 % 2 == parity]
    return lax.ppermute(value, "frame", [(source, source ^ 2) for source in sources])


def other_core(value):
    count = lax.axis_size("frame")
    return lax.ppermute(value, "frame", [(source, source ^ 1) for source in range(count)])


def along_mod(value, step, odd_pairs=False):
    frames, mods = lax.axis_size("frame"), lax.axis_size("mod")
    pairs = [
        (frame * mods + mod, (frame - 2 * odd_pairs) * mods + (mod + step) % mods)
        for frame in range(frames)
        for mod in range(mods)
        if not odd_pairs or frame // 2 % 2
    ]
    return lax.ppermute(value, ("frame", "mod"), pairs)


def shards(frames, cycle_label, good_pixel):
    mods = lax.axis_size("mod")
    cycle_dev = CYCLES // mods
    group_cycles = cycle_dev // 2
    mod, frame = lax.axis_index("mod"), lax.axis_index("frame")
    core, chip = frame % 2, frame // 2
    block, pix_count = frames.shape
    frame_count = block * lax.axis_size("frame")
    assert LAG == 8 * block and block == LANES and pix_count == CYCLES * CHUNK
    place = jnp.stack([core, chip, mod]).astype(jnp.int32)
    half = group_cycles // 2
    parts = [half, group_cycles - half] if half else [group_cycles]
    offsets = [sum(parts[:number]) for number in range(len(parts))]

    halves = len(parts)
    own_units = halves if OWN_SPLIT else 1
    other = other_core(frames)
    used = jnp.where(good_pixel > 0, cycle_label, CYCLES)
    key, counts, own_frames = rank_pixels(used, frames)
    done = {}

    def tied(value, name):
        ties = [get(tie) for tie in TIES.get(name, ()) if known(tie)]
        ties = [tie[0] if isinstance(tie, (list, tuple)) else tie for tie in ties]
        return lax.optimization_barrier((value, *ties))[0] if ties else value

    def known(name):
        limits = dict(g=halves, s=halves, y=halves, k=mods, o=2, c=1)
        return all(int(at) < limits.get(name[0], own_units + halves) for at in name[-1])

    def get(name):
        if name not in done:
            done[name] = make(name[0], name, *(int(at) for at in name[1:]))
        return done[name]

    def make(kind, name, first, second=0):
        if kind == "k":
            joined = [own_frames, other] if first == 0 else [get("k0")[-1]]
            split = halves > 1 and (first > 0 or own_units > 1)
            return order_pixels(place, tied(key, name), joined, first, mods, parts, split)
        if kind == "y":
            at = 1 + first if halves > 1 else 0
            return jnp.stack(
                [along_mod(tied(get(f"k{step}")[at], name), step) for step in range(1, mods)]
            )
        if kind == "c":
            value = tied(counts, name)
            return sum([value] + [along_mod(value, step) for step in range(1, mods)])
        if kind == "u":
            if first >= own_units:
                return get(f"y{first - own_units}")
            return get("k0")[1 + first if own_units > 1 else 0][None]
        if kind == "z":
            return shifted(tied(get(f"u{first}"), name), 2)
        if kind == "w":
            return shifted(tied(get(f"z{first}"), name), 2)
        if kind == "x":
            return other_pair(tied(get(f"z{first}"), name))
        if kind == "v":
            return other_pair(tied(get(f"w{first}"), name), 0)
        if kind == "o":
            if first == 0:
                return other_pair(tied(get("k0")[0], name), 1)[None]
            return jnp.stack(
                [along_mod(tied(get(f"k{step}")[0], name), step, True) for step in range(1, mods)]
            )
        if kind == "s":
            return other_core(get(f"g{first}{second}")[1])
        assert kind == "g"
        phase, part = first, second

        def both(letter):
            early = (get(f"{letter}{part}"), 0) if own_units > 1 else (get(f"{letter}0"), offsets[part])
            return [early, (get(f"{letter}{own_units + part}"), 0)]

        if phase == 0:
            neighbour = [(get(f"o{at}"), offsets[part]) for at in range(2)]
            windows, choice = [both("u"), both("z"), neighbour, both("x")], (1, 2, 3)
        else:
            windows = [both(letter) for letter in "uzwxv"]
            choice = (1, 3, 4)
        before = phase * halves + part - 1
        whole = get(f"g{before // halves}{before % halves}")[0] if before >= 0 else None
        filled = [spot(0, at) for at in range(halves)] if phase and not part else []
        sizes = (group_cycles, cycle_dev, offsets[part], parts[part])
        return grams(
            place, tied(get("c0"), name), whole, windows, choice, sizes, phase, frame_count, filled
        )

    def spot(phase, part):
        return get(f"s{phase}{part}"), (group_cycles, offsets[part], phase * (LAG // 2))

    whole = get(f"g1{halves - 1}")[0]
    return fill(place, whole, [spot(1, part) for part in range(halves)])


def solution(mesh):
    placed = (P("frame", "mod"), P("mod"), P("mod"))
    return jax.shard_map(
        shards, mesh=mesh, in_specs=placed, out_specs=P("mod", "frame", None), check_vma=False
    )
```

time: 90.7 us -> 94.4 us (1.041)
  the two profiles are of different devices: /device:TPU:0 before, /device:TPU:27 now
where the time goes in v3:
time: 94.4 us; the launch traced here: 93.8 us
  starting transfers between devices  47.2 us (50%)
  waiting for transfers between devices  25.9 us (27%)
  Pallas kernels  19.7 us (21%)
    ppermute x8, starting transfers between devices, shifted(): lax.ppermute(value, 'frame', [(source, source - step) for source in range...  22.7 us
    ppermute x9, starting transfers between devices, other_pair(): lax.ppermute(value, 'frame', [(source, source ^ 2) for source in sources])  13.1 us
    ppermute x9, waiting for transfers between devices, other_pair(): lax.ppermute(value, 'frame', [(source, source ^ 2) for source in sources])  12.4 us
    pallas_call x4, Pallas kernels, grams(): pl.pallas_call(kernel, out_shape=[jax.ShapeDtypeStruct((cycle_dev, block,...  10.9 us
    ppermute x8, waiting for transfers between devices, shifted(): lax.ppermute(value, 'frame', [(source, source - step) for source in range...  8.78 us
    pallas_call x2, Pallas kernels, order_pixels(): pl.pallas_call(functools.partial(order_kernel, step=step, mods=mods, part...  5.95 us
    ppermute x5, starting transfers between devices, other_core(): lax.ppermute(value, 'frame', [(source, source ^ 1) for source in range(co...  5.8 us
    ppermute x4, starting transfers between devices, along_mod(): return lax.ppermute(value, ('frame', 'mod'), pairs)  5.55 us
  transfers between devices with their start and end apart: 26, of which 12 were waited for; matrix products, arithmetic and copies ran while one was open for 1% of the time, Pallas kernels for 13%

profile of v3, /device:TPU:27, one launch (start us, length us, event | category | flops | bytes accessed | tf_op | source)
XLA Modules:
  0.0 93.8 jit_solution(15128271318392995298)
XLA Ops:
  0.0 0.7 collective-permute-start.1
  0.7 0.7 compare_select_fusion.label_ref
  1.4 1.2 %shard_map.37 = (f32[256,256]{1,0:T(8,128)S(1)}, f32[16,128]{1,0:T(8,128)S(1)}, bf16[128,4096]{1,0:T(8,128)(2,1)S(1)}) custom-call(s32[4096]{0:T(1024)S(1)} %compare_select_fusion.label_ref, bf16[128,4096]{1,0:T(8,128)(2,1)} %frames_hbm.1), custom_call_target="tpu_custom_call" | custom-call | flops 100663296 | bytes 32768 | tf_op jit(solution)/shard_map/pallas_call | solution.py:85
  2.7 0.1 pad_add_fusion.place_ref
  2.7 0.4 collective-permute-done.1.rest_1_
  3.2 3.0 %shard_map.38 = (bf16[1024,256]{1,0:T(8,128)(2,1)S(1)}, bf16[512,256]{1,0:T(8,128)(2,1)S(1)}, bf16[512,256]{1,0:T(8,128)(2,1)S(1)}, bf16[256,4096]{1,0:T(8,128)(2,1)S(1)}) custom-call(s32[3]{0:T(128)S(1)} %pad_add_fusion.place_ref, f32[256,256]{1,0:T(8,128)S(1)} %get-tuple-element.39.key_ref, bf16[128,4096]{1,0:T(8,128)(2,1)S(1)} %get-tuple-element.40.rest_0_, ...), custom_call_target="tpu_custom_call" | custom-call | flops 2147483648 | bytes 2097152 | tf_op jit(solution)/shard_map/pallas_call | solution.py:152
  6.2 2.1 %collective-permute-start.3 = (bf16[1,512,256]{2,1,0:T(8,128)(2,1)S(1)}, bf16[1,512,256]{2,1,0:T(8,128)(2,1)S(1)}, u32[]{:S(2)}, u32[]{:S(2)}) collective-permute-start(bf16[1,512,256]{2,1,0:T(8,128)(2,1)S(1)} %bitcast.16), channel_id=1, source_target_pairs={{8,0},{10,2},{12,4},{14,6},{16,8},{18,10},{20,12},{22,14},{24,16},... | collective-permute-start | bytes 786440 | tf_op jit(solution)/shard_map/ppermute | solution.py:334
  8.3 2.1 %collective-permute-start.5 = (bf16[1,512,256]{2,1,0:T(8,128)(2,1)S(1)}, bf16[1,512,256]{2,1,0:T(8,128)(2,1)S(1)}, u32[]{:S(2)}, u32[]{:S(2)}) collective-permute-start(bf16[1,512,256]{2,1,0:T(8,128)(2,1)S(1)} %bitcast.13), channel_id=1, source_target_pairs={{8,0},{10,2},{12,4},{14,6},{16,8},{18,10},{20,12},{22,14},{24,16},... | collective-permute-start | bytes 786440 | tf_op jit(solution)/shard_map/ppermute | solution.py:334
  10.4 2.9 %shard_map.39 = (bf16[1024,256]{1,0:T(8,128)(2,1)S(1)}, bf16[512,256]{1,0:T(8,128)(2,1)S(1)}, bf16[512,256]{1,0:T(8,128)(2,1)S(1)}) custom-call(s32[3]{0:T(128)S(1)} %pad_add_fusion.place_ref, f32[256,256]{1,0:T(8,128)S(1)} %get-tuple-element.39.key_ref, bf16[256,4096]{1,0:T(8,128)(2,1)S(1)} %get-tuple-element.42.rest_0_), custom_call_target="tpu_custom_call" | custom-call | flops 2147483648 | bytes 2097152 | tf_op jit(solution)/shard_map/pallas_call | solution.py:152
  13.3 1.3 %collective-permute-start.2 = (bf16[512,256]{1,0:T(8,128)(2,1)S(1)}, bf16[512,256]{1,0:T(8,128)(2,1)S(1)}, u32[]{:S(2)}, u32[]{:S(2)}) collective-permute-start(bf16[512,256]{1,0:T(8,128)(2,1)S(1)} %get-tuple-element.43), channel_id=1, source_target_pairs={{0,1},{1,0},{2,3},{3,2},{4,5},{5,4},{6,7},{7,6},{8,9},{9,8},{10,11... | collective-permute-start | bytes 786440 | tf_op jit(solution)/shard_map/ppermute | solution.py:356
  14.6 2.2 %collective-permute-start.11 = (bf16[1024,256]{1,0:T(8,128)(2,1)S(1)}, bf16[1024,256]{1,0:T(8,128)(2,1)S(1)}, u32[]{:S(2)}, u32[]{:S(2)}) collective-permute-start(bf16[1024,256]{1,0:T(8,128)(2,1)S(1)} %get-tuple-element.50), channel_id=1, source_target_pairs={{4,0},{6,2},{12,8},{14,10},{20,16},{22,18},{28,24},{30,26},{5,1},{... | collective-permute-start | bytes 1572872 | tf_op jit(solution)/shard_map/ppermute | solution.py:340
  16.8 0.3 collective-permute-start.7
  17.1 0.0 collective-permute-done.3.rest_2_
  17.1 2.1 %collective-permute-done.5.rest_2_ = bf16[1,512,256]{2,1,0:T(8,128)(2,1)S(1)} collective-permute-done((bf16[1,512,256]{2,1,0:T(8,128)(2,1)S(1)}, bf16[1,512,256]{2,1,0:T(8,128)(2,1)S(1)}, u32[]{:S(2)}, u32[]{:S(2)}) %collective-permute-start.5) | collective-permute-done | bytes 262176 | tf_op jit(solution)/shard_map/ppermute | solution.py:334
  19.2 4.1 %collective-permute-start.6 = (bf16[1,512,256]{2,1,0:T(8,128)(2,1)S(1)}, bf16[1,512,256]{2,1,0:T(8,128)(2,1)S(1)}, u32[]{:S(2)}, u32[]{:S(2)}) collective-permute-start(bf16[1,512,256]{2,1,0:T(8,128)(2,1)S(1)} %collective-permute-done.3.rest_2_), channel_id=1, source_target_pairs={{8,0},{10,2},{12,4},{14,6},{16,8},{18,10},{20,12},{22,14},{24,16},... | collective-permute-start | bytes 786440 | tf_op jit(solution)/shard_map/ppermute | solution.py:334
  23.3 0.0 collective-permute-done.2
  23.4 2.1 %collective-permute-start.4 = (bf16[1,512,256]{2,1,0:T(8,128)(2,1)S(1)}, bf16[1,512,256]{2,1,0:T(8,128)(2,1)S(1)}, u32[]{:S(2)}, u32[]{:S(2)}) collective-permute-start(bf16[1,512,256]{2,1,0:T(8,128)(2,1)S(1)} %bitcast.22), channel_id=1, source_target_pairs={{8,0},{10,2},{12,4},{14,6},{16,8},{18,10},{20,12},{22,14},{24,16},... | collective-permute-start | bytes 786440 | tf_op jit(solution)/shard_map/ppermute | solution.py:334
  25.4 0.3 collective-permute-start.13
  25.8 0.1 collective-permute-done.7
  25.9 1.1 %collective-permute-start.10 = (bf16[1,512,256]{2,1,0:T(8,128)(2,1)S(1)}, bf16[1,512,256]{2,1,0:T(8,128)(2,1)S(1)}, u32[]{:S(2)}, u32[]{:S(2)}) collective-permute-start(bf16[1,512,256]{2,1,0:T(8,128)(2,1)S(1)} %collective-permute-done.3.rest_2_), channel_id=1, source_target_pairs={{0,4},{2,6},{4,0},{6,2},{8,12},{10,14},{12,8},{14,10},{16,20},{18,... | collective-permute-start | bytes 786440 | tf_op jit(solution)/shard_map/ppermute | solution.py:340
  27.0 0.7 collective-permute-done.6.rest_4_
  27.7 3.1 %collective-permute-start.15 = (bf16[1024,256]{1,0:T(8,128)(2,1)S(1)}, bf16[1024,256]{1,0:T(8,128)(2,1)S(1)}, u32[]{:S(2)}, u32[]{:S(2)}) collective-permute-start(bf16[1024,256]{1,0:T(8,128)(2,1)S(1)} %get-tuple-element.54), channel_id=1, source_target_pairs={{4,1},{5,0},{6,3},{7,2},{12,9},{13,8},{14,11},{15,10},{20,17},{21,... | collective-permute-start | bytes 1572872 | tf_op jit(solution)/shard_map/ppermute | solution.py:356
  30.9 2.5 %collective-permute-done.4.rest_3_ = bf16[1,512,256]{2,1,0:T(8,128)(2,1)S(1)} collective-permute-done((bf16[1,512,256]{2,1,0:T(8,128)(2,1)S(1)}, bf16[1,512,256]{2,1,0:T(8,128)(2,1)S(1)}, u32[]{:S(2)}, u32[]{:S(2)}) %collective-permute-start.4) | collective-permute-done | bytes 262176 | tf_op jit(solution)/shard_map/ppermute | solution.py:334
  33.3 4.1 %collective-permute-start.18 = (bf16[1,512,256]{2,1,0:T(8,128)(2,1)S(1)}, bf16[1,512,256]{2,1,0:T(8,128)(2,1)S(1)}, u32[]{:S(2)}, u32[]{:S(2)}) collective-permute-start(bf16[1,512,256]{2,1,0:T(8,128)(2,1)S(1)} %collective-permute-done.5.rest_2_), channel_id=1, source_target_pairs={{8,0},{10,2},{12,4},{14,6},{16,8},{18,10},{20,12},{22,14},{24,16},... | collective-permute-start | bytes 786440 | tf_op jit(solution)/shard_map/ppermute | solution.py:334
  37.4 0.0 collective-permute-done.13.rest_6_
  37.4 2.1 %collective-permute-start.8 = (bf16[1,512,256]{2,1,0:T(8,128)(2,1)S(1)}, bf16[1,512,256]{2,1,0:T(8,128)(2,1)S(1)}, u32[]{:S(2)}, u32[]{:S(2)}) collective-permute-start(bf16[1,512,256]{2,1,0:T(8,128)(2,1)S(1)} %bitcast.19), channel_id=1, source_target_pairs={{8,0},{10,2},{12,4},{14,6},{16,8},{18,10},{20,12},{22,14},{24,16},... | collective-permute-start | bytes 786440 | tf_op jit(solution)/shard_map/ppermute | solution.py:334
  39.5 0.0 collective-permute-done.11
  39.5 1.3 %collective-permute-start.14 = (bf16[1,512,256]{2,1,0:T(8,128)(2,1)S(1)}, bf16[1,512,256]{2,1,0:T(8,128)(2,1)S(1)}, u32[]{:S(2)}, u32[]{:S(2)}) collective-permute-start(bf16[1,512,256]{2,1,0:T(8,128)(2,1)S(1)} %collective-permute-done.6.rest_4_), channel_id=1, source_target_pairs={{0,4},{2,6},{8,12},{10,14},{16,20},{18,22},{24,28},{26,30},{1,5},{... | collective-permute-start | bytes 786440 | tf_op jit(solution)/shard_map/ppermute | solution.py:340
  40.8 0.0 collective-permute-done.10.rest_6_
  40.9 2.2 %collective-permute-start.12 = (bf16[1,512,256]{2,1,0:T(8,128)(2,1)S(1)}, bf16[1,512,256]{2,1,0:T(8,128)(2,1)S(1)}, u32[]{:S(2)}, u32[]{:S(2)}) collective-permute-start(bf16[1,512,256]{2,1,0:T(8,128)(2,1)S(1)} %collective-permute-done.4.rest_3_), channel_id=1, source_target_pairs={{0,4},{2,6},{4,0},{6,2},{8,12},{10,14},{12,8},{14,10},{16,20},{18,... | collective-permute-start | bytes 786440 | tf_op jit(solution)/shard_map/ppermute | solution.py:340
  43.0 0.0 collective-permute-done.18.rest_4_
  43.0 3.5 %collective-permute-done.8.rest_3_ = bf16[1,512,256]{2,1,0:T(8,128)(2,1)S(1)} collective-permute-done((bf16[1,512,256]{2,1,0:T(8,128)(2,1)S(1)}, bf16[1,512,256]{2,1,0:T(8,128)(2,1)S(1)}, u32[]{:S(2)}, u32[]{:S(2)}) %collective-permute-start.8) | collective-permute-done | bytes 262176 | tf_op jit(solution)/shard_map/ppermute | solution.py:334
  46.5 4.1 %collective-permute-start.21 = (bf16[1,512,256]{2,1,0:T(8,128)(2,1)S(1)}, bf16[1,512,256]{2,1,0:T(8,128)(2,1)S(1)}, u32[]{:S(2)}, u32[]{:S(2)}) collective-permute-start(bf16[1,512,256]{2,1,0:T(8,128)(2,1)S(1)} %collective-permute-done.8.rest_3_), channel_id=1, source_target_pairs={{8,0},{10,2},{12,4},{14,6},{16,8},{18,10},{20,12},{22,14},{24,16},... | collective-permute-start | bytes 786440 | tf_op jit(solution)/shard_map/ppermute | solution.py:334
  50.6 0.0 collective-permute-done.14.rest_8_
  50.6 1.3 %collective-permute-start.19 = (bf16[1,512,256]{2,1,0:T(8,128)(2,1)S(1)}, bf16[1,512,256]{2,1,0:T(8,128)(2,1)S(1)}, u32[]{:S(2)}, u32[]{:S(2)}) collective-permute-start(bf16[1,512,256]{2,1,0:T(8,128)(2,1)S(1)} %collective-permute-done.18.rest_4_), channel_id=1, source_target_pairs={{0,4},{2,6},{8,12},{10,14},{16,20},{18,22},{24,28},{26,30},{1,5},{... | collective-permute-start | bytes 786440 | tf_op jit(solution)/shard_map/ppermute | solution.py:340
  51.9 0.0 collective-permute-done.15
  51.9 2.9 %collective-permute-done.12.rest_7_ = bf16[1,512,256]{2,1,0:T(8,128)(2,1)S(1)} collective-permute-done((bf16[1,512,256]{2,1,0:T(8,128)(2,1)S(1)}, bf16[1,512,256]{2,1,0:T(8,128)(2,1)S(1)}, u32[]{:S(2)}, u32[]{:S(2)}) %collective-permute-start.12) | collective-permute-done | bytes 262176 | tf_op jit(solution)/shard_map/ppermute | solution.py:340
  54.9 2.2 %collective-permute-start.16 = (bf16[1,512,256]{2,1,0:T(8,128)(2,1)S(1)}, bf16[1,512,256]{2,1,0:T(8,128)(2,1)S(1)}, u32[]{:S(2)}, u32[]{:S(2)}) collective-permute-start(bf16[1,512,256]{2,1,0:T(8,128)(2,1)S(1)} %collective-permute-done.8.rest_3_), channel_id=1, source_target_pairs={{0,4},{2,6},{4,0},{6,2},{8,12},{10,14},{12,8},{14,10},{16,20},{18,... | collective-permute-start | bytes 786440 | tf_op jit(solution)/shard_map/ppermute | solution.py:340
  57.1 0.8 collective-permute-start
  57.9 2.0 %collective-permute-done = f32[16,128]{1,0:T(8,128)S(1)} collective-permute-done((f32[16,128]{1,0:T(8,128)S(1)}, f32[16,128]{1,0:T(8,128)S(1)}, u32[]{:S(2)}, u32[]{:S(2)}) %collective-permute-start) | collective-permute-done | bytes 8224 | tf_op jit(solution)/shard_map/ppermute | solution.py:356
  59.9 2.1 %collective-permute-start.9 = (bf16[1,512,256]{2,1,0:T(8,128)(2,1)S(1)}, bf16[1,512,256]{2,1,0:T(8,128)(2,1)S(1)}, u32[]{:S(2)}, u32[]{:S(2)}) collective-permute-start(bf16[1,512,256]{2,1,0:T(8,128)(2,1)S(1)} %collective-permute-done.4.rest_3_), channel_id=1, source_target_pairs={{8,0},{10,2},{12,4},{14,6},{16,8},{18,10},{20,12},{22,14},{24,16},... | collective-permute-start | bytes 786440 | tf_op jit(solution)/shard_map/ppermute | solution.py:334
  61.9 0.0 collective-permute-done.21.rest_5_
  61.9 0.0 collective-permute-done.19.rest_8_
  62.0 2.7 %shard_map.40 = (f32[8,128,1024]{2,1,0:T(8,128)}, f32[2,128,512]{2,1,0:T(8,128)S(1)}) custom-call(s32[3]{0:T(128)S(1)} %pad_add_fusion.place_ref, f32[16,128]{1,0:T(8,128)S(1)} %add.9.counts_ref, bf16[1,512,256]{2,1,0:T(8,128)(2,1)S(1)} %bitcast.17, bf16[1,512,256]{2,1,0:T(8,128)(2,1)S(1)} %bitcast.23, ...), custom_call_target="tpu_custom_call" | custom-call | flops 402653184 | bytes 1048576 | tf_op jit(solution)/shard_map/pallas_call | solution.py:269
  64.6 0.0 collective-permute-done.16.rest_7_
  64.6 2.7 %shard_map.41 = (f32[8,128,1024]{2,1,0:T(8,128)}, f32[2,128,512]{2,1,0:T(8,128)S(1)}) custom-call(s32[3]{0:T(128)S(1)} %pad_add_fusion.place_ref, f32[16,128]{1,0:T(8,128)S(1)} %add.9.counts_ref, bf16[1,512,256]{2,1,0:T(8,128)(2,1)S(1)} %bitcast.14, bf16[1,512,256]{2,1,0:T(8,128)(2,1)S(1)} %bitcast.20, ...), custom_call_target="tpu_custom_call", output_to_operand_aliasing={{0}: (10, {})} | custom-call | flops 402653184 | bytes 1048576 | tf_op jit(solution)/shard_map/pallas_call | solution.py:269
  67.3 3.6 %collective-permute-start.22 = (f32[2,128,512]{2,1,0:T(8,128)S(1)}, f32[2,128,512]{2,1,0:T(8,128)S(1)}, u32[]{:S(2)}, u32[]{:S(2)}) collective-permute-start(f32[2,128,512]{2,1,0:T(8,128)S(1)} %get-tuple-element.64), channel_id=1, source_target_pairs={{0,2},{2,0},{4,6},{6,4},{8,10},{10,8},{12,14},{14,12},{16,18},{18,... | collective-permute-start | bytes 1572872 | tf_op jit(solution)/shard_map/ppermute | solution.py:345
  71.0 0.1 collective-permute-start.20
  71.0 0.0 collective-permute-done.9.rest_5_
  71.0 1.3 %collective-permute-start.17 = (bf16[1,512,256]{2,1,0:T(8,128)(2,1)S(1)}, bf16[1,512,256]{2,1,0:T(8,128)(2,1)S(1)}, u32[]{:S(2)}, u32[]{:S(2)}) collective-permute-start(bf16[1,512,256]{2,1,0:T(8,128)(2,1)S(1)} %collective-permute-done.9.rest_5_), channel_id=1, source_target_pairs={{0,4},{2,6},{8,12},{10,14},{16,20},{18,22},{24,28},{26,30},{1,5},{... | collective-permute-start | bytes 786440 | tf_op jit(solution)/shard_map/ppermute | solution.py:340
  72.3 1.3 %collective-permute-start.24 = (bf16[1,512,256]{2,1,0:T(8,128)(2,1)S(1)}, bf16[1,512,256]{2,1,0:T(8,128)(2,1)S(1)}, u32[]{:S(2)}, u32[]{:S(2)}) collective-permute-start(bf16[1,512,256]{2,1,0:T(8,128)(2,1)S(1)} %collective-permute-done.21.rest_5_), channel_id=1, source_target_pairs={{0,4},{2,6},{8,12},{10,14},{16,20},{18,22},{24,28},{26,30},{1,5},{... | collective-permute-start | bytes 786440 | tf_op jit(solution)/shard_map/ppermute | solution.py:340
  73.6 6.7 %collective-permute-done.17.rest_9_ = bf16[1,512,256]{2,1,0:T(8,128)(2,1)S(1)} collective-permute-done((bf16[1,512,256]{2,1,0:T(8,128)(2,1)S(1)}, bf16[1,512,256]{2,1,0:T(8,128)(2,1)S(1)}, u32[]{:S(2)}, u32[]{:S(2)}) %collective-permute-start.17) | collective-permute-done | bytes 262176 | tf_op jit(solution)/shard_map/ppermute | solution.py:340
  80.4 0.0 collective-permute-done.22.rest_11_
  80.4 0.0 collective-permute-done.20.rest_10_
  80.4 2.9 %shard_map.42 = (f32[8,128,1024]{2,1,0:T(8,128)}, f32[2,128,512]{2,1,0:T(8,128)S(1)}) custom-call(s32[3]{0:T(128)S(1)} %pad_add_fusion.place_ref, f32[16,128]{1,0:T(8,128)S(1)} %add.9.counts_ref, bf16[1,512,256]{2,1,0:T(8,128)(2,1)S(1)} %bitcast.18, bf16[1,512,256]{2,1,0:T(8,128)(2,1)S(1)} %bitcast.24, ...), custom_call_target="tpu_custom_call", output_to_operand_aliasing={{0}: (14, {})} | custom-call | flops 402653184 | bytes 1048576 | tf_op jit(solution)/shard_map/pallas_call | solution.py:269
  83.3 2.7 %collective-permute-done.24.rest_9_ = bf16[1,512,256]{2,1,0:T(8,128)(2,1)S(1)} collective-permute-done((bf16[1,512,256]{2,1,0:T(8,128)(2,1)S(1)}, bf16[1,512,256]{2,1,0:T(8,128)(2,1)S(1)}, u32[]{:S(2)}, u32[]{:S(2)}) %collective-permute-start.24) | collective-permute-done | bytes 262176 | tf_op jit(solution)/shard_map/ppermute | solution.py:340
  86.0 2.7 %shard_map.43 = (f32[8,128,1024]{2,1,0:T(8,128)}, f32[2,128,512]{2,1,0:T(8,128)S(1)}) custom-call(s32[3]{0:T(128)S(1)} %pad_add_fusion.place_ref, f32[16,128]{1,0:T(8,128)S(1)} %add.9.counts_ref, bf16[1,512,256]{2,1,0:T(8,128)(2,1)S(1)} %bitcast.15, bf16[1,512,256]{2,1,0:T(8,128)(2,1)S(1)} %bitcast.21, ...), custom_call_target="tpu_custom_call", output_to_operand_aliasing={{0}: (12, {})} | custom-call | flops 402653184 | bytes 1048576 | tf_op jit(solution)/shard_map/pallas_call | solution.py:269
  88.7 1.3 %collective-permute-start.25 = (f32[2,128,512]{2,1,0:T(8,128)S(1)}, f32[2,128,512]{2,1,0:T(8,128)S(1)}, u32[]{:S(2)}, u32[]{:S(2)}) collective-permute-start(f32[2,128,512]{2,1,0:T(8,128)S(1)} %get-tuple-element.69), channel_id=1, source_target_pairs={{0,2},{2,0},{4,6},{6,4},{8,10},{10,8},{12,14},{14,12},{16,18},{18,... | collective-permute-start | bytes 1572872 | tf_op jit(solution)/shard_map/ppermute | solution.py:345
  90.0 0.1 collective-permute-start.23
  90.1 1.5 %collective-permute-done.25.rest_1_ = f32[2,128,512]{2,1,0:T(8,128)S(1)} collective-permute-done((f32[2,128,512]{2,1,0:T(8,128)S(1)}, f32[2,128,512]{2,1,0:T(8,128)S(1)}, u32[]{:S(2)}, u32[]{:S(2)}) %collective-permute-start.25) | collective-permute-done | bytes 524320 | tf_op jit(solution)/shard_map/ppermute | solution.py:345
  91.6 0.7 collective-permute-done.23.rest_0_
  92.3 1.5 %shard_map.44 = f32[8,128,1024]{2,1,0:T(8,128)} custom-call(s32[3]{0:T(128)S(1)} %pad_add_fusion.place_ref, f32[2,128,512]{2,1,0:T(8,128)S(1)} %collective-permute-done.23.rest_0_, f32[2,128,512]{2,1,0:T(8,128)S(1)} %collective-permute-done.25.rest_1_, f32[8,128,1024]{2,1,0:T(8,128)} %get-tuple-element.70.rest_2_), custom_call_target="tpu_custom_call", output_to_operand_aliasing={{}: (3, {})} | custom-call | bytes 2097152 | tf_op jit(solution)/shard_map/pallas_call | solution.py:319
  (1 shorter events, 0.0 us)
Async XLA Ops:
  0.0 3.2 %collective-permute-start.1 = (bf16[128,4096]{1,0:T(8,128)(2,1)}, bf16[128,4096]{1,0:T(8,128)(2,1)S(1)}, u32[]{:S(2)}, u32[]{:S(2)}) collective-permute-start(bf16[128,4096]{1,0:T(8,128)(2,1)} %frames_hbm.1), channel_id=1, source_target_pairs={{0,2},{2,0},{4,6},{6,4},{8,10},{10,8},{12,14},{14,12},{16,18},{18,... | collective-permute-start | bytes 3145736 | tf_op jit(solution)/shard_map/ppermute | solution.py:345
  6.2 10.9 %collective-permute-start.3 = (bf16[1,512,256]{2,1,0:T(8,128)(2,1)S(1)}, bf16[1,512,256]{2,1,0:T(8,128)(2,1)S(1)}, u32[]{:S(2)}, u32[]{:S(2)}) collective-permute-start(bf16[1,512,256]{2,1,0:T(8,128)(2,1)S(1)} %bitcast.16), channel_id=1, source_target_pairs={{8,0},{10,2},{12,4},{14,6},{16,8},{18,10},{20,12},{22,14},{24,16},... | collective-permute-start | bytes 786440 | tf_op jit(solution)/shard_map/ppermute | solution.py:334
  8.3 10.9 %collective-permute-start.5 = (bf16[1,512,256]{2,1,0:T(8,128)(2,1)S(1)}, bf16[1,512,256]{2,1,0:T(8,128)(2,1)S(1)}, u32[]{:S(2)}, u32[]{:S(2)}) collective-permute-start(bf16[1,512,256]{2,1,0:T(8,128)(2,1)S(1)} %bitcast.13), channel_id=1, source_target_pairs={{8,0},{10,2},{12,4},{14,6},{16,8},{18,10},{20,12},{22,14},{24,16},... | collective-permute-start | bytes 786440 | tf_op jit(solution)/shard_map/ppermute | solution.py:334
  13.3 10.0 %collective-permute-start.2 = (bf16[512,256]{1,0:T(8,128)(2,1)S(1)}, bf16[512,256]{1,0:T(8,128)(2,1)S(1)}, u32[]{:S(2)}, u32[]{:S(2)}) collective-permute-start(bf16[512,256]{1,0:T(8,128)(2,1)S(1)} %get-tuple-element.43), channel_id=1, source_target_pairs={{0,1},{1,0},{2,3},{3,2},{4,5},{5,4},{6,7},{7,6},{8,9},{9,8},{10,11... | collective-permute-start | bytes 786440 | tf_op jit(solution)/shard_map/ppermute | solution.py:356
  14.6 24.9 %collective-permute-start.11 = (bf16[1024,256]{1,0:T(8,128)(2,1)S(1)}, bf16[1024,256]{1,0:T(8,128)(2,1)S(1)}, u32[]{:S(2)}, u32[]{:S(2)}) collective-permute-start(bf16[1024,256]{1,0:T(8,128)(2,1)S(1)} %get-tuple-element.50), channel_id=1, source_target_pairs={{4,0},{6,2},{12,8},{14,10},{20,16},{22,18},{28,24},{30,26},{5,1},{... | collective-permute-start | bytes 1572872 | tf_op jit(solution)/shard_map/ppermute | solution.py:340
  16.8 9.1 %collective-permute-start.7 = (bf16[512,256]{1,0:T(8,128)(2,1)S(1)}, bf16[512,256]{1,0:T(8,128)(2,1)S(1)}, u32[]{:S(2)}, u32[]{:S(2)}) collective-permute-start(bf16[512,256]{1,0:T(8,128)(2,1)S(1)} %get-tuple-element.47), channel_id=1, source_target_pairs={{0,1},{1,0},{2,3},{3,2},{4,5},{5,4},{6,7},{7,6},{8,9},{9,8},{10,11... | collective-permute-start | bytes 786440 | tf_op jit(solution)/shard_map/ppermute | solution.py:356
  19.2 8.5 %collective-permute-start.6 = (bf16[1,512,256]{2,1,0:T(8,128)(2,1)S(1)}, bf16[1,512,256]{2,1,0:T(8,128)(2,1)S(1)}, u32[]{:S(2)}, u32[]{:S(2)}) collective-permute-start(bf16[1,512,256]{2,1,0:T(8,128)(2,1)S(1)} %collective-permute-done.3.rest_2_), channel_id=1, source_target_pairs={{8,0},{10,2},{12,4},{14,6},{16,8},{18,10},{20,12},{22,14},{24,16},... | collective-permute-start | bytes 786440 | tf_op jit(solution)/shard_map/ppermute | solution.py:334
  23.4 10.0 %collective-permute-start.4 = (bf16[1,512,256]{2,1,0:T(8,128)(2,1)S(1)}, bf16[1,512,256]{2,1,0:T(8,128)(2,1)S(1)}, u32[]{:S(2)}, u32[]{:S(2)}) collective-permute-start(bf16[1,512,256]{2,1,0:T(8,128)(2,1)S(1)} %bitcast.22), channel_id=1, source_target_pairs={{8,0},{10,2},{12,4},{14,6},{16,8},{18,10},{20,12},{22,14},{24,16},... | collective-permute-start | bytes 786440 | tf_op jit(solution)/shard_map/ppermute | solution.py:334
  25.4 12.0 %collective-permute-start.13 = (bf16[1,512,256]{2,1,0:T(8,128)(2,1)S(1)}, bf16[1,512,256]{2,1,0:T(8,128)(2,1)S(1)}, u32[]{:S(2)}, u32[]{:S(2)}) collective-permute-start(bf16[1,512,256]{2,1,0:T(8,128)(2,1)S(1)} %collective-permute-done.5.rest_2_), channel_id=1, source_target_pairs={{0,4},{2,6},{4,0},{6,2},{8,12},{10,14},{12,8},{14,10},{16,20},{18,... | collective-permute-start | bytes 786440 | tf_op jit(solution)/shard_map/ppermute | solution.py:340
  25.9 15.0 %collective-permute-start.10 = (bf16[1,512,256]{2,1,0:T(8,128)(2,1)S(1)}, bf16[1,512,256]{2,1,0:T(8,128)(2,1)S(1)}, u32[]{:S(2)}, u32[]{:S(2)}) collective-permute-start(bf16[1,512,256]{2,1,0:T(8,128)(2,1)S(1)} %collective-permute-done.3.rest_2_), channel_id=1, source_target_pairs={{0,4},{2,6},{4,0},{6,2},{8,12},{10,14},{12,8},{14,10},{16,20},{18,... | collective-permute-start | bytes 786440 | tf_op jit(solution)/shard_map/ppermute | solution.py:340
  27.7 24.2 %collective-permute-start.15 = (bf16[1024,256]{1,0:T(8,128)(2,1)S(1)}, bf16[1024,256]{1,0:T(8,128)(2,1)S(1)}, u32[]{:S(2)}, u32[]{:S(2)}) collective-permute-start(bf16[1024,256]{1,0:T(8,128)(2,1)S(1)} %get-tuple-element.54), channel_id=1, source_target_pairs={{4,1},{5,0},{6,3},{7,2},{12,9},{13,8},{14,11},{15,10},{20,17},{21,... | collective-permute-start | bytes 1572872 | tf_op jit(solution)/shard_map/ppermute | solution.py:356
  33.3 9.7 %collective-permute-start.18 = (bf16[1,512,256]{2,1,0:T(8,128)(2,1)S(1)}, bf16[1,512,256]{2,1,0:T(8,128)(2,1)S(1)}, u32[]{:S(2)}, u32[]{:S(2)}) collective-permute-start(bf16[1,512,256]{2,1,0:T(8,128)(2,1)S(1)} %collective-permute-done.5.rest_2_), channel_id=1, source_target_pairs={{8,0},{10,2},{12,4},{14,6},{16,8},{18,10},{20,12},{22,14},{24,16},... | collective-permute-start | bytes 786440 | tf_op jit(solution)/shard_map/ppermute | solution.py:334
  37.4 9.0 %collective-permute-start.8 = (bf16[1,512,256]{2,1,0:T(8,128)(2,1)S(1)}, bf16[1,512,256]{2,1,0:T(8,128)(2,1)S(1)}, u32[]{:S(2)}, u32[]{:S(2)}) collective-permute-start(bf16[1,512,256]{2,1,0:T(8,128)(2,1)S(1)} %bitcast.19), channel_id=1, source_target_pairs={{8,0},{10,2},{12,4},{14,6},{16,8},{18,10},{20,12},{22,14},{24,16},... | collective-permute-start | bytes 786440 | tf_op jit(solution)/shard_map/ppermute | solution.py:334
  39.5 11.1 %collective-permute-start.14 = (bf16[1,512,256]{2,1,0:T(8,128)(2,1)S(1)}, bf16[1,512,256]{2,1,0:T(8,128)(2,1)S(1)}, u32[]{:S(2)}, u32[]{:S(2)}) collective-permute-start(bf16[1,512,256]{2,1,0:T(8,128)(2,1)S(1)} %collective-permute-done.6.rest_4_), channel_id=1, source_target_pairs={{0,4},{2,6},{8,12},{10,14},{16,20},{18,22},{24,28},{26,30},{1,5},{... | collective-permute-start | bytes 786440 | tf_op jit(solution)/shard_map/ppermute | solution.py:340
  40.9 14.0 %collective-permute-start.12 = (bf16[1,512,256]{2,1,0:T(8,128)(2,1)S(1)}, bf16[1,512,256]{2,1,0:T(8,128)(2,1)S(1)}, u32[]{:S(2)}, u32[]{:S(2)}) collective-permute-start(bf16[1,512,256]{2,1,0:T(8,128)(2,1)S(1)} %collective-permute-done.4.rest_3_), channel_id=1, source_target_pairs={{0,4},{2,6},{4,0},{6,2},{8,12},{10,14},{12,8},{14,10},{16,20},{18,... | collective-permute-start | bytes 786440 | tf_op jit(solution)/shard_map/ppermute | solution.py:340
  46.5 15.4 %collective-permute-start.21 = (bf16[1,512,256]{2,1,0:T(8,128)(2,1)S(1)}, bf16[1,512,256]{2,1,0:T(8,128)(2,1)S(1)}, u32[]{:S(2)}, u32[]{:S(2)}) collective-permute-start(bf16[1,512,256]{2,1,0:T(8,128)(2,1)S(1)} %collective-permute-done.8.rest_3_), channel_id=1, source_target_pairs={{8,0},{10,2},{12,4},{14,6},{16,8},{18,10},{20,12},{22,14},{24,16},... | collective-permute-start | bytes 786440 | tf_op jit(solution)/shard_map/ppermute | solution.py:334
  50.6 11.3 %collective-permute-start.19 = (bf16[1,512,256]{2,1,0:T(8,128)(2,1)S(1)}, bf16[1,512,256]{2,1,0:T(8,128)(2,1)S(1)}, u32[]{:S(2)}, u32[]{:S(2)}) collective-permute-start(bf16[1,512,256]{2,1,0:T(8,128)(2,1)S(1)} %collective-permute-done.18.rest_4_), channel_id=1, source_target_pairs={{0,4},{2,6},{8,12},{10,14},{16,20},{18,22},{24,28},{26,30},{1,5},{... | collective-permute-start | bytes 786440 | tf_op jit(solution)/shard_map/ppermute | solution.py:340
  54.9 9.8 %collective-permute-start.16 = (bf16[1,512,256]{2,1,0:T(8,128)(2,1)S(1)}, bf16[1,512,256]{2,1,0:T(8,128)(2,1)S(1)}, u32[]{:S(2)}, u32[]{:S(2)}) collective-permute-start(bf16[1,512,256]{2,1,0:T(8,128)(2,1)S(1)} %collective-permute-done.8.rest_3_), channel_id=1, source_target_pairs={{0,4},{2,6},{4,0},{6,2},{8,12},{10,14},{12,8},{14,10},{16,20},{18,... | collective-permute-start | bytes 786440 | tf_op jit(solution)/shard_map/ppermute | solution.py:340
  57.1 2.8 %collective-permute-start = (f32[16,128]{1,0:T(8,128)S(1)}, f32[16,128]{1,0:T(8,128)S(1)}, u32[]{:S(2)}, u32[]{:S(2)}) collective-permute-start(f32[16,128]{1,0:T(8,128)S(1)} %get-tuple-element.38), channel_id=1, source_target_pairs={{0,1},{1,0},{2,3},{3,2},{4,5},{5,4},{6,7},{7,6},{8,9},{9,8},{10,11... | collective-permute-start | bytes 24584 | tf_op jit(solution)/shard_map/ppermute | solution.py:356
  59.9 11.2 %collective-permute-start.9 = (bf16[1,512,256]{2,1,0:T(8,128)(2,1)S(1)}, bf16[1,512,256]{2,1,0:T(8,128)(2,1)S(1)}, u32[]{:S(2)}, u32[]{:S(2)}) collective-permute-start(bf16[1,512,256]{2,1,0:T(8,128)(2,1)S(1)} %collective-permute-done.4.rest_3_), channel_id=1, source_target_pairs={{8,0},{10,2},{12,4},{14,6},{16,8},{18,10},{20,12},{22,14},{24,16},... | collective-permute-start | bytes 786440 | tf_op jit(solution)/shard_map/ppermute | solution.py:334
  67.3 13.0 %collective-permute-start.22 = (f32[2,128,512]{2,1,0:T(8,128)S(1)}, f32[2,128,512]{2,1,0:T(8,128)S(1)}, u32[]{:S(2)}, u32[]{:S(2)}) collective-permute-start(f32[2,128,512]{2,1,0:T(8,128)S(1)} %get-tuple-element.64), channel_id=1, source_target_pairs={{0,2},{2,0},{4,6},{6,4},{8,10},{10,8},{12,14},{14,12},{16,18},{18,... | collective-permute-start | bytes 1572872 | tf_op jit(solution)/shard_map/ppermute | solution.py:345
  71.0 9.4 %collective-permute-start.20 = (f32[2,128,512]{2,1,0:T(8,128)S(1)}, f32[2,128,512]{2,1,0:T(8,128)S(1)}, u32[]{:S(2)}, u32[]{:S(2)}) collective-permute-start(f32[2,128,512]{2,1,0:T(8,128)S(1)} %get-tuple-element.60), channel_id=1, source_target_pairs={{0,2},{2,0},{4,6},{6,4},{8,10},{10,8},{12,14},{14,12},{16,18},{18,... | collective-permute-start | bytes 1572872 | tf_op jit(solution)/shard_map/ppermute | solution.py:345
  71.0 9.3 %collective-permute-start.17 = (bf16[1,512,256]{2,1,0:T(8,128)(2,1)S(1)}, bf16[1,512,256]{2,1,0:T(8,128)(2,1)S(1)}, u32[]{:S(2)}, u32[]{:S(2)}) collective-permute-start(bf16[1,512,256]{2,1,0:T(8,128)(2,1)S(1)} %collective-permute-done.9.rest_5_), channel_id=1, source_target_pairs={{0,4},{2,6},{8,12},{10,14},{16,20},{18,22},{24,28},{26,30},{1,5},{... | collective-permute-start | bytes 786440 | tf_op jit(solution)/shard_map/ppermute | solution.py:340
  72.3 13.7 %collective-permute-start.24 = (bf16[1,512,256]{2,1,0:T(8,128)(2,1)S(1)}, bf16[1,512,256]{2,1,0:T(8,128)(2,1)S(1)}, u32[]{:S(2)}, u32[]{:S(2)}) collective-permute-start(bf16[1,512,256]{2,1,0:T(8,128)(2,1)S(1)} %collective-permute-done.21.rest_5_), channel_id=1, source_target_pairs={{0,4},{2,6},{8,12},{10,14},{16,20},{18,22},{24,28},{26,30},{1,5},{... | collective-permute-start | bytes 786440 | tf_op jit(solution)/shard_map/ppermute | solution.py:340
  88.7 2.9 %collective-permute-start.25 = (f32[2,128,512]{2,1,0:T(8,128)S(1)}, f32[2,128,512]{2,1,0:T(8,128)S(1)}, u32[]{:S(2)}, u32[]{:S(2)}) collective-permute-start(f32[2,128,512]{2,1,0:T(8,128)S(1)} %get-tuple-element.69), channel_id=1, source_target_pairs={{0,2},{2,0},{4,6},{6,4},{8,10},{10,8},{12,14},{14,12},{16,18},{18,... | collective-permute-start | bytes 1572872 | tf_op jit(solution)/shard_map/ppermute | solution.py:345
  90.0 2.3 %collective-permute-start.23 = (f32[2,128,512]{2,1,0:T(8,128)S(1)}, f32[2,128,512]{2,1,0:T(8,128)S(1)}, u32[]{:S(2)}, u32[]{:S(2)}) collective-permute-start(f32[2,128,512]{2,1,0:T(8,128)S(1)} %get-tuple-element.66), channel_id=1, source_target_pairs={{0,2},{2,0},{4,6},{6,4},{8,10},{10,8},{12,14},{14,12},{16,18},{18,... | collective-permute-start | bytes 1572872 | tf_op jit(solution)/shard_map/ppermute | solution.py:345

commit v4 on v3

--- a/solution.py
+++ b/solution.py
@@ -12,25 +12,22 @@
 LANES = 128
 SUBLANES = 8
 PACKED = 16
+BATCH = 64
 CHUNK = 256
 VMEM_LIMIT = 24 * 1024 * 1024
 
 TIES = {
-    "z2": ("z0",),
-    "w0": ("z1",),
-    "z3": ("z2",),
-    "w1": ("w0",),
-    "w2": ("z3",),
-    "w3": ("w1",),
-    "x2": ("x0", "o0"),
-    "v0": ("x1",),
+    "z3": ("x1", "y1", "y0", "z2"),
+    "x2": ("x0", "o0", "y1"),
+    "v0": ("x1", "k1"),
     "x3": ("x2", "o1"),
-    "v1": ("v0",),
-    "v2": ("x3",),
-    "v3": ("v1",),
-    "o1": ("y1",),
+    "v1": ("v0", "y1", "o0", "w1"),
     "g00": ("v1",),
-    "g01": ("w3", "v1"),
+    "g01": ("w3", "v1", "v2", "v0"),
+    "w3": ("z1",),
+    "x1": ("z1", "o0"),
+    "w0": ("z0",),
+    "y0": ("k1",),
 }
 OWN_SPLIT = True
 
@@ -97,7 +94,7 @@
     )(label, pltpu.with_memory_space_constraint(frames, pltpu.HBM))
 
 
-def order_kernel(place_ref, key_ref, *rest, step, mods, parts, joined):
+def order_kernel(place_ref, key_ref, counts_ref, *rest, step, mods, parts, joined):
     rest = list(rest)
     core, mod = place_ref[0], place_ref[2]
     if joined:
@@ -112,6 +109,10 @@
     chunks = key_ref.shape[0] // CYCLES
     per_cycle = frames.shape[1] // CYCLES
     first_cycle = (lax.rem(mod + step, mods) * 2 + core) * sum(parts)
+    if step:
+        row = parts[0] * per_cycle
+        sent = jnp.concatenate([counts_ref[...]] * (frames.shape[0] // LANES), axis=1)
+        part_refs[0][row : row + CYCLES, :] = sent.astype(jnp.bfloat16)
     slots = [
         (iota((PACKED, CHUNK), 0) + first).astype(jnp.float32).astype(jnp.bfloat16)
         for first in range(0, per_cycle, PACKED)
@@ -138,30 +139,30 @@
             part_refs[number][at * per_cycle : (at + 1) * per_cycle, :] = picked
 
 
-def order_pixels(place, key, frames, step, mods, parts, split):
+def order_pixels(place, key, counts, frames, step, mods, parts, split):
     joined = len(frames) == 1
     chip_block = frames[0].shape[0] * (1 if joined else 2)
     pix_count = frames[0].shape[1]
     per_cycle = pix_count // CYCLES
-    counts = [sum(parts)] + (list(parts) if split else [])
-    out_shape = [
-        jax.ShapeDtypeStruct((count * per_cycle, chip_block), jnp.bfloat16) for count in counts
-    ]
+    heights = [part * per_cycle for part in [sum(parts)] + (list(parts) if split else [])]
+    if step:
+        heights[1] += CYCLES
+    out_shape = [jax.ShapeDtypeStruct((height, chip_block), jnp.bfloat16) for height in heights]
     if not joined:
         out_shape.append(jax.ShapeDtypeStruct((chip_block, pix_count), jnp.bfloat16))
     return pl.pallas_call(
         functools.partial(order_kernel, step=step, mods=mods, parts=parts, joined=joined),
         out_shape=out_shape,
-        in_specs=[SMEM_SPEC] + [VMEM_SPEC] * (1 + len(frames)),
+        in_specs=[SMEM_SPEC] + [VMEM_SPEC] * (2 + len(frames)),
         out_specs=[VMEM_SPEC] * len(out_shape),
         compiler_params=params(),
         cost_estimate=estimate(
             2 * sum(parts) * per_cycle * pix_count * chip_block, 2 * pix_count * chip_block
         ),
-    )(place, key, *frames)
-
-
-def gram_kernel(place_ref, counts_ref, *rest, layout, choice, frame_count, group, offset, count, phase, spots, chained):
+    )(place, key, counts, *frames)
+
+
+def gram_kernel(place_ref, counts_ref, sent_ref, *rest, layout, choice, frame_count, group, offset, count, phase, spots, chained):
     rest = list(rest)
     windows = [[(rest.pop(0), first) for first in pieces] for pieces in layout]
     ready_refs = [rest.pop(0) for _ in spots]
@@ -209,25 +210,41 @@
         later[cycle] = jnp.where(frame_at < frame_count, 1.0 / sums, 0.0)
         label = (mod * 2 + core) * group + offset + cycle
         total = counts_ref[pl.ds(label, 1), :]
+        for source in range(sent_ref.shape[0]):
+            sent = sent_ref[source, sent_ref.shape[1] - CYCLES :, :LANES].astype(jnp.float32)
+            total += jnp.sum(
+                jnp.where(iota((CYCLES, LANES), 0) == label, sent, 0.0), axis=0, keepdims=True
+            )
         earlier[cycle] = total / dot(own_rows, jnp.ones((depth, LANES), jnp.bfloat16))
         for target, position in ((theirs_ref, 1 - core), (mine_ref, core)):
             base = pl.multiple_of(position * block, block)
-            for first in range(0, block, SUBLANES):
-                factor = earlier[cycle, pl.ds(base + first, SUBLANES), :]
-                kept = lane + sublane < LANES - first
-                turned = lax.rem(lane + sublane + first, LANES)
-                rolled = []
-                for tile in range(tiles + 1):
-                    column = pl.multiple_of(base + tile * LANES, LANES)
-                    value = gram[cycle, pl.ds(base + first, SUBLANES), pl.ds(column, LANES)]
-                    value = value * factor * later[cycle, :, pl.ds(column, LANES)]
-                    rolled.append(
-                        jnp.take_along_axis(value, turned, axis=1, mode="promise_in_bounds")
-                    )
-                for tile in range(tiles):
-                    target[
-                        cycle, first : first + SUBLANES, tile * LANES : (tile + 1) * LANES
-                    ] = jnp.where(kept, rolled[tile], rolled[tile + 1])
+            scales = [
+                later[cycle, :, pl.ds(pl.multiple_of(base + tile * LANES, LANES), LANES)]
+                for tile in range(tiles + 1)
+            ]
+            for batch in range(0, block, BATCH):
+                results = []
+                for first in range(batch, batch + BATCH, SUBLANES):
+                    factor = earlier[cycle, pl.ds(base + first, SUBLANES), :]
+                    kept = lane + sublane < LANES - first
+                    turned = lax.rem(lane + sublane + first, LANES)
+                    rolled = []
+                    for tile in range(tiles + 1):
+                        column = pl.multiple_of(base + tile * LANES, LANES)
+                        value = gram[cycle, pl.ds(base + first, SUBLANES), pl.ds(column, LANES)]
+                        value = value * factor * scales[tile]
+                        rolled.append(
+                            jnp.take_along_axis(value, turned, axis=1, mode="promise_in_bounds")
+                        )
+                    for tile in range(tiles):
+                        results.append(jnp.where(kept, rolled[tile], rolled[tile + 1]))
+                at = 0
+                for first in range(batch, batch + BATCH, SUBLANES):
+                    for tile in range(tiles):
+                        target[
+                            cycle, first : first + SUBLANES, tile * LANES : (tile + 1) * LANES
+                        ] = results[at]
+                        at += 1
         store = pltpu.make_async_copy(
             mine_ref.at[cycle],
             out_ref.at[core * group + offset + cycle, :, pl.ds(phase * lags, lags)],
@@ -239,7 +256,7 @@
         copy.wait()
 
 
-def grams(place, counts, whole, windows, choice, sizes, phase, frame_count, ready):
+def grams(place, counts, sent, whole, windows, choice, sizes, phase, frame_count, ready):
     group_cycles, cycle_dev, offset, count = sizes
     flat = [piece for pieces in windows for piece, _ in pieces]
     chip_block = flat[0].shape[-1]
@@ -259,8 +276,8 @@
         spots=[spot for _, spot in ready],
         chained=whole is not None,
     )
-    operands = [place, counts] + flat + [part for part, _ in ready]
-    in_specs = [SMEM_SPEC] + [VMEM_SPEC] * (1 + len(flat)) + [ANY_SPEC] * len(ready)
+    operands = [place, counts, sent] + flat + [part for part, _ in ready]
+    in_specs = [SMEM_SPEC] + [VMEM_SPEC] * (2 + len(flat)) + [ANY_SPEC] * len(ready)
     aliases = {}
     if whole is not None:
         aliases = {len(operands): 0}
@@ -383,7 +400,7 @@
         return lax.optimization_barrier((value, *ties))[0] if ties else value
 
     def known(name):
-        limits = dict(g=halves, s=halves, y=halves, k=mods, o=2, c=1)
+        limits = dict(g=halves, s=halves, y=halves, k=mods, o=2)
         return all(int(at) < limits.get(name[0], own_units + halves) for at in name[-1])
 
     def get(name):
@@ -394,16 +411,12 @@
     def make(kind, name, first, second=0):
         if kind == "k":
             joined = [own_frames, other] if first == 0 else [get("k0")[-1]]
-            split = halves > 1 and (first > 0 or own_units > 1)
-            return order_pixels(place, tied(key, name), joined, first, mods, parts, split)
+            split = first > 0 or own_units > 1
+            return order_pixels(place, tied(key, name), counts, joined, first, mods, parts, split)
         if kind == "y":
-            at = 1 + first if halves > 1 else 0
             return jnp.stack(
-                [along_mod(tied(get(f"k{step}")[at], name), step) for step in range(1, mods)]
-            )
-        if kind == "c":
-            value = tied(counts, name)
-            return sum([value] + [along_mod(value, step) for step in range(1, mods)])
+                [along_mod(tied(get(f"k{step}")[1 + first], name), step) for step in range(1, mods)]
+            )
         if kind == "u":
             if first >= own_units:
                 return get(f"y{first - own_units}")
@@ -442,7 +455,7 @@
         filled = [spot(0, at) for at in range(halves)] if phase and not part else []
         sizes = (group_cycles, cycle_dev, offsets[part], parts[part])
         return grams(
-            place, tied(get("c0"), name), whole, windows, choice, sizes, phase, frame_count, filled
+            place, tied(counts, name), get(f"u{own_units}"), whole, windows, choice, sizes, phase, frame_count, filled
         )
 
     def spot(phase, part):

time: 94.4 us -> 86.6 us (0.917)
  the two profiles are of different devices: /device:TPU:27 before, /device:TPU:0 now
where the time goes in v4:
time: 86.6 us; the launch traced here: 85.4 us
  starting transfers between devices  40.4 us (47%)
  waiting for transfers between devices  24.2 us (28%)
  Pallas kernels  19.6 us (23%)
    ppermute x9, starting transfers between devices, other_pair(): lax.ppermute(value, 'frame', [(source, source ^ 2) for source in sources])  22.9 us
    ppermute x9, waiting for transfers between devices, other_pair(): lax.ppermute(value, 'frame', [(source, source ^ 2) for source in sources])  13.6 us
    pallas_call x4, Pallas kernels, grams(): pl.pallas_call(kernel, out_shape=[jax.ShapeDtypeStruct((cycle_dev, block,...  10.9 us
    ppermute x8, starting transfers between devices, shifted(): lax.ppermute(value, 'frame', [(source, source - step) for source in range...  10.3 us
    ppermute x8, waiting for transfers between devices, shifted(): lax.ppermute(value, 'frame', [(source, source - step) for source in range...  8.29 us
    ppermute x3, starting transfers between devices, along_mod(): return lax.ppermute(value, ('frame', 'mod'), pairs)  6.23 us
    pallas_call x2, Pallas kernels, order_pixels(): pl.pallas_call(functools.partial(order_kernel, step=step, mods=mods, part...  5.96 us
    ppermute x5, waiting for transfers between devices, other_core(): lax.ppermute(value, 'frame', [(source, source ^ 1) for source in range(co...  2.32 us
  transfers between devices with their start and end apart: 25, of which 12 were waited for; matrix products, arithmetic and copies ran while one was open for 1% of the time, Pallas kernels for 18%

profile of v4, /device:TPU:0, one launch (start us, length us, event | category | flops | bytes accessed | tf_op | source)
XLA Modules:
  0.0 85.4 jit_solution(9269025418829833463)
XLA Ops:
  0.0 0.5 collective-permute-start
  0.5 0.7 compare_select_fusion.label_ref
  1.2 1.2 %shard_map.37 = (f32[256,256]{1,0:T(8,128)S(1)}, f32[16,128]{1,0:T(8,128)S(1)}, bf16[128,4096]{1,0:T(8,128)(2,1)S(1)}) custom-call(s32[4096]{0:T(1024)S(1)} %compare_select_fusion.label_ref, bf16[128,4096]{1,0:T(8,128)(2,1)} %frames_hbm.1), custom_call_target="tpu_custom_call" | custom-call | flops 100663296 | bytes 32768 | tf_op jit(solution)/shard_map/pallas_call | solution.py:82
  2.4 0.1 pad_add_fusion.place_ref
  2.5 0.4 collective-permute-done.rest_1_
  3.0 3.0 %shard_map.38 = (bf16[1024,256]{1,0:T(8,128)(2,1)S(1)}, bf16[512,256]{1,0:T(8,128)(2,1)S(1)}, bf16[512,256]{1,0:T(8,128)(2,1)S(1)}, bf16[256,4096]{1,0:T(8,128)(2,1)S(1)}) custom-call(s32[3]{0:T(128)S(1)} %pad_add_fusion.place_ref, f32[256,256]{1,0:T(8,128)S(1)} %get-tuple-element.35.key_ref, f32[16,128]{1,0:T(8,128)S(1)} %get-tuple-element.54.counts_ref, ...), custom_call_target="tpu_custom_call" | custom-call | flops 2147483648 | bytes 2097152 | tf_op jit(solution)/shard_map/pallas_call | solution.py:153
  6.0 1.3 %collective-permute-start.7 = (bf16[1024,256]{1,0:T(8,128)(2,1)S(1)}, bf16[1024,256]{1,0:T(8,128)(2,1)S(1)}, u32[]{:S(2)}, u32[]{:S(2)}) collective-permute-start(bf16[1024,256]{1,0:T(8,128)(2,1)S(1)} %get-tuple-element.43), channel_id=1, source_target_pairs={{4,0},{6,2},{12,8},{14,10},{20,16},{22,18},{28,24},{30,26},{5,1},{... | collective-permute-start | bytes 1572872 | tf_op jit(solution)/shard_map/ppermute | solution.py:357
  7.3 1.3 %collective-permute-start.2 = (bf16[1,512,256]{2,1,0:T(8,128)(2,1)S(1)}, bf16[1,512,256]{2,1,0:T(8,128)(2,1)S(1)}, u32[]{:S(2)}, u32[]{:S(2)}) collective-permute-start(bf16[1,512,256]{2,1,0:T(8,128)(2,1)S(1)} %bitcast.26), channel_id=1, source_target_pairs={{8,0},{10,2},{12,4},{14,6},{16,8},{18,10},{20,12},{22,14},{24,16},... | collective-permute-start | bytes 786440 | tf_op jit(solution)/shard_map/ppermute | solution.py:351
  8.6 1.3 %collective-permute-start.10 = (bf16[1,512,256]{2,1,0:T(8,128)(2,1)S(1)}, bf16[1,512,256]{2,1,0:T(8,128)(2,1)S(1)}, u32[]{:S(2)}, u32[]{:S(2)}) collective-permute-start(bf16[1,512,256]{2,1,0:T(8,128)(2,1)S(1)} %bitcast.20), channel_id=1, source_target_pairs={{8,0},{10,2},{12,4},{14,6},{16,8},{18,10},{20,12},{22,14},{24,16},... | collective-permute-start | bytes 786440 | tf_op jit(solution)/shard_map/ppermute | solution.py:351
  9.9 2.9 %shard_map.39 = (bf16[1024,256]{1,0:T(8,128)(2,1)S(1)}, bf16[528,256]{1,0:T(8,128)(2,1)S(1)}, bf16[512,256]{1,0:T(8,128)(2,1)S(1)}) custom-call(s32[3]{0:T(128)S(1)} %pad_add_fusion.place_ref, f32[256,256]{1,0:T(8,128)S(1)} %get-tuple-element.35.key_ref, f32[16,128]{1,0:T(8,128)S(1)} %get-tuple-element.54.counts_ref, ...), custom_call_target="tpu_custom_call" | custom-call | flops 2147483648 | bytes 2097152 | tf_op jit(solution)/shard_map/pallas_call | solution.py:153
  12.8 3.0 %collective-permute-start.1 = (bf16[528,256]{1,0:T(8,128)(2,1)S(1)}, bf16[528,256]{1,0:T(8,128)(2,1)S(1)}, u32[]{:S(2)}, u32[]{:S(2)}) collective-permute-start(bf16[528,256]{1,0:T(8,128)(2,1)S(1)} %get-tuple-element.40), channel_id=1, source_target_pairs={{0,1},{1,0},{2,3},{3,2},{4,5},{5,4},{6,7},{7,6},{8,9},{9,8},{10,11... | collective-permute-start | bytes 811016 | tf_op jit(solution)/shard_map/ppermute | solution.py:373
  15.8 3.5 %collective-permute-done.2.rest_2_ = bf16[1,512,256]{2,1,0:T(8,128)(2,1)S(1)} collective-permute-done((bf16[1,512,256]{2,1,0:T(8,128)(2,1)S(1)}, bf16[1,512,256]{2,1,0:T(8,128)(2,1)S(1)}, u32[]{:S(2)}, u32[]{:S(2)}) %collective-permute-start.2) | collective-permute-done | bytes 262176 | tf_op jit(solution)/shard_map/ppermute | solution.py:351
  19.2 1.3 %collective-permute-start.4 = (bf16[1,512,256]{2,1,0:T(8,128)(2,1)S(1)}, bf16[1,512,256]{2,1,0:T(8,128)(2,1)S(1)}, u32[]{:S(2)}, u32[]{:S(2)}) collective-permute-start(bf16[1,512,256]{2,1,0:T(8,128)(2,1)S(1)} %collective-permute-done.2.rest_2_), channel_id=1, source_target_pairs={{8,0},{10,2},{12,4},{14,6},{16,8},{18,10},{20,12},{22,14},{24,16},... | collective-permute-start | bytes 786440 | tf_op jit(solution)/shard_map/ppermute | solution.py:351
  20.5 4.3 %collective-permute-done.10.rest_2_ = bf16[1,512,256]{2,1,0:T(8,128)(2,1)S(1)} collective-permute-done((bf16[1,512,256]{2,1,0:T(8,128)(2,1)S(1)}, bf16[1,512,256]{2,1,0:T(8,128)(2,1)S(1)}, u32[]{:S(2)}, u32[]{:S(2)}) %collective-permute-start.10) | collective-permute-done | bytes 262176 | tf_op jit(solution)/shard_map/ppermute | solution.py:351
  24.9 0.0 collective-permute-done.7
  24.9 2.7 %collective-permute-start.11 = (bf16[1,512,256]{2,1,0:T(8,128)(2,1)S(1)}, bf16[1,512,256]{2,1,0:T(8,128)(2,1)S(1)}, u32[]{:S(2)}, u32[]{:S(2)}) collective-permute-start(bf16[1,512,256]{2,1,0:T(8,128)(2,1)S(1)} %collective-permute-done.10.rest_2_), channel_id=1, source_target_pairs={{0,4},{2,6},{4,0},{6,2},{8,12},{10,14},{12,8},{14,10},{16,20},{18,... | collective-permute-start | bytes 786440 | tf_op jit(solution)/shard_map/ppermute | solution.py:357
  27.6 2.0 %collective-permute-start.8 = (bf16[512,256]{1,0:T(8,128)(2,1)S(1)}, bf16[512,256]{1,0:T(8,128)(2,1)S(1)}, u32[]{:S(2)}, u32[]{:S(2)}) collective-permute-start(bf16[512,256]{1,0:T(8,128)(2,1)S(1)} %get-tuple-element.44), channel_id=1, source_target_pairs={{0,1},{1,0},{2,3},{3,2},{4,5},{5,4},{6,7},{7,6},{8,9},{9,8},{10,11... | collective-permute-start | bytes 786440 | tf_op jit(solution)/shard_map/ppermute | solution.py:373
  29.6 0.0 collective-permute-done.1
  29.6 1.3 %collective-permute-start.3 = (bf16[1,528,256]{2,1,0:T(8,128)(2,1)S(1)}, bf16[1,528,256]{2,1,0:T(8,128)(2,1)S(1)}, u32[]{:S(2)}, u32[]{:S(2)}) collective-permute-start(bf16[1,528,256]{2,1,0:T(8,128)(2,1)S(1)} %bitcast.9), channel_id=1, source_target_pairs={{8,0},{10,2},{12,4},{14,6},{16,8},{18,10},{20,12},{22,14},{24,16},... | collective-permute-start | bytes 811016 | tf_op jit(solution)/shard_map/ppermute | solution.py:351
  30.9 0.1 collective-permute-start.6
  30.9 0.0 collective-permute-done.4.rest_4_
  31.0 1.3 %collective-permute-start.14 = (bf16[1,512,256]{2,1,0:T(8,128)(2,1)S(1)}, bf16[1,512,256]{2,1,0:T(8,128)(2,1)S(1)}, u32[]{:S(2)}, u32[]{:S(2)}) collective-permute-start(bf16[1,512,256]{2,1,0:T(8,128)(2,1)S(1)} %collective-permute-done.10.rest_2_), channel_id=1, source_target_pairs={{8,0},{10,2},{12,4},{14,6},{16,8},{18,10},{20,12},{22,14},{24,16},... | collective-permute-start | bytes 786440 | tf_op jit(solution)/shard_map/ppermute | solution.py:351
  32.3 2.1 %collective-permute-done.11.rest_6_ = bf16[1,512,256]{2,1,0:T(8,128)(2,1)S(1)} collective-permute-done((bf16[1,512,256]{2,1,0:T(8,128)(2,1)S(1)}, bf16[1,512,256]{2,1,0:T(8,128)(2,1)S(1)}, u32[]{:S(2)}, u32[]{:S(2)}) %collective-permute-start.11) | collective-permute-done | bytes 262176 | tf_op jit(solution)/shard_map/ppermute | solution.py:357
  34.3 1.3 %collective-permute-start.16 = (bf16[1024,256]{1,0:T(8,128)(2,1)S(1)}, bf16[1024,256]{1,0:T(8,128)(2,1)S(1)}, u32[]{:S(2)}, u32[]{:S(2)}) collective-permute-start(bf16[1024,256]{1,0:T(8,128)(2,1)S(1)} %get-tuple-element.39), channel_id=1, source_target_pairs={{4,1},{5,0},{6,3},{7,2},{12,9},{13,8},{14,11},{15,10},{20,17},{21,... | collective-permute-start | bytes 1572872 | tf_op jit(solution)/shard_map/ppermute | solution.py:373
  35.6 0.0 collective-permute-done.8
  35.6 6.1 %collective-permute-start.12 = (bf16[1,512,256]{2,1,0:T(8,128)(2,1)S(1)}, bf16[1,512,256]{2,1,0:T(8,128)(2,1)S(1)}, u32[]{:S(2)}, u32[]{:S(2)}) collective-permute-start(bf16[1,512,256]{2,1,0:T(8,128)(2,1)S(1)} %collective-permute-done.4.rest_4_), channel_id=1, source_target_pairs={{0,4},{2,6},{8,12},{10,14},{16,20},{18,22},{24,28},{26,30},{1,5},{... | collective-permute-start | bytes 786440 | tf_op jit(solution)/shard_map/ppermute | solution.py:357
  41.8 0.0 collective-permute-done.3.rest_3_
  41.8 1.3 %collective-permute-start.5 = (bf16[1,528,256]{2,1,0:T(8,128)(2,1)S(1)}, bf16[1,528,256]{2,1,0:T(8,128)(2,1)S(1)}, u32[]{:S(2)}, u32[]{:S(2)}) collective-permute-start(bf16[1,528,256]{2,1,0:T(8,128)(2,1)S(1)} %collective-permute-done.3.rest_3_), channel_id=1, source_target_pairs={{8,0},{10,2},{12,4},{14,6},{16,8},{18,10},{20,12},{22,14},{24,16},... | collective-permute-start | bytes 811016 | tf_op jit(solution)/shard_map/ppermute | solution.py:351
  43.1 0.0 collective-permute-done.6.rest_6_
  43.1 0.1 collective-permute-start.9
  43.2 0.1 collective-permute-done.14.rest_4_
  43.3 1.3 %collective-permute-start.18 = (bf16[1,512,256]{2,1,0:T(8,128)(2,1)S(1)}, bf16[1,512,256]{2,1,0:T(8,128)(2,1)S(1)}, u32[]{:S(2)}, u32[]{:S(2)}) collective-permute-start(bf16[1,512,256]{2,1,0:T(8,128)(2,1)S(1)} %bitcast.23), channel_id=1, source_target_pairs={{8,0},{10,2},{12,4},{14,6},{16,8},{18,10},{20,12},{22,14},{24,16},... | collective-permute-start | bytes 786440 | tf_op jit(solution)/shard_map/ppermute | solution.py:351
  44.6 2.0 %collective-permute-done.12.rest_8_ = bf16[1,512,256]{2,1,0:T(8,128)(2,1)S(1)} collective-permute-done((bf16[1,512,256]{2,1,0:T(8,128)(2,1)S(1)}, bf16[1,512,256]{2,1,0:T(8,128)(2,1)S(1)}, u32[]{:S(2)}, u32[]{:S(2)}) %collective-permute-start.12) | collective-permute-done | bytes 262176 | tf_op jit(solution)/shard_map/ppermute | solution.py:357
  46.6 4.4 %collective-permute-start.15 = (bf16[1,512,256]{2,1,0:T(8,128)(2,1)S(1)}, bf16[1,512,256]{2,1,0:T(8,128)(2,1)S(1)}, u32[]{:S(2)}, u32[]{:S(2)}) collective-permute-start(bf16[1,512,256]{2,1,0:T(8,128)(2,1)S(1)} %collective-permute-done.14.rest_4_), channel_id=1, source_target_pairs={{0,4},{2,6},{8,12},{10,14},{16,20},{18,22},{24,28},{26,30},{1,5},{... | collective-permute-start | bytes 786440 | tf_op jit(solution)/shard_map/ppermute | solution.py:357
  51.0 0.4 collective-permute-done.5.rest_5_
  51.4 2.9 %collective-permute-start.13 = (bf16[1,528,256]{2,1,0:T(8,128)(2,1)S(1)}, bf16[1,528,256]{2,1,0:T(8,128)(2,1)S(1)}, u32[]{:S(2)}, u32[]{:S(2)}) collective-permute-start(bf16[1,528,256]{2,1,0:T(8,128)(2,1)S(1)} %collective-permute-done.5.rest_5_), channel_id=1, source_target_pairs={{0,4},{2,6},{8,12},{10,14},{16,20},{18,22},{24,28},{26,30},{1,5},{... | collective-permute-start | bytes 811016 | tf_op jit(solution)/shard_map/ppermute | solution.py:357
  54.3 0.0 collective-permute-done.18.rest_3_
  54.3 1.3 %collective-permute-start.19 = (bf16[1,512,256]{2,1,0:T(8,128)(2,1)S(1)}, bf16[1,512,256]{2,1,0:T(8,128)(2,1)S(1)}, u32[]{:S(2)}, u32[]{:S(2)}) collective-permute-start(bf16[1,512,256]{2,1,0:T(8,128)(2,1)S(1)} %collective-permute-done.18.rest_3_), channel_id=1, source_target_pairs={{8,0},{10,2},{12,4},{14,6},{16,8},{18,10},{20,12},{22,14},{24,16},... | collective-permute-start | bytes 786440 | tf_op jit(solution)/shard_map/ppermute | solution.py:351
  55.6 0.0 collective-permute-done.16
  55.6 0.0 collective-permute-done.9.rest_7_
  55.6 0.9 %collective-permute-start.20 = (bf16[1,512,256]{2,1,0:T(8,128)(2,1)S(1)}, bf16[1,512,256]{2,1,0:T(8,128)(2,1)S(1)}, u32[]{:S(2)}, u32[]{:S(2)}) collective-permute-start(bf16[1,512,256]{2,1,0:T(8,128)(2,1)S(1)} %collective-permute-done.18.rest_3_), channel_id=1, source_target_pairs={{0,4},{2,6},{4,0},{6,2},{8,12},{10,14},{12,8},{14,10},{16,20},{18,... | collective-permute-start | bytes 786440 | tf_op jit(solution)/shard_map/ppermute | solution.py:357
  56.6 1.4 %collective-permute-done.15.rest_8_ = bf16[1,512,256]{2,1,0:T(8,128)(2,1)S(1)} collective-permute-done((bf16[1,512,256]{2,1,0:T(8,128)(2,1)S(1)}, bf16[1,512,256]{2,1,0:T(8,128)(2,1)S(1)}, u32[]{:S(2)}, u32[]{:S(2)}) %collective-permute-start.15) | collective-permute-done | bytes 262176 | tf_op jit(solution)/shard_map/ppermute | solution.py:357
  58.0 2.7 %shard_map.40 = (f32[8,128,1024]{2,1,0:T(8,128)}, f32[2,128,512]{2,1,0:T(8,128)S(1)}) custom-call(s32[3]{0:T(128)S(1)} %pad_add_fusion.place_ref, f32[16,128]{1,0:T(8,128)S(1)} %get-tuple-element.54.counts_ref, bf16[1,528,256]{2,1,0:T(8,128)(2,1)S(1)} %bitcast.10, bf16[1,512,256]{2,1,0:T(8,128)(2,1)S(1)} %bitcast.27, bf16[1,528,256]{2,1,0:T(8,128)(2,1)S(1)} %bitcast.11, ...), custom_call_target="tpu_custom_call" | custom-call | flops 402653184 | bytes 1048576 | tf_op jit(solution)/shard_map/pallas_call | solution.py:286
  60.7 0.1 collective-permute-start.17
  60.8 2.3 %collective-permute-done.13.rest_9_ = bf16[1,528,256]{2,1,0:T(8,128)(2,1)S(1)} collective-permute-done((bf16[1,528,256]{2,1,0:T(8,128)(2,1)S(1)}, bf16[1,528,256]{2,1,0:T(8,128)(2,1)S(1)}, u32[]{:S(2)}, u32[]{:S(2)}) %collective-permute-start.13) | collective-permute-done | bytes 270368 | tf_op jit(solution)/shard_map/ppermute | solution.py:357
  63.1 0.0 collective-permute-done.19.rest_5_
  63.1 2.8 %collective-permute-done.20.rest_7_ = bf16[1,512,256]{2,1,0:T(8,128)(2,1)S(1)} collective-permute-done((bf16[1,512,256]{2,1,0:T(8,128)(2,1)S(1)}, bf16[1,512,256]{2,1,0:T(8,128)(2,1)S(1)}, u32[]{:S(2)}, u32[]{:S(2)}) %collective-permute-start.20) | collective-permute-done | bytes 262176 | tf_op jit(solution)/shard_map/ppermute | solution.py:357
  65.9 2.7 %shard_map.41 = (f32[8,128,1024]{2,1,0:T(8,128)}, f32[2,128,512]{2,1,0:T(8,128)S(1)}) custom-call(s32[3]{0:T(128)S(1)} %pad_add_fusion.place_ref, f32[16,128]{1,0:T(8,128)S(1)} %get-tuple-element.54.counts_ref, bf16[1,528,256]{2,1,0:T(8,128)(2,1)S(1)} %bitcast.12, bf16[1,512,256]{2,1,0:T(8,128)(2,1)S(1)} %bitcast.21, ...), custom_call_target="tpu_custom_call", output_to_operand_aliasing={{0}: (11, {})} | custom-call | flops 402653184 | bytes 1048576 | tf_op jit(solution)/shard_map/pallas_call | solution.py:286
  68.5 0.1 collective-permute-start.21
  68.6 4.4 %collective-permute-start.23 = (bf16[1,512,256]{2,1,0:T(8,128)(2,1)S(1)}, bf16[1,512,256]{2,1,0:T(8,128)(2,1)S(1)}, u32[]{:S(2)}, u32[]{:S(2)}) collective-permute-start(bf16[1,512,256]{2,1,0:T(8,128)(2,1)S(1)} %collective-permute-done.19.rest_5_), channel_id=1, source_target_pairs={{0,4},{2,6},{8,12},{10,14},{16,20},{18,22},{24,28},{26,30},{1,5},{... | collective-permute-start | bytes 786440 | tf_op jit(solution)/shard_map/ppermute | solution.py:357
  73.0 0.0 collective-permute-done.17.rest_10_
  73.0 0.0 collective-permute-done.21.rest_11_
  73.1 2.9 %shard_map.42 = (f32[8,128,1024]{2,1,0:T(8,128)}, f32[2,128,512]{2,1,0:T(8,128)S(1)}) custom-call(s32[3]{0:T(128)S(1)} %pad_add_fusion.place_ref, f32[16,128]{1,0:T(8,128)S(1)} %get-tuple-element.54.counts_ref, bf16[1,528,256]{2,1,0:T(8,128)(2,1)S(1)} %bitcast.13, bf16[1,512,256]{2,1,0:T(8,128)(2,1)S(1)} %bitcast.28, ...), custom_call_target="tpu_custom_call", output_to_operand_aliasing={{0}: (15, {})} | custom-call | flops 402653184 | bytes 1048576 | tf_op jit(solution)/shard_map/pallas_call | solution.py:286
  76.0 0.3 collective-permute-start.22
  76.2 3.0 %collective-permute-done.23.rest_9_ = bf16[1,512,256]{2,1,0:T(8,128)(2,1)S(1)} collective-permute-done((bf16[1,512,256]{2,1,0:T(8,128)(2,1)S(1)}, bf16[1,512,256]{2,1,0:T(8,128)(2,1)S(1)}, u32[]{:S(2)}, u32[]{:S(2)}) %collective-permute-start.23) | collective-permute-done | bytes 262176 | tf_op jit(solution)/shard_map/ppermute | solution.py:357
  79.2 2.7 %shard_map.43 = (f32[8,128,1024]{2,1,0:T(8,128)}, f32[2,128,512]{2,1,0:T(8,128)S(1)}) custom-call(s32[3]{0:T(128)S(1)} %pad_add_fusion.place_ref, f32[16,128]{1,0:T(8,128)S(1)} %get-tuple-element.54.counts_ref, bf16[1,528,256]{2,1,0:T(8,128)(2,1)S(1)} %bitcast.15, bf16[1,512,256]{2,1,0:T(8,128)(2,1)S(1)} %bitcast.22, ...), custom_call_target="tpu_custom_call", output_to_operand_aliasing={{0}: (13, {})} | custom-call | flops 402653184 | bytes 1048576 | tf_op jit(solution)/shard_map/pallas_call | solution.py:286
  81.9 0.1 collective-permute-start.24
  82.0 0.0 collective-permute-done.22.rest_0_
  82.0 1.9 %collective-permute-done.24.rest_1_ = f32[2,128,512]{2,1,0:T(8,128)S(1)} collective-permute-done((f32[2,128,512]{2,1,0:T(8,128)S(1)}, f32[2,128,512]{2,1,0:T(8,128)S(1)}, u32[]{:S(2)}, u32[]{:S(2)}) %collective-permute-start.24) | collective-permute-done | bytes 524320 | tf_op jit(solution)/shard_map/ppermute | solution.py:362
  83.9 1.5 %shard_map.44 = f32[8,128,1024]{2,1,0:T(8,128)} custom-call(s32[3]{0:T(128)S(1)} %pad_add_fusion.place_ref, f32[2,128,512]{2,1,0:T(8,128)S(1)} %collective-permute-done.22.rest_0_, f32[2,128,512]{2,1,0:T(8,128)S(1)} %collective-permute-done.24.rest_1_, f32[8,128,1024]{2,1,0:T(8,128)} %get-tuple-element.62.rest_2_), custom_call_target="tpu_custom_call", output_to_operand_aliasing={{}: (3, {})} | custom-call | bytes 2097152 | tf_op jit(solution)/shard_map/pallas_call | solution.py:336
Async XLA Ops:
  0.0 3.0 %collective-permute-start = (bf16[128,4096]{1,0:T(8,128)(2,1)}, bf16[128,4096]{1,0:T(8,128)(2,1)S(1)}, u32[]{:S(2)}, u32[]{:S(2)}) collective-permute-start(bf16[128,4096]{1,0:T(8,128)(2,1)} %frames_hbm.1), channel_id=1, source_target_pairs={{0,2},{2,0},{4,6},{6,4},{8,10},{10,8},{12,14},{14,12},{16,18},{18,... | collective-permute-start | bytes 3145736 | tf_op jit(solution)/shard_map/ppermute | solution.py:362
  6.0 18.9 %collective-permute-start.7 = (bf16[1024,256]{1,0:T(8,128)(2,1)S(1)}, bf16[1024,256]{1,0:T(8,128)(2,1)S(1)}, u32[]{:S(2)}, u32[]{:S(2)}) collective-permute-start(bf16[1024,256]{1,0:T(8,128)(2,1)S(1)} %get-tuple-element.43), channel_id=1, source_target_pairs={{4,0},{6,2},{12,8},{14,10},{20,16},{22,18},{28,24},{30,26},{5,1},{... | collective-permute-start | bytes 1572872 | tf_op jit(solution)/shard_map/ppermute | solution.py:357
  7.3 11.9 %collective-permute-start.2 = (bf16[1,512,256]{2,1,0:T(8,128)(2,1)S(1)}, bf16[1,512,256]{2,1,0:T(8,128)(2,1)S(1)}, u32[]{:S(2)}, u32[]{:S(2)}) collective-permute-start(bf16[1,512,256]{2,1,0:T(8,128)(2,1)S(1)} %bitcast.26), channel_id=1, source_target_pairs={{8,0},{10,2},{12,4},{14,6},{16,8},{18,10},{20,12},{22,14},{24,16},... | collective-permute-start | bytes 786440 | tf_op jit(solution)/shard_map/ppermute | solution.py:351
  8.6 16.3 %collective-permute-start.10 = (bf16[1,512,256]{2,1,0:T(8,128)(2,1)S(1)}, bf16[1,512,256]{2,1,0:T(8,128)(2,1)S(1)}, u32[]{:S(2)}, u32[]{:S(2)}) collective-permute-start(bf16[1,512,256]{2,1,0:T(8,128)(2,1)S(1)} %bitcast.20), channel_id=1, source_target_pairs={{8,0},{10,2},{12,4},{14,6},{16,8},{18,10},{20,12},{22,14},{24,16},... | collective-permute-start | bytes 786440 | tf_op jit(solution)/shard_map/ppermute | solution.py:351
  12.8 16.8 %collective-permute-start.1 = (bf16[528,256]{1,0:T(8,128)(2,1)S(1)}, bf16[528,256]{1,0:T(8,128)(2,1)S(1)}, u32[]{:S(2)}, u32[]{:S(2)}) collective-permute-start(bf16[528,256]{1,0:T(8,128)(2,1)S(1)} %get-tuple-element.40), channel_id=1, source_target_pairs={{0,1},{1,0},{2,3},{3,2},{4,5},{5,4},{6,7},{7,6},{8,9},{9,8},{10,11... | collective-permute-start | bytes 811016 | tf_op jit(solution)/shard_map/ppermute | solution.py:373
  19.2 11.7 %collective-permute-start.4 = (bf16[1,512,256]{2,1,0:T(8,128)(2,1)S(1)}, bf16[1,512,256]{2,1,0:T(8,128)(2,1)S(1)}, u32[]{:S(2)}, u32[]{:S(2)}) collective-permute-start(bf16[1,512,256]{2,1,0:T(8,128)(2,1)S(1)} %collective-permute-done.2.rest_2_), channel_id=1, source_target_pairs={{8,0},{10,2},{12,4},{14,6},{16,8},{18,10},{20,12},{22,14},{24,16},... | collective-permute-start | bytes 786440 | tf_op jit(solution)/shard_map/ppermute | solution.py:351
  24.9 9.5 %collective-permute-start.11 = (bf16[1,512,256]{2,1,0:T(8,128)(2,1)S(1)}, bf16[1,512,256]{2,1,0:T(8,128)(2,1)S(1)}, u32[]{:S(2)}, u32[]{:S(2)}) collective-permute-start(bf16[1,512,256]{2,1,0:T(8,128)(2,1)S(1)} %collective-permute-done.10.rest_2_), channel_id=1, source_target_pairs={{0,4},{2,6},{4,0},{6,2},{8,12},{10,14},{12,8},{14,10},{16,20},{18,... | collective-permute-start | bytes 786440 | tf_op jit(solution)/shard_map/ppermute | solution.py:357
  27.6 8.1 %collective-permute-start.8 = (bf16[512,256]{1,0:T(8,128)(2,1)S(1)}, bf16[512,256]{1,0:T(8,128)(2,1)S(1)}, u32[]{:S(2)}, u32[]{:S(2)}) collective-permute-start(bf16[512,256]{1,0:T(8,128)(2,1)S(1)} %get-tuple-element.44), channel_id=1, source_target_pairs={{0,1},{1,0},{2,3},{3,2},{4,5},{5,4},{6,7},{7,6},{8,9},{9,8},{10,11... | collective-permute-start | bytes 786440 | tf_op jit(solution)/shard_map/ppermute | solution.py:373
  29.6 12.2 %collective-permute-start.3 = (bf16[1,528,256]{2,1,0:T(8,128)(2,1)S(1)}, bf16[1,528,256]{2,1,0:T(8,128)(2,1)S(1)}, u32[]{:S(2)}, u32[]{:S(2)}) collective-permute-start(bf16[1,528,256]{2,1,0:T(8,128)(2,1)S(1)} %bitcast.9), channel_id=1, source_target_pairs={{8,0},{10,2},{12,4},{14,6},{16,8},{18,10},{20,12},{22,14},{24,16},... | collective-permute-start | bytes 811016 | tf_op jit(solution)/shard_map/ppermute | solution.py:351
  30.9 12.2 %collective-permute-start.6 = (bf16[1,512,256]{2,1,0:T(8,128)(2,1)S(1)}, bf16[1,512,256]{2,1,0:T(8,128)(2,1)S(1)}, u32[]{:S(2)}, u32[]{:S(2)}) collective-permute-start(bf16[1,512,256]{2,1,0:T(8,128)(2,1)S(1)} %collective-permute-done.2.rest_2_), channel_id=1, source_target_pairs={{0,4},{2,6},{4,0},{6,2},{8,12},{10,14},{12,8},{14,10},{16,20},{18,... | collective-permute-start | bytes 786440 | tf_op jit(solution)/shard_map/ppermute | solution.py:357
  31.0 12.3 %collective-permute-start.14 = (bf16[1,512,256]{2,1,0:T(8,128)(2,1)S(1)}, bf16[1,512,256]{2,1,0:T(8,128)(2,1)S(1)}, u32[]{:S(2)}, u32[]{:S(2)}) collective-permute-start(bf16[1,512,256]{2,1,0:T(8,128)(2,1)S(1)} %collective-permute-done.10.rest_2_), channel_id=1, source_target_pairs={{8,0},{10,2},{12,4},{14,6},{16,8},{18,10},{20,12},{22,14},{24,16},... | collective-permute-start | bytes 786440 | tf_op jit(solution)/shard_map/ppermute | solution.py:351
  34.3 21.3 %collective-permute-start.16 = (bf16[1024,256]{1,0:T(8,128)(2,1)S(1)}, bf16[1024,256]{1,0:T(8,128)(2,1)S(1)}, u32[]{:S(2)}, u32[]{:S(2)}) collective-permute-start(bf16[1024,256]{1,0:T(8,128)(2,1)S(1)} %get-tuple-element.39), channel_id=1, source_target_pairs={{4,1},{5,0},{6,3},{7,2},{12,9},{13,8},{14,11},{15,10},{20,17},{21,... | collective-permute-start | bytes 1572872 | tf_op jit(solution)/shard_map/ppermute | solution.py:373
  35.6 11.0 %collective-permute-start.12 = (bf16[1,512,256]{2,1,0:T(8,128)(2,1)S(1)}, bf16[1,512,256]{2,1,0:T(8,128)(2,1)S(1)}, u32[]{:S(2)}, u32[]{:S(2)}) collective-permute-start(bf16[1,512,256]{2,1,0:T(8,128)(2,1)S(1)} %collective-permute-done.4.rest_4_), channel_id=1, source_target_pairs={{0,4},{2,6},{8,12},{10,14},{16,20},{18,22},{24,28},{26,30},{1,5},{... | collective-permute-start | bytes 786440 | tf_op jit(solution)/shard_map/ppermute | solution.py:357
  41.8 9.6 %collective-permute-start.5 = (bf16[1,528,256]{2,1,0:T(8,128)(2,1)S(1)}, bf16[1,528,256]{2,1,0:T(8,128)(2,1)S(1)}, u32[]{:S(2)}, u32[]{:S(2)}) collective-permute-start(bf16[1,528,256]{2,1,0:T(8,128)(2,1)S(1)} %collective-permute-done.3.rest_3_), channel_id=1, source_target_pairs={{8,0},{10,2},{12,4},{14,6},{16,8},{18,10},{20,12},{22,14},{24,16},... | collective-permute-start | bytes 811016 | tf_op jit(solution)/shard_map/ppermute | solution.py:351
  43.1 12.5 %collective-permute-start.9 = (bf16[1,528,256]{2,1,0:T(8,128)(2,1)S(1)}, bf16[1,528,256]{2,1,0:T(8,128)(2,1)S(1)}, u32[]{:S(2)}, u32[]{:S(2)}) collective-permute-start(bf16[1,528,256]{2,1,0:T(8,128)(2,1)S(1)} %collective-permute-done.3.rest_3_), channel_id=1, source_target_pairs={{0,4},{2,6},{4,0},{6,2},{8,12},{10,14},{12,8},{14,10},{16,20},{18,... | collective-permute-start | bytes 811016 | tf_op jit(solution)/shard_map/ppermute | solution.py:357
  43.3 11.0 %collective-permute-start.18 = (bf16[1,512,256]{2,1,0:T(8,128)(2,1)S(1)}, bf16[1,512,256]{2,1,0:T(8,128)(2,1)S(1)}, u32[]{:S(2)}, u32[]{:S(2)}) collective-permute-start(bf16[1,512,256]{2,1,0:T(8,128)(2,1)S(1)} %bitcast.23), channel_id=1, source_target_pairs={{8,0},{10,2},{12,4},{14,6},{16,8},{18,10},{20,12},{22,14},{24,16},... | collective-permute-start | bytes 786440 | tf_op jit(solution)/shard_map/ppermute | solution.py:351
  46.6 11.4 %collective-permute-start.15 = (bf16[1,512,256]{2,1,0:T(8,128)(2,1)S(1)}, bf16[1,512,256]{2,1,0:T(8,128)(2,1)S(1)}, u32[]{:S(2)}, u32[]{:S(2)}) collective-permute-start(bf16[1,512,256]{2,1,0:T(8,128)(2,1)S(1)} %collective-permute-done.14.rest_4_), channel_id=1, source_target_pairs={{0,4},{2,6},{8,12},{10,14},{16,20},{18,22},{24,28},{26,30},{1,5},{... | collective-permute-start | bytes 786440 | tf_op jit(solution)/shard_map/ppermute | solution.py:357
  51.4 11.7 %collective-permute-start.13 = (bf16[1,528,256]{2,1,0:T(8,128)(2,1)S(1)}, bf16[1,528,256]{2,1,0:T(8,128)(2,1)S(1)}, u32[]{:S(2)}, u32[]{:S(2)}) collective-permute-start(bf16[1,528,256]{2,1,0:T(8,128)(2,1)S(1)} %collective-permute-done.5.rest_5_), channel_id=1, source_target_pairs={{0,4},{2,6},{8,12},{10,14},{16,20},{18,22},{24,28},{26,30},{1,5},{... | collective-permute-start | bytes 811016 | tf_op jit(solution)/shard_map/ppermute | solution.py:357
  54.3 8.7 %collective-permute-start.19 = (bf16[1,512,256]{2,1,0:T(8,128)(2,1)S(1)}, bf16[1,512,256]{2,1,0:T(8,128)(2,1)S(1)}, u32[]{:S(2)}, u32[]{:S(2)}) collective-permute-start(bf16[1,512,256]{2,1,0:T(8,128)(2,1)S(1)} %collective-permute-done.18.rest_3_), channel_id=1, source_target_pairs={{8,0},{10,2},{12,4},{14,6},{16,8},{18,10},{20,12},{22,14},{24,16},... | collective-permute-start | bytes 786440 | tf_op jit(solution)/shard_map/ppermute | solution.py:351
  55.6 10.2 %collective-permute-start.20 = (bf16[1,512,256]{2,1,0:T(8,128)(2,1)S(1)}, bf16[1,512,256]{2,1,0:T(8,128)(2,1)S(1)}, u32[]{:S(2)}, u32[]{:S(2)}) collective-permute-start(bf16[1,512,256]{2,1,0:T(8,128)(2,1)S(1)} %collective-permute-done.18.rest_3_), channel_id=1, source_target_pairs={{0,4},{2,6},{4,0},{6,2},{8,12},{10,14},{12,8},{14,10},{16,20},{18,... | collective-permute-start | bytes 786440 | tf_op jit(solution)/shard_map/ppermute | solution.py:357
  60.7 12.4 %collective-permute-start.17 = (f32[2,128,512]{2,1,0:T(8,128)S(1)}, f32[2,128,512]{2,1,0:T(8,128)S(1)}, u32[]{:S(2)}, u32[]{:S(2)}) collective-permute-start(f32[2,128,512]{2,1,0:T(8,128)S(1)} %get-tuple-element.51), channel_id=1, source_target_pairs={{0,2},{2,0},{4,6},{6,4},{8,10},{10,8},{12,14},{14,12},{16,18},{18,... | collective-permute-start | bytes 1572872 | tf_op jit(solution)/shard_map/ppermute | solution.py:362
  68.5 4.5 %collective-permute-start.21 = (f32[2,128,512]{2,1,0:T(8,128)S(1)}, f32[2,128,512]{2,1,0:T(8,128)S(1)}, u32[]{:S(2)}, u32[]{:S(2)}) collective-permute-start(f32[2,128,512]{2,1,0:T(8,128)S(1)} %get-tuple-element.57), channel_id=1, source_target_pairs={{0,2},{2,0},{4,6},{6,4},{8,10},{10,8},{12,14},{14,12},{16,18},{18,... | collective-permute-start | bytes 1572872 | tf_op jit(solution)/shard_map/ppermute | solution.py:362
  68.6 10.6 %collective-permute-start.23 = (bf16[1,512,256]{2,1,0:T(8,128)(2,1)S(1)}, bf16[1,512,256]{2,1,0:T(8,128)(2,1)S(1)}, u32[]{:S(2)}, u32[]{:S(2)}) collective-permute-start(bf16[1,512,256]{2,1,0:T(8,128)(2,1)S(1)} %collective-permute-done.19.rest_5_), channel_id=1, source_target_pairs={{0,4},{2,6},{8,12},{10,14},{16,20},{18,22},{24,28},{26,30},{1,5},{... | collective-permute-start | bytes 786440 | tf_op jit(solution)/shard_map/ppermute | solution.py:357
  76.0 6.0 %collective-permute-start.22 = (f32[2,128,512]{2,1,0:T(8,128)S(1)}, f32[2,128,512]{2,1,0:T(8,128)S(1)}, u32[]{:S(2)}, u32[]{:S(2)}) collective-permute-start(f32[2,128,512]{2,1,0:T(8,128)S(1)} %get-tuple-element.59), channel_id=1, source_target_pairs={{0,2},{2,0},{4,6},{6,4},{8,10},{10,8},{12,14},{14,12},{16,18},{18,... | collective-permute-start | bytes 1572872 | tf_op jit(solution)/shard_map/ppermute | solution.py:362
  81.9 2.0 %collective-permute-start.24 = (f32[2,128,512]{2,1,0:T(8,128)S(1)}, f32[2,128,512]{2,1,0:T(8,128)S(1)}, u32[]{:S(2)}, u32[]{:S(2)}) collective-permute-start(f32[2,128,512]{2,1,0:T(8,128)S(1)} %get-tuple-element.61), channel_id=1, source_target_pairs={{0,2},{2,0},{4,6},{6,4},{8,10},{10,8},{12,14},{14,12},{16,18},{18,... | collective-permute-start | bytes 1572872 | tf_op jit(solution)/shard_map/ppermute | solution.py:362

commit v5 on v4

--- a/solution.py
+++ b/solution.py
@@ -204,8 +204,9 @@
         whole = jnp.concatenate(columns, axis=1)
         depth, width = whole.shape
         own_rows = own.T
-        gram[cycle] = dot(own_rows, whole)
-        sums = dot(jnp.ones((PACKED, depth), jnp.bfloat16), whole)[:SUBLANES]
+        ones = jnp.ones((PACKED, depth), jnp.bfloat16)
+        gram[cycle] = dot(jnp.concatenate([own_rows, ones], axis=0), whole)
+        sums = gram[cycle, chip_block : chip_block + SUBLANES, :]
         frame_at = chip * chip_block + phase * lags + iota((SUBLANES, width), 1)
         later[cycle] = jnp.where(frame_at < frame_count, 1.0 / sums, 0.0)
         label = (mod * 2 + core) * group + offset + cycle
@@ -215,7 +216,8 @@
             total += jnp.sum(
                 jnp.where(iota((CYCLES, LANES), 0) == label, sent, 0.0), axis=0, keepdims=True
             )
-        earlier[cycle] = total / dot(own_rows, jnp.ones((depth, LANES), jnp.bfloat16))
+        own_sums = jnp.sum(own_rows.astype(jnp.float32), axis=1, keepdims=True)
+        earlier[cycle] = jnp.broadcast_to(total / own_sums, (chip_block, LANES))
         for target, position in ((theirs_ref, 1 - core), (mine_ref, core)):
             base = pl.multiple_of(position * block, block)
             scales = [
@@ -293,7 +295,7 @@
         out_specs=[ANY_SPEC, VMEM_SPEC],
         scratch_shapes=[
             pltpu.VMEM((count, block, lags), jnp.float32),
-            pltpu.VMEM((count, chip_block, width), jnp.float32),
+            pltpu.VMEM((count, chip_block + PACKED, width), jnp.float32),
             pltpu.VMEM((count, SUBLANES, width), jnp.float32),
             pltpu.VMEM((count, chip_block, LANES), jnp.float32),
             pltpu.SemaphoreType.DMA((count,)),

time: 86.6 us -> 86.5 us (level)
  transfers between devices with their start and end apart: 25 -> 25, of which waited for: 12 -> 12; matrix products, arithmetic and copies ran while one was open for 1% -> 1% of each run, Pallas kernels for 18% -> 17%
where the time goes in v5:
time: 86.5 us; the launch traced here: 85.3 us
  starting transfers between devices  40.4 us (47%)
  waiting for transfers between devices  24.4 us (28%)
  Pallas kernels  19.4 us (22%)
    ppermute x9, starting transfers between devices, other_pair(): lax.ppermute(value, 'frame', [(source, source ^ 2) for source in sources])  22.9 us
    ppermute x9, waiting for transfers between devices, other_pair(): lax.ppermute(value, 'frame', [(source, source ^ 2) for source in sources])  13.7 us
    pallas_call x4, Pallas kernels, grams(): pl.pallas_call(kernel, out_shape=[jax.ShapeDtypeStruct((cycle_dev, block,...  10.7 us
    ppermute x8, starting transfers between devices, shifted(): lax.ppermute(value, 'frame', [(source, source - step) for source in range...  10.3 us
    ppermute x8, waiting for transfers between devices, shifted(): lax.ppermute(value, 'frame', [(source, source - step) for source in range...  8.29 us
    ppermute x3, starting transfers between devices, along_mod(): return lax.ppermute(value, ('frame', 'mod'), pairs)  6.23 us
    pallas_call x2, Pallas kernels, order_pixels(): pl.pallas_call(functools.partial(order_kernel, step=step, mods=mods, part...  5.96 us
    ppermute x5, waiting for transfers between devices, other_core(): lax.ppermute(value, 'frame', [(source, source ^ 1) for source in range(co...  2.32 us
  transfers between devices with their start and end apart: 25, of which 12 were waited for; matrix products, arithmetic and copies ran while one was open for 1% of the time, Pallas kernels for 17%

profile of v5, /device:TPU:0, one launch (start us, length us, event | category | flops | bytes accessed | tf_op | source)
XLA Modules:
  0.0 85.3 jit_solution(15244114664911285587)
XLA Ops:
  0.0 0.5 collective-permute-start
  0.5 0.7 compare_select_fusion.label_ref
  1.2 1.2 %shard_map.37 = (f32[256,256]{1,0:T(8,128)S(1)}, f32[16,128]{1,0:T(8,128)S(1)}, bf16[128,4096]{1,0:T(8,128)(2,1)S(1)}) custom-call(s32[4096]{0:T(1024)S(1)} %compare_select_fusion.label_ref, bf16[128,4096]{1,0:T(8,128)(2,1)} %frames_hbm.1), custom_call_target="tpu_custom_call" | custom-call | flops 100663296 | bytes 32768 | tf_op jit(solution)/shard_map/pallas_call | solution.py:82
  2.4 0.1 pad_add_fusion.place_ref
  2.5 0.4 collective-permute-done.rest_1_
  3.0 3.0 %shard_map.38 = (bf16[1024,256]{1,0:T(8,128)(2,1)S(1)}, bf16[512,256]{1,0:T(8,128)(2,1)S(1)}, bf16[512,256]{1,0:T(8,128)(2,1)S(1)}, bf16[256,4096]{1,0:T(8,128)(2,1)S(1)}) custom-call(s32[3]{0:T(128)S(1)} %pad_add_fusion.place_ref, f32[256,256]{1,0:T(8,128)S(1)} %get-tuple-element.35.key_ref, f32[16,128]{1,0:T(8,128)S(1)} %get-tuple-element.54.counts_ref, ...), custom_call_target="tpu_custom_call" | custom-call | flops 2147483648 | bytes 2097152 | tf_op jit(solution)/shard_map/pallas_call | solution.py:153
  6.0 1.3 %collective-permute-start.7 = (bf16[1024,256]{1,0:T(8,128)(2,1)S(1)}, bf16[1024,256]{1,0:T(8,128)(2,1)S(1)}, u32[]{:S(2)}, u32[]{:S(2)}) collective-permute-start(bf16[1024,256]{1,0:T(8,128)(2,1)S(1)} %get-tuple-element.43), channel_id=1, source_target_pairs={{4,0},{6,2},{12,8},{14,10},{20,16},{22,18},{28,24},{30,26},{5,1},{... | collective-permute-start | bytes 1572872 | tf_op jit(solution)/shard_map/ppermute | solution.py:359
  7.3 1.3 %collective-permute-start.2 = (bf16[1,512,256]{2,1,0:T(8,128)(2,1)S(1)}, bf16[1,512,256]{2,1,0:T(8,128)(2,1)S(1)}, u32[]{:S(2)}, u32[]{:S(2)}) collective-permute-start(bf16[1,512,256]{2,1,0:T(8,128)(2,1)S(1)} %bitcast.26), channel_id=1, source_target_pairs={{8,0},{10,2},{12,4},{14,6},{16,8},{18,10},{20,12},{22,14},{24,16},... | collective-permute-start | bytes 786440 | tf_op jit(solution)/shard_map/ppermute | solution.py:353
  8.6 1.3 %collective-permute-start.10 = (bf16[1,512,256]{2,1,0:T(8,128)(2,1)S(1)}, bf16[1,512,256]{2,1,0:T(8,128)(2,1)S(1)}, u32[]{:S(2)}, u32[]{:S(2)}) collective-permute-start(bf16[1,512,256]{2,1,0:T(8,128)(2,1)S(1)} %bitcast.20), channel_id=1, source_target_pairs={{8,0},{10,2},{12,4},{14,6},{16,8},{18,10},{20,12},{22,14},{24,16},... | collective-permute-start | bytes 786440 | tf_op jit(solution)/shard_map/ppermute | solution.py:353
  9.9 2.9 %shard_map.39 = (bf16[1024,256]{1,0:T(8,128)(2,1)S(1)}, bf16[528,256]{1,0:T(8,128)(2,1)S(1)}, bf16[512,256]{1,0:T(8,128)(2,1)S(1)}) custom-call(s32[3]{0:T(128)S(1)} %pad_add_fusion.place_ref, f32[256,256]{1,0:T(8,128)S(1)} %get-tuple-element.35.key_ref, f32[16,128]{1,0:T(8,128)S(1)} %get-tuple-element.54.counts_ref, ...), custom_call_target="tpu_custom_call" | custom-call | flops 2147483648 | bytes 2097152 | tf_op jit(solution)/shard_map/pallas_call | solution.py:153
  12.8 3.0 %collective-permute-start.1 = (bf16[528,256]{1,0:T(8,128)(2,1)S(1)}, bf16[528,256]{1,0:T(8,128)(2,1)S(1)}, u32[]{:S(2)}, u32[]{:S(2)}) collective-permute-start(bf16[528,256]{1,0:T(8,128)(2,1)S(1)} %get-tuple-element.40), channel_id=1, source_target_pairs={{0,1},{1,0},{2,3},{3,2},{4,5},{5,4},{6,7},{7,6},{8,9},{9,8},{10,11... | collective-permute-start | bytes 811016 | tf_op jit(solution)/shard_map/ppermute | solution.py:375
  15.8 3.5 %collective-permute-done.2.rest_2_ = bf16[1,512,256]{2,1,0:T(8,128)(2,1)S(1)} collective-permute-done((bf16[1,512,256]{2,1,0:T(8,128)(2,1)S(1)}, bf16[1,512,256]{2,1,0:T(8,128)(2,1)S(1)}, u32[]{:S(2)}, u32[]{:S(2)}) %collective-permute-start.2) | collective-permute-done | bytes 262176 | tf_op jit(solution)/shard_map/ppermute | solution.py:353
  19.2 1.3 %collective-permute-start.4 = (bf16[1,512,256]{2,1,0:T(8,128)(2,1)S(1)}, bf16[1,512,256]{2,1,0:T(8,128)(2,1)S(1)}, u32[]{:S(2)}, u32[]{:S(2)}) collective-permute-start(bf16[1,512,256]{2,1,0:T(8,128)(2,1)S(1)} %collective-permute-done.2.rest_2_), channel_id=1, source_target_pairs={{8,0},{10,2},{12,4},{14,6},{16,8},{18,10},{20,12},{22,14},{24,16},... | collective-permute-start | bytes 786440 | tf_op jit(solution)/shard_map/ppermute | solution.py:353
  20.5 4.3 %collective-permute-done.10.rest_2_ = bf16[1,512,256]{2,1,0:T(8,128)(2,1)S(1)} collective-permute-done((bf16[1,512,256]{2,1,0:T(8,128)(2,1)S(1)}, bf16[1,512,256]{2,1,0:T(8,128)(2,1)S(1)}, u32[]{:S(2)}, u32[]{:S(2)}) %collective-permute-start.10) | collective-permute-done | bytes 262176 | tf_op jit(solution)/shard_map/ppermute | solution.py:353
  24.9 0.0 collective-permute-done.7
  24.9 2.7 %collective-permute-start.11 = (bf16[1,512,256]{2,1,0:T(8,128)(2,1)S(1)}, bf16[1,512,256]{2,1,0:T(8,128)(2,1)S(1)}, u32[]{:S(2)}, u32[]{:S(2)}) collective-permute-start(bf16[1,512,256]{2,1,0:T(8,128)(2,1)S(1)} %collective-permute-done.10.rest_2_), channel_id=1, source_target_pairs={{0,4},{2,6},{4,0},{6,2},{8,12},{10,14},{12,8},{14,10},{16,20},{18,... | collective-permute-start | bytes 786440 | tf_op jit(solution)/shard_map/ppermute | solution.py:359
  27.6 2.0 %collective-permute-start.8 = (bf16[512,256]{1,0:T(8,128)(2,1)S(1)}, bf16[512,256]{1,0:T(8,128)(2,1)S(1)}, u32[]{:S(2)}, u32[]{:S(2)}) collective-permute-start(bf16[512,256]{1,0:T(8,128)(2,1)S(1)} %get-tuple-element.44), channel_id=1, source_target_pairs={{0,1},{1,0},{2,3},{3,2},{4,5},{5,4},{6,7},{7,6},{8,9},{9,8},{10,11... | collective-permute-start | bytes 786440 | tf_op jit(solution)/shard_map/ppermute | solution.py:375
  29.6 0.0 collective-permute-done.1
  29.6 1.3 %collective-permute-start.3 = (bf16[1,528,256]{2,1,0:T(8,128)(2,1)S(1)}, bf16[1,528,256]{2,1,0:T(8,128)(2,1)S(1)}, u32[]{:S(2)}, u32[]{:S(2)}) collective-permute-start(bf16[1,528,256]{2,1,0:T(8,128)(2,1)S(1)} %bitcast.9), channel_id=1, source_target_pairs={{8,0},{10,2},{12,4},{14,6},{16,8},{18,10},{20,12},{22,14},{24,16},... | collective-permute-start | bytes 811016 | tf_op jit(solution)/shard_map/ppermute | solution.py:353
  30.9 0.1 collective-permute-start.6
  30.9 0.0 collective-permute-done.4.rest_4_
  31.0 1.3 %collective-permute-start.14 = (bf16[1,512,256]{2,1,0:T(8,128)(2,1)S(1)}, bf16[1,512,256]{2,1,0:T(8,128)(2,1)S(1)}, u32[]{:S(2)}, u32[]{:S(2)}) collective-permute-start(bf16[1,512,256]{2,1,0:T(8,128)(2,1)S(1)} %collective-permute-done.10.rest_2_), channel_id=1, source_target_pairs={{8,0},{10,2},{12,4},{14,6},{16,8},{18,10},{20,12},{22,14},{24,16},... | collective-permute-start | bytes 786440 | tf_op jit(solution)/shard_map/ppermute | solution.py:353
  32.3 2.1 %collective-permute-done.11.rest_6_ = bf16[1,512,256]{2,1,0:T(8,128)(2,1)S(1)} collective-permute-done((bf16[1,512,256]{2,1,0:T(8,128)(2,1)S(1)}, bf16[1,512,256]{2,1,0:T(8,128)(2,1)S(1)}, u32[]{:S(2)}, u32[]{:S(2)}) %collective-permute-start.11) | collective-permute-done | bytes 262176 | tf_op jit(solution)/shard_map/ppermute | solution.py:359
  34.3 1.3 %collective-permute-start.16 = (bf16[1024,256]{1,0:T(8,128)(2,1)S(1)}, bf16[1024,256]{1,0:T(8,128)(2,1)S(1)}, u32[]{:S(2)}, u32[]{:S(2)}) collective-permute-start(bf16[1024,256]{1,0:T(8,128)(2,1)S(1)} %get-tuple-element.39), channel_id=1, source_target_pairs={{4,1},{5,0},{6,3},{7,2},{12,9},{13,8},{14,11},{15,10},{20,17},{21,... | collective-permute-start | bytes 1572872 | tf_op jit(solution)/shard_map/ppermute | solution.py:375
  35.6 0.0 collective-permute-done.8
  35.6 6.1 %collective-permute-start.12 = (bf16[1,512,256]{2,1,0:T(8,128)(2,1)S(1)}, bf16[1,512,256]{2,1,0:T(8,128)(2,1)S(1)}, u32[]{:S(2)}, u32[]{:S(2)}) collective-permute-start(bf16[1,512,256]{2,1,0:T(8,128)(2,1)S(1)} %collective-permute-done.4.rest_4_), channel_id=1, source_target_pairs={{0,4},{2,6},{8,12},{10,14},{16,20},{18,22},{24,28},{26,30},{1,5},{... | collective-permute-start | bytes 786440 | tf_op jit(solution)/shard_map/ppermute | solution.py:359
  41.8 0.0 collective-permute-done.3.rest_3_
  41.8 1.3 %collective-permute-start.5 = (bf16[1,528,256]{2,1,0:T(8,128)(2,1)S(1)}, bf16[1,528,256]{2,1,0:T(8,128)(2,1)S(1)}, u32[]{:S(2)}, u32[]{:S(2)}) collective-permute-start(bf16[1,528,256]{2,1,0:T(8,128)(2,1)S(1)} %collective-permute-done.3.rest_3_), channel_id=1, source_target_pairs={{8,0},{10,2},{12,4},{14,6},{16,8},{18,10},{20,12},{22,14},{24,16},... | collective-permute-start | bytes 811016 | tf_op jit(solution)/shard_map/ppermute | solution.py:353
  43.1 0.0 collective-permute-done.6.rest_6_
  43.1 0.1 collective-permute-start.9
  43.2 0.1 collective-permute-done.14.rest_4_
  43.3 1.3 %collective-permute-start.18 = (bf16[1,512,256]{2,1,0:T(8,128)(2,1)S(1)}, bf16[1,512,256]{2,1,0:T(8,128)(2,1)S(1)}, u32[]{:S(2)}, u32[]{:S(2)}) collective-permute-start(bf16[1,512,256]{2,1,0:T(8,128)(2,1)S(1)} %bitcast.23), channel_id=1, source_target_pairs={{8,0},{10,2},{12,4},{14,6},{16,8},{18,10},{20,12},{22,14},{24,16},... | collective-permute-start | bytes 786440 | tf_op jit(solution)/shard_map/ppermute | solution.py:353
  44.6 2.0 %collective-permute-done.12.rest_8_ = bf16[1,512,256]{2,1,0:T(8,128)(2,1)S(1)} collective-permute-done((bf16[1,512,256]{2,1,0:T(8,128)(2,1)S(1)}, bf16[1,512,256]{2,1,0:T(8,128)(2,1)S(1)}, u32[]{:S(2)}, u32[]{:S(2)}) %collective-permute-start.12) | collective-permute-done | bytes 262176 | tf_op jit(solution)/shard_map/ppermute | solution.py:359
  46.6 4.4 %collective-permute-start.15 = (bf16[1,512,256]{2,1,0:T(8,128)(2,1)S(1)}, bf16[1,512,256]{2,1,0:T(8,128)(2,1)S(1)}, u32[]{:S(2)}, u32[]{:S(2)}) collective-permute-start(bf16[1,512,256]{2,1,0:T(8,128)(2,1)S(1)} %collective-permute-done.14.rest_4_), channel_id=1, source_target_pairs={{0,4},{2,6},{8,12},{10,14},{16,20},{18,22},{24,28},{26,30},{1,5},{... | collective-permute-start | bytes 786440 | tf_op jit(solution)/shard_map/ppermute | solution.py:359
  51.0 0.4 collective-permute-done.5.rest_5_
  51.4 2.9 %collective-permute-start.13 = (bf16[1,528,256]{2,1,0:T(8,128)(2,1)S(1)}, bf16[1,528,256]{2,1,0:T(8,128)(2,1)S(1)}, u32[]{:S(2)}, u32[]{:S(2)}) collective-permute-start(bf16[1,528,256]{2,1,0:T(8,128)(2,1)S(1)} %collective-permute-done.5.rest_5_), channel_id=1, source_target_pairs={{0,4},{2,6},{8,12},{10,14},{16,20},{18,22},{24,28},{26,30},{1,5},{... | collective-permute-start | bytes 811016 | tf_op jit(solution)/shard_map/ppermute | solution.py:359
  54.3 0.0 collective-permute-done.18.rest_3_
  54.3 1.3 %collective-permute-start.19 = (bf16[1,512,256]{2,1,0:T(8,128)(2,1)S(1)}, bf16[1,512,256]{2,1,0:T(8,128)(2,1)S(1)}, u32[]{:S(2)}, u32[]{:S(2)}) collective-permute-start(bf16[1,512,256]{2,1,0:T(8,128)(2,1)S(1)} %collective-permute-done.18.rest_3_), channel_id=1, source_target_pairs={{8,0},{10,2},{12,4},{14,6},{16,8},{18,10},{20,12},{22,14},{24,16},... | collective-permute-start | bytes 786440 | tf_op jit(solution)/shard_map/ppermute | solution.py:353
  55.6 0.0 collective-permute-done.16
  55.6 0.0 collective-permute-done.9.rest_7_
  55.6 0.9 %collective-permute-start.20 = (bf16[1,512,256]{2,1,0:T(8,128)(2,1)S(1)}, bf16[1,512,256]{2,1,0:T(8,128)(2,1)S(1)}, u32[]{:S(2)}, u32[]{:S(2)}) collective-permute-start(bf16[1,512,256]{2,1,0:T(8,128)(2,1)S(1)} %collective-permute-done.18.rest_3_), channel_id=1, source_target_pairs={{0,4},{2,6},{4,0},{6,2},{8,12},{10,14},{12,8},{14,10},{16,20},{18,... | collective-permute-start | bytes 786440 | tf_op jit(solution)/shard_map/ppermute | solution.py:359
  56.6 1.4 %collective-permute-done.15.rest_8_ = bf16[1,512,256]{2,1,0:T(8,128)(2,1)S(1)} collective-permute-done((bf16[1,512,256]{2,1,0:T(8,128)(2,1)S(1)}, bf16[1,512,256]{2,1,0:T(8,128)(2,1)S(1)}, u32[]{:S(2)}, u32[]{:S(2)}) %collective-permute-start.15) | collective-permute-done | bytes 262176 | tf_op jit(solution)/shard_map/ppermute | solution.py:359
  58.0 2.6 %shard_map.40 = (f32[8,128,1024]{2,1,0:T(8,128)}, f32[2,128,512]{2,1,0:T(8,128)S(1)}) custom-call(s32[3]{0:T(128)S(1)} %pad_add_fusion.place_ref, f32[16,128]{1,0:T(8,128)S(1)} %get-tuple-element.54.counts_ref, bf16[1,528,256]{2,1,0:T(8,128)(2,1)S(1)} %bitcast.10, bf16[1,512,256]{2,1,0:T(8,128)(2,1)S(1)} %bitcast.27, bf16[1,528,256]{2,1,0:T(8,128)(2,1)S(1)} %bitcast.11, ...), custom_call_target="tpu_custom_call" | custom-call | flops 402653184 | bytes 1048576 | tf_op jit(solution)/shard_map/pallas_call | solution.py:288
  60.7 0.1 collective-permute-start.17
  60.7 2.3 %collective-permute-done.13.rest_9_ = bf16[1,528,256]{2,1,0:T(8,128)(2,1)S(1)} collective-permute-done((bf16[1,528,256]{2,1,0:T(8,128)(2,1)S(1)}, bf16[1,528,256]{2,1,0:T(8,128)(2,1)S(1)}, u32[]{:S(2)}, u32[]{:S(2)}) %collective-permute-start.13) | collective-permute-done | bytes 270368 | tf_op jit(solution)/shard_map/ppermute | solution.py:359
  63.1 0.0 collective-permute-done.19.rest_5_
  63.1 2.8 %collective-permute-done.20.rest_7_ = bf16[1,512,256]{2,1,0:T(8,128)(2,1)S(1)} collective-permute-done((bf16[1,512,256]{2,1,0:T(8,128)(2,1)S(1)}, bf16[1,512,256]{2,1,0:T(8,128)(2,1)S(1)}, u32[]{:S(2)}, u32[]{:S(2)}) %collective-permute-start.20) | collective-permute-done | bytes 262176 | tf_op jit(solution)/shard_map/ppermute | solution.py:359
  65.9 2.6 %shard_map.41 = (f32[8,128,1024]{2,1,0:T(8,128)}, f32[2,128,512]{2,1,0:T(8,128)S(1)}) custom-call(s32[3]{0:T(128)S(1)} %pad_add_fusion.place_ref, f32[16,128]{1,0:T(8,128)S(1)} %get-tuple-element.54.counts_ref, bf16[1,528,256]{2,1,0:T(8,128)(2,1)S(1)} %bitcast.12, bf16[1,512,256]{2,1,0:T(8,128)(2,1)S(1)} %bitcast.21, ...), custom_call_target="tpu_custom_call", output_to_operand_aliasing={{0}: (11, {})} | custom-call | flops 402653184 | bytes 1048576 | tf_op jit(solution)/shard_map/pallas_call | solution.py:288
  68.5 0.1 collective-permute-start.21
  68.6 4.4 %collective-permute-start.23 = (bf16[1,512,256]{2,1,0:T(8,128)(2,1)S(1)}, bf16[1,512,256]{2,1,0:T(8,128)(2,1)S(1)}, u32[]{:S(2)}, u32[]{:S(2)}) collective-permute-start(bf16[1,512,256]{2,1,0:T(8,128)(2,1)S(1)} %collective-permute-done.19.rest_5_), channel_id=1, source_target_pairs={{0,4},{2,6},{8,12},{10,14},{16,20},{18,22},{24,28},{26,30},{1,5},{... | collective-permute-start | bytes 786440 | tf_op jit(solution)/shard_map/ppermute | solution.py:359
  73.0 0.0 collective-permute-done.17.rest_10_
  73.0 0.0 collective-permute-done.21.rest_11_
  73.0 2.8 %shard_map.42 = (f32[8,128,1024]{2,1,0:T(8,128)}, f32[2,128,512]{2,1,0:T(8,128)S(1)}) custom-call(s32[3]{0:T(128)S(1)} %pad_add_fusion.place_ref, f32[16,128]{1,0:T(8,128)S(1)} %get-tuple-element.54.counts_ref, bf16[1,528,256]{2,1,0:T(8,128)(2,1)S(1)} %bitcast.13, bf16[1,512,256]{2,1,0:T(8,128)(2,1)S(1)} %bitcast.28, ...), custom_call_target="tpu_custom_call", output_to_operand_aliasing={{0}: (15, {})} | custom-call | flops 402653184 | bytes 1048576 | tf_op jit(solution)/shard_map/pallas_call | solution.py:288
  75.8 0.3 collective-permute-start.22
  76.1 3.1 %collective-permute-done.23.rest_9_ = bf16[1,512,256]{2,1,0:T(8,128)(2,1)S(1)} collective-permute-done((bf16[1,512,256]{2,1,0:T(8,128)(2,1)S(1)}, bf16[1,512,256]{2,1,0:T(8,128)(2,1)S(1)}, u32[]{:S(2)}, u32[]{:S(2)}) %collective-permute-start.23) | collective-permute-done | bytes 262176 | tf_op jit(solution)/shard_map/ppermute | solution.py:359
  79.2 2.6 %shard_map.43 = (f32[8,128,1024]{2,1,0:T(8,128)}, f32[2,128,512]{2,1,0:T(8,128)S(1)}) custom-call(s32[3]{0:T(128)S(1)} %pad_add_fusion.place_ref, f32[16,128]{1,0:T(8,128)S(1)} %get-tuple-element.54.counts_ref, bf16[1,528,256]{2,1,0:T(8,128)(2,1)S(1)} %bitcast.15, bf16[1,512,256]{2,1,0:T(8,128)(2,1)S(1)} %bitcast.22, ...), custom_call_target="tpu_custom_call", output_to_operand_aliasing={{0}: (13, {})} | custom-call | flops 402653184 | bytes 1048576 | tf_op jit(solution)/shard_map/pallas_call | solution.py:288
  81.8 0.1 collective-permute-start.24
  81.9 0.0 collective-permute-done.22.rest_0_
  81.9 1.9 %collective-permute-done.24.rest_1_ = f32[2,128,512]{2,1,0:T(8,128)S(1)} collective-permute-done((f32[2,128,512]{2,1,0:T(8,128)S(1)}, f32[2,128,512]{2,1,0:T(8,128)S(1)}, u32[]{:S(2)}, u32[]{:S(2)}) %collective-permute-start.24) | collective-permute-done | bytes 524320 | tf_op jit(solution)/shard_map/ppermute | solution.py:364
  83.8 1.5 %shard_map.44 = f32[8,128,1024]{2,1,0:T(8,128)} custom-call(s32[3]{0:T(128)S(1)} %pad_add_fusion.place_ref, f32[2,128,512]{2,1,0:T(8,128)S(1)} %collective-permute-done.22.rest_0_, f32[2,128,512]{2,1,0:T(8,128)S(1)} %collective-permute-done.24.rest_1_, f32[8,128,1024]{2,1,0:T(8,128)} %get-tuple-element.62.rest_2_), custom_call_target="tpu_custom_call", output_to_operand_aliasing={{}: (3, {})} | custom-call | bytes 2097152 | tf_op jit(solution)/shard_map/pallas_call | solution.py:338
Async XLA Ops:
  0.0 3.0 %collective-permute-start = (bf16[128,4096]{1,0:T(8,128)(2,1)}, bf16[128,4096]{1,0:T(8,128)(2,1)S(1)}, u32[]{:S(2)}, u32[]{:S(2)}) collective-permute-start(bf16[128,4096]{1,0:T(8,128)(2,1)} %frames_hbm.1), channel_id=1, source_target_pairs={{0,2},{2,0},{4,6},{6,4},{8,10},{10,8},{12,14},{14,12},{16,18},{18,... | collective-permute-start | bytes 3145736 | tf_op jit(solution)/shard_map/ppermute | solution.py:364
  6.0 18.9 %collective-permute-start.7 = (bf16[1024,256]{1,0:T(8,128)(2,1)S(1)}, bf16[1024,256]{1,0:T(8,128)(2,1)S(1)}, u32[]{:S(2)}, u32[]{:S(2)}) collective-permute-start(bf16[1024,256]{1,0:T(8,128)(2,1)S(1)} %get-tuple-element.43), channel_id=1, source_target_pairs={{4,0},{6,2},{12,8},{14,10},{20,16},{22,18},{28,24},{30,26},{5,1},{... | collective-permute-start | bytes 1572872 | tf_op jit(solution)/shard_map/ppermute | solution.py:359
  7.3 11.9 %collective-permute-start.2 = (bf16[1,512,256]{2,1,0:T(8,128)(2,1)S(1)}, bf16[1,512,256]{2,1,0:T(8,128)(2,1)S(1)}, u32[]{:S(2)}, u32[]{:S(2)}) collective-permute-start(bf16[1,512,256]{2,1,0:T(8,128)(2,1)S(1)} %bitcast.26), channel_id=1, source_target_pairs={{8,0},{10,2},{12,4},{14,6},{16,8},{18,10},{20,12},{22,14},{24,16},... | collective-permute-start | bytes 786440 | tf_op jit(solution)/shard_map/ppermute | solution.py:353
  8.6 16.3 %collective-permute-start.10 = (bf16[1,512,256]{2,1,0:T(8,128)(2,1)S(1)}, bf16[1,512,256]{2,1,0:T(8,128)(2,1)S(1)}, u32[]{:S(2)}, u32[]{:S(2)}) collective-permute-start(bf16[1,512,256]{2,1,0:T(8,128)(2,1)S(1)} %bitcast.20), channel_id=1, source_target_pairs={{8,0},{10,2},{12,4},{14,6},{16,8},{18,10},{20,12},{22,14},{24,16},... | collective-permute-start | bytes 786440 | tf_op jit(solution)/shard_map/ppermute | solution.py:353
  12.8 16.8 %collective-permute-start.1 = (bf16[528,256]{1,0:T(8,128)(2,1)S(1)}, bf16[528,256]{1,0:T(8,128)(2,1)S(1)}, u32[]{:S(2)}, u32[]{:S(2)}) collective-permute-start(bf16[528,256]{1,0:T(8,128)(2,1)S(1)} %get-tuple-element.40), channel_id=1, source_target_pairs={{0,1},{1,0},{2,3},{3,2},{4,5},{5,4},{6,7},{7,6},{8,9},{9,8},{10,11... | collective-permute-start | bytes 811016 | tf_op jit(solution)/shard_map/ppermute | solution.py:375
  19.2 11.7 %collective-permute-start.4 = (bf16[1,512,256]{2,1,0:T(8,128)(2,1)S(1)}, bf16[1,512,256]{2,1,0:T(8,128)(2,1)S(1)}, u32[]{:S(2)}, u32[]{:S(2)}) collective-permute-start(bf16[1,512,256]{2,1,0:T(8,128)(2,1)S(1)} %collective-permute-done.2.rest_2_), channel_id=1, source_target_pairs={{8,0},{10,2},{12,4},{14,6},{16,8},{18,10},{20,12},{22,14},{24,16},... | collective-permute-start | bytes 786440 | tf_op jit(solution)/shard_map/ppermute | solution.py:353
  24.9 9.5 %collective-permute-start.11 = (bf16[1,512,256]{2,1,0:T(8,128)(2,1)S(1)}, bf16[1,512,256]{2,1,0:T(8,128)(2,1)S(1)}, u32[]{:S(2)}, u32[]{:S(2)}) collective-permute-start(bf16[1,512,256]{2,1,0:T(8,128)(2,1)S(1)} %collective-permute-done.10.rest_2_), channel_id=1, source_target_pairs={{0,4},{2,6},{4,0},{6,2},{8,12},{10,14},{12,8},{14,10},{16,20},{18,... | collective-permute-start | bytes 786440 | tf_op jit(solution)/shard_map/ppermute | solution.py:359
  27.6 8.1 %collective-permute-start.8 = (bf16[512,256]{1,0:T(8,128)(2,1)S(1)}, bf16[512,256]{1,0:T(8,128)(2,1)S(1)}, u32[]{:S(2)}, u32[]{:S(2)}) collective-permute-start(bf16[512,256]{1,0:T(8,128)(2,1)S(1)} %get-tuple-element.44), channel_id=1, source_target_pairs={{0,1},{1,0},{2,3},{3,2},{4,5},{5,4},{6,7},{7,6},{8,9},{9,8},{10,11... | collective-permute-start | bytes 786440 | tf_op jit(solution)/shard_map/ppermute | solution.py:375
  29.6 12.2 %collective-permute-start.3 = (bf16[1,528,256]{2,1,0:T(8,128)(2,1)S(1)}, bf16[1,528,256]{2,1,0:T(8,128)(2,1)S(1)}, u32[]{:S(2)}, u32[]{:S(2)}) collective-permute-start(bf16[1,528,256]{2,1,0:T(8,128)(2,1)S(1)} %bitcast.9), channel_id=1, source_target_pairs={{8,0},{10,2},{12,4},{14,6},{16,8},{18,10},{20,12},{22,14},{24,16},... | collective-permute-start | bytes 811016 | tf_op jit(solution)/shard_map/ppermute | solution.py:353
  30.9 12.2 %collective-permute-start.6 = (bf16[1,512,256]{2,1,0:T(8,128)(2,1)S(1)}, bf16[1,512,256]{2,1,0:T(8,128)(2,1)S(1)}, u32[]{:S(2)}, u32[]{:S(2)}) collective-permute-start(bf16[1,512,256]{2,1,0:T(8,128)(2,1)S(1)} %collective-permute-done.2.rest_2_), channel_id=1, source_target_pairs={{0,4},{2,6},{4,0},{6,2},{8,12},{10,14},{12,8},{14,10},{16,20},{18,... | collective-permute-start | bytes 786440 | tf_op jit(solution)/shard_map/ppermute | solution.py:359
  31.0 12.3 %collective-permute-start.14 = (bf16[1,512,256]{2,1,0:T(8,128)(2,1)S(1)}, bf16[1,512,256]{2,1,0:T(8,128)(2,1)S(1)}, u32[]{:S(2)}, u32[]{:S(2)}) collective-permute-start(bf16[1,512,256]{2,1,0:T(8,128)(2,1)S(1)} %collective-permute-done.10.rest_2_), channel_id=1, source_target_pairs={{8,0},{10,2},{12,4},{14,6},{16,8},{18,10},{20,12},{22,14},{24,16},... | collective-permute-start | bytes 786440 | tf_op jit(solution)/shard_map/ppermute | solution.py:353
  34.3 21.3 %collective-permute-start.16 = (bf16[1024,256]{1,0:T(8,128)(2,1)S(1)}, bf16[1024,256]{1,0:T(8,128)(2,1)S(1)}, u32[]{:S(2)}, u32[]{:S(2)}) collective-permute-start(bf16[1024,256]{1,0:T(8,128)(2,1)S(1)} %get-tuple-element.39), channel_id=1, source_target_pairs={{4,1},{5,0},{6,3},{7,2},{12,9},{13,8},{14,11},{15,10},{20,17},{21,... | collective-permute-start | bytes 1572872 | tf_op jit(solution)/shard_map/ppermute | solution.py:375
  35.6 11.0 %collective-permute-start.12 = (bf16[1,512,256]{2,1,0:T(8,128)(2,1)S(1)}, bf16[1,512,256]{2,1,0:T(8,128)(2,1)S(1)}, u32[]{:S(2)}, u32[]{:S(2)}) collective-permute-start(bf16[1,512,256]{2,1,0:T(8,128)(2,1)S(1)} %collective-permute-done.4.rest_4_), channel_id=1, source_target_pairs={{0,4},{2,6},{8,12},{10,14},{16,20},{18,22},{24,28},{26,30},{1,5},{... | collective-permute-start | bytes 786440 | tf_op jit(solution)/shard_map/ppermute | solution.py:359
  41.8 9.6 %collective-permute-start.5 = (bf16[1,528,256]{2,1,0:T(8,128)(2,1)S(1)}, bf16[1,528,256]{2,1,0:T(8,128)(2,1)S(1)}, u32[]{:S(2)}, u32[]{:S(2)}) collective-permute-start(bf16[1,528,256]{2,1,0:T(8,128)(2,1)S(1)} %collective-permute-done.3.rest_3_), channel_id=1, source_target_pairs={{8,0},{10,2},{12,4},{14,6},{16,8},{18,10},{20,12},{22,14},{24,16},... | collective-permute-start | bytes 811016 | tf_op jit(solution)/shard_map/ppermute | solution.py:353
  43.1 12.5 %collective-permute-start.9 = (bf16[1,528,256]{2,1,0:T(8,128)(2,1)S(1)}, bf16[1,528,256]{2,1,0:T(8,128)(2,1)S(1)}, u32[]{:S(2)}, u32[]{:S(2)}) collective-permute-start(bf16[1,528,256]{2,1,0:T(8,128)(2,1)S(1)} %collective-permute-done.3.rest_3_), channel_id=1, source_target_pairs={{0,4},{2,6},{4,0},{6,2},{8,12},{10,14},{12,8},{14,10},{16,20},{18,... | collective-permute-start | bytes 811016 | tf_op jit(solution)/shard_map/ppermute | solution.py:359
  43.3 11.0 %collective-permute-start.18 = (bf16[1,512,256]{2,1,0:T(8,128)(2,1)S(1)}, bf16[1,512,256]{2,1,0:T(8,128)(2,1)S(1)}, u32[]{:S(2)}, u32[]{:S(2)}) collective-permute-start(bf16[1,512,256]{2,1,0:T(8,128)(2,1)S(1)} %bitcast.23), channel_id=1, source_target_pairs={{8,0},{10,2},{12,4},{14,6},{16,8},{18,10},{20,12},{22,14},{24,16},... | collective-permute-start | bytes 786440 | tf_op jit(solution)/shard_map/ppermute | solution.py:353
  46.6 11.4 %collective-permute-start.15 = (bf16[1,512,256]{2,1,0:T(8,128)(2,1)S(1)}, bf16[1,512,256]{2,1,0:T(8,128)(2,1)S(1)}, u32[]{:S(2)}, u32[]{:S(2)}) collective-permute-start(bf16[1,512,256]{2,1,0:T(8,128)(2,1)S(1)} %collective-permute-done.14.rest_4_), channel_id=1, source_target_pairs={{0,4},{2,6},{8,12},{10,14},{16,20},{18,22},{24,28},{26,30},{1,5},{... | collective-permute-start | bytes 786440 | tf_op jit(solution)/shard_map/ppermute | solution.py:359
  51.4 11.7 %collective-permute-start.13 = (bf16[1,528,256]{2,1,0:T(8,128)(2,1)S(1)}, bf16[1,528,256]{2,1,0:T(8,128)(2,1)S(1)}, u32[]{:S(2)}, u32[]{:S(2)}) collective-permute-start(bf16[1,528,256]{2,1,0:T(8,128)(2,1)S(1)} %collective-permute-done.5.rest_5_), channel_id=1, source_target_pairs={{0,4},{2,6},{8,12},{10,14},{16,20},{18,22},{24,28},{26,30},{1,5},{... | collective-permute-start | bytes 811016 | tf_op jit(solution)/shard_map/ppermute | solution.py:359
  54.3 8.7 %collective-permute-start.19 = (bf16[1,512,256]{2,1,0:T(8,128)(2,1)S(1)}, bf16[1,512,256]{2,1,0:T(8,128)(2,1)S(1)}, u32[]{:S(2)}, u32[]{:S(2)}) collective-permute-start(bf16[1,512,256]{2,1,0:T(8,128)(2,1)S(1)} %collective-permute-done.18.rest_3_), channel_id=1, source_target_pairs={{8,0},{10,2},{12,4},{14,6},{16,8},{18,10},{20,12},{22,14},{24,16},... | collective-permute-start | bytes 786440 | tf_op jit(solution)/shard_map/ppermute | solution.py:353
  55.6 10.2 %collective-permute-start.20 = (bf16[1,512,256]{2,1,0:T(8,128)(2,1)S(1)}, bf16[1,512,256]{2,1,0:T(8,128)(2,1)S(1)}, u32[]{:S(2)}, u32[]{:S(2)}) collective-permute-start(bf16[1,512,256]{2,1,0:T(8,128)(2,1)S(1)} %collective-permute-done.18.rest_3_), channel_id=1, source_target_pairs={{0,4},{2,6},{4,0},{6,2},{8,12},{10,14},{12,8},{14,10},{16,20},{18,... | collective-permute-start | bytes 786440 | tf_op jit(solution)/shard_map/ppermute | solution.py:359
  60.7 12.3 %collective-permute-start.17 = (f32[2,128,512]{2,1,0:T(8,128)S(1)}, f32[2,128,512]{2,1,0:T(8,128)S(1)}, u32[]{:S(2)}, u32[]{:S(2)}) collective-permute-start(f32[2,128,512]{2,1,0:T(8,128)S(1)} %get-tuple-element.51), channel_id=1, source_target_pairs={{0,2},{2,0},{4,6},{6,4},{8,10},{10,8},{12,14},{14,12},{16,18},{18,... | collective-permute-start | bytes 1572872 | tf_op jit(solution)/shard_map/ppermute | solution.py:364
  68.5 4.5 %collective-permute-start.21 = (f32[2,128,512]{2,1,0:T(8,128)S(1)}, f32[2,128,512]{2,1,0:T(8,128)S(1)}, u32[]{:S(2)}, u32[]{:S(2)}) collective-permute-start(f32[2,128,512]{2,1,0:T(8,128)S(1)} %get-tuple-element.57), channel_id=1, source_target_pairs={{0,2},{2,0},{4,6},{6,4},{8,10},{10,8},{12,14},{14,12},{16,18},{18,... | collective-permute-start | bytes 1572872 | tf_op jit(solution)/shard_map/ppermute | solution.py:364
  68.6 10.6 %collective-permute-start.23 = (bf16[1,512,256]{2,1,0:T(8,128)(2,1)S(1)}, bf16[1,512,256]{2,1,0:T(8,128)(2,1)S(1)}, u32[]{:S(2)}, u32[]{:S(2)}) collective-permute-start(bf16[1,512,256]{2,1,0:T(8,128)(2,1)S(1)} %collective-permute-done.19.rest_5_), channel_id=1, source_target_pairs={{0,4},{2,6},{8,12},{10,14},{16,20},{18,22},{24,28},{26,30},{1,5},{... | collective-permute-start | bytes 786440 | tf_op jit(solution)/shard_map/ppermute | solution.py:359
  75.8 6.1 %collective-permute-start.22 = (f32[2,128,512]{2,1,0:T(8,128)S(1)}, f32[2,128,512]{2,1,0:T(8,128)S(1)}, u32[]{:S(2)}, u32[]{:S(2)}) collective-permute-start(f32[2,128,512]{2,1,0:T(8,128)S(1)} %get-tuple-element.59), channel_id=1, source_target_pairs={{0,2},{2,0},{4,6},{6,4},{8,10},{10,8},{12,14},{14,12},{16,18},{18,... | collective-permute-start | bytes 1572872 | tf_op jit(solution)/shard_map/ppermute | solution.py:364
  81.8 2.0 %collective-permute-start.24 = (f32[2,128,512]{2,1,0:T(8,128)S(1)}, f32[2,128,512]{2,1,0:T(8,128)S(1)}, u32[]{:S(2)}, u32[]{:S(2)}) collective-permute-start(f32[2,128,512]{2,1,0:T(8,128)S(1)} %get-tuple-element.61), channel_id=1, source_target_pairs={{0,2},{2,0},{4,6},{6,4},{8,10},{10,8},{12,14},{14,12},{16,18},{18,... | collective-permute-start | bytes 1572872 | tf_op jit(solution)/shard_map/ppermute | solution.py:364

commit v6 on v5

--- a/solution.py
+++ b/solution.py
@@ -16,19 +16,38 @@
 CHUNK = 256
 VMEM_LIMIT = 24 * 1024 * 1024
 
-TIES = {
-    "z3": ("x1", "y1", "y0", "z2"),
-    "x2": ("x0", "o0", "y1"),
-    "v0": ("x1", "k1"),
-    "x3": ("x2", "o1"),
-    "v1": ("v0", "y1", "o0", "w1"),
-    "g00": ("v1",),
-    "g01": ("w3", "v1", "v2", "v0"),
-    "w3": ("z1",),
-    "x1": ("z1", "o0"),
-    "w0": ("z0",),
-    "y0": ("k1",),
-}
+ORDER = (
+    ("start", "o0", "z0", "y0"),
+    ("wait", "k1"),
+    ("start", "z1"),
+    ("wait", "z0"),
+    ("pause", 1000000000),
+    ("start", "w0", "x0"),
+    ("wait", "y0"),
+    ("start", "z2"),
+    ("wait", "o0"),
+    ("start", "x1", "w1"),
+    ("wait", "w0"),
+    ("start", "v0"),
+    ("wait", "z1", "x0"),
+    ("start", "y1", "x2", "w2"),
+    ("wait", "x1"),
+    ("start", "v1", "o1"),
+    ("wait", "z2", "y1", "v0", "w1"),
+    ("start", "z3"),
+    ("pause", 100000000),
+    ("pause", 300000000),
+    ("pause", 0),
+    ("wait", "w0", "x2"),
+    ("pause", 100000000),
+    ("start", "v2"),
+    ("wait", "w2", "v1"),
+    ("start", "w3", "x3"),
+    ("pause", 300000000),
+    ("wait", "o1", "v2", "g00"),
+    ("start", "v3"),
+    ("wait", "x3", "g01", "g11", "v3", "g10"),
+)
 OWN_SPLIT = True
 
 SMEM_SPEC = pl.BlockSpec(memory_space=pltpu.SMEM)
@@ -333,18 +352,32 @@
         copy.wait()
 
 
-def fill(place, whole, ready):
+def fill(place, token, whole, ready):
     parts, spots = zip(*ready)
     return pl.pallas_call(
         functools.partial(fill_kernel, spots=spots),
         out_shape=jax.ShapeDtypeStruct(whole.shape, whole.dtype),
-        in_specs=[SMEM_SPEC] + [ANY_SPEC] * (len(parts) + 1),
+        in_specs=[SMEM_SPEC] + [ANY_SPEC] * (len(parts) + 2),
         out_specs=ANY_SPEC,
         scratch_shapes=[pltpu.SemaphoreType.DMA((len(parts),))],
-        input_output_aliases={1 + len(parts): 0},
+        input_output_aliases={2 + len(parts): 0},
         compiler_params=params(),
         cost_estimate=estimate(0, 8 * sum(part.size for part in parts)),
-    )(place, *parts, whole)
+    )(place, *parts, token, whole)
+
+
+def pause_kernel(value_ref, out_ref):
+    out_ref[...] = value_ref[...]
+
+
+def pause(value, weight):
+    return pl.pallas_call(
+        pause_kernel,
+        out_shape=jax.ShapeDtypeStruct(value.shape, value.dtype),
+        in_specs=[VMEM_SPEC],
+        out_specs=VMEM_SPEC,
+        cost_estimate=estimate(weight, 0),
+    )(value)
 
 
 def shifted(value, pairs_down):
@@ -396,10 +429,12 @@
     key, counts, own_frames = rank_pixels(used, frames)
     done = {}
 
+    token = counts
+
     def tied(value, name):
-        ties = [get(tie) for tie in TIES.get(name, ()) if known(tie)]
-        ties = [tie[0] if isinstance(tie, (list, tuple)) else tie for tie in ties]
-        return lax.optimization_barrier((value, *ties))[0] if ties else value
+        nonlocal token
+        value, token = lax.optimization_barrier((value, token))
+        return value
 
     def known(name):
         limits = dict(g=halves, s=halves, y=halves, k=mods, o=2)
@@ -463,8 +498,20 @@
     def spot(phase, part):
         return get(f"s{phase}{part}"), (group_cycles, offsets[part], phase * (LAG // 2))
 
+    for step, *names in ORDER:
+        if step == "pause":
+            token = pause(token, *names)
+            continue
+        for name in filter(known, names):
+            value = get(name)
+            if step == "wait":
+                if isinstance(value, (list, tuple)):
+                    head, token = lax.optimization_barrier((value[0], token))
+                    done[name] = [head, *value[1:]]
+                else:
+                    done[name], token = lax.optimization_barrier((value, token))
     whole = get(f"g1{halves - 1}")[0]
-    return fill(place, whole, [spot(1, part) for part in range(halves)])
+    return fill(place, token, whole, [spot(1, part) for part in range(halves)])
 
 
 def solution(mesh):

time: 86.5 us -> 94.8 us (1.096)
  the two profiles are of different devices: /device:TPU:0 before, /device:TPU:27 now
where the time goes in v6:
time: 94.8 us; the launch traced here: 93.9 us
  starting transfers between devices  45.8 us (48%)
  Pallas kernels  27.9 us (29%)
  local copies, waits for them, and re-layouts  9.98 us (11%)
  waiting for transfers between devices  9.02 us (10%)
    ppermute x8, starting transfers between devices, shifted(): lax.ppermute(value, 'frame', [(source, source - step) for source in range...  20.5 us
    ppermute x9, starting transfers between devices, other_pair(): lax.ppermute(value, 'frame', [(source, source ^ 2) for source in sources])  12 us
    pallas_call x4, Pallas kernels, grams(): pl.pallas_call(kernel, out_shape=[jax.ShapeDtypeStruct((cycle_dev, block,...  10.7 us
    unnamed x41, local copies, waits for them, and re-layouts  9.98 us
    pallas_call x6, Pallas kernels, pause(): pl.pallas_call(pause_kernel, out_shape=jax.ShapeDtypeStruct(value.shape,...  7.75 us
    ppermute x5, starting transfers between devices, other_core(): lax.ppermute(value, 'frame', [(source, source ^ 1) for source in range(co...  7.49 us
    pallas_call x2, Pallas kernels, order_pixels(): pl.pallas_call(functools.partial(order_kernel, step=step, mods=mods, part...  6.66 us
    ppermute x3, starting transfers between devices, along_mod(): return lax.ppermute(value, ('frame', 'mod'), pairs)  5.79 us
  transfers between devices with their start and end apart: 25, of which 9 were waited for; matrix products, arithmetic and copies ran while one was open for 3% of the time, Pallas kernels for 22%

profile of v6, /device:TPU:27, one launch (start us, length us, event | category | flops | bytes accessed | tf_op | source)
XLA Modules:
  0.0 93.9 jit_solution(11761740724335823223)
XLA Ops:
  0.0 0.7 collective-permute-start
  0.7 0.7 compare_select_fusion.label_ref
  1.4 1.2 %shard_map.37 = (f32[256,256]{1,0:T(8,128)S(1)}, f32[16,128]{1,0:T(8,128)S(1)}, bf16[128,4096]{1,0:T(8,128)(2,1)S(1)}) custom-call(s32[4096]{0:T(1024)S(1)} %compare_select_fusion.label_ref, bf16[128,4096]{1,0:T(8,128)(2,1)} %frames_hbm.1), custom_call_target="tpu_custom_call" | custom-call | flops 100663296 | bytes 32768 | tf_op jit(solution)/shard_map/pallas_call | solution.py:101
  2.7 0.0 copy-start.17
  2.7 1.0 %copy-done.17 = bf16[128,4096]{1,0:T(8,128)(2,1)} copy-done((bf16[128,4096]{1,0:T(8,128)(2,1)}, bf16[128,4096]{1,0:T(8,128)(2,1)S(1)}, u32[]{:S(2)}) %copy-start.17) | copy-done | bytes 1048600
  3.6 0.1 pad_add_fusion.place_ref
  3.7 0.0 collective-permute-done.rest_1_
  3.7 1.2 %copy-done.18 = bf16[128,4096]{1,0:T(8,128)(2,1)S(1)} copy-done((bf16[128,4096]{1,0:T(8,128)(2,1)S(1)}, bf16[128,4096]{1,0:T(8,128)(2,1)}, u32[]{:S(2)}) %copy-start.18) | copy-done | bytes 1048600
  5.0 3.0 %shard_map.38 = (bf16[1024,256]{1,0:T(8,128)(2,1)S(1)}, bf16[512,256]{1,0:T(8,128)(2,1)S(1)}, bf16[512,256]{1,0:T(8,128)(2,1)S(1)}, bf16[256,4096]{1,0:T(8,128)(2,1)S(1)}) custom-call(s32[3]{0:T(128)S(1)} %pad_add_fusion.place_ref, f32[256,256]{1,0:T(8,128)S(1)} %get-tuple-element.128.key_ref, f32[16,128]{1,0:T(8,128)S(1)} %get-tuple-element.221.counts_ref.value_ref, ...), custom_call_target="tpu_custom_call" | custom-call | flops 2147483648 | bytes 2097152 | tf_op jit(solution)/shard_map/pallas_call | solution.py:172
  8.0 2.1 %collective-permute-start.1 = (bf16[1,512,256]{2,1,0:T(8,128)(2,1)S(1)}, bf16[1,512,256]{2,1,0:T(8,128)(2,1)S(1)}, u32[]{:S(2)}, u32[]{:S(2)}) collective-permute-start(bf16[1,512,256]{2,1,0:T(8,128)(2,1)S(1)} %bitcast.26), channel_id=1, source_target_pairs={{8,0},{10,2},{12,4},{14,6},{16,8},{18,10},{20,12},{22,14},{24,16},... | collective-permute-start | bytes 786440 | tf_op jit(solution)/shard_map/ppermute | solution.py:386
  10.1 2.2 %collective-permute-start.5 = (bf16[1024,256]{1,0:T(8,128)(2,1)S(1)}, bf16[1024,256]{1,0:T(8,128)(2,1)S(1)}, u32[]{:S(2)}, u32[]{:S(2)}) collective-permute-start(bf16[1024,256]{1,0:T(8,128)(2,1)S(1)} %get-tuple-element.145), channel_id=1, source_target_pairs={{4,0},{6,2},{12,8},{14,10},{20,16},{22,18},{28,24},{30,26},{5,1},{... | collective-permute-start | bytes 1572872 | tf_op jit(solution)/shard_map/ppermute | solution.py:392
  12.3 3.6 %shard_map.39 = (bf16[1024,256]{1,0:T(8,128)(2,1)S(1)}, bf16[528,256]{1,0:T(8,128)(2,1)S(1)}, bf16[512,256]{1,0:T(8,128)(2,1)}) custom-call(s32[3]{0:T(128)S(1)} %pad_add_fusion.place_ref, f32[256,256]{1,0:T(8,128)S(1)} %get-tuple-element.128.key_ref, f32[16,128]{1,0:T(8,128)S(1)} %get-tuple-element.221.counts_ref.value_ref, ...), custom_call_target="tpu_custom_call" | custom-call | flops 2147483648 | bytes 2097152 | tf_op jit(solution)/shard_map/pallas_call | solution.py:172
  15.9 0.8 copy-done.19
  16.7 2.2 %collective-permute-start.3 = (bf16[1,512,256]{2,1,0:T(8,128)(2,1)S(1)}, bf16[1,512,256]{2,1,0:T(8,128)(2,1)S(1)}, u32[]{:S(2)}, u32[]{:S(2)}) collective-permute-start(bf16[1,512,256]{2,1,0:T(8,128)(2,1)S(1)} %bitcast.20), channel_id=1, source_target_pairs={{8,0},{10,2},{12,4},{14,6},{16,8},{18,10},{20,12},{22,14},{24,16},... | collective-permute-start | bytes 786440 | tf_op jit(solution)/shard_map/ppermute | solution.py:386
  18.9 1.3 %collective-permute-start.6 = (bf16[528,256]{1,0:T(8,128)(2,1)S(1)}, bf16[528,256]{1,0:T(8,128)(2,1)S(1)}, u32[]{:S(2)}, u32[]{:S(2)}) collective-permute-start(bf16[528,256]{1,0:T(8,128)(2,1)S(1)} %get-tuple-element.146), channel_id=1, source_target_pairs={{0,1},{1,0},{2,3},{3,2},{4,5},{5,4},{6,7},{7,6},{8,9},{9,8},{10,11... | collective-permute-start | bytes 811016 | tf_op jit(solution)/shard_map/ppermute | solution.py:408
  20.2 1.3 %shard_map.40.value_ref = f32[16,128]{1,0:T(8,128)} custom-call(f32[16,128]{1,0:T(8,128)} %copy-done.14), custom_call_target="tpu_custom_call" | custom-call | flops 1000000000 | tf_op jit(solution)/shard_map/pallas_call | solution.py:374
  21.5 2.1 %collective-permute-start.4 = (bf16[1,512,256]{2,1,0:T(8,128)(2,1)S(1)}, bf16[1,512,256]{2,1,0:T(8,128)(2,1)S(1)}, u32[]{:S(2)}, u32[]{:S(2)}) collective-permute-start(bf16[1,512,256]{2,1,0:T(8,128)(2,1)S(1)} %collective-permute-done.1.rest_2_), channel_id=1, source_target_pairs={{8,0},{10,2},{12,4},{14,6},{16,8},{18,10},{20,12},{22,14},{24,16},... | collective-permute-start | bytes 786440 | tf_op jit(solution)/shard_map/ppermute | solution.py:386
  23.6 0.1 collective-permute-start.2
  23.7 2.5 %collective-permute-done.6 = bf16[528,256]{1,0:T(8,128)(2,1)S(1)} collective-permute-done((bf16[528,256]{1,0:T(8,128)(2,1)S(1)}, bf16[528,256]{1,0:T(8,128)(2,1)S(1)}, u32[]{:S(2)}, u32[]{:S(2)}) %collective-permute-start.6) | collective-permute-done | bytes 270368 | tf_op jit(solution)/shard_map/ppermute | solution.py:408
  26.1 2.2 %collective-permute-start.8 = (bf16[1,528,256]{2,1,0:T(8,128)(2,1)S(1)}, bf16[1,528,256]{2,1,0:T(8,128)(2,1)S(1)}, u32[]{:S(2)}, u32[]{:S(2)}) collective-permute-start(bf16[1,528,256]{2,1,0:T(8,128)(2,1)S(1)} %bitcast.9), channel_id=1, source_target_pairs={{8,0},{10,2},{12,4},{14,6},{16,8},{18,10},{20,12},{22,14},{24,16},... | collective-permute-start | bytes 811016 | tf_op jit(solution)/shard_map/ppermute | solution.py:386
  28.4 0.0 collective-permute-done.3.rest_2_
  28.4 0.1 collective-permute-start.10
  28.5 2.2 %collective-permute-start.9 = (bf16[1,512,256]{2,1,0:T(8,128)(2,1)S(1)}, bf16[1,512,256]{2,1,0:T(8,128)(2,1)S(1)}, u32[]{:S(2)}, u32[]{:S(2)}) collective-permute-start(bf16[1,512,256]{2,1,0:T(8,128)(2,1)S(1)} %collective-permute-done.3.rest_2_), channel_id=1, source_target_pairs={{8,0},{10,2},{12,4},{14,6},{16,8},{18,10},{20,12},{22,14},{24,16},... | collective-permute-start | bytes 786440 | tf_op jit(solution)/shard_map/ppermute | solution.py:386
  30.8 0.7 copy-done.5
  31.5 1.1 %collective-permute-start.7 = (bf16[512,256]{1,0:T(8,128)(2,1)}, bf16[512,256]{1,0:T(8,128)(2,1)S(1)}, u32[]{:S(2)}, u32[]{:S(2)}) collective-permute-start(bf16[512,256]{1,0:T(8,128)(2,1)} %get-tuple-element.155), channel_id=1, source_target_pairs={{0,1},{1,0},{2,3},{3,2},{4,5},{5,4},{6,7},{7,6},{8,9},{9,8},{10,11... | collective-permute-start | bytes 786440 | tf_op jit(solution)/shard_map/ppermute | solution.py:408
  32.5 1.3 %collective-permute-start.11 = (bf16[1,512,256]{2,1,0:T(8,128)(2,1)S(1)}, bf16[1,512,256]{2,1,0:T(8,128)(2,1)S(1)}, u32[]{:S(2)}, u32[]{:S(2)}) collective-permute-start(bf16[1,512,256]{2,1,0:T(8,128)(2,1)S(1)} %collective-permute-done.4.rest_4_), channel_id=1, source_target_pairs={{0,4},{2,6},{8,12},{10,14},{16,20},{18,22},{24,28},{26,30},{1,5},{... | collective-permute-start | bytes 786440 | tf_op jit(solution)/shard_map/ppermute | solution.py:392
  33.8 0.7 copy-done.10
  34.5 1.0 %collective-permute-done.8.rest_3_ = bf16[1,528,256]{2,1,0:T(8,128)(2,1)S(1)} collective-permute-done((bf16[1,528,256]{2,1,0:T(8,128)(2,1)S(1)}, bf16[1,528,256]{2,1,0:T(8,128)(2,1)S(1)}, u32[]{:S(2)}, u32[]{:S(2)}) %collective-permute-start.8) | collective-permute-done | bytes 270368 | tf_op jit(solution)/shard_map/ppermute | solution.py:386
  35.6 1.1 %collective-permute-start.15 = (bf16[1,528,256]{2,1,0:T(8,128)(2,1)S(1)}, bf16[1,528,256]{2,1,0:T(8,128)(2,1)S(1)}, u32[]{:S(2)}, u32[]{:S(2)}) collective-permute-start(bf16[1,528,256]{2,1,0:T(8,128)(2,1)S(1)} %collective-permute-done.8.rest_3_), channel_id=1, source_target_pairs={{0,4},{2,6},{4,0},{6,2},{8,12},{10,14},{12,8},{14,10},{16,20},{18,... | collective-permute-start | bytes 811016 | tf_op jit(solution)/shard_map/ppermute | solution.py:392
  36.6 0.0 collective-permute-done.10.rest_6_
  36.6 3.8 %collective-permute-start.14 = (bf16[1,528,256]{2,1,0:T(8,128)(2,1)S(1)}, bf16[1,528,256]{2,1,0:T(8,128)(2,1)}, u32[]{:S(2)}, u32[]{:S(2)}) collective-permute-start(bf16[1,528,256]{2,1,0:T(8,128)(2,1)S(1)} %collective-permute-done.8.rest_3_), channel_id=1, source_target_pairs={{8,0},{10,2},{12,4},{14,6},{16,8},{18,10},{20,12},{22,14},{24,16},... | collective-permute-start | bytes 811016 | tf_op jit(solution)/shard_map/ppermute | solution.py:386
  40.5 0.7 collective-permute-done.9.rest_4_
  41.2 3.4 %collective-permute-start.19 = (bf16[1024,256]{1,0:T(8,128)(2,1)}, bf16[1024,256]{1,0:T(8,128)(2,1)S(1)}, u32[]{:S(2)}, u32[]{:S(2)}) collective-permute-start(bf16[1024,256]{1,0:T(8,128)(2,1)} %copy-done.19), channel_id=1, source_target_pairs={{4,1},{5,0},{6,3},{7,2},{12,9},{13,8},{14,11},{15,10},{20,17},{21,... | collective-permute-start | bytes 1572872 | tf_op jit(solution)/shard_map/ppermute | solution.py:408
  44.6 1.3 %collective-permute-start.13 = (bf16[1,512,256]{2,1,0:T(8,128)(2,1)S(1)}, bf16[1,512,256]{2,1,0:T(8,128)(2,1)}, u32[]{:S(2)}, u32[]{:S(2)}) collective-permute-start(bf16[1,512,256]{2,1,0:T(8,128)(2,1)S(1)} %collective-permute-done.9.rest_4_), channel_id=1, source_target_pairs={{0,4},{2,6},{8,12},{10,14},{16,20},{18,22},{24,28},{26,30},{1,5},{... | collective-permute-start | bytes 786440 | tf_op jit(solution)/shard_map/ppermute | solution.py:392
  45.9 0.7 copy-done.12
  46.6 3.1 %collective-permute-start.12 = (bf16[1,512,256]{2,1,0:T(8,128)(2,1)S(1)}, bf16[1,512,256]{2,1,0:T(8,128)(2,1)S(1)}, u32[]{:S(2)}, u32[]{:S(2)}) collective-permute-start(bf16[1,512,256]{2,1,0:T(8,128)(2,1)S(1)} %bitcast.23), channel_id=1, source_target_pairs={{8,0},{10,2},{12,4},{14,6},{16,8},{18,10},{20,12},{22,14},{24,16},... | collective-permute-start | bytes 786440 | tf_op jit(solution)/shard_map/ppermute | solution.py:386
  49.7 1.3 %shard_map.41.value_ref = f32[16,128]{1,0:T(8,128)} custom-call(f32[16,128]{1,0:T(8,128)} %shard_map.40.value_ref), custom_call_target="tpu_custom_call" | custom-call | flops 100000000 | tf_op jit(solution)/shard_map/pallas_call | solution.py:374
  51.0 1.3 %shard_map.42.value_ref = f32[16,128]{1,0:T(8,128)} custom-call(f32[16,128]{1,0:T(8,128)} %shard_map.41.value_ref), custom_call_target="tpu_custom_call" | custom-call | flops 300000000 | tf_op jit(solution)/shard_map/pallas_call | solution.py:374
  52.3 1.3 %shard_map.43.value_ref = f32[16,128]{1,0:T(8,128)} custom-call(f32[16,128]{1,0:T(8,128)} %shard_map.42.value_ref), custom_call_target="tpu_custom_call" | custom-call | tf_op jit(solution)/shard_map/pallas_call | solution.py:374
  53.6 1.3 %shard_map.44.value_ref = f32[16,128]{1,0:T(8,128)} custom-call(f32[16,128]{1,0:T(8,128)} %shard_map.43.value_ref), custom_call_target="tpu_custom_call" | custom-call | flops 100000000 | tf_op jit(solution)/shard_map/pallas_call | solution.py:374
  54.9 1.3 %collective-permute-start.18 = (bf16[1,528,256]{2,1,0:T(8,128)(2,1)}, bf16[1,528,256]{2,1,0:T(8,128)(2,1)}, u32[]{:S(2)}, u32[]{:S(2)}) collective-permute-start(bf16[1,528,256]{2,1,0:T(8,128)(2,1)} %collective-permute-done.14.rest_5_), channel_id=1, source_target_pairs={{0,4},{2,6},{8,12},{10,14},{16,20},{18,22},{24,28},{26,30},{1,5},{... | collective-permute-start | bytes 811016 | tf_op jit(solution)/shard_map/ppermute | solution.py:392
  56.2 2.8 %collective-permute-start.17 = (bf16[1,512,256]{2,1,0:T(8,128)(2,1)S(1)}, bf16[1,512,256]{2,1,0:T(8,128)(2,1)}, u32[]{:S(2)}, u32[]{:S(2)}) collective-permute-start(bf16[1,512,256]{2,1,0:T(8,128)(2,1)S(1)} %collective-permute-done.12.rest_3_), channel_id=1, source_target_pairs={{8,0},{10,2},{12,4},{14,6},{16,8},{18,10},{20,12},{22,14},{24,16},... | collective-permute-start | bytes 786440 | tf_op jit(solution)/shard_map/ppermute | solution.py:386
  59.0 3.5 %collective-permute-start.16 = (bf16[1,512,256]{2,1,0:T(8,128)(2,1)S(1)}, bf16[1,512,256]{2,1,0:T(8,128)(2,1)S(1)}, u32[]{:S(2)}, u32[]{:S(2)}) collective-permute-start(bf16[1,512,256]{2,1,0:T(8,128)(2,1)S(1)} %collective-permute-done.12.rest_3_), channel_id=1, source_target_pairs={{0,4},{2,6},{4,0},{6,2},{8,12},{10,14},{12,8},{14,10},{16,20},{18,... | collective-permute-start | bytes 786440 | tf_op jit(solution)/shard_map/ppermute | solution.py:392
  62.5 1.3 %shard_map.45.rest_2_ = f32[16,128]{1,0:T(8,128)} custom-call(f32[16,128]{1,0:T(8,128)} %shard_map.44.value_ref), custom_call_target="tpu_custom_call" | custom-call | flops 300000000 | tf_op jit(solution)/shard_map/pallas_call | solution.py:374
  63.8 0.2 collective-permute-done.18.rest_9_
  63.9 0.9 %copy-done.1 = bf16[512,256]{1,0:T(8,128)(2,1)S(1)} copy-done((bf16[512,256]{1,0:T(8,128)(2,1)S(1)}, bf16[512,256]{1,0:T(8,128)(2,1)}, u32[]{:S(2)}) %copy-start.1) | copy-done | bytes 262168
  64.9 0.9 %copy-done.3 = bf16[1,512,256]{2,1,0:T(8,128)(2,1)S(1)} copy-done((bf16[1,512,256]{2,1,0:T(8,128)(2,1)S(1)}, bf16[1,512,256]{2,1,0:T(8,128)(2,1)}, u32[]{:S(2)}) %copy-start.3) | copy-done | bytes 262168
  65.8 0.9 %copy-done.6 = bf16[1,512,256]{2,1,0:T(8,128)(2,1)S(1)} copy-done((bf16[1,512,256]{2,1,0:T(8,128)(2,1)S(1)}, bf16[1,512,256]{2,1,0:T(8,128)(2,1)}, u32[]{:S(2)}) %copy-start.6) | copy-done | bytes 262168
  66.8 2.3 %shard_map.46 = (f32[8,128,1024]{2,1,0:T(8,128)S(1)}, f32[2,128,512]{2,1,0:T(8,128)S(1)}) custom-call(s32[3]{0:T(128)S(1)} %pad_add_fusion.place_ref, f32[16,128]{1,0:T(8,128)S(1)} %copy-done.15, bf16[1,528,256]{2,1,0:T(8,128)(2,1)S(1)} %bitcast.10, bf16[1,512,256]{2,1,0:T(8,128)(2,1)S(1)} %bitcast.27, bf16[1,528,256]{2,1,0:T(8,128)(2,1)S(1)} %bitcast.11, ...), custom_call_target="tpu_custom_call" | custom-call | flops 402653184 | bytes 1048576 | tf_op jit(solution)/shard_map/pallas_call | solution.py:307
  69.2 0.3 collective-permute-done.16.rest_7_
  69.4 2.3 %shard_map.47 = (f32[8,128,1024]{2,1,0:T(8,128)S(1)}, f32[2,128,512]{2,1,0:T(8,128)S(1)}) custom-call(s32[3]{0:T(128)S(1)} %pad_add_fusion.place_ref, f32[16,128]{1,0:T(8,128)S(1)} %copy-done.15, bf16[1,528,256]{2,1,0:T(8,128)(2,1)S(1)} %bitcast.12, bf16[1,512,256]{2,1,0:T(8,128)(2,1)S(1)} %bitcast.21, ...), custom_call_target="tpu_custom_call", output_to_operand_aliasing={{0}: (11, {})} | custom-call | flops 402653184 | bytes 1048576 | tf_op jit(solution)/shard_map/pallas_call | solution.py:307
  71.8 5.0 %collective-permute-start.21 = (f32[2,128,512]{2,1,0:T(8,128)S(1)}, f32[2,128,512]{2,1,0:T(8,128)S(1)}, u32[]{:S(2)}, u32[]{:S(2)}) collective-permute-start(f32[2,128,512]{2,1,0:T(8,128)S(1)} %get-tuple-element.217), channel_id=1, source_target_pairs={{0,2},{2,0},{4,6},{6,4},{8,10},{10,8},{12,14},{14,12},{16,18},{18,... | collective-permute-start | bytes 1572872 | tf_op jit(solution)/shard_map/ppermute | solution.py:397
  76.7 0.1 collective-permute-start.20
  76.8 1.3 %collective-permute-start.23 = (bf16[1,512,256]{2,1,0:T(8,128)(2,1)}, bf16[1,512,256]{2,1,0:T(8,128)(2,1)S(1)}, u32[]{:S(2)}, u32[]{:S(2)}) collective-permute-start(bf16[1,512,256]{2,1,0:T(8,128)(2,1)} %collective-permute-done.17.rest_5_), channel_id=1, source_target_pairs={{0,4},{2,6},{8,12},{10,14},{16,20},{18,22},{24,28},{26,30},{1,5},{... | collective-permute-start | bytes 786440 | tf_op jit(solution)/shard_map/ppermute | solution.py:392
  78.1 0.2 collective-permute-done.21.rest_11_
  78.3 0.7 collective-permute-done.20.rest_10_
  79.0 3.0 %shard_map.48 = (f32[8,128,1024]{2,1,0:T(8,128)S(1)}, f32[2,128,512]{2,1,0:T(8,128)S(1)}) custom-call(s32[3]{0:T(128)S(1)} %pad_add_fusion.place_ref, f32[16,128]{1,0:T(8,128)S(1)} %copy-done.15, bf16[1,528,256]{2,1,0:T(8,128)(2,1)S(1)} %bitcast.13, bf16[1,512,256]{2,1,0:T(8,128)(2,1)S(1)} %bitcast.28, ...), custom_call_target="tpu_custom_call", output_to_operand_aliasing={{0}: (15, {})} | custom-call | flops 402653184 | bytes 1048576 | tf_op jit(solution)/shard_map/pallas_call | solution.py:307
  82.0 0.4 collective-permute-start.22
  82.4 2.0 %copy.10.rest_10_ = f32[8,128,1024]{2,1,0:T(8,128)} copy(f32[8,128,1024]{2,1,0:T(8,128)S(1)} %get-tuple-element.225) | data formatting | bytes 8388608
  84.5 1.9 %collective-permute-done.23.rest_9_ = bf16[1,512,256]{2,1,0:T(8,128)(2,1)S(1)} collective-permute-done((bf16[1,512,256]{2,1,0:T(8,128)(2,1)}, bf16[1,512,256]{2,1,0:T(8,128)(2,1)S(1)}, u32[]{:S(2)}, u32[]{:S(2)}) %collective-permute-start.23) | collective-permute-done | bytes 262176 | tf_op jit(solution)/shard_map/ppermute | solution.py:392
  86.4 3.1 %shard_map.49 = (f32[8,128,1024]{2,1,0:T(8,128)}, f32[2,128,512]{2,1,0:T(8,128)S(1)}) custom-call(s32[3]{0:T(128)S(1)} %pad_add_fusion.place_ref, f32[16,128]{1,0:T(8,128)S(1)} %copy-done.15, bf16[1,528,256]{2,1,0:T(8,128)(2,1)S(1)} %bitcast.15, bf16[1,512,256]{2,1,0:T(8,128)(2,1)S(1)} %bitcast.22, ...), custom_call_target="tpu_custom_call", output_to_operand_aliasing={{0}: (13, {})} | custom-call | flops 402653184 | bytes 1048576 | tf_op jit(solution)/shard_map/pallas_call | solution.py:307
  89.5 1.3 %collective-permute-start.24 = (f32[2,128,512]{2,1,0:T(8,128)S(1)}, f32[2,128,512]{2,1,0:T(8,128)S(1)}, u32[]{:S(2)}, u32[]{:S(2)}) collective-permute-start(f32[2,128,512]{2,1,0:T(8,128)S(1)} %get-tuple-element.226), channel_id=1, source_target_pairs={{0,2},{2,0},{4,6},{6,4},{8,10},{10,8},{12,14},{14,12},{16,18},{18,... | collective-permute-start | bytes 1572872 | tf_op jit(solution)/shard_map/ppermute | solution.py:397
  90.8 1.5 %collective-permute-done.24.rest_1_ = f32[2,128,512]{2,1,0:T(8,128)S(1)} collective-permute-done((f32[2,128,512]{2,1,0:T(8,128)S(1)}, f32[2,128,512]{2,1,0:T(8,128)S(1)}, u32[]{:S(2)}, u32[]{:S(2)}) %collective-permute-start.24) | collective-permute-done | bytes 524320 | tf_op jit(solution)/shard_map/ppermute | solution.py:397
  92.4 1.5 %shard_map.50 = f32[8,128,1024]{2,1,0:T(8,128)} custom-call(s32[3]{0:T(128)S(1)} %pad_add_fusion.place_ref, f32[2,128,512]{2,1,0:T(8,128)S(1)} %collective-permute-done.22.rest_0_, f32[2,128,512]{2,1,0:T(8,128)S(1)} %collective-permute-done.24.rest_1_, f32[16,128]{1,0:T(8,128)S(1)} %copy-done.16, ...), custom_call_target="tpu_custom_call", output_to_operand_aliasing={{}: (4, {})} | custom-call | bytes 2097152 | tf_op jit(solution)/shard_map/pallas_call | solution.py:357
  (43 shorter events, 0.1 us)
Async XLA Ops:
  0.0 3.7 %collective-permute-start = (bf16[128,4096]{1,0:T(8,128)(2,1)}, bf16[128,4096]{1,0:T(8,128)(2,1)S(1)}, u32[]{:S(2)}, u32[]{:S(2)}) collective-permute-start(bf16[128,4096]{1,0:T(8,128)(2,1)} %frames_hbm.1), channel_id=1, source_target_pairs={{0,2},{2,0},{4,6},{6,4},{8,10},{10,8},{12,14},{14,12},{16,18},{18,... | collective-permute-start | bytes 3145736 | tf_op jit(solution)/shard_map/ppermute | solution.py:397
  2.7 1.0 %copy-start.17 = (bf16[128,4096]{1,0:T(8,128)(2,1)}, bf16[128,4096]{1,0:T(8,128)(2,1)S(1)}, u32[]{:S(2)}) copy-start(bf16[128,4096]{1,0:T(8,128)(2,1)S(1)} %get-tuple-element.122.rest_0_) | copy-start | bytes 3145732
  3.6 12.3 %copy-start.14 = (f32[16,128]{1,0:T(8,128)}, f32[16,128]{1,0:T(8,128)S(1)}, u32[]{:S(2)}) copy-start(f32[16,128]{1,0:T(8,128)S(1)} %get-tuple-element.221.counts_ref.value_ref) | copy-start | bytes 24580
  3.7 1.2 %copy-start.18 = (bf16[128,4096]{1,0:T(8,128)(2,1)S(1)}, bf16[128,4096]{1,0:T(8,128)(2,1)}, u32[]{:S(2)}) copy-start(bf16[128,4096]{1,0:T(8,128)(2,1)} %copy-done.17) | copy-start | bytes 3145732
  8.0 13.5 %copy-start = (bf16[512,256]{1,0:T(8,128)(2,1)}, bf16[512,256]{1,0:T(8,128)(2,1)S(1)}, u32[]{:S(2)}) copy-start(bf16[512,256]{1,0:T(8,128)(2,1)S(1)} %get-tuple-element.123) | copy-start | bytes 786436
  8.0 12.2 %collective-permute-start.1 = (bf16[1,512,256]{2,1,0:T(8,128)(2,1)S(1)}, bf16[1,512,256]{2,1,0:T(8,128)(2,1)S(1)}, u32[]{:S(2)}, u32[]{:S(2)}) collective-permute-start(bf16[1,512,256]{2,1,0:T(8,128)(2,1)S(1)} %bitcast.26), channel_id=1, source_target_pairs={{8,0},{10,2},{12,4},{14,6},{16,8},{18,10},{20,12},{22,14},{24,16},... | collective-permute-start | bytes 786440 | tf_op jit(solution)/shard_map/ppermute | solution.py:386
  10.1 18.3 %collective-permute-start.5 = (bf16[1024,256]{1,0:T(8,128)(2,1)S(1)}, bf16[1024,256]{1,0:T(8,128)(2,1)S(1)}, u32[]{:S(2)}, u32[]{:S(2)}) collective-permute-start(bf16[1024,256]{1,0:T(8,128)(2,1)S(1)} %get-tuple-element.145), channel_id=1, source_target_pairs={{4,0},{6,2},{12,8},{14,10},{20,16},{22,18},{28,24},{30,26},{5,1},{... | collective-permute-start | bytes 1572872 | tf_op jit(solution)/shard_map/ppermute | solution.py:392
  15.9 0.8 copy-start.19
  16.7 47.2 %copy-start.15 = (f32[16,128]{1,0:T(8,128)S(1)}, f32[16,128]{1,0:T(8,128)}, u32[]{:S(2)}) copy-start(f32[16,128]{1,0:T(8,128)} %copy-done.14) | copy-start | bytes 24580
  16.7 11.7 %collective-permute-start.3 = (bf16[1,512,256]{2,1,0:T(8,128)(2,1)S(1)}, bf16[1,512,256]{2,1,0:T(8,128)(2,1)S(1)}, u32[]{:S(2)}, u32[]{:S(2)}) collective-permute-start(bf16[1,512,256]{2,1,0:T(8,128)(2,1)S(1)} %bitcast.20), channel_id=1, source_target_pairs={{8,0},{10,2},{12,4},{14,6},{16,8},{18,10},{20,12},{22,14},{24,16},... | collective-permute-start | bytes 786440 | tf_op jit(solution)/shard_map/ppermute | solution.py:386
  18.9 7.2 %collective-permute-start.6 = (bf16[528,256]{1,0:T(8,128)(2,1)S(1)}, bf16[528,256]{1,0:T(8,128)(2,1)S(1)}, u32[]{:S(2)}, u32[]{:S(2)}) collective-permute-start(bf16[528,256]{1,0:T(8,128)(2,1)S(1)} %get-tuple-element.146), channel_id=1, source_target_pairs={{0,1},{1,0},{2,3},{3,2},{4,5},{5,4},{6,7},{7,6},{8,9},{9,8},{10,11... | collective-permute-start | bytes 811016 | tf_op jit(solution)/shard_map/ppermute | solution.py:408
  20.2 20.2 %copy-start.2 = (bf16[1,512,256]{2,1,0:T(8,128)(2,1)}, bf16[1,512,256]{2,1,0:T(8,128)(2,1)S(1)}, u32[]{:S(2)}) copy-start(bf16[1,512,256]{2,1,0:T(8,128)(2,1)S(1)} %collective-permute-done.1.rest_2_) | copy-start | bytes 786436
  21.5 9.2 %collective-permute-start.4 = (bf16[1,512,256]{2,1,0:T(8,128)(2,1)S(1)}, bf16[1,512,256]{2,1,0:T(8,128)(2,1)S(1)}, u32[]{:S(2)}, u32[]{:S(2)}) collective-permute-start(bf16[1,512,256]{2,1,0:T(8,128)(2,1)S(1)} %collective-permute-done.1.rest_2_), channel_id=1, source_target_pairs={{8,0},{10,2},{12,4},{14,6},{16,8},{18,10},{20,12},{22,14},{24,16},... | collective-permute-start | bytes 786440 | tf_op jit(solution)/shard_map/ppermute | solution.py:386
  23.6 7.1 %collective-permute-start.2 = (bf16[1,512,256]{2,1,0:T(8,128)(2,1)S(1)}, bf16[1,512,256]{2,1,0:T(8,128)(2,1)S(1)}, u32[]{:S(2)}, u32[]{:S(2)}) collective-permute-start(bf16[1,512,256]{2,1,0:T(8,128)(2,1)S(1)} %collective-permute-done.1.rest_2_), channel_id=1, source_target_pairs={{0,4},{2,6},{4,0},{6,2},{8,12},{10,14},{12,8},{14,10},{16,20},{18,... | collective-permute-start | bytes 786440 | tf_op jit(solution)/shard_map/ppermute | solution.py:392
  26.1 9.4 %collective-permute-start.8 = (bf16[1,528,256]{2,1,0:T(8,128)(2,1)S(1)}, bf16[1,528,256]{2,1,0:T(8,128)(2,1)S(1)}, u32[]{:S(2)}, u32[]{:S(2)}) collective-permute-start(bf16[1,528,256]{2,1,0:T(8,128)(2,1)S(1)} %bitcast.9), channel_id=1, source_target_pairs={{8,0},{10,2},{12,4},{14,6},{16,8},{18,10},{20,12},{22,14},{24,16},... | collective-permute-start | bytes 811016 | tf_op jit(solution)/shard_map/ppermute | solution.py:386
  28.4 8.2 %collective-permute-start.10 = (bf16[1,512,256]{2,1,0:T(8,128)(2,1)S(1)}, bf16[1,512,256]{2,1,0:T(8,128)(2,1)S(1)}, u32[]{:S(2)}, u32[]{:S(2)}) collective-permute-start(bf16[1,512,256]{2,1,0:T(8,128)(2,1)S(1)} %collective-permute-done.3.rest_2_), channel_id=1, source_target_pairs={{0,4},{2,6},{4,0},{6,2},{8,12},{10,14},{12,8},{14,10},{16,20},{18,... | collective-permute-start | bytes 786440 | tf_op jit(solution)/shard_map/ppermute | solution.py:392
  28.5 12.7 %collective-permute-start.9 = (bf16[1,512,256]{2,1,0:T(8,128)(2,1)S(1)}, bf16[1,512,256]{2,1,0:T(8,128)(2,1)S(1)}, u32[]{:S(2)}, u32[]{:S(2)}) collective-permute-start(bf16[1,512,256]{2,1,0:T(8,128)(2,1)S(1)} %collective-permute-done.3.rest_2_), channel_id=1, source_target_pairs={{8,0},{10,2},{12,4},{14,6},{16,8},{18,10},{20,12},{22,14},{24,16},... | collective-permute-start | bytes 786440 | tf_op jit(solution)/shard_map/ppermute | solution.py:386
  30.8 0.7 copy-start.5
  31.5 13.1 %collective-permute-start.7 = (bf16[512,256]{1,0:T(8,128)(2,1)}, bf16[512,256]{1,0:T(8,128)(2,1)S(1)}, u32[]{:S(2)}, u32[]{:S(2)}) collective-permute-start(bf16[512,256]{1,0:T(8,128)(2,1)} %get-tuple-element.155), channel_id=1, source_target_pairs={{0,1},{1,0},{2,3},{3,2},{4,5},{5,4},{6,7},{7,6},{8,9},{9,8},{10,11... | collective-permute-start | bytes 786440 | tf_op jit(solution)/shard_map/ppermute | solution.py:408
  32.5 13.3 %collective-permute-start.11 = (bf16[1,512,256]{2,1,0:T(8,128)(2,1)S(1)}, bf16[1,512,256]{2,1,0:T(8,128)(2,1)S(1)}, u32[]{:S(2)}, u32[]{:S(2)}) collective-permute-start(bf16[1,512,256]{2,1,0:T(8,128)(2,1)S(1)} %collective-permute-done.4.rest_4_), channel_id=1, source_target_pairs={{0,4},{2,6},{8,12},{10,14},{16,20},{18,22},{24,28},{26,30},{1,5},{... | collective-permute-start | bytes 786440 | tf_op jit(solution)/shard_map/ppermute | solution.py:392
  33.8 0.7 copy-start.10
  35.6 18.1 %collective-permute-start.15 = (bf16[1,528,256]{2,1,0:T(8,128)(2,1)S(1)}, bf16[1,528,256]{2,1,0:T(8,128)(2,1)S(1)}, u32[]{:S(2)}, u32[]{:S(2)}) collective-permute-start(bf16[1,528,256]{2,1,0:T(8,128)(2,1)S(1)} %collective-permute-done.8.rest_3_), channel_id=1, source_target_pairs={{0,4},{2,6},{4,0},{6,2},{8,12},{10,14},{12,8},{14,10},{16,20},{18,... | collective-permute-start | bytes 811016 | tf_op jit(solution)/shard_map/ppermute | solution.py:392
  36.6 18.3 %collective-permute-start.14 = (bf16[1,528,256]{2,1,0:T(8,128)(2,1)S(1)}, bf16[1,528,256]{2,1,0:T(8,128)(2,1)}, u32[]{:S(2)}, u32[]{:S(2)}) collective-permute-start(bf16[1,528,256]{2,1,0:T(8,128)(2,1)S(1)} %collective-permute-done.8.rest_3_), channel_id=1, source_target_pairs={{8,0},{10,2},{12,4},{14,6},{16,8},{18,10},{20,12},{22,14},{24,16},... | collective-permute-start | bytes 811016 | tf_op jit(solution)/shard_map/ppermute | solution.py:386
  41.2 15.0 %copy-start.8 = (bf16[1,512,256]{2,1,0:T(8,128)(2,1)}, bf16[1,512,256]{2,1,0:T(8,128)(2,1)S(1)}, u32[]{:S(2)}) copy-start(bf16[1,512,256]{2,1,0:T(8,128)(2,1)S(1)} %collective-permute-done.9.rest_4_) | copy-start | bytes 786436
  41.2 22.6 %collective-permute-start.19 = (bf16[1024,256]{1,0:T(8,128)(2,1)}, bf16[1024,256]{1,0:T(8,128)(2,1)S(1)}, u32[]{:S(2)}, u32[]{:S(2)}) collective-permute-start(bf16[1024,256]{1,0:T(8,128)(2,1)} %copy-done.19), channel_id=1, source_target_pairs={{4,1},{5,0},{6,3},{7,2},{12,9},{13,8},{14,11},{15,10},{20,17},{21,... | collective-permute-start | bytes 1572872 | tf_op jit(solution)/shard_map/ppermute | solution.py:408
  44.6 11.6 %collective-permute-start.13 = (bf16[1,512,256]{2,1,0:T(8,128)(2,1)S(1)}, bf16[1,512,256]{2,1,0:T(8,128)(2,1)}, u32[]{:S(2)}, u32[]{:S(2)}) collective-permute-start(bf16[1,512,256]{2,1,0:T(8,128)(2,1)S(1)} %collective-permute-done.9.rest_4_), channel_id=1, source_target_pairs={{0,4},{2,6},{8,12},{10,14},{16,20},{18,22},{24,28},{26,30},{1,5},{... | collective-permute-start | bytes 786440 | tf_op jit(solution)/shard_map/ppermute | solution.py:392
  45.9 0.7 copy-start.12
  46.6 9.6 %collective-permute-start.12 = (bf16[1,512,256]{2,1,0:T(8,128)(2,1)S(1)}, bf16[1,512,256]{2,1,0:T(8,128)(2,1)S(1)}, u32[]{:S(2)}, u32[]{:S(2)}) collective-permute-start(bf16[1,512,256]{2,1,0:T(8,128)(2,1)S(1)} %bitcast.23), channel_id=1, source_target_pairs={{8,0},{10,2},{12,4},{14,6},{16,8},{18,10},{20,12},{22,14},{24,16},... | collective-permute-start | bytes 786440 | tf_op jit(solution)/shard_map/ppermute | solution.py:386
  54.9 9.0 %collective-permute-start.18 = (bf16[1,528,256]{2,1,0:T(8,128)(2,1)}, bf16[1,528,256]{2,1,0:T(8,128)(2,1)}, u32[]{:S(2)}, u32[]{:S(2)}) collective-permute-start(bf16[1,528,256]{2,1,0:T(8,128)(2,1)} %collective-permute-done.14.rest_5_), channel_id=1, source_target_pairs={{0,4},{2,6},{8,12},{10,14},{16,20},{18,22},{24,28},{26,30},{1,5},{... | collective-permute-start | bytes 811016 | tf_op jit(solution)/shard_map/ppermute | solution.py:392
  56.2 12.9 %collective-permute-start.17 = (bf16[1,512,256]{2,1,0:T(8,128)(2,1)S(1)}, bf16[1,512,256]{2,1,0:T(8,128)(2,1)}, u32[]{:S(2)}, u32[]{:S(2)}) collective-permute-start(bf16[1,512,256]{2,1,0:T(8,128)(2,1)S(1)} %collective-permute-done.12.rest_3_), channel_id=1, source_target_pairs={{8,0},{10,2},{12,4},{14,6},{16,8},{18,10},{20,12},{22,14},{24,16},... | collective-permute-start | bytes 786440 | tf_op jit(solution)/shard_map/ppermute | solution.py:386
  59.0 10.4 %collective-permute-start.16 = (bf16[1,512,256]{2,1,0:T(8,128)(2,1)S(1)}, bf16[1,512,256]{2,1,0:T(8,128)(2,1)S(1)}, u32[]{:S(2)}, u32[]{:S(2)}) collective-permute-start(bf16[1,512,256]{2,1,0:T(8,128)(2,1)S(1)} %collective-permute-done.12.rest_3_), channel_id=1, source_target_pairs={{0,4},{2,6},{4,0},{6,2},{8,12},{10,14},{12,8},{14,10},{16,20},{18,... | collective-permute-start | bytes 786440 | tf_op jit(solution)/shard_map/ppermute | solution.py:392
  63.9 1.0 %copy-start.1 = (bf16[512,256]{1,0:T(8,128)(2,1)S(1)}, bf16[512,256]{1,0:T(8,128)(2,1)}, u32[]{:S(2)}) copy-start(bf16[512,256]{1,0:T(8,128)(2,1)} %copy-done) | copy-start | bytes 786436
  64.9 0.9 %copy-start.3 = (bf16[1,512,256]{2,1,0:T(8,128)(2,1)S(1)}, bf16[1,512,256]{2,1,0:T(8,128)(2,1)}, u32[]{:S(2)}) copy-start(bf16[1,512,256]{2,1,0:T(8,128)(2,1)} %copy-done.2) | copy-start | bytes 786436
  65.8 0.9 %copy-start.6 = (bf16[1,512,256]{2,1,0:T(8,128)(2,1)S(1)}, bf16[1,512,256]{2,1,0:T(8,128)(2,1)}, u32[]{:S(2)}) copy-start(bf16[1,512,256]{2,1,0:T(8,128)(2,1)} %copy-done.5) | copy-start | bytes 786436
  69.1 9.9 %copy-start.4 = (bf16[1,512,256]{2,1,0:T(8,128)(2,1)S(1)}, bf16[1,512,256]{2,1,0:T(8,128)(2,1)}, u32[]{:S(2)}) copy-start(bf16[1,512,256]{2,1,0:T(8,128)(2,1)} %copy-done.2) | copy-start | bytes 786436
  69.1 9.9 %copy-start.7 = (bf16[1,512,256]{2,1,0:T(8,128)(2,1)S(1)}, bf16[1,512,256]{2,1,0:T(8,128)(2,1)}, u32[]{:S(2)}) copy-start(bf16[1,512,256]{2,1,0:T(8,128)(2,1)} %copy-done.5) | copy-start | bytes 786436
  69.1 9.9 %copy-start.11 = (bf16[1,512,256]{2,1,0:T(8,128)(2,1)S(1)}, bf16[1,512,256]{2,1,0:T(8,128)(2,1)}, u32[]{:S(2)}) copy-start(bf16[1,512,256]{2,1,0:T(8,128)(2,1)} %copy-done.10) | copy-start | bytes 786436
  69.1 9.9 %copy-start.13 = (bf16[1,512,256]{2,1,0:T(8,128)(2,1)S(1)}, bf16[1,512,256]{2,1,0:T(8,128)(2,1)}, u32[]{:S(2)}) copy-start(bf16[1,512,256]{2,1,0:T(8,128)(2,1)} %copy-done.12) | copy-start | bytes 786436
  71.8 6.5 %collective-permute-start.21 = (f32[2,128,512]{2,1,0:T(8,128)S(1)}, f32[2,128,512]{2,1,0:T(8,128)S(1)}, u32[]{:S(2)}, u32[]{:S(2)}) collective-permute-start(f32[2,128,512]{2,1,0:T(8,128)S(1)} %get-tuple-element.217), channel_id=1, source_target_pairs={{0,2},{2,0},{4,6},{6,4},{8,10},{10,8},{12,14},{14,12},{16,18},{18,... | collective-permute-start | bytes 1572872 | tf_op jit(solution)/shard_map/ppermute | solution.py:397
  76.7 2.3 %collective-permute-start.20 = (f32[2,128,512]{2,1,0:T(8,128)S(1)}, f32[2,128,512]{2,1,0:T(8,128)S(1)}, u32[]{:S(2)}, u32[]{:S(2)}) collective-permute-start(f32[2,128,512]{2,1,0:T(8,128)S(1)} %get-tuple-element.216), channel_id=1, source_target_pairs={{0,2},{2,0},{4,6},{6,4},{8,10},{10,8},{12,14},{14,12},{16,18},{18,... | collective-permute-start | bytes 1572872 | tf_op jit(solution)/shard_map/ppermute | solution.py:397
  76.8 9.5 %collective-permute-start.23 = (bf16[1,512,256]{2,1,0:T(8,128)(2,1)}, bf16[1,512,256]{2,1,0:T(8,128)(2,1)S(1)}, u32[]{:S(2)}, u32[]{:S(2)}) collective-permute-start(bf16[1,512,256]{2,1,0:T(8,128)(2,1)} %collective-permute-done.17.rest_5_), channel_id=1, source_target_pairs={{0,4},{2,6},{8,12},{10,14},{16,20},{18,22},{24,28},{26,30},{1,5},{... | collective-permute-start | bytes 786440 | tf_op jit(solution)/shard_map/ppermute | solution.py:392
  82.0 8.8 %collective-permute-start.22 = (f32[2,128,512]{2,1,0:T(8,128)S(1)}, f32[2,128,512]{2,1,0:T(8,128)S(1)}, u32[]{:S(2)}, u32[]{:S(2)}) collective-permute-start(f32[2,128,512]{2,1,0:T(8,128)S(1)} %get-tuple-element.219), channel_id=1, source_target_pairs={{0,2},{2,0},{4,6},{6,4},{8,10},{10,8},{12,14},{14,12},{16,18},{18,... | collective-permute-start | bytes 1572872 | tf_op jit(solution)/shard_map/ppermute | solution.py:397
  82.4 3.9 %copy-start.9 = (bf16[1,512,256]{2,1,0:T(8,128)(2,1)S(1)}, bf16[1,512,256]{2,1,0:T(8,128)(2,1)}, u32[]{:S(2)}) copy-start(bf16[1,512,256]{2,1,0:T(8,128)(2,1)} %copy-done.8) | copy-start | bytes 786436
  84.5 7.9 %copy-start.16 = (f32[16,128]{1,0:T(8,128)S(1)}, f32[16,128]{1,0:T(8,128)}, u32[]{:S(2)}) copy-start(f32[16,128]{1,0:T(8,128)} %shard_map.45.rest_2_) | copy-start | bytes 24580
  89.5 2.9 %collective-permute-start.24 = (f32[2,128,512]{2,1,0:T(8,128)S(1)}, f32[2,128,512]{2,1,0:T(8,128)S(1)}, u32[]{:S(2)}, u32[]{:S(2)}) collective-permute-start(f32[2,128,512]{2,1,0:T(8,128)S(1)} %get-tuple-element.226), channel_id=1, source_target_pairs={{0,2},{2,0},{4,6},{6,4},{8,10},{10,8},{12,14},{14,12},{16,18},{18,... | collective-permute-start | bytes 1572872 | tf_op jit(solution)/shard_map/ppermute | solution.py:397

commit v7 on v6

--- a/solution.py
+++ b/solution.py
@@ -237,7 +237,7 @@
             )
         own_sums = jnp.sum(own_rows.astype(jnp.float32), axis=1, keepdims=True)
         earlier[cycle] = jnp.broadcast_to(total / own_sums, (chip_block, LANES))
-        for target, position in ((theirs_ref, 1 - core), (mine_ref, core)):
+        for target, position in ((mine_ref, core), (theirs_ref, 1 - core)):
             base = pl.multiple_of(position * block, block)
             scales = [
                 later[cycle, :, pl.ds(pl.multiple_of(base + tile * LANES, LANES), LANES)]
@@ -266,13 +266,15 @@
                             cycle, first : first + SUBLANES, tile * LANES : (tile + 1) * LANES
                         ] = results[at]
                         at += 1
-        store = pltpu.make_async_copy(
-            mine_ref.at[cycle],
-            out_ref.at[core * group + offset + cycle, :, pl.ds(phase * lags, lags)],
-            sems.at[cycle],
-        )
-        store.start()
-        stores.append(store)
+            if target is theirs_ref:
+                continue
+            store = pltpu.make_async_copy(
+                mine_ref.at[cycle],
+                out_ref.at[core * group + offset + cycle, :, pl.ds(phase * lags, lags)],
+                sems.at[cycle],
+            )
+            store.start()
+            stores.append(store)
     for copy in stores + fills:
         copy.wait()
 
@@ -376,6 +378,7 @@
         out_shape=jax.ShapeDtypeStruct(value.shape, value.dtype),
         in_specs=[VMEM_SPEC],
         out_specs=VMEM_SPEC,
+        compiler_params=pltpu.CompilerParams(vmem_limit_bytes=1024 * 1024),
         cost_estimate=estimate(weight, 0),
     )(value)
 

time: 94.8 us -> 83.4 us (0.88)
  the two profiles are of different devices: /device:TPU:27 before, /device:TPU:0 now
where the time goes in v7:
time: 83.4 us; the launch traced here: 82.8 us
  starting transfers between devices  41 us (49%)
  waiting for transfers between devices  20.6 us (25%)
  Pallas kernels  18.1 us (22%)
  local copies, waits for them, and re-layouts  2.02 us (2%)
    ppermute x9, starting transfers between devices, other_pair(): lax.ppermute(value, 'frame', [(source, source ^ 2) for source in sources])  22.6 us
    ppermute x8, starting transfers between devices, shifted(): lax.ppermute(value, 'frame', [(source, source - step) for source in range...  10.3 us
    pallas_call x4, Pallas kernels, grams(): pl.pallas_call(kernel, out_shape=[jax.ShapeDtypeStruct((cycle_dev, block,...  9.38 us
    ppermute x8, waiting for transfers between devices, shifted(): lax.ppermute(value, 'frame', [(source, source - step) for source in range...  8.92 us
    ppermute x9, waiting for transfers between devices, other_pair(): lax.ppermute(value, 'frame', [(source, source ^ 2) for source in sources])  7.25 us
    ppermute x3, starting transfers between devices, along_mod(): return lax.ppermute(value, ('frame', 'mod'), pairs)  6.93 us
    pallas_call x2, Pallas kernels, order_pixels(): pl.pallas_call(functools.partial(order_kernel, step=step, mods=mods, part...  5.95 us
    ppermute x5, waiting for transfers between devices, other_core(): lax.ppermute(value, 'frame', [(source, source ^ 1) for source in range(co...  2.3 us
  transfers between devices with their start and end apart: 25, of which 13 were waited for; matrix products, arithmetic and copies ran while one was open for 3% of the time, Pallas kernels for 14%

profile of v7, /device:TPU:0, one launch (start us, length us, event | category | flops | bytes accessed | tf_op | source)
XLA Modules:
  0.0 82.8 jit_solution(11872382132992484652)
XLA Ops:
  0.0 0.5 collective-permute-start
  0.5 0.7 compare_select_fusion.label_ref
  1.2 1.2 %shard_map.37 = (f32[256,256]{1,0:T(8,128)S(1)}, f32[16,128]{1,0:T(8,128)S(1)}, bf16[128,4096]{1,0:T(8,128)(2,1)S(1)}) custom-call(s32[4096]{0:T(1024)S(1)} %compare_select_fusion.label_ref, bf16[128,4096]{1,0:T(8,128)(2,1)} %frames_hbm.1), custom_call_target="tpu_custom_call" | custom-call | flops 100663296 | bytes 32768 | tf_op jit(solution)/shard_map/pallas_call | solution.py:101
  2.5 0.1 pad_add_fusion.place_ref
  2.5 0.4 collective-permute-done.rest_1_
  3.0 3.0 %shard_map.38 = (bf16[1024,256]{1,0:T(8,128)(2,1)S(1)}, bf16[512,256]{1,0:T(8,128)(2,1)S(1)}, bf16[512,256]{1,0:T(8,128)(2,1)S(1)}, bf16[256,4096]{1,0:T(8,128)(2,1)S(1)}) custom-call(s32[3]{0:T(128)S(1)} %pad_add_fusion.place_ref, f32[256,256]{1,0:T(8,128)S(1)} %get-tuple-element.128.key_ref, f32[16,128]{1,0:T(8,128)S(1)} %get-tuple-element.221.counts_ref.value_ref, ...), custom_call_target="tpu_custom_call" | custom-call | flops 2147483648 | bytes 2097152 | tf_op jit(solution)/shard_map/pallas_call | solution.py:172
  6.0 1.3 %collective-permute-start.1 = (bf16[1,512,256]{2,1,0:T(8,128)(2,1)S(1)}, bf16[1,512,256]{2,1,0:T(8,128)(2,1)S(1)}, u32[]{:S(2)}, u32[]{:S(2)}) collective-permute-start(bf16[1,512,256]{2,1,0:T(8,128)(2,1)S(1)} %bitcast.26), channel_id=1, source_target_pairs={{8,0},{10,2},{12,4},{14,6},{16,8},{18,10},{20,12},{22,14},{24,16},... | collective-permute-start | bytes 786440 | tf_op jit(solution)/shard_map/ppermute | solution.py:389
  7.3 1.3 %collective-permute-start.5 = (bf16[1024,256]{1,0:T(8,128)(2,1)S(1)}, bf16[1024,256]{1,0:T(8,128)(2,1)S(1)}, u32[]{:S(2)}, u32[]{:S(2)}) collective-permute-start(bf16[1024,256]{1,0:T(8,128)(2,1)S(1)} %get-tuple-element.145), channel_id=1, source_target_pairs={{4,0},{6,2},{12,8},{14,10},{20,16},{22,18},{28,24},{30,26},{5,1},{... | collective-permute-start | bytes 1572872 | tf_op jit(solution)/shard_map/ppermute | solution.py:395
  8.6 2.9 %shard_map.39 = (bf16[1024,256]{1,0:T(8,128)(2,1)S(1)}, bf16[528,256]{1,0:T(8,128)(2,1)S(1)}, bf16[512,256]{1,0:T(8,128)(2,1)S(1)}) custom-call(s32[3]{0:T(128)S(1)} %pad_add_fusion.place_ref, f32[256,256]{1,0:T(8,128)S(1)} %get-tuple-element.128.key_ref, f32[16,128]{1,0:T(8,128)S(1)} %get-tuple-element.221.counts_ref.value_ref, ...), custom_call_target="tpu_custom_call" | custom-call | flops 2147483648 | bytes 2097152 | tf_op jit(solution)/shard_map/pallas_call | solution.py:172
  11.5 1.3 %collective-permute-start.3 = (bf16[1,512,256]{2,1,0:T(8,128)(2,1)S(1)}, bf16[1,512,256]{2,1,0:T(8,128)(2,1)S(1)}, u32[]{:S(2)}, u32[]{:S(2)}) collective-permute-start(bf16[1,512,256]{2,1,0:T(8,128)(2,1)S(1)} %bitcast.20), channel_id=1, source_target_pairs={{8,0},{10,2},{12,4},{14,6},{16,8},{18,10},{20,12},{22,14},{24,16},... | collective-permute-start | bytes 786440 | tf_op jit(solution)/shard_map/ppermute | solution.py:389
  12.8 3.0 %collective-permute-start.6 = (bf16[528,256]{1,0:T(8,128)(2,1)S(1)}, bf16[528,256]{1,0:T(8,128)(2,1)S(1)}, u32[]{:S(2)}, u32[]{:S(2)}) collective-permute-start(bf16[528,256]{1,0:T(8,128)(2,1)S(1)} %get-tuple-element.146), channel_id=1, source_target_pairs={{0,1},{1,0},{2,3},{3,2},{4,5},{5,4},{6,7},{7,6},{8,9},{9,8},{10,11... | collective-permute-start | bytes 811016 | tf_op jit(solution)/shard_map/ppermute | solution.py:411
  15.8 1.7 %collective-permute-done.1.rest_2_ = bf16[1,512,256]{2,1,0:T(8,128)(2,1)S(1)} collective-permute-done((bf16[1,512,256]{2,1,0:T(8,128)(2,1)S(1)}, bf16[1,512,256]{2,1,0:T(8,128)(2,1)S(1)}, u32[]{:S(2)}, u32[]{:S(2)}) %collective-permute-start.1) | collective-permute-done | bytes 262176 | tf_op jit(solution)/shard_map/ppermute | solution.py:389
  17.5 1.3 %collective-permute-start.4 = (bf16[1,512,256]{2,1,0:T(8,128)(2,1)S(1)}, bf16[1,512,256]{2,1,0:T(8,128)(2,1)S(1)}, u32[]{:S(2)}, u32[]{:S(2)}) collective-permute-start(bf16[1,512,256]{2,1,0:T(8,128)(2,1)S(1)} %collective-permute-done.1.rest_2_), channel_id=1, source_target_pairs={{8,0},{10,2},{12,4},{14,6},{16,8},{18,10},{20,12},{22,14},{24,16},... | collective-permute-start | bytes 786440 | tf_op jit(solution)/shard_map/ppermute | solution.py:389
  18.8 1.7 %collective-permute-start.2 = (bf16[1,512,256]{2,1,0:T(8,128)(2,1)S(1)}, bf16[1,512,256]{2,1,0:T(8,128)(2,1)S(1)}, u32[]{:S(2)}, u32[]{:S(2)}) collective-permute-start(bf16[1,512,256]{2,1,0:T(8,128)(2,1)S(1)} %collective-permute-done.1.rest_2_), channel_id=1, source_target_pairs={{0,4},{2,6},{4,0},{6,2},{8,12},{10,14},{12,8},{14,10},{16,20},{18,... | collective-permute-start | bytes 786440 | tf_op jit(solution)/shard_map/ppermute | solution.py:395
  20.5 2.1 %collective-permute-done.6 = bf16[528,256]{1,0:T(8,128)(2,1)S(1)} collective-permute-done((bf16[528,256]{1,0:T(8,128)(2,1)S(1)}, bf16[528,256]{1,0:T(8,128)(2,1)S(1)}, u32[]{:S(2)}, u32[]{:S(2)}) %collective-permute-start.6) | collective-permute-done | bytes 270368 | tf_op jit(solution)/shard_map/ppermute | solution.py:411
  22.6 1.3 %collective-permute-start.8 = (bf16[1,528,256]{2,1,0:T(8,128)(2,1)S(1)}, bf16[1,528,256]{2,1,0:T(8,128)(2,1)S(1)}, u32[]{:S(2)}, u32[]{:S(2)}) collective-permute-start(bf16[1,528,256]{2,1,0:T(8,128)(2,1)S(1)} %bitcast.9), channel_id=1, source_target_pairs={{8,0},{10,2},{12,4},{14,6},{16,8},{18,10},{20,12},{22,14},{24,16},... | collective-permute-start | bytes 811016 | tf_op jit(solution)/shard_map/ppermute | solution.py:389
  23.8 0.3 collective-permute-done.5
  24.2 0.0 collective-permute-done.3.rest_2_
  24.2 2.6 %collective-permute-start.10 = (bf16[1,512,256]{2,1,0:T(8,128)(2,1)S(1)}, bf16[1,512,256]{2,1,0:T(8,128)(2,1)S(1)}, u32[]{:S(2)}, u32[]{:S(2)}) collective-permute-start(bf16[1,512,256]{2,1,0:T(8,128)(2,1)S(1)} %collective-permute-done.3.rest_2_), channel_id=1, source_target_pairs={{0,4},{2,6},{4,0},{6,2},{8,12},{10,14},{12,8},{14,10},{16,20},{18,... | collective-permute-start | bytes 786440 | tf_op jit(solution)/shard_map/ppermute | solution.py:395
  26.8 1.3 %collective-permute-start.9 = (bf16[1,512,256]{2,1,0:T(8,128)(2,1)S(1)}, bf16[1,512,256]{2,1,0:T(8,128)(2,1)S(1)}, u32[]{:S(2)}, u32[]{:S(2)}) collective-permute-start(bf16[1,512,256]{2,1,0:T(8,128)(2,1)S(1)} %collective-permute-done.3.rest_2_), channel_id=1, source_target_pairs={{8,0},{10,2},{12,4},{14,6},{16,8},{18,10},{20,12},{22,14},{24,16},... | collective-permute-start | bytes 786440 | tf_op jit(solution)/shard_map/ppermute | solution.py:389
  28.1 1.6 %collective-permute-done.4.rest_4_ = bf16[1,512,256]{2,1,0:T(8,128)(2,1)S(1)} collective-permute-done((bf16[1,512,256]{2,1,0:T(8,128)(2,1)S(1)}, bf16[1,512,256]{2,1,0:T(8,128)(2,1)S(1)}, u32[]{:S(2)}, u32[]{:S(2)}) %collective-permute-start.4) | collective-permute-done | bytes 262176 | tf_op jit(solution)/shard_map/ppermute | solution.py:389
  29.7 0.1 collective-permute-done.2.rest_6_
  29.8 2.7 %collective-permute-start.7 = (bf16[512,256]{1,0:T(8,128)(2,1)S(1)}, bf16[512,256]{1,0:T(8,128)(2,1)S(1)}, u32[]{:S(2)}, u32[]{:S(2)}) collective-permute-start(bf16[512,256]{1,0:T(8,128)(2,1)S(1)} %get-tuple-element.155), channel_id=1, source_target_pairs={{0,1},{1,0},{2,3},{3,2},{4,5},{5,4},{6,7},{7,6},{8,9},{9,8},{10,11... | collective-permute-start | bytes 786440 | tf_op jit(solution)/shard_map/ppermute | solution.py:411
  32.5 3.9 %collective-permute-start.11 = (bf16[1,512,256]{2,1,0:T(8,128)(2,1)S(1)}, bf16[1,512,256]{2,1,0:T(8,128)(2,1)S(1)}, u32[]{:S(2)}, u32[]{:S(2)}) collective-permute-start(bf16[1,512,256]{2,1,0:T(8,128)(2,1)S(1)} %collective-permute-done.4.rest_4_), channel_id=1, source_target_pairs={{0,4},{2,6},{8,12},{10,14},{16,20},{18,22},{24,28},{26,30},{1,5},{... | collective-permute-start | bytes 786440 | tf_op jit(solution)/shard_map/ppermute | solution.py:395
  36.3 0.0 collective-permute-done.8.rest_3_
  36.3 1.9 %collective-permute-start.15 = (bf16[1,528,256]{2,1,0:T(8,128)(2,1)S(1)}, bf16[1,528,256]{2,1,0:T(8,128)(2,1)S(1)}, u32[]{:S(2)}, u32[]{:S(2)}) collective-permute-start(bf16[1,528,256]{2,1,0:T(8,128)(2,1)S(1)} %collective-permute-done.8.rest_3_), channel_id=1, source_target_pairs={{0,4},{2,6},{4,0},{6,2},{8,12},{10,14},{12,8},{14,10},{16,20},{18,... | collective-permute-start | bytes 811016 | tf_op jit(solution)/shard_map/ppermute | solution.py:395
  38.2 0.0 collective-permute-done.10.rest_6_
  38.2 1.3 %collective-permute-start.14 = (bf16[1,528,256]{2,1,0:T(8,128)(2,1)S(1)}, bf16[1,528,256]{2,1,0:T(8,128)(2,1)S(1)}, u32[]{:S(2)}, u32[]{:S(2)}) collective-permute-start(bf16[1,528,256]{2,1,0:T(8,128)(2,1)S(1)} %collective-permute-done.8.rest_3_), channel_id=1, source_target_pairs={{8,0},{10,2},{12,4},{14,6},{16,8},{18,10},{20,12},{22,14},{24,16},... | collective-permute-start | bytes 811016 | tf_op jit(solution)/shard_map/ppermute | solution.py:389
  39.5 1.1 %collective-permute-done.9.rest_4_ = bf16[1,512,256]{2,1,0:T(8,128)(2,1)S(1)} collective-permute-done((bf16[1,512,256]{2,1,0:T(8,128)(2,1)S(1)}, bf16[1,512,256]{2,1,0:T(8,128)(2,1)S(1)}, u32[]{:S(2)}, u32[]{:S(2)}) %collective-permute-start.9) | collective-permute-done | bytes 262176 | tf_op jit(solution)/shard_map/ppermute | solution.py:389
  40.6 1.3 %collective-permute-start.19 = (bf16[1024,256]{1,0:T(8,128)(2,1)S(1)}, bf16[1024,256]{1,0:T(8,128)(2,1)S(1)}, u32[]{:S(2)}, u32[]{:S(2)}) collective-permute-start(bf16[1024,256]{1,0:T(8,128)(2,1)S(1)} %get-tuple-element.187), channel_id=1, source_target_pairs={{4,1},{5,0},{6,3},{7,2},{12,9},{13,8},{14,11},{15,10},{20,17},{21,... | collective-permute-start | bytes 1572872 | tf_op jit(solution)/shard_map/ppermute | solution.py:411
  41.9 0.0 collective-permute-done.7
  41.9 5.7 %collective-permute-start.13 = (bf16[1,512,256]{2,1,0:T(8,128)(2,1)S(1)}, bf16[1,512,256]{2,1,0:T(8,128)(2,1)S(1)}, u32[]{:S(2)}, u32[]{:S(2)}) collective-permute-start(bf16[1,512,256]{2,1,0:T(8,128)(2,1)S(1)} %collective-permute-done.9.rest_4_), channel_id=1, source_target_pairs={{0,4},{2,6},{8,12},{10,14},{16,20},{18,22},{24,28},{26,30},{1,5},{... | collective-permute-start | bytes 786440 | tf_op jit(solution)/shard_map/ppermute | solution.py:395
  47.6 0.0 collective-permute-done.11.rest_8_
  47.6 1.3 %collective-permute-start.12 = (bf16[1,512,256]{2,1,0:T(8,128)(2,1)S(1)}, bf16[1,512,256]{2,1,0:T(8,128)(2,1)S(1)}, u32[]{:S(2)}, u32[]{:S(2)}) collective-permute-start(bf16[1,512,256]{2,1,0:T(8,128)(2,1)S(1)} %bitcast.23), channel_id=1, source_target_pairs={{8,0},{10,2},{12,4},{14,6},{16,8},{18,10},{20,12},{22,14},{24,16},... | collective-permute-start | bytes 786440 | tf_op jit(solution)/shard_map/ppermute | solution.py:389
  49.0 0.0 collective-permute-done.15.rest_7_
  49.0 0.0 collective-permute-done.14.rest_5_
  49.0 1.7 %collective-permute-start.18 = (bf16[1,528,256]{2,1,0:T(8,128)(2,1)S(1)}, bf16[1,528,256]{2,1,0:T(8,128)(2,1)S(1)}, u32[]{:S(2)}, u32[]{:S(2)}) collective-permute-start(bf16[1,528,256]{2,1,0:T(8,128)(2,1)S(1)} %collective-permute-done.14.rest_5_), channel_id=1, source_target_pairs={{0,4},{2,6},{8,12},{10,14},{16,20},{18,22},{24,28},{26,30},{1,5},{... | collective-permute-start | bytes 811016 | tf_op jit(solution)/shard_map/ppermute | solution.py:395
  50.7 3.6 %collective-permute-done.13.rest_8_ = bf16[1,512,256]{2,1,0:T(8,128)(2,1)S(1)} collective-permute-done((bf16[1,512,256]{2,1,0:T(8,128)(2,1)S(1)}, bf16[1,512,256]{2,1,0:T(8,128)(2,1)S(1)}, u32[]{:S(2)}, u32[]{:S(2)}) %collective-permute-start.13) | collective-permute-done | bytes 262176 | tf_op jit(solution)/shard_map/ppermute | solution.py:395
  54.4 2.1 %collective-permute-done.12.rest_3_ = bf16[1,512,256]{2,1,0:T(8,128)(2,1)S(1)} collective-permute-done((bf16[1,512,256]{2,1,0:T(8,128)(2,1)S(1)}, bf16[1,512,256]{2,1,0:T(8,128)(2,1)S(1)}, u32[]{:S(2)}, u32[]{:S(2)}) %collective-permute-start.12) | collective-permute-done | bytes 262176 | tf_op jit(solution)/shard_map/ppermute | solution.py:389
  56.5 1.3 %collective-permute-start.17 = (bf16[1,512,256]{2,1,0:T(8,128)(2,1)S(1)}, bf16[1,512,256]{2,1,0:T(8,128)(2,1)S(1)}, u32[]{:S(2)}, u32[]{:S(2)}) collective-permute-start(bf16[1,512,256]{2,1,0:T(8,128)(2,1)S(1)} %collective-permute-done.12.rest_3_), channel_id=1, source_target_pairs={{8,0},{10,2},{12,4},{14,6},{16,8},{18,10},{20,12},{22,14},{24,16},... | collective-permute-start | bytes 786440 | tf_op jit(solution)/shard_map/ppermute | solution.py:389
  57.8 0.4 collective-permute-start.16
  58.2 0.0 collective-permute-done.19
  58.2 1.9 %collective-permute-done.18.rest_9_ = bf16[1,528,256]{2,1,0:T(8,128)(2,1)S(1)} collective-permute-done((bf16[1,528,256]{2,1,0:T(8,128)(2,1)S(1)}, bf16[1,528,256]{2,1,0:T(8,128)(2,1)S(1)}, u32[]{:S(2)}, u32[]{:S(2)}) %collective-permute-start.18) | collective-permute-done | bytes 270368 | tf_op jit(solution)/shard_map/ppermute | solution.py:395
  60.2 2.2 %shard_map.46 = (f32[8,128,1024]{2,1,0:T(8,128)S(1)}, f32[2,128,512]{2,1,0:T(8,128)S(1)}) custom-call(s32[3]{0:T(128)S(1)} %pad_add_fusion.place_ref, f32[16,128]{1,0:T(8,128)S(1)} %get-tuple-element.221.counts_ref.value_ref, bf16[1,528,256]{2,1,0:T(8,128)(2,1)S(1)} %bitcast.10, bf16[1,512,256]{2,1,0:T(8,128)(2,1)S(1)} %bitcast.27, ...), custom_call_target="tpu_custom_call" | custom-call | flops 402653184 | bytes 1048576 | tf_op jit(solution)/shard_map/pallas_call | solution.py:309
  62.4 2.3 %collective-permute-done.17.rest_5_ = bf16[1,512,256]{2,1,0:T(8,128)(2,1)S(1)} collective-permute-done((bf16[1,512,256]{2,1,0:T(8,128)(2,1)S(1)}, bf16[1,512,256]{2,1,0:T(8,128)(2,1)S(1)}, u32[]{:S(2)}, u32[]{:S(2)}) %collective-permute-start.17) | collective-permute-done | bytes 262176 | tf_op jit(solution)/shard_map/ppermute | solution.py:389
  64.8 0.0 collective-permute-done.16.rest_7_
  64.8 2.2 %shard_map.47 = (f32[8,128,1024]{2,1,0:T(8,128)S(1)}, f32[2,128,512]{2,1,0:T(8,128)S(1)}) custom-call(s32[3]{0:T(128)S(1)} %pad_add_fusion.place_ref, f32[16,128]{1,0:T(8,128)S(1)} %get-tuple-element.221.counts_ref.value_ref, bf16[1,528,256]{2,1,0:T(8,128)(2,1)S(1)} %bitcast.12, bf16[1,512,256]{2,1,0:T(8,128)(2,1)S(1)} %bitcast.21, ...), custom_call_target="tpu_custom_call", output_to_operand_aliasing={{0}: (11, {})} | custom-call | flops 402653184 | bytes 1048576 | tf_op jit(solution)/shard_map/pallas_call | solution.py:309
  67.0 0.1 collective-permute-start.21
  67.1 0.5 collective-permute-start.20
  67.6 3.4 %collective-permute-start.23 = (bf16[1,512,256]{2,1,0:T(8,128)(2,1)S(1)}, bf16[1,512,256]{2,1,0:T(8,128)(2,1)S(1)}, u32[]{:S(2)}, u32[]{:S(2)}) collective-permute-start(bf16[1,512,256]{2,1,0:T(8,128)(2,1)S(1)} %collective-permute-done.17.rest_5_), channel_id=1, source_target_pairs={{0,4},{2,6},{8,12},{10,14},{16,20},{18,22},{24,28},{26,30},{1,5},{... | collective-permute-start | bytes 786440 | tf_op jit(solution)/shard_map/ppermute | solution.py:395
  71.0 0.0 collective-permute-done.21.rest_11_
  71.0 0.0 collective-permute-done.20.rest_10_
  71.0 2.4 %shard_map.48 = (f32[8,128,1024]{2,1,0:T(8,128)S(1)}, f32[2,128,512]{2,1,0:T(8,128)S(1)}) custom-call(s32[3]{0:T(128)S(1)} %pad_add_fusion.place_ref, f32[16,128]{1,0:T(8,128)S(1)} %get-tuple-element.221.counts_ref.value_ref, bf16[1,528,256]{2,1,0:T(8,128)(2,1)S(1)} %bitcast.13, bf16[1,512,256]{2,1,0:T(8,128)(2,1)S(1)} %bitcast.28, ...), custom_call_target="tpu_custom_call", output_to_operand_aliasing={{0}: (15, {})} | custom-call | flops 402653184 | bytes 1048576 | tf_op jit(solution)/shard_map/pallas_call | solution.py:309
  73.4 0.1 collective-permute-start.22
  73.5 2.0 %copy.10.rest_10_ = f32[8,128,1024]{2,1,0:T(8,128)} copy(f32[8,128,1024]{2,1,0:T(8,128)S(1)} %get-tuple-element.225) | data formatting | bytes 8388608
  75.5 1.3 %collective-permute-done.23.rest_9_ = bf16[1,512,256]{2,1,0:T(8,128)(2,1)S(1)} collective-permute-done((bf16[1,512,256]{2,1,0:T(8,128)(2,1)S(1)}, bf16[1,512,256]{2,1,0:T(8,128)(2,1)S(1)}, u32[]{:S(2)}, u32[]{:S(2)}) %collective-permute-start.23) | collective-permute-done | bytes 262176 | tf_op jit(solution)/shard_map/ppermute | solution.py:395
  76.8 2.5 %shard_map.49 = (f32[8,128,1024]{2,1,0:T(8,128)}, f32[2,128,512]{2,1,0:T(8,128)S(1)}) custom-call(s32[3]{0:T(128)S(1)} %pad_add_fusion.place_ref, f32[16,128]{1,0:T(8,128)S(1)} %get-tuple-element.221.counts_ref.value_ref, bf16[1,528,256]{2,1,0:T(8,128)(2,1)S(1)} %bitcast.15, bf16[1,512,256]{2,1,0:T(8,128)(2,1)S(1)} %bitcast.22, ...), custom_call_target="tpu_custom_call", output_to_operand_aliasing={{0}: (13, {})} | custom-call | flops 402653184 | bytes 1048576 | tf_op jit(solution)/shard_map/pallas_call | solution.py:309
  79.3 0.1 collective-permute-start.24
  79.4 0.0 collective-permute-done.22.rest_0_
  79.4 1.9 %collective-permute-done.24.rest_1_ = f32[2,128,512]{2,1,0:T(8,128)S(1)} collective-permute-done((f32[2,128,512]{2,1,0:T(8,128)S(1)}, f32[2,128,512]{2,1,0:T(8,128)S(1)}, u32[]{:S(2)}, u32[]{:S(2)}) %collective-permute-start.24) | collective-permute-done | bytes 524320 | tf_op jit(solution)/shard_map/ppermute | solution.py:400
  81.3 1.5 %shard_map.50 = f32[8,128,1024]{2,1,0:T(8,128)} custom-call(s32[3]{0:T(128)S(1)} %pad_add_fusion.place_ref, f32[2,128,512]{2,1,0:T(8,128)S(1)} %collective-permute-done.22.rest_0_, f32[2,128,512]{2,1,0:T(8,128)S(1)} %collective-permute-done.24.rest_1_, f32[16,128]{1,0:T(8,128)S(1)} %shard_map.45.rest_2_, ...), custom_call_target="tpu_custom_call", output_to_operand_aliasing={{}: (4, {})} | custom-call | bytes 2097152 | tf_op jit(solution)/shard_map/pallas_call | solution.py:359
  (6 shorter events, 0.0 us)
Async XLA Ops:
  0.0 3.0 %collective-permute-start = (bf16[128,4096]{1,0:T(8,128)(2,1)}, bf16[128,4096]{1,0:T(8,128)(2,1)S(1)}, u32[]{:S(2)}, u32[]{:S(2)}) collective-permute-start(bf16[128,4096]{1,0:T(8,128)(2,1)} %frames_hbm.1), channel_id=1, source_target_pairs={{0,2},{2,0},{4,6},{6,4},{8,10},{10,8},{12,14},{14,12},{16,18},{18,... | collective-permute-start | bytes 3145736 | tf_op jit(solution)/shard_map/ppermute | solution.py:400
  6.0 11.5 %collective-permute-start.1 = (bf16[1,512,256]{2,1,0:T(8,128)(2,1)S(1)}, bf16[1,512,256]{2,1,0:T(8,128)(2,1)S(1)}, u32[]{:S(2)}, u32[]{:S(2)}) collective-permute-start(bf16[1,512,256]{2,1,0:T(8,128)(2,1)S(1)} %bitcast.26), channel_id=1, source_target_pairs={{8,0},{10,2},{12,4},{14,6},{16,8},{18,10},{20,12},{22,14},{24,16},... | collective-permute-start | bytes 786440 | tf_op jit(solution)/shard_map/ppermute | solution.py:389
  7.3 16.8 %collective-permute-start.5 = (bf16[1024,256]{1,0:T(8,128)(2,1)S(1)}, bf16[1024,256]{1,0:T(8,128)(2,1)S(1)}, u32[]{:S(2)}, u32[]{:S(2)}) collective-permute-start(bf16[1024,256]{1,0:T(8,128)(2,1)S(1)} %get-tuple-element.145), channel_id=1, source_target_pairs={{4,0},{6,2},{12,8},{14,10},{20,16},{22,18},{28,24},{30,26},{5,1},{... | collective-permute-start | bytes 1572872 | tf_op jit(solution)/shard_map/ppermute | solution.py:395
  11.5 12.6 %collective-permute-start.3 = (bf16[1,512,256]{2,1,0:T(8,128)(2,1)S(1)}, bf16[1,512,256]{2,1,0:T(8,128)(2,1)S(1)}, u32[]{:S(2)}, u32[]{:S(2)}) collective-permute-start(bf16[1,512,256]{2,1,0:T(8,128)(2,1)S(1)} %bitcast.20), channel_id=1, source_target_pairs={{8,0},{10,2},{12,4},{14,6},{16,8},{18,10},{20,12},{22,14},{24,16},... | collective-permute-start | bytes 786440 | tf_op jit(solution)/shard_map/ppermute | solution.py:389
  12.8 9.7 %collective-permute-start.6 = (bf16[528,256]{1,0:T(8,128)(2,1)S(1)}, bf16[528,256]{1,0:T(8,128)(2,1)S(1)}, u32[]{:S(2)}, u32[]{:S(2)}) collective-permute-start(bf16[528,256]{1,0:T(8,128)(2,1)S(1)} %get-tuple-element.146), channel_id=1, source_target_pairs={{0,1},{1,0},{2,3},{3,2},{4,5},{5,4},{6,7},{7,6},{8,9},{9,8},{10,11... | collective-permute-start | bytes 811016 | tf_op jit(solution)/shard_map/ppermute | solution.py:411
  17.5 12.2 %collective-permute-start.4 = (bf16[1,512,256]{2,1,0:T(8,128)(2,1)S(1)}, bf16[1,512,256]{2,1,0:T(8,128)(2,1)S(1)}, u32[]{:S(2)}, u32[]{:S(2)}) collective-permute-start(bf16[1,512,256]{2,1,0:T(8,128)(2,1)S(1)} %collective-permute-done.1.rest_2_), channel_id=1, source_target_pairs={{8,0},{10,2},{12,4},{14,6},{16,8},{18,10},{20,12},{22,14},{24,16},... | collective-permute-start | bytes 786440 | tf_op jit(solution)/shard_map/ppermute | solution.py:389
  18.8 11.0 %collective-permute-start.2 = (bf16[1,512,256]{2,1,0:T(8,128)(2,1)S(1)}, bf16[1,512,256]{2,1,0:T(8,128)(2,1)S(1)}, u32[]{:S(2)}, u32[]{:S(2)}) collective-permute-start(bf16[1,512,256]{2,1,0:T(8,128)(2,1)S(1)} %collective-permute-done.1.rest_2_), channel_id=1, source_target_pairs={{0,4},{2,6},{4,0},{6,2},{8,12},{10,14},{12,8},{14,10},{16,20},{18,... | collective-permute-start | bytes 786440 | tf_op jit(solution)/shard_map/ppermute | solution.py:395
  22.6 13.8 %collective-permute-start.8 = (bf16[1,528,256]{2,1,0:T(8,128)(2,1)S(1)}, bf16[1,528,256]{2,1,0:T(8,128)(2,1)S(1)}, u32[]{:S(2)}, u32[]{:S(2)}) collective-permute-start(bf16[1,528,256]{2,1,0:T(8,128)(2,1)S(1)} %bitcast.9), channel_id=1, source_target_pairs={{8,0},{10,2},{12,4},{14,6},{16,8},{18,10},{20,12},{22,14},{24,16},... | collective-permute-start | bytes 811016 | tf_op jit(solution)/shard_map/ppermute | solution.py:389
  24.2 14.1 %collective-permute-start.10 = (bf16[1,512,256]{2,1,0:T(8,128)(2,1)S(1)}, bf16[1,512,256]{2,1,0:T(8,128)(2,1)S(1)}, u32[]{:S(2)}, u32[]{:S(2)}) collective-permute-start(bf16[1,512,256]{2,1,0:T(8,128)(2,1)S(1)} %collective-permute-done.3.rest_2_), channel_id=1, source_target_pairs={{0,4},{2,6},{4,0},{6,2},{8,12},{10,14},{12,8},{14,10},{16,20},{18,... | collective-permute-start | bytes 786440 | tf_op jit(solution)/shard_map/ppermute | solution.py:395
  26.8 13.8 %collective-permute-start.9 = (bf16[1,512,256]{2,1,0:T(8,128)(2,1)S(1)}, bf16[1,512,256]{2,1,0:T(8,128)(2,1)S(1)}, u32[]{:S(2)}, u32[]{:S(2)}) collective-permute-start(bf16[1,512,256]{2,1,0:T(8,128)(2,1)S(1)} %collective-permute-done.3.rest_2_), channel_id=1, source_target_pairs={{8,0},{10,2},{12,4},{14,6},{16,8},{18,10},{20,12},{22,14},{24,16},... | collective-permute-start | bytes 786440 | tf_op jit(solution)/shard_map/ppermute | solution.py:389
  29.8 12.1 %collective-permute-start.7 = (bf16[512,256]{1,0:T(8,128)(2,1)S(1)}, bf16[512,256]{1,0:T(8,128)(2,1)S(1)}, u32[]{:S(2)}, u32[]{:S(2)}) collective-permute-start(bf16[512,256]{1,0:T(8,128)(2,1)S(1)} %get-tuple-element.155), channel_id=1, source_target_pairs={{0,1},{1,0},{2,3},{3,2},{4,5},{5,4},{6,7},{7,6},{8,9},{9,8},{10,11... | collective-permute-start | bytes 786440 | tf_op jit(solution)/shard_map/ppermute | solution.py:411
  32.5 15.2 %collective-permute-start.11 = (bf16[1,512,256]{2,1,0:T(8,128)(2,1)S(1)}, bf16[1,512,256]{2,1,0:T(8,128)(2,1)S(1)}, u32[]{:S(2)}, u32[]{:S(2)}) collective-permute-start(bf16[1,512,256]{2,1,0:T(8,128)(2,1)S(1)} %collective-permute-done.4.rest_4_), channel_id=1, source_target_pairs={{0,4},{2,6},{8,12},{10,14},{16,20},{18,22},{24,28},{26,30},{1,5},{... | collective-permute-start | bytes 786440 | tf_op jit(solution)/shard_map/ppermute | solution.py:395
  36.3 12.6 %collective-permute-start.15 = (bf16[1,528,256]{2,1,0:T(8,128)(2,1)S(1)}, bf16[1,528,256]{2,1,0:T(8,128)(2,1)S(1)}, u32[]{:S(2)}, u32[]{:S(2)}) collective-permute-start(bf16[1,528,256]{2,1,0:T(8,128)(2,1)S(1)} %collective-permute-done.8.rest_3_), channel_id=1, source_target_pairs={{0,4},{2,6},{4,0},{6,2},{8,12},{10,14},{12,8},{14,10},{16,20},{18,... | collective-permute-start | bytes 811016 | tf_op jit(solution)/shard_map/ppermute | solution.py:395
  38.2 10.8 %collective-permute-start.14 = (bf16[1,528,256]{2,1,0:T(8,128)(2,1)S(1)}, bf16[1,528,256]{2,1,0:T(8,128)(2,1)S(1)}, u32[]{:S(2)}, u32[]{:S(2)}) collective-permute-start(bf16[1,528,256]{2,1,0:T(8,128)(2,1)S(1)} %collective-permute-done.8.rest_3_), channel_id=1, source_target_pairs={{8,0},{10,2},{12,4},{14,6},{16,8},{18,10},{20,12},{22,14},{24,16},... | collective-permute-start | bytes 811016 | tf_op jit(solution)/shard_map/ppermute | solution.py:389
  40.6 17.6 %collective-permute-start.19 = (bf16[1024,256]{1,0:T(8,128)(2,1)S(1)}, bf16[1024,256]{1,0:T(8,128)(2,1)S(1)}, u32[]{:S(2)}, u32[]{:S(2)}) collective-permute-start(bf16[1024,256]{1,0:T(8,128)(2,1)S(1)} %get-tuple-element.187), channel_id=1, source_target_pairs={{4,1},{5,0},{6,3},{7,2},{12,9},{13,8},{14,11},{15,10},{20,17},{21,... | collective-permute-start | bytes 1572872 | tf_op jit(solution)/shard_map/ppermute | solution.py:411
  41.9 12.4 %collective-permute-start.13 = (bf16[1,512,256]{2,1,0:T(8,128)(2,1)S(1)}, bf16[1,512,256]{2,1,0:T(8,128)(2,1)S(1)}, u32[]{:S(2)}, u32[]{:S(2)}) collective-permute-start(bf16[1,512,256]{2,1,0:T(8,128)(2,1)S(1)} %collective-permute-done.9.rest_4_), channel_id=1, source_target_pairs={{0,4},{2,6},{8,12},{10,14},{16,20},{18,22},{24,28},{26,30},{1,5},{... | collective-permute-start | bytes 786440 | tf_op jit(solution)/shard_map/ppermute | solution.py:395
  47.6 8.8 %collective-permute-start.12 = (bf16[1,512,256]{2,1,0:T(8,128)(2,1)S(1)}, bf16[1,512,256]{2,1,0:T(8,128)(2,1)S(1)}, u32[]{:S(2)}, u32[]{:S(2)}) collective-permute-start(bf16[1,512,256]{2,1,0:T(8,128)(2,1)S(1)} %bitcast.23), channel_id=1, source_target_pairs={{8,0},{10,2},{12,4},{14,6},{16,8},{18,10},{20,12},{22,14},{24,16},... | collective-permute-start | bytes 786440 | tf_op jit(solution)/shard_map/ppermute | solution.py:389
  49.0 11.1 %collective-permute-start.18 = (bf16[1,528,256]{2,1,0:T(8,128)(2,1)S(1)}, bf16[1,528,256]{2,1,0:T(8,128)(2,1)S(1)}, u32[]{:S(2)}, u32[]{:S(2)}) collective-permute-start(bf16[1,528,256]{2,1,0:T(8,128)(2,1)S(1)} %collective-permute-done.14.rest_5_), channel_id=1, source_target_pairs={{0,4},{2,6},{8,12},{10,14},{16,20},{18,22},{24,28},{26,30},{1,5},{... | collective-permute-start | bytes 811016 | tf_op jit(solution)/shard_map/ppermute | solution.py:395
  56.5 8.3 %collective-permute-start.17 = (bf16[1,512,256]{2,1,0:T(8,128)(2,1)S(1)}, bf16[1,512,256]{2,1,0:T(8,128)(2,1)S(1)}, u32[]{:S(2)}, u32[]{:S(2)}) collective-permute-start(bf16[1,512,256]{2,1,0:T(8,128)(2,1)S(1)} %collective-permute-done.12.rest_3_), channel_id=1, source_target_pairs={{8,0},{10,2},{12,4},{14,6},{16,8},{18,10},{20,12},{22,14},{24,16},... | collective-permute-start | bytes 786440 | tf_op jit(solution)/shard_map/ppermute | solution.py:389
  57.8 7.0 %collective-permute-start.16 = (bf16[1,512,256]{2,1,0:T(8,128)(2,1)S(1)}, bf16[1,512,256]{2,1,0:T(8,128)(2,1)S(1)}, u32[]{:S(2)}, u32[]{:S(2)}) collective-permute-start(bf16[1,512,256]{2,1,0:T(8,128)(2,1)S(1)} %collective-permute-done.12.rest_3_), channel_id=1, source_target_pairs={{0,4},{2,6},{4,0},{6,2},{8,12},{10,14},{12,8},{14,10},{16,20},{18,... | collective-permute-start | bytes 786440 | tf_op jit(solution)/shard_map/ppermute | solution.py:395
  67.0 4.0 %collective-permute-start.21 = (f32[2,128,512]{2,1,0:T(8,128)S(1)}, f32[2,128,512]{2,1,0:T(8,128)S(1)}, u32[]{:S(2)}, u32[]{:S(2)}) collective-permute-start(f32[2,128,512]{2,1,0:T(8,128)S(1)} %get-tuple-element.217), channel_id=1, source_target_pairs={{0,2},{2,0},{4,6},{6,4},{8,10},{10,8},{12,14},{14,12},{16,18},{18,... | collective-permute-start | bytes 1572872 | tf_op jit(solution)/shard_map/ppermute | solution.py:400
  67.1 3.9 %collective-permute-start.20 = (f32[2,128,512]{2,1,0:T(8,128)S(1)}, f32[2,128,512]{2,1,0:T(8,128)S(1)}, u32[]{:S(2)}, u32[]{:S(2)}) collective-permute-start(f32[2,128,512]{2,1,0:T(8,128)S(1)} %get-tuple-element.216), channel_id=1, source_target_pairs={{0,2},{2,0},{4,6},{6,4},{8,10},{10,8},{12,14},{14,12},{16,18},{18,... | collective-permute-start | bytes 1572872 | tf_op jit(solution)/shard_map/ppermute | solution.py:400
  67.6 9.2 %collective-permute-start.23 = (bf16[1,512,256]{2,1,0:T(8,128)(2,1)S(1)}, bf16[1,512,256]{2,1,0:T(8,128)(2,1)S(1)}, u32[]{:S(2)}, u32[]{:S(2)}) collective-permute-start(bf16[1,512,256]{2,1,0:T(8,128)(2,1)S(1)} %collective-permute-done.17.rest_5_), channel_id=1, source_target_pairs={{0,4},{2,6},{8,12},{10,14},{16,20},{18,22},{24,28},{26,30},{1,5},{... | collective-permute-start | bytes 786440 | tf_op jit(solution)/shard_map/ppermute | solution.py:395
  73.4 6.0 %collective-permute-start.22 = (f32[2,128,512]{2,1,0:T(8,128)S(1)}, f32[2,128,512]{2,1,0:T(8,128)S(1)}, u32[]{:S(2)}, u32[]{:S(2)}) collective-permute-start(f32[2,128,512]{2,1,0:T(8,128)S(1)} %get-tuple-element.219), channel_id=1, source_target_pairs={{0,2},{2,0},{4,6},{6,4},{8,10},{10,8},{12,14},{14,12},{16,18},{18,... | collective-permute-start | bytes 1572872 | tf_op jit(solution)/shard_map/ppermute | solution.py:400
  79.3 2.0 %collective-permute-start.24 = (f32[2,128,512]{2,1,0:T(8,128)S(1)}, f32[2,128,512]{2,1,0:T(8,128)S(1)}, u32[]{:S(2)}, u32[]{:S(2)}) collective-permute-start(f32[2,128,512]{2,1,0:T(8,128)S(1)} %get-tuple-element.226), channel_id=1, source_target_pairs={{0,2},{2,0},{4,6},{6,4},{8,10},{10,8},{12,14},{14,12},{16,18},{18,... | collective-permute-start | bytes 1572872 | tf_op jit(solution)/shard_map/ppermute | solution.py:400

commit v8 on v7

--- a/solution.py
+++ b/solution.py
@@ -44,9 +44,12 @@
     ("wait", "w2", "v1"),
     ("start", "w3", "x3"),
     ("pause", 300000000),
-    ("wait", "o1", "v2", "g00"),
+    ("wait", "o1", "v2", "g00", "w3"),
     ("start", "v3"),
-    ("wait", "x3", "g01", "g11", "v3", "g10"),
+    ("pause", 0),
+    ("wait", "x3", "g01"),
+    ("pause", 0),
+    ("wait", "g10", "v3", "g11"),
 )
 OWN_SPLIT = True
 
@@ -324,9 +327,7 @@
         ],
         input_output_aliases=aliases,
         compiler_params=params(),
-        cost_estimate=estimate(
-            2 * count * depth * width * chip_block, 4 * count * chip_block * lags
-        ),
+        cost_estimate=estimate(0, 0),
     )(*operands)
 
 
@@ -492,7 +493,7 @@
             choice = (1, 3, 4)
         before = phase * halves + part - 1
         whole = get(f"g{before // halves}{before % halves}")[0] if before >= 0 else None
-        filled = [spot(0, at) for at in range(halves)] if phase and not part else []
+        filled = []
         sizes = (group_cycles, cycle_dev, offsets[part], parts[part])
         return grams(
             place, tied(counts, name), get(f"u{own_units}"), whole, windows, choice, sizes, phase, frame_count, filled
@@ -508,13 +509,17 @@
         for name in filter(known, names):
             value = get(name)
             if step == "wait":
-                if isinstance(value, (list, tuple)):
+                if name[0] == "g":
+                    theirs, token = lax.optimization_barrier((value[1], token))
+                    done[name] = [value[0], theirs]
+                elif isinstance(value, (list, tuple)):
                     head, token = lax.optimization_barrier((value[0], token))
                     done[name] = [head, *value[1:]]
                 else:
                     done[name], token = lax.optimization_barrier((value, token))
     whole = get(f"g1{halves - 1}")[0]
-    return fill(place, token, whole, [spot(1, part) for part in range(halves)])
+    spots = [spot(phase, part) for phase in range(2) for part in range(halves)]
+    return fill(place, token, whole, spots)
 
 
 def solution(mesh):

time: 83.4 us -> 79.9 us (0.958)
  local copies, waits for them, and re-layouts: 2.02 us -> 0 us
  waiting for transfers between devices: 20.6 us -> 18.6 us
  Pallas kernels: 18.1 us -> 19.2 us
    unnamed x1 -> x0, local copies, waits for them, and re-layouts: 2.02 us -> none
    ppermute x9, waiting for transfers between devices: 7.25 us -> 5.97 us  [other_pair(): lax.ppermute(value, 'frame', [(source, source ^ 2) for source in sources])]
    ppermute x9, starting transfers between devices: 22.6 us -> 21.5 us  [other_pair(): lax.ppermute(value, 'frame', [(source, source ^ 2) for source in sources])]
  transfers between devices with their start and end apart: 25 -> 25, of which waited for: 13 -> 12; matrix products, arithmetic and copies ran while one was open for 3% -> 1% of each run, Pallas kernels for 14% -> 18%
where the time goes in v8:
time: 79.9 us; the launch traced here: 79.3 us
  starting transfers between devices  40.3 us (50%)
  Pallas kernels  19.2 us (24%)
  waiting for transfers between devices  18.6 us (23%)
  other arithmetic  0.82 us (1%)
    ppermute x9, starting transfers between devices, other_pair(): lax.ppermute(value, 'frame', [(source, source ^ 2) for source in sources])  21.5 us
    ppermute x8, starting transfers between devices, shifted(): lax.ppermute(value, 'frame', [(source, source - step) for source in range...  10.3 us
    pallas_call x4, Pallas kernels, grams(): pl.pallas_call(kernel, out_shape=[jax.ShapeDtypeStruct((cycle_dev, block,...  10.1 us
    ppermute x8, waiting for transfers between devices, shifted(): lax.ppermute(value, 'frame', [(source, source - step) for source in range...  8.64 us
    ppermute x3, starting transfers between devices, along_mod(): return lax.ppermute(value, ('frame', 'mod'), pairs)  6.93 us
    ppermute x9, waiting for transfers between devices, other_pair(): lax.ppermute(value, 'frame', [(source, source ^ 2) for source in sources])  5.97 us
    pallas_call x2, Pallas kernels, order_pixels(): pl.pallas_call(functools.partial(order_kernel, step=step, mods=mods, part...  5.95 us
    ppermute x3, waiting for transfers between devices, along_mod(): return lax.ppermute(value, ('frame', 'mod'), pairs)  2.09 us
  transfers between devices with their start and end apart: 25, of which 12 were waited for; matrix products, arithmetic and copies ran while one was open for 1% of the time, Pallas kernels for 18%

profile of v8, /device:TPU:0, one launch (start us, length us, event | category | flops | bytes accessed | tf_op | source)
XLA Modules:
  0.0 79.3 jit_solution(18036885492469559125)
XLA Ops:
  0.0 0.5 collective-permute-start
  0.5 0.7 compare_select_fusion.label_ref
  1.2 1.2 %shard_map.37 = (f32[256,256]{1,0:T(8,128)S(1)}, f32[16,128]{1,0:T(8,128)S(1)}, bf16[128,4096]{1,0:T(8,128)(2,1)S(1)}) custom-call(s32[4096]{0:T(1024)S(1)} %compare_select_fusion.label_ref, bf16[128,4096]{1,0:T(8,128)(2,1)} %frames_hbm.1), custom_call_target="tpu_custom_call" | custom-call | flops 100663296 | bytes 32768 | tf_op jit(solution)/shard_map/pallas_call | solution.py:104
  2.5 0.1 pad_add_fusion.place_ref
  2.5 0.4 collective-permute-done.rest_1_
  3.0 3.0 %shard_map.38 = (bf16[1024,256]{1,0:T(8,128)(2,1)S(1)}, bf16[512,256]{1,0:T(8,128)(2,1)S(1)}, bf16[512,256]{1,0:T(8,128)(2,1)S(1)}, bf16[256,4096]{1,0:T(8,128)(2,1)S(1)}) custom-call(s32[3]{0:T(128)S(1)} %pad_add_fusion.place_ref, f32[256,256]{1,0:T(8,128)S(1)} %get-tuple-element.131.key_ref, f32[16,128]{1,0:T(8,128)S(1)} %get-tuple-element.228.counts_ref.value_ref, ...), custom_call_target="tpu_custom_call" | custom-call | flops 2147483648 | bytes 2097152 | tf_op jit(solution)/shard_map/pallas_call | solution.py:175
  6.0 1.3 %collective-permute-start.2 = (bf16[1,512,256]{2,1,0:T(8,128)(2,1)S(1)}, bf16[1,512,256]{2,1,0:T(8,128)(2,1)S(1)}, u32[]{:S(2)}, u32[]{:S(2)}) collective-permute-start(bf16[1,512,256]{2,1,0:T(8,128)(2,1)S(1)} %bitcast.26), channel_id=1, source_target_pairs={{8,0},{10,2},{12,4},{14,6},{16,8},{18,10},{20,12},{22,14},{24,16},... | collective-permute-start | bytes 786440 | tf_op jit(solution)/shard_map/ppermute | solution.py:390
  7.3 1.3 %collective-permute-start.7 = (bf16[1024,256]{1,0:T(8,128)(2,1)S(1)}, bf16[1024,256]{1,0:T(8,128)(2,1)S(1)}, u32[]{:S(2)}, u32[]{:S(2)}) collective-permute-start(bf16[1024,256]{1,0:T(8,128)(2,1)S(1)} %get-tuple-element.151), channel_id=1, source_target_pairs={{4,0},{6,2},{12,8},{14,10},{20,16},{22,18},{28,24},{30,26},{5,1},{... | collective-permute-start | bytes 1572872 | tf_op jit(solution)/shard_map/ppermute | solution.py:396
  8.6 2.9 %shard_map.39 = (bf16[1024,256]{1,0:T(8,128)(2,1)S(1)}, bf16[528,256]{1,0:T(8,128)(2,1)S(1)}, bf16[512,256]{1,0:T(8,128)(2,1)S(1)}) custom-call(s32[3]{0:T(128)S(1)} %pad_add_fusion.place_ref, f32[256,256]{1,0:T(8,128)S(1)} %get-tuple-element.131.key_ref, f32[16,128]{1,0:T(8,128)S(1)} %get-tuple-element.228.counts_ref.value_ref, ...), custom_call_target="tpu_custom_call" | custom-call | flops 2147483648 | bytes 2097152 | tf_op jit(solution)/shard_map/pallas_call | solution.py:175
  11.5 1.3 %collective-permute-start.5 = (bf16[1,512,256]{2,1,0:T(8,128)(2,1)S(1)}, bf16[1,512,256]{2,1,0:T(8,128)(2,1)S(1)}, u32[]{:S(2)}, u32[]{:S(2)}) collective-permute-start(bf16[1,512,256]{2,1,0:T(8,128)(2,1)S(1)} %bitcast.20), channel_id=1, source_target_pairs={{8,0},{10,2},{12,4},{14,6},{16,8},{18,10},{20,12},{22,14},{24,16},... | collective-permute-start | bytes 786440 | tf_op jit(solution)/shard_map/ppermute | solution.py:390
  12.8 3.0 %collective-permute-start.1 = (bf16[528,256]{1,0:T(8,128)(2,1)S(1)}, bf16[528,256]{1,0:T(8,128)(2,1)S(1)}, u32[]{:S(2)}, u32[]{:S(2)}) collective-permute-start(bf16[528,256]{1,0:T(8,128)(2,1)S(1)} %get-tuple-element.135), channel_id=1, source_target_pairs={{0,1},{1,0},{2,3},{3,2},{4,5},{5,4},{6,7},{7,6},{8,9},{9,8},{10,11... | collective-permute-start | bytes 811016 | tf_op jit(solution)/shard_map/ppermute | solution.py:412
  15.8 1.7 %collective-permute-done.2.rest_2_ = bf16[1,512,256]{2,1,0:T(8,128)(2,1)S(1)} collective-permute-done((bf16[1,512,256]{2,1,0:T(8,128)(2,1)S(1)}, bf16[1,512,256]{2,1,0:T(8,128)(2,1)S(1)}, u32[]{:S(2)}, u32[]{:S(2)}) %collective-permute-start.2) | collective-permute-done | bytes 262176 | tf_op jit(solution)/shard_map/ppermute | solution.py:390
  17.5 1.3 %collective-permute-start.6 = (bf16[1,512,256]{2,1,0:T(8,128)(2,1)S(1)}, bf16[1,512,256]{2,1,0:T(8,128)(2,1)S(1)}, u32[]{:S(2)}, u32[]{:S(2)}) collective-permute-start(bf16[1,512,256]{2,1,0:T(8,128)(2,1)S(1)} %collective-permute-done.2.rest_2_), channel_id=1, source_target_pairs={{8,0},{10,2},{12,4},{14,6},{16,8},{18,10},{20,12},{22,14},{24,16},... | collective-permute-start | bytes 786440 | tf_op jit(solution)/shard_map/ppermute | solution.py:390
  18.8 1.7 %collective-permute-start.4 = (bf16[1,512,256]{2,1,0:T(8,128)(2,1)S(1)}, bf16[1,512,256]{2,1,0:T(8,128)(2,1)S(1)}, u32[]{:S(2)}, u32[]{:S(2)}) collective-permute-start(bf16[1,512,256]{2,1,0:T(8,128)(2,1)S(1)} %collective-permute-done.2.rest_2_), channel_id=1, source_target_pairs={{0,4},{2,6},{4,0},{6,2},{8,12},{10,14},{12,8},{14,10},{16,20},{18,... | collective-permute-start | bytes 786440 | tf_op jit(solution)/shard_map/ppermute | solution.py:396
  20.5 2.1 %collective-permute-done.1 = bf16[528,256]{1,0:T(8,128)(2,1)S(1)} collective-permute-done((bf16[528,256]{1,0:T(8,128)(2,1)S(1)}, bf16[528,256]{1,0:T(8,128)(2,1)S(1)}, u32[]{:S(2)}, u32[]{:S(2)}) %collective-permute-start.1) | collective-permute-done | bytes 270368 | tf_op jit(solution)/shard_map/ppermute | solution.py:412
  22.6 1.3 %collective-permute-start.3 = (bf16[1,528,256]{2,1,0:T(8,128)(2,1)S(1)}, bf16[1,528,256]{2,1,0:T(8,128)(2,1)S(1)}, u32[]{:S(2)}, u32[]{:S(2)}) collective-permute-start(bf16[1,528,256]{2,1,0:T(8,128)(2,1)S(1)} %bitcast.9), channel_id=1, source_target_pairs={{8,0},{10,2},{12,4},{14,6},{16,8},{18,10},{20,12},{22,14},{24,16},... | collective-permute-start | bytes 811016 | tf_op jit(solution)/shard_map/ppermute | solution.py:390
  23.8 0.3 collective-permute-done.7
  24.2 0.0 collective-permute-done.5.rest_2_
  24.2 2.6 %collective-permute-start.12 = (bf16[1,512,256]{2,1,0:T(8,128)(2,1)S(1)}, bf16[1,512,256]{2,1,0:T(8,128)(2,1)S(1)}, u32[]{:S(2)}, u32[]{:S(2)}) collective-permute-start(bf16[1,512,256]{2,1,0:T(8,128)(2,1)S(1)} %collective-permute-done.5.rest_2_), channel_id=1, source_target_pairs={{0,4},{2,6},{4,0},{6,2},{8,12},{10,14},{12,8},{14,10},{16,20},{18,... | collective-permute-start | bytes 786440 | tf_op jit(solution)/shard_map/ppermute | solution.py:396
  26.8 1.3 %collective-permute-start.11 = (bf16[1,512,256]{2,1,0:T(8,128)(2,1)S(1)}, bf16[1,512,256]{2,1,0:T(8,128)(2,1)S(1)}, u32[]{:S(2)}, u32[]{:S(2)}) collective-permute-start(bf16[1,512,256]{2,1,0:T(8,128)(2,1)S(1)} %collective-permute-done.5.rest_2_), channel_id=1, source_target_pairs={{8,0},{10,2},{12,4},{14,6},{16,8},{18,10},{20,12},{22,14},{24,16},... | collective-permute-start | bytes 786440 | tf_op jit(solution)/shard_map/ppermute | solution.py:390
  28.1 1.6 %collective-permute-done.6.rest_4_ = bf16[1,512,256]{2,1,0:T(8,128)(2,1)S(1)} collective-permute-done((bf16[1,512,256]{2,1,0:T(8,128)(2,1)S(1)}, bf16[1,512,256]{2,1,0:T(8,128)(2,1)S(1)}, u32[]{:S(2)}, u32[]{:S(2)}) %collective-permute-start.6) | collective-permute-done | bytes 262176 | tf_op jit(solution)/shard_map/ppermute | solution.py:390
  29.7 0.1 collective-permute-done.4.rest_6_
  29.8 2.7 %collective-permute-start.10 = (bf16[512,256]{1,0:T(8,128)(2,1)S(1)}, bf16[512,256]{1,0:T(8,128)(2,1)S(1)}, u32[]{:S(2)}, u32[]{:S(2)}) collective-permute-start(bf16[512,256]{1,0:T(8,128)(2,1)S(1)} %get-tuple-element.164), channel_id=1, source_target_pairs={{0,1},{1,0},{2,3},{3,2},{4,5},{5,4},{6,7},{7,6},{8,9},{9,8},{10,11... | collective-permute-start | bytes 786440 | tf_op jit(solution)/shard_map/ppermute | solution.py:412
  32.5 3.9 %collective-permute-start.13 = (bf16[1,512,256]{2,1,0:T(8,128)(2,1)S(1)}, bf16[1,512,256]{2,1,0:T(8,128)(2,1)S(1)}, u32[]{:S(2)}, u32[]{:S(2)}) collective-permute-start(bf16[1,512,256]{2,1,0:T(8,128)(2,1)S(1)} %collective-permute-done.6.rest_4_), channel_id=1, source_target_pairs={{0,4},{2,6},{8,12},{10,14},{16,20},{18,22},{24,28},{26,30},{1,5},{... | collective-permute-start | bytes 786440 | tf_op jit(solution)/shard_map/ppermute | solution.py:396
  36.3 0.0 collective-permute-done.3.rest_3_
  36.3 1.9 %collective-permute-start.9 = (bf16[1,528,256]{2,1,0:T(8,128)(2,1)S(1)}, bf16[1,528,256]{2,1,0:T(8,128)(2,1)S(1)}, u32[]{:S(2)}, u32[]{:S(2)}) collective-permute-start(bf16[1,528,256]{2,1,0:T(8,128)(2,1)S(1)} %collective-permute-done.3.rest_3_), channel_id=1, source_target_pairs={{0,4},{2,6},{4,0},{6,2},{8,12},{10,14},{12,8},{14,10},{16,20},{18,... | collective-permute-start | bytes 811016 | tf_op jit(solution)/shard_map/ppermute | solution.py:396
  38.2 0.0 collective-permute-done.12.rest_6_
  38.2 1.3 %collective-permute-start.8 = (bf16[1,528,256]{2,1,0:T(8,128)(2,1)S(1)}, bf16[1,528,256]{2,1,0:T(8,128)(2,1)S(1)}, u32[]{:S(2)}, u32[]{:S(2)}) collective-permute-start(bf16[1,528,256]{2,1,0:T(8,128)(2,1)S(1)} %collective-permute-done.3.rest_3_), channel_id=1, source_target_pairs={{8,0},{10,2},{12,4},{14,6},{16,8},{18,10},{20,12},{22,14},{24,16},... | collective-permute-start | bytes 811016 | tf_op jit(solution)/shard_map/ppermute | solution.py:390
  39.5 1.1 %collective-permute-done.11.rest_4_ = bf16[1,512,256]{2,1,0:T(8,128)(2,1)S(1)} collective-permute-done((bf16[1,512,256]{2,1,0:T(8,128)(2,1)S(1)}, bf16[1,512,256]{2,1,0:T(8,128)(2,1)S(1)}, u32[]{:S(2)}, u32[]{:S(2)}) %collective-permute-start.11) | collective-permute-done | bytes 262176 | tf_op jit(solution)/shard_map/ppermute | solution.py:390
  40.6 1.3 %collective-permute-start.15 = (bf16[1024,256]{1,0:T(8,128)(2,1)S(1)}, bf16[1024,256]{1,0:T(8,128)(2,1)S(1)}, u32[]{:S(2)}, u32[]{:S(2)}) collective-permute-start(bf16[1024,256]{1,0:T(8,128)(2,1)S(1)} %get-tuple-element.182), channel_id=1, source_target_pairs={{4,1},{5,0},{6,3},{7,2},{12,9},{13,8},{14,11},{15,10},{20,17},{21,... | collective-permute-start | bytes 1572872 | tf_op jit(solution)/shard_map/ppermute | solution.py:412
  41.9 0.0 collective-permute-done.10
  41.9 5.7 %collective-permute-start.17 = (bf16[1,512,256]{2,1,0:T(8,128)(2,1)S(1)}, bf16[1,512,256]{2,1,0:T(8,128)(2,1)S(1)}, u32[]{:S(2)}, u32[]{:S(2)}) collective-permute-start(bf16[1,512,256]{2,1,0:T(8,128)(2,1)S(1)} %collective-permute-done.11.rest_4_), channel_id=1, source_target_pairs={{0,4},{2,6},{8,12},{10,14},{16,20},{18,22},{24,28},{26,30},{1,5},{... | collective-permute-start | bytes 786440 | tf_op jit(solution)/shard_map/ppermute | solution.py:396
  47.6 0.0 collective-permute-done.13.rest_8_
  47.6 1.3 %collective-permute-start.16 = (bf16[1,512,256]{2,1,0:T(8,128)(2,1)S(1)}, bf16[1,512,256]{2,1,0:T(8,128)(2,1)S(1)}, u32[]{:S(2)}, u32[]{:S(2)}) collective-permute-start(bf16[1,512,256]{2,1,0:T(8,128)(2,1)S(1)} %bitcast.23), channel_id=1, source_target_pairs={{8,0},{10,2},{12,4},{14,6},{16,8},{18,10},{20,12},{22,14},{24,16},... | collective-permute-start | bytes 786440 | tf_op jit(solution)/shard_map/ppermute | solution.py:390
  49.0 0.0 collective-permute-done.9.rest_7_
  49.0 0.0 collective-permute-done.8.rest_5_
  49.0 1.7 %collective-permute-start.14 = (bf16[1,528,256]{2,1,0:T(8,128)(2,1)S(1)}, bf16[1,528,256]{2,1,0:T(8,128)(2,1)S(1)}, u32[]{:S(2)}, u32[]{:S(2)}) collective-permute-start(bf16[1,528,256]{2,1,0:T(8,128)(2,1)S(1)} %collective-permute-done.8.rest_5_), channel_id=1, source_target_pairs={{0,4},{2,6},{8,12},{10,14},{16,20},{18,22},{24,28},{26,30},{1,5},{... | collective-permute-start | bytes 811016 | tf_op jit(solution)/shard_map/ppermute | solution.py:396
  50.7 3.6 %collective-permute-done.17.rest_8_ = bf16[1,512,256]{2,1,0:T(8,128)(2,1)S(1)} collective-permute-done((bf16[1,512,256]{2,1,0:T(8,128)(2,1)S(1)}, bf16[1,512,256]{2,1,0:T(8,128)(2,1)S(1)}, u32[]{:S(2)}, u32[]{:S(2)}) %collective-permute-start.17) | collective-permute-done | bytes 262176 | tf_op jit(solution)/shard_map/ppermute | solution.py:396
  54.4 2.1 %collective-permute-done.16.rest_3_ = bf16[1,512,256]{2,1,0:T(8,128)(2,1)S(1)} collective-permute-done((bf16[1,512,256]{2,1,0:T(8,128)(2,1)S(1)}, bf16[1,512,256]{2,1,0:T(8,128)(2,1)S(1)}, u32[]{:S(2)}, u32[]{:S(2)}) %collective-permute-start.16) | collective-permute-done | bytes 262176 | tf_op jit(solution)/shard_map/ppermute | solution.py:390
  56.5 1.3 %collective-permute-start.20 = (bf16[1,512,256]{2,1,0:T(8,128)(2,1)S(1)}, bf16[1,512,256]{2,1,0:T(8,128)(2,1)S(1)}, u32[]{:S(2)}, u32[]{:S(2)}) collective-permute-start(bf16[1,512,256]{2,1,0:T(8,128)(2,1)S(1)} %collective-permute-done.16.rest_3_), channel_id=1, source_target_pairs={{8,0},{10,2},{12,4},{14,6},{16,8},{18,10},{20,12},{22,14},{24,16},... | collective-permute-start | bytes 786440 | tf_op jit(solution)/shard_map/ppermute | solution.py:390
  57.8 0.4 collective-permute-start.19
  58.2 0.0 collective-permute-done.15
  58.2 1.9 %collective-permute-done.14.rest_9_ = bf16[1,528,256]{2,1,0:T(8,128)(2,1)S(1)} collective-permute-done((bf16[1,528,256]{2,1,0:T(8,128)(2,1)S(1)}, bf16[1,528,256]{2,1,0:T(8,128)(2,1)S(1)}, u32[]{:S(2)}, u32[]{:S(2)}) %collective-permute-start.14) | collective-permute-done | bytes 270368 | tf_op jit(solution)/shard_map/ppermute | solution.py:396
  60.2 2.5 %shard_map.46 = (f32[8,128,1024]{2,1,0:T(8,128)}, f32[2,128,512]{2,1,0:T(8,128)S(1)}) custom-call(s32[3]{0:T(128)S(1)} %pad_add_fusion.place_ref, f32[16,128]{1,0:T(8,128)S(1)} %get-tuple-element.228.counts_ref.value_ref, bf16[1,528,256]{2,1,0:T(8,128)(2,1)S(1)} %bitcast.10, bf16[1,512,256]{2,1,0:T(8,128)(2,1)S(1)} %bitcast.27, ...), custom_call_target="tpu_custom_call" | custom-call | tf_op jit(solution)/shard_map/pallas_call | solution.py:312
  62.7 2.1 %collective-permute-done.20.rest_5_ = bf16[1,512,256]{2,1,0:T(8,128)(2,1)S(1)} collective-permute-done((bf16[1,512,256]{2,1,0:T(8,128)(2,1)S(1)}, bf16[1,512,256]{2,1,0:T(8,128)(2,1)S(1)}, u32[]{:S(2)}, u32[]{:S(2)}) %collective-permute-start.20) | collective-permute-done | bytes 262176 | tf_op jit(solution)/shard_map/ppermute | solution.py:390
  64.8 2.4 %collective-permute-start.23 = (bf16[1,512,256]{2,1,0:T(8,128)(2,1)S(1)}, bf16[1,512,256]{2,1,0:T(8,128)(2,1)S(1)}, u32[]{:S(2)}, u32[]{:S(2)}) collective-permute-start(bf16[1,512,256]{2,1,0:T(8,128)(2,1)S(1)} %collective-permute-done.20.rest_5_), channel_id=1, source_target_pairs={{0,4},{2,6},{8,12},{10,14},{16,20},{18,22},{24,28},{26,30},{1,5},{... | collective-permute-start | bytes 786440 | tf_op jit(solution)/shard_map/ppermute | solution.py:396
  67.1 0.0 collective-permute-done.19.rest_7_
  67.1 2.5 %shard_map.48 = (f32[8,128,1024]{2,1,0:T(8,128)}, f32[2,128,512]{2,1,0:T(8,128)S(1)}) custom-call(s32[3]{0:T(128)S(1)} %pad_add_fusion.place_ref, f32[16,128]{1,0:T(8,128)S(1)} %get-tuple-element.228.counts_ref.value_ref, bf16[1,528,256]{2,1,0:T(8,128)(2,1)S(1)} %bitcast.12, bf16[1,512,256]{2,1,0:T(8,128)(2,1)S(1)} %bitcast.21, ...), custom_call_target="tpu_custom_call", output_to_operand_aliasing={{0}: (11, {})} | custom-call | tf_op jit(solution)/shard_map/pallas_call | solution.py:312
  69.7 2.5 %shard_map.50 = (f32[8,128,1024]{2,1,0:T(8,128)}, f32[2,128,512]{2,1,0:T(8,128)S(1)}) custom-call(s32[3]{0:T(128)S(1)} %pad_add_fusion.place_ref, f32[16,128]{1,0:T(8,128)S(1)} %get-tuple-element.228.counts_ref.value_ref, bf16[1,528,256]{2,1,0:T(8,128)(2,1)S(1)} %bitcast.13, bf16[1,512,256]{2,1,0:T(8,128)(2,1)S(1)} %bitcast.28, ...), custom_call_target="tpu_custom_call", output_to_operand_aliasing={{0}: (13, {})} | custom-call | tf_op jit(solution)/shard_map/pallas_call | solution.py:312
  72.2 0.1 collective-permute-start.22
  72.3 0.5 collective-permute-start.21
  72.8 0.1 collective-permute-start.18
  72.9 0.0 collective-permute-done.23.rest_9_
  72.9 2.5 %shard_map.51 = (f32[8,128,1024]{2,1,0:T(8,128)}, f32[2,128,512]{2,1,0:T(8,128)S(1)}) custom-call(s32[3]{0:T(128)S(1)} %pad_add_fusion.place_ref, f32[16,128]{1,0:T(8,128)S(1)} %get-tuple-element.228.counts_ref.value_ref, bf16[1,528,256]{2,1,0:T(8,128)(2,1)S(1)} %bitcast.15, bf16[1,512,256]{2,1,0:T(8,128)(2,1)S(1)} %bitcast.22, ...), custom_call_target="tpu_custom_call", output_to_operand_aliasing={{0}: (13, {})} | custom-call | tf_op jit(solution)/shard_map/pallas_call | solution.py:312
  75.4 0.5 collective-permute-start.24
  75.9 0.0 collective-permute-done.22.rest_2_
  75.9 0.0 collective-permute-done.21.rest_1_
  75.9 0.0 collective-permute-done.18.rest_0_
  75.9 1.5 %collective-permute-done.24.rest_3_ = f32[2,128,512]{2,1,0:T(8,128)S(1)} collective-permute-done((f32[2,128,512]{2,1,0:T(8,128)S(1)}, f32[2,128,512]{2,1,0:T(8,128)S(1)}, u32[]{:S(2)}, u32[]{:S(2)}) %collective-permute-start.24) | collective-permute-done | bytes 524320 | tf_op jit(solution)/shard_map/ppermute | solution.py:401
  77.4 1.9 %shard_map.52 = f32[8,128,1024]{2,1,0:T(8,128)} custom-call(s32[3]{0:T(128)S(1)} %pad_add_fusion.place_ref, f32[2,128,512]{2,1,0:T(8,128)S(1)} %collective-permute-done.18.rest_0_, f32[2,128,512]{2,1,0:T(8,128)S(1)} %collective-permute-done.21.rest_1_, f32[2,128,512]{2,1,0:T(8,128)S(1)} %collective-permute-done.22.rest_2_, ...), custom_call_target="tpu_custom_call", output_to_operand_aliasing={{}: (6, {})} | custom-call | bytes 4194304 | tf_op jit(solution)/shard_map/pallas_call | solution.py:360
  (8 shorter events, 0.0 us)
Async XLA Ops:
  0.0 3.0 %collective-permute-start = (bf16[128,4096]{1,0:T(8,128)(2,1)}, bf16[128,4096]{1,0:T(8,128)(2,1)S(1)}, u32[]{:S(2)}, u32[]{:S(2)}) collective-permute-start(bf16[128,4096]{1,0:T(8,128)(2,1)} %frames_hbm.1), channel_id=1, source_target_pairs={{0,2},{2,0},{4,6},{6,4},{8,10},{10,8},{12,14},{14,12},{16,18},{18,... | collective-permute-start | bytes 3145736 | tf_op jit(solution)/shard_map/ppermute | solution.py:401
  6.0 11.5 %collective-permute-start.2 = (bf16[1,512,256]{2,1,0:T(8,128)(2,1)S(1)}, bf16[1,512,256]{2,1,0:T(8,128)(2,1)S(1)}, u32[]{:S(2)}, u32[]{:S(2)}) collective-permute-start(bf16[1,512,256]{2,1,0:T(8,128)(2,1)S(1)} %bitcast.26), channel_id=1, source_target_pairs={{8,0},{10,2},{12,4},{14,6},{16,8},{18,10},{20,12},{22,14},{24,16},... | collective-permute-start | bytes 786440 | tf_op jit(solution)/shard_map/ppermute | solution.py:390
  7.3 16.8 %collective-permute-start.7 = (bf16[1024,256]{1,0:T(8,128)(2,1)S(1)}, bf16[1024,256]{1,0:T(8,128)(2,1)S(1)}, u32[]{:S(2)}, u32[]{:S(2)}) collective-permute-start(bf16[1024,256]{1,0:T(8,128)(2,1)S(1)} %get-tuple-element.151), channel_id=1, source_target_pairs={{4,0},{6,2},{12,8},{14,10},{20,16},{22,18},{28,24},{30,26},{5,1},{... | collective-permute-start | bytes 1572872 | tf_op jit(solution)/shard_map/ppermute | solution.py:396
  11.5 12.6 %collective-permute-start.5 = (bf16[1,512,256]{2,1,0:T(8,128)(2,1)S(1)}, bf16[1,512,256]{2,1,0:T(8,128)(2,1)S(1)}, u32[]{:S(2)}, u32[]{:S(2)}) collective-permute-start(bf16[1,512,256]{2,1,0:T(8,128)(2,1)S(1)} %bitcast.20), channel_id=1, source_target_pairs={{8,0},{10,2},{12,4},{14,6},{16,8},{18,10},{20,12},{22,14},{24,16},... | collective-permute-start | bytes 786440 | tf_op jit(solution)/shard_map/ppermute | solution.py:390
  12.8 9.7 %collective-permute-start.1 = (bf16[528,256]{1,0:T(8,128)(2,1)S(1)}, bf16[528,256]{1,0:T(8,128)(2,1)S(1)}, u32[]{:S(2)}, u32[]{:S(2)}) collective-permute-start(bf16[528,256]{1,0:T(8,128)(2,1)S(1)} %get-tuple-element.135), channel_id=1, source_target_pairs={{0,1},{1,0},{2,3},{3,2},{4,5},{5,4},{6,7},{7,6},{8,9},{9,8},{10,11... | collective-permute-start | bytes 811016 | tf_op jit(solution)/shard_map/ppermute | solution.py:412
  17.5 12.2 %collective-permute-start.6 = (bf16[1,512,256]{2,1,0:T(8,128)(2,1)S(1)}, bf16[1,512,256]{2,1,0:T(8,128)(2,1)S(1)}, u32[]{:S(2)}, u32[]{:S(2)}) collective-permute-start(bf16[1,512,256]{2,1,0:T(8,128)(2,1)S(1)} %collective-permute-done.2.rest_2_), channel_id=1, source_target_pairs={{8,0},{10,2},{12,4},{14,6},{16,8},{18,10},{20,12},{22,14},{24,16},... | collective-permute-start | bytes 786440 | tf_op jit(solution)/shard_map/ppermute | solution.py:390
  18.8 11.0 %collective-permute-start.4 = (bf16[1,512,256]{2,1,0:T(8,128)(2,1)S(1)}, bf16[1,512,256]{2,1,0:T(8,128)(2,1)S(1)}, u32[]{:S(2)}, u32[]{:S(2)}) collective-permute-start(bf16[1,512,256]{2,1,0:T(8,128)(2,1)S(1)} %collective-permute-done.2.rest_2_), channel_id=1, source_target_pairs={{0,4},{2,6},{4,0},{6,2},{8,12},{10,14},{12,8},{14,10},{16,20},{18,... | collective-permute-start | bytes 786440 | tf_op jit(solution)/shard_map/ppermute | solution.py:396
  22.6 13.8 %collective-permute-start.3 = (bf16[1,528,256]{2,1,0:T(8,128)(2,1)S(1)}, bf16[1,528,256]{2,1,0:T(8,128)(2,1)S(1)}, u32[]{:S(2)}, u32[]{:S(2)}) collective-permute-start(bf16[1,528,256]{2,1,0:T(8,128)(2,1)S(1)} %bitcast.9), channel_id=1, source_target_pairs={{8,0},{10,2},{12,4},{14,6},{16,8},{18,10},{20,12},{22,14},{24,16},... | collective-permute-start | bytes 811016 | tf_op jit(solution)/shard_map/ppermute | solution.py:390
  24.2 14.1 %collective-permute-start.12 = (bf16[1,512,256]{2,1,0:T(8,128)(2,1)S(1)}, bf16[1,512,256]{2,1,0:T(8,128)(2,1)S(1)}, u32[]{:S(2)}, u32[]{:S(2)}) collective-permute-start(bf16[1,512,256]{2,1,0:T(8,128)(2,1)S(1)} %collective-permute-done.5.rest_2_), channel_id=1, source_target_pairs={{0,4},{2,6},{4,0},{6,2},{8,12},{10,14},{12,8},{14,10},{16,20},{18,... | collective-permute-start | bytes 786440 | tf_op jit(solution)/shard_map/ppermute | solution.py:396
  26.8 13.8 %collective-permute-start.11 = (bf16[1,512,256]{2,1,0:T(8,128)(2,1)S(1)}, bf16[1,512,256]{2,1,0:T(8,128)(2,1)S(1)}, u32[]{:S(2)}, u32[]{:S(2)}) collective-permute-start(bf16[1,512,256]{2,1,0:T(8,128)(2,1)S(1)} %collective-permute-done.5.rest_2_), channel_id=1, source_target_pairs={{8,0},{10,2},{12,4},{14,6},{16,8},{18,10},{20,12},{22,14},{24,16},... | collective-permute-start | bytes 786440 | tf_op jit(solution)/shard_map/ppermute | solution.py:390
  29.8 12.1 %collective-permute-start.10 = (bf16[512,256]{1,0:T(8,128)(2,1)S(1)}, bf16[512,256]{1,0:T(8,128)(2,1)S(1)}, u32[]{:S(2)}, u32[]{:S(2)}) collective-permute-start(bf16[512,256]{1,0:T(8,128)(2,1)S(1)} %get-tuple-element.164), channel_id=1, source_target_pairs={{0,1},{1,0},{2,3},{3,2},{4,5},{5,4},{6,7},{7,6},{8,9},{9,8},{10,11... | collective-permute-start | bytes 786440 | tf_op jit(solution)/shard_map/ppermute | solution.py:412
  32.5 15.2 %collective-permute-start.13 = (bf16[1,512,256]{2,1,0:T(8,128)(2,1)S(1)}, bf16[1,512,256]{2,1,0:T(8,128)(2,1)S(1)}, u32[]{:S(2)}, u32[]{:S(2)}) collective-permute-start(bf16[1,512,256]{2,1,0:T(8,128)(2,1)S(1)} %collective-permute-done.6.rest_4_), channel_id=1, source_target_pairs={{0,4},{2,6},{8,12},{10,14},{16,20},{18,22},{24,28},{26,30},{1,5},{... | collective-permute-start | bytes 786440 | tf_op jit(solution)/shard_map/ppermute | solution.py:396
  36.3 12.6 %collective-permute-start.9 = (bf16[1,528,256]{2,1,0:T(8,128)(2,1)S(1)}, bf16[1,528,256]{2,1,0:T(8,128)(2,1)S(1)}, u32[]{:S(2)}, u32[]{:S(2)}) collective-permute-start(bf16[1,528,256]{2,1,0:T(8,128)(2,1)S(1)} %collective-permute-done.3.rest_3_), channel_id=1, source_target_pairs={{0,4},{2,6},{4,0},{6,2},{8,12},{10,14},{12,8},{14,10},{16,20},{18,... | collective-permute-start | bytes 811016 | tf_op jit(solution)/shard_map/ppermute | solution.py:396
  38.2 10.8 %collective-permute-start.8 = (bf16[1,528,256]{2,1,0:T(8,128)(2,1)S(1)}, bf16[1,528,256]{2,1,0:T(8,128)(2,1)S(1)}, u32[]{:S(2)}, u32[]{:S(2)}) collective-permute-start(bf16[1,528,256]{2,1,0:T(8,128)(2,1)S(1)} %collective-permute-done.3.rest_3_), channel_id=1, source_target_pairs={{8,0},{10,2},{12,4},{14,6},{16,8},{18,10},{20,12},{22,14},{24,16},... | collective-permute-start | bytes 811016 | tf_op jit(solution)/shard_map/ppermute | solution.py:390
  40.6 17.6 %collective-permute-start.15 = (bf16[1024,256]{1,0:T(8,128)(2,1)S(1)}, bf16[1024,256]{1,0:T(8,128)(2,1)S(1)}, u32[]{:S(2)}, u32[]{:S(2)}) collective-permute-start(bf16[1024,256]{1,0:T(8,128)(2,1)S(1)} %get-tuple-element.182), channel_id=1, source_target_pairs={{4,1},{5,0},{6,3},{7,2},{12,9},{13,8},{14,11},{15,10},{20,17},{21,... | collective-permute-start | bytes 1572872 | tf_op jit(solution)/shard_map/ppermute | solution.py:412
  41.9 12.4 %collective-permute-start.17 = (bf16[1,512,256]{2,1,0:T(8,128)(2,1)S(1)}, bf16[1,512,256]{2,1,0:T(8,128)(2,1)S(1)}, u32[]{:S(2)}, u32[]{:S(2)}) collective-permute-start(bf16[1,512,256]{2,1,0:T(8,128)(2,1)S(1)} %collective-permute-done.11.rest_4_), channel_id=1, source_target_pairs={{0,4},{2,6},{8,12},{10,14},{16,20},{18,22},{24,28},{26,30},{1,5},{... | collective-permute-start | bytes 786440 | tf_op jit(solution)/shard_map/ppermute | solution.py:396
  47.6 8.8 %collective-permute-start.16 = (bf16[1,512,256]{2,1,0:T(8,128)(2,1)S(1)}, bf16[1,512,256]{2,1,0:T(8,128)(2,1)S(1)}, u32[]{:S(2)}, u32[]{:S(2)}) collective-permute-start(bf16[1,512,256]{2,1,0:T(8,128)(2,1)S(1)} %bitcast.23), channel_id=1, source_target_pairs={{8,0},{10,2},{12,4},{14,6},{16,8},{18,10},{20,12},{22,14},{24,16},... | collective-permute-start | bytes 786440 | tf_op jit(solution)/shard_map/ppermute | solution.py:390
  49.0 11.1 %collective-permute-start.14 = (bf16[1,528,256]{2,1,0:T(8,128)(2,1)S(1)}, bf16[1,528,256]{2,1,0:T(8,128)(2,1)S(1)}, u32[]{:S(2)}, u32[]{:S(2)}) collective-permute-start(bf16[1,528,256]{2,1,0:T(8,128)(2,1)S(1)} %collective-permute-done.8.rest_5_), channel_id=1, source_target_pairs={{0,4},{2,6},{8,12},{10,14},{16,20},{18,22},{24,28},{26,30},{1,5},{... | collective-permute-start | bytes 811016 | tf_op jit(solution)/shard_map/ppermute | solution.py:396
  56.5 8.3 %collective-permute-start.20 = (bf16[1,512,256]{2,1,0:T(8,128)(2,1)S(1)}, bf16[1,512,256]{2,1,0:T(8,128)(2,1)S(1)}, u32[]{:S(2)}, u32[]{:S(2)}) collective-permute-start(bf16[1,512,256]{2,1,0:T(8,128)(2,1)S(1)} %collective-permute-done.16.rest_3_), channel_id=1, source_target_pairs={{8,0},{10,2},{12,4},{14,6},{16,8},{18,10},{20,12},{22,14},{24,16},... | collective-permute-start | bytes 786440 | tf_op jit(solution)/shard_map/ppermute | solution.py:390
  57.8 9.3 %collective-permute-start.19 = (bf16[1,512,256]{2,1,0:T(8,128)(2,1)S(1)}, bf16[1,512,256]{2,1,0:T(8,128)(2,1)S(1)}, u32[]{:S(2)}, u32[]{:S(2)}) collective-permute-start(bf16[1,512,256]{2,1,0:T(8,128)(2,1)S(1)} %collective-permute-done.16.rest_3_), channel_id=1, source_target_pairs={{0,4},{2,6},{4,0},{6,2},{8,12},{10,14},{12,8},{14,10},{16,20},{18,... | collective-permute-start | bytes 786440 | tf_op jit(solution)/shard_map/ppermute | solution.py:396
  64.8 8.1 %collective-permute-start.23 = (bf16[1,512,256]{2,1,0:T(8,128)(2,1)S(1)}, bf16[1,512,256]{2,1,0:T(8,128)(2,1)S(1)}, u32[]{:S(2)}, u32[]{:S(2)}) collective-permute-start(bf16[1,512,256]{2,1,0:T(8,128)(2,1)S(1)} %collective-permute-done.20.rest_5_), channel_id=1, source_target_pairs={{0,4},{2,6},{8,12},{10,14},{16,20},{18,22},{24,28},{26,30},{1,5},{... | collective-permute-start | bytes 786440 | tf_op jit(solution)/shard_map/ppermute | solution.py:396
  72.2 3.7 %collective-permute-start.22 = (f32[2,128,512]{2,1,0:T(8,128)S(1)}, f32[2,128,512]{2,1,0:T(8,128)S(1)}, u32[]{:S(2)}, u32[]{:S(2)}) collective-permute-start(f32[2,128,512]{2,1,0:T(8,128)S(1)} %get-tuple-element.224), channel_id=1, source_target_pairs={{0,2},{2,0},{4,6},{6,4},{8,10},{10,8},{12,14},{14,12},{16,18},{18,... | collective-permute-start | bytes 1572872 | tf_op jit(solution)/shard_map/ppermute | solution.py:401
  72.3 3.6 %collective-permute-start.21 = (f32[2,128,512]{2,1,0:T(8,128)S(1)}, f32[2,128,512]{2,1,0:T(8,128)S(1)}, u32[]{:S(2)}, u32[]{:S(2)}) collective-permute-start(f32[2,128,512]{2,1,0:T(8,128)S(1)} %get-tuple-element.214), channel_id=1, source_target_pairs={{0,2},{2,0},{4,6},{6,4},{8,10},{10,8},{12,14},{14,12},{16,18},{18,... | collective-permute-start | bytes 1572872 | tf_op jit(solution)/shard_map/ppermute | solution.py:401
  72.8 3.1 %collective-permute-start.18 = (f32[2,128,512]{2,1,0:T(8,128)S(1)}, f32[2,128,512]{2,1,0:T(8,128)S(1)}, u32[]{:S(2)}, u32[]{:S(2)}) collective-permute-start(f32[2,128,512]{2,1,0:T(8,128)S(1)} %get-tuple-element.201), channel_id=1, source_target_pairs={{0,2},{2,0},{4,6},{6,4},{8,10},{10,8},{12,14},{14,12},{16,18},{18,... | collective-permute-start | bytes 1572872 | tf_op jit(solution)/shard_map/ppermute | solution.py:401
  75.4 2.0 %collective-permute-start.24 = (f32[2,128,512]{2,1,0:T(8,128)S(1)}, f32[2,128,512]{2,1,0:T(8,128)S(1)}, u32[]{:S(2)}, u32[]{:S(2)}) collective-permute-start(f32[2,128,512]{2,1,0:T(8,128)S(1)} %get-tuple-element.236), channel_id=1, source_target_pairs={{0,2},{2,0},{4,6},{6,4},{8,10},{10,8},{12,14},{14,12},{16,18},{18,... | collective-permute-start | bytes 1572872 | tf_op jit(solution)/shard_map/ppermute | solution.py:401

commit v9 on v8

--- a/solution.py
+++ b/solution.py
@@ -200,6 +200,10 @@
     per_cycle = CHUNK
     lane, sublane = iota((SUBLANES, LANES), 1), iota((SUBLANES, LANES), 0)
     tiles = lags // LANES
+    skews = [
+        (lane + sublane < LANES - first, (lane + sublane + first) & (LANES - 1))
+        for first in range(0, block, SUBLANES)
+    ]
     stores = []
     for cycle in range(count):
 
@@ -250,8 +254,7 @@
                 results = []
                 for first in range(batch, batch + BATCH, SUBLANES):
                     factor = earlier[cycle, pl.ds(base + first, SUBLANES), :]
-                    kept = lane + sublane < LANES - first
-                    turned = lax.rem(lane + sublane + first, LANES)
+                    kept, turned = skews[first // SUBLANES]
                     rolled = []
                     for tile in range(tiles + 1):
                         column = pl.multiple_of(base + tile * LANES, LANES)
@@ -519,7 +522,8 @@
                     done[name], token = lax.optimization_barrier((value, token))
     whole = get(f"g1{halves - 1}")[0]
     spots = [spot(phase, part) for phase in range(2) for part in range(halves)]
-    return fill(place, token, whole, spots)
+    whole = fill(place, token, whole, spots[:-1])
+    return fill(place, token, whole, spots[-1:])
 
 
 def solution(mesh):

time: 79.9 us -> 79.5 us (level)
  waiting for transfers between devices: 18.6 us -> 17.1 us
  Pallas kernels: 19.2 us -> 20.4 us
    ppermute x5, waiting for transfers between devices: 1.94 us -> 0.42 us  [other_core(): lax.ppermute(value, 'frame', [(source, source ^ 1) for source in range(co...]
    pallas_call x1 -> x2, Pallas kernels: 1.89 us -> 3.06 us  [fill(): pl.pallas_call(functools.partial(fill_kernel, spots=spots), out_shape=jax...]
  transfers between devices with their start and end apart: 25 -> 25, of which waited for: 12 -> 11; matrix products, arithmetic and copies ran while one was open for 1% -> 1% of each run, Pallas kernels for 18% -> 20%
where the time goes in v9:
time: 79.5 us; the launch traced here: 79 us
  starting transfers between devices  40.3 us (51%)
  Pallas kernels  20.4 us (26%)
  waiting for transfers between devices  17.1 us (22%)
  other arithmetic  0.82 us (1%)
    ppermute x9, starting transfers between devices, other_pair(): lax.ppermute(value, 'frame', [(source, source ^ 2) for source in sources])  21.5 us
    ppermute x8, starting transfers between devices, shifted(): lax.ppermute(value, 'frame', [(source, source - step) for source in range...  10.3 us
    pallas_call x4, Pallas kernels, grams(): pl.pallas_call(kernel, out_shape=[jax.ShapeDtypeStruct((cycle_dev, block,...  10.1 us
    ppermute x8, waiting for transfers between devices, shifted(): lax.ppermute(value, 'frame', [(source, source - step) for source in range...  8.64 us
    ppermute x3, starting transfers between devices, along_mod(): return lax.ppermute(value, ('frame', 'mod'), pairs)  6.93 us
    ppermute x9, waiting for transfers between devices, other_pair(): lax.ppermute(value, 'frame', [(source, source ^ 2) for source in sources])  5.97 us
    pallas_call x2, Pallas kernels, order_pixels(): pl.pallas_call(functools.partial(order_kernel, step=step, mods=mods, part...  5.95 us
    pallas_call x2, Pallas kernels, fill(): pl.pallas_call(functools.partial(fill_kernel, spots=spots), out_shape=jax...  3.06 us
  transfers between devices with their start and end apart: 25, of which 11 were waited for; matrix products, arithmetic and copies ran while one was open for 1% of the time, Pallas kernels for 20%

profile of v9, /device:TPU:0, one launch (start us, length us, event | category | flops | bytes accessed | tf_op | source)
XLA Modules:
  0.0 79.0 jit_solution(10250454939849116733)
XLA Ops:
  0.0 0.5 collective-permute-start
  0.5 0.7 compare_select_fusion.label_ref
  1.2 1.2 %shard_map.37 = (f32[256,256]{1,0:T(8,128)S(1)}, f32[16,128]{1,0:T(8,128)S(1)}, bf16[128,4096]{1,0:T(8,128)(2,1)S(1)}) custom-call(s32[4096]{0:T(1024)S(1)} %compare_select_fusion.label_ref, bf16[128,4096]{1,0:T(8,128)(2,1)} %frames_hbm.1), custom_call_target="tpu_custom_call" | custom-call | flops 100663296 | bytes 32768 | tf_op jit(solution)/shard_map/pallas_call | solution.py:104
  2.5 0.1 pad_add_fusion.place_ref
  2.5 0.4 collective-permute-done.rest_1_
  3.0 3.0 %shard_map.38 = (bf16[1024,256]{1,0:T(8,128)(2,1)S(1)}, bf16[512,256]{1,0:T(8,128)(2,1)S(1)}, bf16[512,256]{1,0:T(8,128)(2,1)S(1)}, bf16[256,4096]{1,0:T(8,128)(2,1)S(1)}) custom-call(s32[3]{0:T(128)S(1)} %pad_add_fusion.place_ref, f32[256,256]{1,0:T(8,128)S(1)} %get-tuple-element.131.key_ref, f32[16,128]{1,0:T(8,128)S(1)} %get-tuple-element.225.counts_ref.value_ref, ...), custom_call_target="tpu_custom_call" | custom-call | flops 2147483648 | bytes 2097152 | tf_op jit(solution)/shard_map/pallas_call | solution.py:175
  6.0 1.3 %collective-permute-start.1 = (bf16[1,512,256]{2,1,0:T(8,128)(2,1)S(1)}, bf16[1,512,256]{2,1,0:T(8,128)(2,1)S(1)}, u32[]{:S(2)}, u32[]{:S(2)}) collective-permute-start(bf16[1,512,256]{2,1,0:T(8,128)(2,1)S(1)} %bitcast.26), channel_id=1, source_target_pairs={{8,0},{10,2},{12,4},{14,6},{16,8},{18,10},{20,12},{22,14},{24,16},... | collective-permute-start | bytes 786440 | tf_op jit(solution)/shard_map/ppermute | solution.py:393
  7.3 1.3 %collective-permute-start.5 = (bf16[1024,256]{1,0:T(8,128)(2,1)S(1)}, bf16[1024,256]{1,0:T(8,128)(2,1)S(1)}, u32[]{:S(2)}, u32[]{:S(2)}) collective-permute-start(bf16[1024,256]{1,0:T(8,128)(2,1)S(1)} %get-tuple-element.148), channel_id=1, source_target_pairs={{4,0},{6,2},{12,8},{14,10},{20,16},{22,18},{28,24},{30,26},{5,1},{... | collective-permute-start | bytes 1572872 | tf_op jit(solution)/shard_map/ppermute | solution.py:399
  8.6 2.9 %shard_map.39 = (bf16[1024,256]{1,0:T(8,128)(2,1)S(1)}, bf16[528,256]{1,0:T(8,128)(2,1)S(1)}, bf16[512,256]{1,0:T(8,128)(2,1)S(1)}) custom-call(s32[3]{0:T(128)S(1)} %pad_add_fusion.place_ref, f32[256,256]{1,0:T(8,128)S(1)} %get-tuple-element.131.key_ref, f32[16,128]{1,0:T(8,128)S(1)} %get-tuple-element.225.counts_ref.value_ref, ...), custom_call_target="tpu_custom_call" | custom-call | flops 2147483648 | bytes 2097152 | tf_op jit(solution)/shard_map/pallas_call | solution.py:175
  11.5 1.3 %collective-permute-start.3 = (bf16[1,512,256]{2,1,0:T(8,128)(2,1)S(1)}, bf16[1,512,256]{2,1,0:T(8,128)(2,1)S(1)}, u32[]{:S(2)}, u32[]{:S(2)}) collective-permute-start(bf16[1,512,256]{2,1,0:T(8,128)(2,1)S(1)} %bitcast.20), channel_id=1, source_target_pairs={{8,0},{10,2},{12,4},{14,6},{16,8},{18,10},{20,12},{22,14},{24,16},... | collective-permute-start | bytes 786440 | tf_op jit(solution)/shard_map/ppermute | solution.py:393
  12.8 3.0 %collective-permute-start.6 = (bf16[528,256]{1,0:T(8,128)(2,1)S(1)}, bf16[528,256]{1,0:T(8,128)(2,1)S(1)}, u32[]{:S(2)}, u32[]{:S(2)}) collective-permute-start(bf16[528,256]{1,0:T(8,128)(2,1)S(1)} %get-tuple-element.149), channel_id=1, source_target_pairs={{0,1},{1,0},{2,3},{3,2},{4,5},{5,4},{6,7},{7,6},{8,9},{9,8},{10,11... | collective-permute-start | bytes 811016 | tf_op jit(solution)/shard_map/ppermute | solution.py:415
  15.8 1.7 %collective-permute-done.1.rest_2_ = bf16[1,512,256]{2,1,0:T(8,128)(2,1)S(1)} collective-permute-done((bf16[1,512,256]{2,1,0:T(8,128)(2,1)S(1)}, bf16[1,512,256]{2,1,0:T(8,128)(2,1)S(1)}, u32[]{:S(2)}, u32[]{:S(2)}) %collective-permute-start.1) | collective-permute-done | bytes 262176 | tf_op jit(solution)/shard_map/ppermute | solution.py:393
  17.5 1.3 %collective-permute-start.4 = (bf16[1,512,256]{2,1,0:T(8,128)(2,1)S(1)}, bf16[1,512,256]{2,1,0:T(8,128)(2,1)S(1)}, u32[]{:S(2)}, u32[]{:S(2)}) collective-permute-start(bf16[1,512,256]{2,1,0:T(8,128)(2,1)S(1)} %collective-permute-done.1.rest_2_), channel_id=1, source_target_pairs={{8,0},{10,2},{12,4},{14,6},{16,8},{18,10},{20,12},{22,14},{24,16},... | collective-permute-start | bytes 786440 | tf_op jit(solution)/shard_map/ppermute | solution.py:393
  18.8 1.7 %collective-permute-start.2 = (bf16[1,512,256]{2,1,0:T(8,128)(2,1)S(1)}, bf16[1,512,256]{2,1,0:T(8,128)(2,1)S(1)}, u32[]{:S(2)}, u32[]{:S(2)}) collective-permute-start(bf16[1,512,256]{2,1,0:T(8,128)(2,1)S(1)} %collective-permute-done.1.rest_2_), channel_id=1, source_target_pairs={{0,4},{2,6},{4,0},{6,2},{8,12},{10,14},{12,8},{14,10},{16,20},{18,... | collective-permute-start | bytes 786440 | tf_op jit(solution)/shard_map/ppermute | solution.py:399
  20.5 2.1 %collective-permute-done.6 = bf16[528,256]{1,0:T(8,128)(2,1)S(1)} collective-permute-done((bf16[528,256]{1,0:T(8,128)(2,1)S(1)}, bf16[528,256]{1,0:T(8,128)(2,1)S(1)}, u32[]{:S(2)}, u32[]{:S(2)}) %collective-permute-start.6) | collective-permute-done | bytes 270368 | tf_op jit(solution)/shard_map/ppermute | solution.py:415
  22.6 1.3 %collective-permute-start.8 = (bf16[1,528,256]{2,1,0:T(8,128)(2,1)S(1)}, bf16[1,528,256]{2,1,0:T(8,128)(2,1)S(1)}, u32[]{:S(2)}, u32[]{:S(2)}) collective-permute-start(bf16[1,528,256]{2,1,0:T(8,128)(2,1)S(1)} %bitcast.9), channel_id=1, source_target_pairs={{8,0},{10,2},{12,4},{14,6},{16,8},{18,10},{20,12},{22,14},{24,16},... | collective-permute-start | bytes 811016 | tf_op jit(solution)/shard_map/ppermute | solution.py:393
  23.8 0.3 collective-permute-done.5
  24.2 0.0 collective-permute-done.3.rest_2_
  24.2 2.6 %collective-permute-start.10 = (bf16[1,512,256]{2,1,0:T(8,128)(2,1)S(1)}, bf16[1,512,256]{2,1,0:T(8,128)(2,1)S(1)}, u32[]{:S(2)}, u32[]{:S(2)}) collective-permute-start(bf16[1,512,256]{2,1,0:T(8,128)(2,1)S(1)} %collective-permute-done.3.rest_2_), channel_id=1, source_target_pairs={{0,4},{2,6},{4,0},{6,2},{8,12},{10,14},{12,8},{14,10},{16,20},{18,... | collective-permute-start | bytes 786440 | tf_op jit(solution)/shard_map/ppermute | solution.py:399
  26.8 1.3 %collective-permute-start.9 = (bf16[1,512,256]{2,1,0:T(8,128)(2,1)S(1)}, bf16[1,512,256]{2,1,0:T(8,128)(2,1)S(1)}, u32[]{:S(2)}, u32[]{:S(2)}) collective-permute-start(bf16[1,512,256]{2,1,0:T(8,128)(2,1)S(1)} %collective-permute-done.3.rest_2_), channel_id=1, source_target_pairs={{8,0},{10,2},{12,4},{14,6},{16,8},{18,10},{20,12},{22,14},{24,16},... | collective-permute-start | bytes 786440 | tf_op jit(solution)/shard_map/ppermute | solution.py:393
  28.1 1.6 %collective-permute-done.4.rest_4_ = bf16[1,512,256]{2,1,0:T(8,128)(2,1)S(1)} collective-permute-done((bf16[1,512,256]{2,1,0:T(8,128)(2,1)S(1)}, bf16[1,512,256]{2,1,0:T(8,128)(2,1)S(1)}, u32[]{:S(2)}, u32[]{:S(2)}) %collective-permute-start.4) | collective-permute-done | bytes 262176 | tf_op jit(solution)/shard_map/ppermute | solution.py:393
  29.7 0.1 collective-permute-done.2.rest_6_
  29.8 2.7 %collective-permute-start.7 = (bf16[512,256]{1,0:T(8,128)(2,1)S(1)}, bf16[512,256]{1,0:T(8,128)(2,1)S(1)}, u32[]{:S(2)}, u32[]{:S(2)}) collective-permute-start(bf16[512,256]{1,0:T(8,128)(2,1)S(1)} %get-tuple-element.158), channel_id=1, source_target_pairs={{0,1},{1,0},{2,3},{3,2},{4,5},{5,4},{6,7},{7,6},{8,9},{9,8},{10,11... | collective-permute-start | bytes 786440 | tf_op jit(solution)/shard_map/ppermute | solution.py:415
  32.5 3.9 %collective-permute-start.11 = (bf16[1,512,256]{2,1,0:T(8,128)(2,1)S(1)}, bf16[1,512,256]{2,1,0:T(8,128)(2,1)S(1)}, u32[]{:S(2)}, u32[]{:S(2)}) collective-permute-start(bf16[1,512,256]{2,1,0:T(8,128)(2,1)S(1)} %collective-permute-done.4.rest_4_), channel_id=1, source_target_pairs={{0,4},{2,6},{8,12},{10,14},{16,20},{18,22},{24,28},{26,30},{1,5},{... | collective-permute-start | bytes 786440 | tf_op jit(solution)/shard_map/ppermute | solution.py:399
  36.3 0.0 collective-permute-done.8.rest_3_
  36.3 1.9 %collective-permute-start.15 = (bf16[1,528,256]{2,1,0:T(8,128)(2,1)S(1)}, bf16[1,528,256]{2,1,0:T(8,128)(2,1)S(1)}, u32[]{:S(2)}, u32[]{:S(2)}) collective-permute-start(bf16[1,528,256]{2,1,0:T(8,128)(2,1)S(1)} %collective-permute-done.8.rest_3_), channel_id=1, source_target_pairs={{0,4},{2,6},{4,0},{6,2},{8,12},{10,14},{12,8},{14,10},{16,20},{18,... | collective-permute-start | bytes 811016 | tf_op jit(solution)/shard_map/ppermute | solution.py:399
  38.2 0.0 collective-permute-done.10.rest_6_
  38.2 1.3 %collective-permute-start.14 = (bf16[1,528,256]{2,1,0:T(8,128)(2,1)S(1)}, bf16[1,528,256]{2,1,0:T(8,128)(2,1)S(1)}, u32[]{:S(2)}, u32[]{:S(2)}) collective-permute-start(bf16[1,528,256]{2,1,0:T(8,128)(2,1)S(1)} %collective-permute-done.8.rest_3_), channel_id=1, source_target_pairs={{8,0},{10,2},{12,4},{14,6},{16,8},{18,10},{20,12},{22,14},{24,16},... | collective-permute-start | bytes 811016 | tf_op jit(solution)/shard_map/ppermute | solution.py:393
  39.5 1.1 %collective-permute-done.9.rest_4_ = bf16[1,512,256]{2,1,0:T(8,128)(2,1)S(1)} collective-permute-done((bf16[1,512,256]{2,1,0:T(8,128)(2,1)S(1)}, bf16[1,512,256]{2,1,0:T(8,128)(2,1)S(1)}, u32[]{:S(2)}, u32[]{:S(2)}) %collective-permute-start.9) | collective-permute-done | bytes 262176 | tf_op jit(solution)/shard_map/ppermute | solution.py:393
  40.6 1.3 %collective-permute-start.18 = (bf16[1024,256]{1,0:T(8,128)(2,1)S(1)}, bf16[1024,256]{1,0:T(8,128)(2,1)S(1)}, u32[]{:S(2)}, u32[]{:S(2)}) collective-permute-start(bf16[1024,256]{1,0:T(8,128)(2,1)S(1)} %get-tuple-element.188), channel_id=1, source_target_pairs={{4,1},{5,0},{6,3},{7,2},{12,9},{13,8},{14,11},{15,10},{20,17},{21,... | collective-permute-start | bytes 1572872 | tf_op jit(solution)/shard_map/ppermute | solution.py:415
  41.9 0.0 collective-permute-done.7
  41.9 5.7 %collective-permute-start.13 = (bf16[1,512,256]{2,1,0:T(8,128)(2,1)S(1)}, bf16[1,512,256]{2,1,0:T(8,128)(2,1)S(1)}, u32[]{:S(2)}, u32[]{:S(2)}) collective-permute-start(bf16[1,512,256]{2,1,0:T(8,128)(2,1)S(1)} %collective-permute-done.9.rest_4_), channel_id=1, source_target_pairs={{0,4},{2,6},{8,12},{10,14},{16,20},{18,22},{24,28},{26,30},{1,5},{... | collective-permute-start | bytes 786440 | tf_op jit(solution)/shard_map/ppermute | solution.py:399
  47.6 0.0 collective-permute-done.11.rest_8_
  47.6 1.3 %collective-permute-start.12 = (bf16[1,512,256]{2,1,0:T(8,128)(2,1)S(1)}, bf16[1,512,256]{2,1,0:T(8,128)(2,1)S(1)}, u32[]{:S(2)}, u32[]{:S(2)}) collective-permute-start(bf16[1,512,256]{2,1,0:T(8,128)(2,1)S(1)} %bitcast.23), channel_id=1, source_target_pairs={{8,0},{10,2},{12,4},{14,6},{16,8},{18,10},{20,12},{22,14},{24,16},... | collective-permute-start | bytes 786440 | tf_op jit(solution)/shard_map/ppermute | solution.py:393
  49.0 0.0 collective-permute-done.15.rest_7_
  49.0 0.0 collective-permute-done.14.rest_5_
  49.0 1.7 %collective-permute-start.17 = (bf16[1,528,256]{2,1,0:T(8,128)(2,1)S(1)}, bf16[1,528,256]{2,1,0:T(8,128)(2,1)S(1)}, u32[]{:S(2)}, u32[]{:S(2)}) collective-permute-start(bf16[1,528,256]{2,1,0:T(8,128)(2,1)S(1)} %collective-permute-done.14.rest_5_), channel_id=1, source_target_pairs={{0,4},{2,6},{8,12},{10,14},{16,20},{18,22},{24,28},{26,30},{1,5},{... | collective-permute-start | bytes 811016 | tf_op jit(solution)/shard_map/ppermute | solution.py:399
  50.7 3.6 %collective-permute-done.13.rest_8_ = bf16[1,512,256]{2,1,0:T(8,128)(2,1)S(1)} collective-permute-done((bf16[1,512,256]{2,1,0:T(8,128)(2,1)S(1)}, bf16[1,512,256]{2,1,0:T(8,128)(2,1)S(1)}, u32[]{:S(2)}, u32[]{:S(2)}) %collective-permute-start.13) | collective-permute-done | bytes 262176 | tf_op jit(solution)/shard_map/ppermute | solution.py:399
  54.4 2.1 %collective-permute-done.12.rest_3_ = bf16[1,512,256]{2,1,0:T(8,128)(2,1)S(1)} collective-permute-done((bf16[1,512,256]{2,1,0:T(8,128)(2,1)S(1)}, bf16[1,512,256]{2,1,0:T(8,128)(2,1)S(1)}, u32[]{:S(2)}, u32[]{:S(2)}) %collective-permute-start.12) | collective-permute-done | bytes 262176 | tf_op jit(solution)/shard_map/ppermute | solution.py:393
  56.5 1.3 %collective-permute-start.16 = (bf16[1,512,256]{2,1,0:T(8,128)(2,1)S(1)}, bf16[1,512,256]{2,1,0:T(8,128)(2,1)S(1)}, u32[]{:S(2)}, u32[]{:S(2)}) collective-permute-start(bf16[1,512,256]{2,1,0:T(8,128)(2,1)S(1)} %collective-permute-done.12.rest_3_), channel_id=1, source_target_pairs={{8,0},{10,2},{12,4},{14,6},{16,8},{18,10},{20,12},{22,14},{24,16},... | collective-permute-start | bytes 786440 | tf_op jit(solution)/shard_map/ppermute | solution.py:393
  57.8 0.4 collective-permute-start.20
  58.2 0.0 collective-permute-done.18
  58.2 1.9 %collective-permute-done.17.rest_9_ = bf16[1,528,256]{2,1,0:T(8,128)(2,1)S(1)} collective-permute-done((bf16[1,528,256]{2,1,0:T(8,128)(2,1)S(1)}, bf16[1,528,256]{2,1,0:T(8,128)(2,1)S(1)}, u32[]{:S(2)}, u32[]{:S(2)}) %collective-permute-start.17) | collective-permute-done | bytes 270368 | tf_op jit(solution)/shard_map/ppermute | solution.py:399
  60.2 2.5 %shard_map.46 = (f32[8,128,1024]{2,1,0:T(8,128)}, f32[2,128,512]{2,1,0:T(8,128)S(1)}) custom-call(s32[3]{0:T(128)S(1)} %pad_add_fusion.place_ref, f32[16,128]{1,0:T(8,128)S(1)} %get-tuple-element.225.counts_ref.value_ref, bf16[1,528,256]{2,1,0:T(8,128)(2,1)S(1)} %bitcast.10, bf16[1,512,256]{2,1,0:T(8,128)(2,1)S(1)} %bitcast.27, ...), custom_call_target="tpu_custom_call" | custom-call | tf_op jit(solution)/shard_map/pallas_call | solution.py:315
  62.7 2.1 %collective-permute-done.16.rest_5_ = bf16[1,512,256]{2,1,0:T(8,128)(2,1)S(1)} collective-permute-done((bf16[1,512,256]{2,1,0:T(8,128)(2,1)S(1)}, bf16[1,512,256]{2,1,0:T(8,128)(2,1)S(1)}, u32[]{:S(2)}, u32[]{:S(2)}) %collective-permute-start.16) | collective-permute-done | bytes 262176 | tf_op jit(solution)/shard_map/ppermute | solution.py:393
  64.8 2.4 %collective-permute-start.19 = (bf16[1,512,256]{2,1,0:T(8,128)(2,1)S(1)}, bf16[1,512,256]{2,1,0:T(8,128)(2,1)S(1)}, u32[]{:S(2)}, u32[]{:S(2)}) collective-permute-start(bf16[1,512,256]{2,1,0:T(8,128)(2,1)S(1)} %collective-permute-done.16.rest_5_), channel_id=1, source_target_pairs={{0,4},{2,6},{8,12},{10,14},{16,20},{18,22},{24,28},{26,30},{1,5},{... | collective-permute-start | bytes 786440 | tf_op jit(solution)/shard_map/ppermute | solution.py:399
  67.1 0.0 collective-permute-done.20.rest_7_
  67.1 2.5 %shard_map.48 = (f32[8,128,1024]{2,1,0:T(8,128)}, f32[2,128,512]{2,1,0:T(8,128)S(1)}) custom-call(s32[3]{0:T(128)S(1)} %pad_add_fusion.place_ref, f32[16,128]{1,0:T(8,128)S(1)} %get-tuple-element.225.counts_ref.value_ref, bf16[1,528,256]{2,1,0:T(8,128)(2,1)S(1)} %bitcast.12, bf16[1,512,256]{2,1,0:T(8,128)(2,1)S(1)} %bitcast.21, ...), custom_call_target="tpu_custom_call", output_to_operand_aliasing={{0}: (11, {})} | custom-call | tf_op jit(solution)/shard_map/pallas_call | solution.py:315
  69.7 2.5 %shard_map.50 = (f32[8,128,1024]{2,1,0:T(8,128)}, f32[2,128,512]{2,1,0:T(8,128)S(1)}) custom-call(s32[3]{0:T(128)S(1)} %pad_add_fusion.place_ref, f32[16,128]{1,0:T(8,128)S(1)} %get-tuple-element.225.counts_ref.value_ref, bf16[1,528,256]{2,1,0:T(8,128)(2,1)S(1)} %bitcast.13, bf16[1,512,256]{2,1,0:T(8,128)(2,1)S(1)} %bitcast.28, ...), custom_call_target="tpu_custom_call", output_to_operand_aliasing={{0}: (13, {})} | custom-call | tf_op jit(solution)/shard_map/pallas_call | solution.py:315
  72.2 0.1 collective-permute-start.24
  72.3 0.5 collective-permute-start.23
  72.8 0.1 collective-permute-start.22
  72.9 0.0 collective-permute-done.19.rest_9_
  72.9 2.5 %shard_map.51 = (f32[8,128,1024]{2,1,0:T(8,128)}, f32[2,128,512]{2,1,0:T(8,128)S(1)}) custom-call(s32[3]{0:T(128)S(1)} %pad_add_fusion.place_ref, f32[16,128]{1,0:T(8,128)S(1)} %get-tuple-element.225.counts_ref.value_ref, bf16[1,528,256]{2,1,0:T(8,128)(2,1)S(1)} %bitcast.15, bf16[1,512,256]{2,1,0:T(8,128)(2,1)S(1)} %bitcast.22, ...), custom_call_target="tpu_custom_call", output_to_operand_aliasing={{0}: (13, {})} | custom-call | tf_op jit(solution)/shard_map/pallas_call | solution.py:315
  75.4 0.5 collective-permute-start.21
  75.9 0.0 collective-permute-done.24.rest_2_
  75.9 0.0 collective-permute-done.23.rest_1_
  75.9 0.0 collective-permute-done.22.rest_0_
  75.9 1.7 %shard_map.52.rest_2_ = f32[8,128,1024]{2,1,0:T(8,128)} custom-call(s32[3]{0:T(128)S(1)} %pad_add_fusion.place_ref, f32[2,128,512]{2,1,0:T(8,128)S(1)} %collective-permute-done.22.rest_0_, f32[2,128,512]{2,1,0:T(8,128)S(1)} %collective-permute-done.23.rest_1_, f32[2,128,512]{2,1,0:T(8,128)S(1)} %collective-permute-done.24.rest_2_, ...), custom_call_target="tpu_custom_call", output_to_operand_aliasing={{}: (5, {})} | custom-call | bytes 3145728 | tf_op jit(solution)/shard_map/pallas_call | solution.py:363
  77.6 0.0 collective-permute-done.21.rest_0_
  77.6 1.4 %shard_map.53 = f32[8,128,1024]{2,1,0:T(8,128)} custom-call(s32[3]{0:T(128)S(1)} %pad_add_fusion.place_ref, f32[2,128,512]{2,1,0:T(8,128)S(1)} %collective-permute-done.21.rest_0_, f32[16,128]{1,0:T(8,128)S(1)} %shard_map.49.rest_3_.rest_1_, f32[8,128,1024]{2,1,0:T(8,128)} %shard_map.52.rest_2_), custom_call_target="tpu_custom_call", output_to_operand_aliasing={{}: (3, {})} | custom-call | bytes 1048576 | tf_op jit(solution)/shard_map/pallas_call | solution.py:363
  (8 shorter events, 0.0 us)
Async XLA Ops:
  0.0 3.0 %collective-permute-start = (bf16[128,4096]{1,0:T(8,128)(2,1)}, bf16[128,4096]{1,0:T(8,128)(2,1)S(1)}, u32[]{:S(2)}, u32[]{:S(2)}) collective-permute-start(bf16[128,4096]{1,0:T(8,128)(2,1)} %frames_hbm.1), channel_id=1, source_target_pairs={{0,2},{2,0},{4,6},{6,4},{8,10},{10,8},{12,14},{14,12},{16,18},{18,... | collective-permute-start | bytes 3145736 | tf_op jit(solution)/shard_map/ppermute | solution.py:404
  6.0 11.5 %collective-permute-start.1 = (bf16[1,512,256]{2,1,0:T(8,128)(2,1)S(1)}, bf16[1,512,256]{2,1,0:T(8,128)(2,1)S(1)}, u32[]{:S(2)}, u32[]{:S(2)}) collective-permute-start(bf16[1,512,256]{2,1,0:T(8,128)(2,1)S(1)} %bitcast.26), channel_id=1, source_target_pairs={{8,0},{10,2},{12,4},{14,6},{16,8},{18,10},{20,12},{22,14},{24,16},... | collective-permute-start | bytes 786440 | tf_op jit(solution)/shard_map/ppermute | solution.py:393
  7.3 16.8 %collective-permute-start.5 = (bf16[1024,256]{1,0:T(8,128)(2,1)S(1)}, bf16[1024,256]{1,0:T(8,128)(2,1)S(1)}, u32[]{:S(2)}, u32[]{:S(2)}) collective-permute-start(bf16[1024,256]{1,0:T(8,128)(2,1)S(1)} %get-tuple-element.148), channel_id=1, source_target_pairs={{4,0},{6,2},{12,8},{14,10},{20,16},{22,18},{28,24},{30,26},{5,1},{... | collective-permute-start | bytes 1572872 | tf_op jit(solution)/shard_map/ppermute | solution.py:399
  11.5 12.6 %collective-permute-start.3 = (bf16[1,512,256]{2,1,0:T(8,128)(2,1)S(1)}, bf16[1,512,256]{2,1,0:T(8,128)(2,1)S(1)}, u32[]{:S(2)}, u32[]{:S(2)}) collective-permute-start(bf16[1,512,256]{2,1,0:T(8,128)(2,1)S(1)} %bitcast.20), channel_id=1, source_target_pairs={{8,0},{10,2},{12,4},{14,6},{16,8},{18,10},{20,12},{22,14},{24,16},... | collective-permute-start | bytes 786440 | tf_op jit(solution)/shard_map/ppermute | solution.py:393
  12.8 9.7 %collective-permute-start.6 = (bf16[528,256]{1,0:T(8,128)(2,1)S(1)}, bf16[528,256]{1,0:T(8,128)(2,1)S(1)}, u32[]{:S(2)}, u32[]{:S(2)}) collective-permute-start(bf16[528,256]{1,0:T(8,128)(2,1)S(1)} %get-tuple-element.149), channel_id=1, source_target_pairs={{0,1},{1,0},{2,3},{3,2},{4,5},{5,4},{6,7},{7,6},{8,9},{9,8},{10,11... | collective-permute-start | bytes 811016 | tf_op jit(solution)/shard_map/ppermute | solution.py:415
  17.5 12.2 %collective-permute-start.4 = (bf16[1,512,256]{2,1,0:T(8,128)(2,1)S(1)}, bf16[1,512,256]{2,1,0:T(8,128)(2,1)S(1)}, u32[]{:S(2)}, u32[]{:S(2)}) collective-permute-start(bf16[1,512,256]{2,1,0:T(8,128)(2,1)S(1)} %collective-permute-done.1.rest_2_), channel_id=1, source_target_pairs={{8,0},{10,2},{12,4},{14,6},{16,8},{18,10},{20,12},{22,14},{24,16},... | collective-permute-start | bytes 786440 | tf_op jit(solution)/shard_map/ppermute | solution.py:393
  18.8 11.0 %collective-permute-start.2 = (bf16[1,512,256]{2,1,0:T(8,128)(2,1)S(1)}, bf16[1,512,256]{2,1,0:T(8,128)(2,1)S(1)}, u32[]{:S(2)}, u32[]{:S(2)}) collective-permute-start(bf16[1,512,256]{2,1,0:T(8,128)(2,1)S(1)} %collective-permute-done.1.rest_2_), channel_id=1, source_target_pairs={{0,4},{2,6},{4,0},{6,2},{8,12},{10,14},{12,8},{14,10},{16,20},{18,... | collective-permute-start | bytes 786440 | tf_op jit(solution)/shard_map/ppermute | solution.py:399
  22.6 13.8 %collective-permute-start.8 = (bf16[1,528,256]{2,1,0:T(8,128)(2,1)S(1)}, bf16[1,528,256]{2,1,0:T(8,128)(2,1)S(1)}, u32[]{:S(2)}, u32[]{:S(2)}) collective-permute-start(bf16[1,528,256]{2,1,0:T(8,128)(2,1)S(1)} %bitcast.9), channel_id=1, source_target_pairs={{8,0},{10,2},{12,4},{14,6},{16,8},{18,10},{20,12},{22,14},{24,16},... | collective-permute-start | bytes 811016 | tf_op jit(solution)/shard_map/ppermute | solution.py:393
  24.2 14.1 %collective-permute-start.10 = (bf16[1,512,256]{2,1,0:T(8,128)(2,1)S(1)}, bf16[1,512,256]{2,1,0:T(8,128)(2,1)S(1)}, u32[]{:S(2)}, u32[]{:S(2)}) collective-permute-start(bf16[1,512,256]{2,1,0:T(8,128)(2,1)S(1)} %collective-permute-done.3.rest_2_), channel_id=1, source_target_pairs={{0,4},{2,6},{4,0},{6,2},{8,12},{10,14},{12,8},{14,10},{16,20},{18,... | collective-permute-start | bytes 786440 | tf_op jit(solution)/shard_map/ppermute | solution.py:399
  26.8 13.8 %collective-permute-start.9 = (bf16[1,512,256]{2,1,0:T(8,128)(2,1)S(1)}, bf16[1,512,256]{2,1,0:T(8,128)(2,1)S(1)}, u32[]{:S(2)}, u32[]{:S(2)}) collective-permute-start(bf16[1,512,256]{2,1,0:T(8,128)(2,1)S(1)} %collective-permute-done.3.rest_2_), channel_id=1, source_target_pairs={{8,0},{10,2},{12,4},{14,6},{16,8},{18,10},{20,12},{22,14},{24,16},... | collective-permute-start | bytes 786440 | tf_op jit(solution)/shard_map/ppermute | solution.py:393
  29.8 12.1 %collective-permute-start.7 = (bf16[512,256]{1,0:T(8,128)(2,1)S(1)}, bf16[512,256]{1,0:T(8,128)(2,1)S(1)}, u32[]{:S(2)}, u32[]{:S(2)}) collective-permute-start(bf16[512,256]{1,0:T(8,128)(2,1)S(1)} %get-tuple-element.158), channel_id=1, source_target_pairs={{0,1},{1,0},{2,3},{3,2},{4,5},{5,4},{6,7},{7,6},{8,9},{9,8},{10,11... | collective-permute-start | bytes 786440 | tf_op jit(solution)/shard_map/ppermute | solution.py:415
  32.5 15.2 %collective-permute-start.11 = (bf16[1,512,256]{2,1,0:T(8,128)(2,1)S(1)}, bf16[1,512,256]{2,1,0:T(8,128)(2,1)S(1)}, u32[]{:S(2)}, u32[]{:S(2)}) collective-permute-start(bf16[1,512,256]{2,1,0:T(8,128)(2,1)S(1)} %collective-permute-done.4.rest_4_), channel_id=1, source_target_pairs={{0,4},{2,6},{8,12},{10,14},{16,20},{18,22},{24,28},{26,30},{1,5},{... | collective-permute-start | bytes 786440 | tf_op jit(solution)/shard_map/ppermute | solution.py:399
  36.3 12.6 %collective-permute-start.15 = (bf16[1,528,256]{2,1,0:T(8,128)(2,1)S(1)}, bf16[1,528,256]{2,1,0:T(8,128)(2,1)S(1)}, u32[]{:S(2)}, u32[]{:S(2)}) collective-permute-start(bf16[1,528,256]{2,1,0:T(8,128)(2,1)S(1)} %collective-permute-done.8.rest_3_), channel_id=1, source_target_pairs={{0,4},{2,6},{4,0},{6,2},{8,12},{10,14},{12,8},{14,10},{16,20},{18,... | collective-permute-start | bytes 811016 | tf_op jit(solution)/shard_map/ppermute | solution.py:399
  38.2 10.8 %collective-permute-start.14 = (bf16[1,528,256]{2,1,0:T(8,128)(2,1)S(1)}, bf16[1,528,256]{2,1,0:T(8,128)(2,1)S(1)}, u32[]{:S(2)}, u32[]{:S(2)}) collective-permute-start(bf16[1,528,256]{2,1,0:T(8,128)(2,1)S(1)} %collective-permute-done.8.rest_3_), channel_id=1, source_target_pairs={{8,0},{10,2},{12,4},{14,6},{16,8},{18,10},{20,12},{22,14},{24,16},... | collective-permute-start | bytes 811016 | tf_op jit(solution)/shard_map/ppermute | solution.py:393
  40.6 17.6 %collective-permute-start.18 = (bf16[1024,256]{1,0:T(8,128)(2,1)S(1)}, bf16[1024,256]{1,0:T(8,128)(2,1)S(1)}, u32[]{:S(2)}, u32[]{:S(2)}) collective-permute-start(bf16[1024,256]{1,0:T(8,128)(2,1)S(1)} %get-tuple-element.188), channel_id=1, source_target_pairs={{4,1},{5,0},{6,3},{7,2},{12,9},{13,8},{14,11},{15,10},{20,17},{21,... | collective-permute-start | bytes 1572872 | tf_op jit(solution)/shard_map/ppermute | solution.py:415
  41.9 12.4 %collective-permute-start.13 = (bf16[1,512,256]{2,1,0:T(8,128)(2,1)S(1)}, bf16[1,512,256]{2,1,0:T(8,128)(2,1)S(1)}, u32[]{:S(2)}, u32[]{:S(2)}) collective-permute-start(bf16[1,512,256]{2,1,0:T(8,128)(2,1)S(1)} %collective-permute-done.9.rest_4_), channel_id=1, source_target_pairs={{0,4},{2,6},{8,12},{10,14},{16,20},{18,22},{24,28},{26,30},{1,5},{... | collective-permute-start | bytes 786440 | tf_op jit(solution)/shard_map/ppermute | solution.py:399
  47.6 8.8 %collective-permute-start.12 = (bf16[1,512,256]{2,1,0:T(8,128)(2,1)S(1)}, bf16[1,512,256]{2,1,0:T(8,128)(2,1)S(1)}, u32[]{:S(2)}, u32[]{:S(2)}) collective-permute-start(bf16[1,512,256]{2,1,0:T(8,128)(2,1)S(1)} %bitcast.23), channel_id=1, source_target_pairs={{8,0},{10,2},{12,4},{14,6},{16,8},{18,10},{20,12},{22,14},{24,16},... | collective-permute-start | bytes 786440 | tf_op jit(solution)/shard_map/ppermute | solution.py:393
  49.0 11.1 %collective-permute-start.17 = (bf16[1,528,256]{2,1,0:T(8,128)(2,1)S(1)}, bf16[1,528,256]{2,1,0:T(8,128)(2,1)S(1)}, u32[]{:S(2)}, u32[]{:S(2)}) collective-permute-start(bf16[1,528,256]{2,1,0:T(8,128)(2,1)S(1)} %collective-permute-done.14.rest_5_), channel_id=1, source_target_pairs={{0,4},{2,6},{8,12},{10,14},{16,20},{18,22},{24,28},{26,30},{1,5},{... | collective-permute-start | bytes 811016 | tf_op jit(solution)/shard_map/ppermute | solution.py:399
  56.5 8.3 %collective-permute-start.16 = (bf16[1,512,256]{2,1,0:T(8,128)(2,1)S(1)}, bf16[1,512,256]{2,1,0:T(8,128)(2,1)S(1)}, u32[]{:S(2)}, u32[]{:S(2)}) collective-permute-start(bf16[1,512,256]{2,1,0:T(8,128)(2,1)S(1)} %collective-permute-done.12.rest_3_), channel_id=1, source_target_pairs={{8,0},{10,2},{12,4},{14,6},{16,8},{18,10},{20,12},{22,14},{24,16},... | collective-permute-start | bytes 786440 | tf_op jit(solution)/shard_map/ppermute | solution.py:393
  57.8 9.3 %collective-permute-start.20 = (bf16[1,512,256]{2,1,0:T(8,128)(2,1)S(1)}, bf16[1,512,256]{2,1,0:T(8,128)(2,1)S(1)}, u32[]{:S(2)}, u32[]{:S(2)}) collective-permute-start(bf16[1,512,256]{2,1,0:T(8,128)(2,1)S(1)} %collective-permute-done.12.rest_3_), channel_id=1, source_target_pairs={{0,4},{2,6},{4,0},{6,2},{8,12},{10,14},{12,8},{14,10},{16,20},{18,... | collective-permute-start | bytes 786440 | tf_op jit(solution)/shard_map/ppermute | solution.py:399
  64.8 8.1 %collective-permute-start.19 = (bf16[1,512,256]{2,1,0:T(8,128)(2,1)S(1)}, bf16[1,512,256]{2,1,0:T(8,128)(2,1)S(1)}, u32[]{:S(2)}, u32[]{:S(2)}) collective-permute-start(bf16[1,512,256]{2,1,0:T(8,128)(2,1)S(1)} %collective-permute-done.16.rest_5_), channel_id=1, source_target_pairs={{0,4},{2,6},{8,12},{10,14},{16,20},{18,22},{24,28},{26,30},{1,5},{... | collective-permute-start | bytes 786440 | tf_op jit(solution)/shard_map/ppermute | solution.py:399
  72.2 3.7 %collective-permute-start.24 = (f32[2,128,512]{2,1,0:T(8,128)S(1)}, f32[2,128,512]{2,1,0:T(8,128)S(1)}, u32[]{:S(2)}, u32[]{:S(2)}) collective-permute-start(f32[2,128,512]{2,1,0:T(8,128)S(1)} %get-tuple-element.237), channel_id=1, source_target_pairs={{0,2},{2,0},{4,6},{6,4},{8,10},{10,8},{12,14},{14,12},{16,18},{18,... | collective-permute-start | bytes 1572872 | tf_op jit(solution)/shard_map/ppermute | solution.py:404
  72.3 3.6 %collective-permute-start.23 = (f32[2,128,512]{2,1,0:T(8,128)S(1)}, f32[2,128,512]{2,1,0:T(8,128)S(1)}, u32[]{:S(2)}, u32[]{:S(2)}) collective-permute-start(f32[2,128,512]{2,1,0:T(8,128)S(1)} %get-tuple-element.236), channel_id=1, source_target_pairs={{0,2},{2,0},{4,6},{6,4},{8,10},{10,8},{12,14},{14,12},{16,18},{18,... | collective-permute-start | bytes 1572872 | tf_op jit(solution)/shard_map/ppermute | solution.py:404
  72.8 3.1 %collective-permute-start.22 = (f32[2,128,512]{2,1,0:T(8,128)S(1)}, f32[2,128,512]{2,1,0:T(8,128)S(1)}, u32[]{:S(2)}, u32[]{:S(2)}) collective-permute-start(f32[2,128,512]{2,1,0:T(8,128)S(1)} %get-tuple-element.235), channel_id=1, source_target_pairs={{0,2},{2,0},{4,6},{6,4},{8,10},{10,8},{12,14},{14,12},{16,18},{18,... | collective-permute-start | bytes 1572872 | tf_op jit(solution)/shard_map/ppermute | solution.py:404
  75.4 2.2 %collective-permute-start.21 = (f32[2,128,512]{2,1,0:T(8,128)S(1)}, f32[2,128,512]{2,1,0:T(8,128)S(1)}, u32[]{:S(2)}, u32[]{:S(2)}) collective-permute-start(f32[2,128,512]{2,1,0:T(8,128)S(1)} %get-tuple-element.233), channel_id=1, source_target_pairs={{0,2},{2,0},{4,6},{6,4},{8,10},{10,8},{12,14},{14,12},{16,18},{18,... | collective-permute-start | bytes 1572872 | tf_op jit(solution)/shard_map/ppermute | solution.py:404
